TPU v7x, 32 devices: a whole 2x2x4 slice. The times are simulated.
32 devices in a mesh: dp: 4 (over x, core), ctx: 2 (over y), fsdp: 4 (over z).
Axes of the slice: x: 2, y: 2, z: 4, core: 2. Of those that a mesh axis runs over, the one named last changes fastest.
Arguments:
- tokens: bfloat16 [4, 1536, 960], P('dp', ('ctx', 'fsdp')), may hold values from -6 to 6
- block_order: int32 [4, 4], P('dp'), may hold values from 0 to 3, each once within a row
- attention_gain: bfloat16 [960], P('fsdp'), may hold values from 0.5 to 1.5
- query_weight: bfloat16 [960, 960], P('fsdp'), may hold values from -0.1875 to 0.1875
- key_weight: bfloat16 [960, 320], P('fsdp'), may hold values from -0.1875 to 0.1875
- value_weight: bfloat16 [960, 320], P('fsdp'), may hold values from -0.1875 to 0.1875
- output_weight: bfloat16 [960, 960], P('fsdp'), may hold values from -1.5 to 1.5
- feedforward_gain: bfloat16 [960], P('fsdp'), may hold values from 0.5 to 1.5
- gate_weight: bfloat16 [960, 2560], P('fsdp'), may hold values from -0.1875 to 0.1875
- up_weight: bfloat16 [960, 2560], P('fsdp'), may hold values from -0.1875 to 0.1875
- down_weight: bfloat16 [2560, 960], P('fsdp'), may hold values from -0.125 to 0.125
- cotangent: bfloat16 [4, 1536, 960], P('dp', ('ctx', 'fsdp')), may hold values from -6 to 6
Outputs:
- result: float32 [4, 1536, 960], P('dp', ('ctx', 'fsdp'))
- input_grad: float32 [4, 1536, 960], P('dp', ('ctx', 'fsdp'))
- attention_gain_grad: float32 [960], P('fsdp')
- query_weight_grad: float32 [960, 960], P('fsdp')
- key_weight_grad: float32 [960, 320], P('fsdp')
- value_weight_grad: float32 [960, 320], P('fsdp')
- output_weight_grad: float32 [960, 960], P('fsdp')
- feedforward_gain_grad: float32 [960], P('fsdp')
- gate_weight_grad: float32 [960, 2560], P('fsdp')
- up_weight_grad: float32 [960, 2560], P('fsdp')
- down_weight_grad: float32 [2560, 960], P('fsdp')
Inputs may be any that keep to these rules, and one draw needn't show every extreme that they name: Each row is a permutation of the 4 blocks: stored block j of a sequence holds the tokens from block_order[j] * 384 on, in order.
All inputs are finite; a program needn't handle non-finite values.
Results may differ from a plain program's by a relative error of at most 0.02.
Values may be sent and summed in bfloat16 or wider, within the bound.
No kernel may reach another device: no remote copies, remote signals or barrier semaphores. Data moves between devices by JAX's collectives and lax.ppermute only.
A program may use at most 192 MiB of HBM per device.

v0:
```python
import math

import jax
import jax.numpy as jnp
from jax import lax
from jax.sharding import PartitionSpec as P

HEADS = 15
KV_HEADS = 5
HEAD_DIM = 64


EPSILON = 1e-05
ROPE_BASE = 100000.0
MASKED = -1e30


def as_sent(x):

    def short(part):
        return part.astype(jnp.bfloat16) if part.dtype == jnp.float32 else part

    return jax.tree.map(short, x)


def from_behind(x, axis, by):
    count = lax.axis_size(axis)
    return lax.ppermute(x, axis, [(i, (i + by) % count) for i in range(count)])


def dot_plain(left, right):
    return jnp.dot(left, right, preferred_element_type=jnp.float32)


def dot_last(left, right):
    return lax.dot_general(
        left, right, (((1,), (1,)), ((), ())), preferred_element_type=jnp.float32
    )


def dot_first(left, right):
    return lax.dot_general(
        left, right, (((0,), (0,)), ((), ())), preferred_element_type=jnp.float32
    )


def norm_rows(values, gain):
    inverse = lax.rsqrt(jnp.mean(values * values, axis=-1, keepdims=True) + EPSILON)
    return (values * inverse * gain, inverse)


def norm_back(gradient, values, inverse, gain):
    scaled = gradient * gain
    inner_mean = jnp.mean(scaled * values, axis=-1, keepdims=True)
    return inverse * scaled - values * (inverse * inverse * inverse) * inner_mean


def rotation(positions):
    half_dim = HEAD_DIM // 2
    exponent = -(jnp.arange(half_dim, dtype=jnp.float32) * 2.0) / HEAD_DIM
    frequency = jnp.power(jnp.float32(ROPE_BASE), exponent)
    angles = positions.astype(jnp.float32)[..., None] * frequency
    cosine_half = jnp.cos(angles)
    sine_half = jnp.sin(angles)
    return (
        jnp.concatenate([cosine_half, cosine_half], axis=-1),
        jnp.concatenate([sine_half, sine_half], axis=-1),
    )


def rotate(values, cosine_table, sine_table):
    half_dim = values.shape[-1] // 2
    turned = jnp.concatenate([-values[..., half_dim:], values[..., :half_dim]], axis=-1)
    return values * cosine_table + turned * sine_table


def positions_of(block_order, offset, amount, block_length):
    stored = offset + jnp.arange(amount, dtype=jnp.int32)
    which_block = stored // block_length
    matches = (
        which_block[:, None] == jnp.arange(block_order.shape[1], dtype=jnp.int32)[None, :]
    ).astype(jnp.int32)
    chosen = jnp.sum(block_order[:, None, :] * matches[None, :, :], axis=-1)
    return chosen * block_length + stored % block_length


def on_device(
    tokens,
    block_order,
    attention_gain,
    query_weight,
    key_weight,
    value_weight,
    output_weight,
    feedforward_gain,
    gate_weight,
    up_weight,
    down_weight,
    cotangent,
):
    sequences, local_rows, model_width = tokens.shape
    shard_count = lax.axis_size("fsdp")
    cycle_count = lax.axis_size("ctx")
    block_rows = local_rows * shard_count
    block_length = block_rows * cycle_count // block_order.shape[1]
    groups = HEADS // KV_HEADS
    kv_width = KV_HEADS * HEAD_DIM
    score_scale = 1.0 / math.sqrt(HEAD_DIM)
    token_count = sequences * local_rows
    cycle_index = lax.axis_index("ctx")
    my_start = (cycle_index * shard_count + lax.axis_index("fsdp")) * local_rows
    gathered = (
        lax.all_gather(attention_gain, "fsdp", axis=0, tiled=True),
        lax.all_gather(query_weight, "fsdp", axis=0, tiled=True),
        lax.all_gather(key_weight, "fsdp", axis=0, tiled=True),
        lax.all_gather(value_weight, "fsdp", axis=0, tiled=True),
        lax.all_gather(output_weight, "fsdp", axis=0, tiled=True),
        lax.all_gather(feedforward_gain, "fsdp", axis=0, tiled=True),
        lax.all_gather(gate_weight, "fsdp", axis=0, tiled=True),
        lax.all_gather(up_weight, "fsdp", axis=0, tiled=True),
        lax.all_gather(down_weight, "fsdp", axis=0, tiled=True),
    )
    (
        first_gain,
        query_full,
        key_full,
        value_full,
        output_full,
        second_gain,
        gate_full,
        up_full,
        down_full,
    ) = gathered
    first_gain = first_gain.astype(jnp.float32)
    second_gain = second_gain.astype(jnp.float32)
    inputs = tokens.reshape(token_count, model_width).astype(jnp.float32)
    normed_one, inverse_one = norm_rows(inputs, first_gain)
    normed_one = normed_one.astype(jnp.bfloat16)
    query_pos = positions_of(block_order, my_start, local_rows, block_length)
    cosine_table, sine_table = rotation(query_pos)
    cosine_table = cosine_table[:, :, None, :]
    sine_table = sine_table[:, :, None, :]
    query_raw = dot_plain(normed_one, query_full).reshape(sequences, local_rows, HEADS, HEAD_DIM)
    queries = rotate(query_raw, cosine_table, sine_table).astype(jnp.bfloat16)
    queries = queries.reshape(sequences, local_rows, KV_HEADS, groups, HEAD_DIM)
    key_raw = dot_plain(normed_one, key_full).reshape(sequences, local_rows, KV_HEADS, HEAD_DIM)
    local_keys = (
        rotate(key_raw, cosine_table, sine_table)
        .astype(jnp.bfloat16)
        .reshape(sequences, local_rows, kv_width)
    )
    local_values = (
        dot_plain(normed_one, value_full)
        .astype(jnp.bfloat16)
        .reshape(sequences, local_rows, kv_width)
    )
    block_keys, block_values = (
        lax.all_gather(local_keys, "fsdp", axis=1, tiled=True),
        lax.all_gather(local_values, "fsdp", axis=1, tiled=True),
    )

    def scores_for(key_grid, offset):
        key_pos = positions_of(block_order, offset, key_grid.shape[1], block_length)
        scores = (
            jnp.einsum("stkgd,sukd->skgtu", queries, key_grid, preferred_element_type=jnp.float32)
            * score_scale
        )
        allowed = query_pos[:, None, None, :, None] >= key_pos[:, None, None, None, :]
        return (jnp.where(allowed, scores, MASKED), allowed)

    def key_slices(key_part, value_part, first_row, block_size):
        key_grid = lax.dynamic_slice_in_dim(key_part, first_row, block_size, 1)
        value_grid = lax.dynamic_slice_in_dim(value_part, first_row, block_size, 1)
        shape_grid = (sequences, block_size, KV_HEADS, HEAD_DIM)
        return (key_grid.reshape(shape_grid), value_grid.reshape(shape_grid))

    stat_shape = (sequences, KV_HEADS, groups, local_rows)
    head_shape = (sequences, local_rows, KV_HEADS, groups, HEAD_DIM)
    start_state = (
        jnp.full(stat_shape, MASKED, jnp.float32),
        jnp.zeros(stat_shape, jnp.float32),
        jnp.zeros(head_shape, jnp.float32),
    )
    key_part = lax.all_gather(block_keys, "ctx", axis=1, tiled=True)
    value_part = lax.all_gather(block_values, "ctx", axis=1, tiled=True)
    block_size = math.gcd(key_part.shape[1], 512)

    def attend_one_block(block_index, inner_state):
        running_max, running_sum, weighted_sum = inner_state
        first_row = block_index * block_size
        key_grid, value_grid = key_slices(key_part, value_part, first_row, block_size)
        scores, allowed = scores_for(key_grid, first_row)
        new_max = jnp.maximum(running_max, jnp.max(scores, axis=-1))
        weights = jnp.where(allowed, jnp.exp(scores - new_max[..., None]), 0.0)
        factor = jnp.exp(running_max - new_max)
        running_sum = running_sum * factor + jnp.sum(weights, axis=-1)
        update = jnp.einsum(
            "skgtu,sukd->stkgd",
            weights.astype(jnp.bfloat16),
            value_grid,
            preferred_element_type=jnp.float32,
        )
        weighted_sum = weighted_sum * jnp.transpose(factor, (0, 3, 1, 2))[..., None] + update
        return (new_max, running_sum, weighted_sum)

    running_max, running_sum, weighted_sum = lax.fori_loop(
        0, key_part.shape[1] // block_size, attend_one_block, start_state
    )
    log_total = running_max + jnp.log(running_sum)
    attended = weighted_sum / jnp.transpose(running_sum, (0, 3, 1, 2))[..., None]
    attended_low = attended.reshape(token_count, HEADS * HEAD_DIM).astype(jnp.bfloat16)
    residual = inputs + dot_plain(attended_low, output_full)
    normed_two, inverse_two = norm_rows(residual, second_gain)
    normed_two = normed_two.astype(jnp.bfloat16)
    gate_value = dot_plain(normed_two, gate_full)
    upward = dot_plain(normed_two, up_full)
    sigmoid_gate = jax.nn.sigmoid(gate_value)
    activated = (gate_value * sigmoid_gate * upward).astype(jnp.bfloat16)
    result = residual + dot_plain(activated, down_full)
    upstream = cotangent.reshape(token_count, model_width)
    act_grad = dot_last(upstream, down_full)
    down_weight_grad = dot_first(activated, upstream)
    gate_grad = (
        act_grad * upward * sigmoid_gate * (1.0 + gate_value * (1.0 - sigmoid_gate))
    ).astype(jnp.bfloat16)
    up_grad = (act_grad * gate_value * sigmoid_gate).astype(jnp.bfloat16)
    normed_two_grad = dot_last(gate_grad, gate_full) + dot_last(up_grad, up_full)
    gate_weight_grad = dot_first(normed_two, gate_grad)
    up_weight_grad = dot_first(normed_two, up_grad)
    second_gain_grad = jnp.sum(normed_two_grad * residual * inverse_two, axis=0)
    residual_grad = upstream.astype(jnp.float32) + norm_back(
        normed_two_grad, residual, inverse_two, second_gain
    )
    residual_low = residual_grad.astype(jnp.bfloat16)
    output_weight_grad = dot_first(attended_low, residual_low)
    attended_grad = dot_last(residual_low, output_full).astype(jnp.bfloat16).reshape(head_shape)
    row_delta = jnp.transpose(
        jnp.sum(attended_grad.astype(jnp.float32) * attended, axis=-1), (0, 2, 3, 1)
    )

    def back_piece(query_grad, key_part, value_part, offset):
        piece_rows = key_part.shape[1]
        block_size = math.gcd(piece_rows, 512)

        def back_one_block(block_index, inner_state):
            query_sum, key_grads, value_grads = inner_state
            first_row = block_index * block_size
            key_grid, value_grid = key_slices(key_part, value_part, first_row, block_size)
            scores, allowed = scores_for(key_grid, offset + first_row)
            probabilities = jnp.where(allowed, jnp.exp(scores - log_total[..., None]), 0.0)
            value_delta = jnp.einsum(
                "skgtu,stkgd->sukd",
                probabilities.astype(jnp.bfloat16),
                attended_grad,
                preferred_element_type=jnp.float32,
            )
            prob_grad = jnp.einsum(
                "stkgd,sukd->skgtu", attended_grad, value_grid, preferred_element_type=jnp.float32
            )
            score_grad = (probabilities * (prob_grad - row_delta[..., None])).astype(jnp.bfloat16)
            query_sum = (
                query_sum
                + jnp.einsum(
                    "skgtu,sukd->stkgd", score_grad, key_grid, preferred_element_type=jnp.float32
                )
                * score_scale
            )
            key_delta = (
                jnp.einsum(
                    "skgtu,stkgd->sukd", score_grad, queries, preferred_element_type=jnp.float32
                )
                * score_scale
            )
            key_grads = lax.dynamic_update_slice_in_dim(
                key_grads, key_delta.reshape(sequences, block_size, kv_width), first_row, 1
            )
            value_grads = lax.dynamic_update_slice_in_dim(
                value_grads, value_delta.reshape(sequences, block_size, kv_width), first_row, 1
            )
            return (query_sum, key_grads, value_grads)

        empty_grads = jnp.zeros((sequences, piece_rows, kv_width), jnp.float32)
        return lax.fori_loop(
            0, piece_rows // block_size, back_one_block, (query_grad, empty_grads, empty_grads)
        )

    query_start = jnp.zeros(head_shape, jnp.float32)

    def pass_grads(grad_pair):
        return jax.tree.map(
            lambda part, own: part.astype(own.dtype),
            from_behind(as_sent(grad_pair), "ctx", 1),
            grad_pair,
        )

    def visit(turn_index, query_grad, key_block, value_block, key_acc, value_acc):
        owner_index = (cycle_index - turn_index + cycle_count) % cycle_count
        query_grad, key_delta, value_delta = back_piece(
            query_grad, key_block, value_block, owner_index * block_rows
        )
        key_acc, value_acc = pass_grads((key_acc + key_delta, value_acc + value_delta))
        return (query_grad, key_acc, value_acc)

    def cycle_turn(turn_index, carry_state):
        query_grad, key_block, value_block, key_acc, value_acc = carry_state
        query_grad, key_acc, value_acc = visit(
            turn_index, query_grad, key_block, value_block, key_acc, value_acc
        )
        key_block, value_block = from_behind((key_block, value_block), "ctx", 1)
        return (query_grad, key_block, value_block, key_acc, value_acc)

    zero_block = jnp.zeros((sequences, block_rows, kv_width), jnp.float32)
    final_state = lax.fori_loop(
        0,
        cycle_count - 1,
        cycle_turn,
        (query_start, block_keys, block_values, zero_block, zero_block),
    )
    query_grad, key_block, value_block, key_acc, value_acc = final_state
    query_grad, key_acc, value_acc = visit(
        cycle_count - 1, query_grad, key_block, value_block, key_acc, value_acc
    )
    key_grad, value_grad = (
        lax.psum_scatter(
            key_acc.astype(jnp.bfloat16), "fsdp", scatter_dimension=1, tiled=True
        ).astype(jnp.float32),
        lax.psum_scatter(
            value_acc.astype(jnp.bfloat16), "fsdp", scatter_dimension=1, tiled=True
        ).astype(jnp.float32),
    )
    query_grad = query_grad.reshape(sequences, local_rows, HEADS, HEAD_DIM)
    query_low = (
        rotate(query_grad, cosine_table, -sine_table)
        .astype(jnp.bfloat16)
        .reshape(token_count, HEADS * HEAD_DIM)
    )
    key_grad = key_grad.reshape(sequences, local_rows, KV_HEADS, HEAD_DIM)
    key_low = (
        rotate(key_grad, cosine_table, -sine_table)
        .astype(jnp.bfloat16)
        .reshape(token_count, kv_width)
    )
    value_low = value_grad.astype(jnp.bfloat16).reshape(token_count, kv_width)
    normed_one_grad = (
        dot_last(query_low, query_full)
        + dot_last(key_low, key_full)
        + dot_last(value_low, value_full)
    )
    query_weight_grad = dot_first(normed_one, query_low)
    key_weight_grad = dot_first(normed_one, key_low)
    value_weight_grad = dot_first(normed_one, value_low)
    first_gain_grad = jnp.sum(normed_one_grad * inputs * inverse_one, axis=0)
    input_grad = residual_grad + norm_back(normed_one_grad, inputs, inverse_one, first_gain)
    shares = (
        lax.psum_scatter(
            first_gain_grad.astype(jnp.bfloat16), "fsdp", scatter_dimension=0, tiled=True
        ).astype(jnp.float32),
        lax.psum_scatter(
            query_weight_grad.astype(jnp.bfloat16), "fsdp", scatter_dimension=0, tiled=True
        ).astype(jnp.float32),
        lax.psum_scatter(
            key_weight_grad.astype(jnp.bfloat16), "fsdp", scatter_dimension=0, tiled=True
        ).astype(jnp.float32),
        lax.psum_scatter(
            value_weight_grad.astype(jnp.bfloat16), "fsdp", scatter_dimension=0, tiled=True
        ).astype(jnp.float32),
        lax.psum_scatter(
            output_weight_grad.astype(jnp.bfloat16), "fsdp", scatter_dimension=0, tiled=True
        ).astype(jnp.float32),
        lax.psum_scatter(
            second_gain_grad.astype(jnp.bfloat16), "fsdp", scatter_dimension=0, tiled=True
        ).astype(jnp.float32),
        lax.psum_scatter(
            gate_weight_grad.astype(jnp.bfloat16), "fsdp", scatter_dimension=0, tiled=True
        ).astype(jnp.float32),
        lax.psum_scatter(
            up_weight_grad.astype(jnp.bfloat16), "fsdp", scatter_dimension=0, tiled=True
        ).astype(jnp.float32),
        lax.psum_scatter(
            down_weight_grad.astype(jnp.bfloat16), "fsdp", scatter_dimension=0, tiled=True
        ).astype(jnp.float32),
    )
    totals = lax.psum(
        (
            shares[0],
            shares[1],
            shares[2],
            shares[3],
            shares[4],
            shares[5],
            shares[6],
            shares[7],
            shares[8],
        ),
        ("dp", "ctx"),
    )
    return (
        result.reshape(sequences, local_rows, model_width),
        input_grad.reshape(sequences, local_rows, model_width),
        totals[0],
        totals[1],
        totals[2],
        totals[3],
        totals[4],
        totals[5],
        totals[6],
        totals[7],
        totals[8],
    )


def solution(mesh):
    return jax.shard_map(
        on_device,
        mesh=mesh,
        in_specs=(
            P("dp", ("ctx", "fsdp"), None),
            P("dp", None),
            P("fsdp"),
            P("fsdp", None),
            P("fsdp", None),
            P("fsdp", None),
            P("fsdp", None),
            P("fsdp"),
            P("fsdp", None),
            P("fsdp", None),
            P("fsdp", None),
            P("dp", ("ctx", "fsdp"), None),
        ),
        out_specs=(
            P("dp", ("ctx", "fsdp"), None),
            P("dp", ("ctx", "fsdp"), None),
            P("fsdp"),
            P("fsdp", None),
            P("fsdp", None),
            P("fsdp", None),
            P("fsdp", None),
            P("fsdp"),
            P("fsdp", None),
            P("fsdp", None),
            P("fsdp", None),
        ),
        check_vma=False,
    )
```

profile of v0, /device:TPU:0, one launch (start us, length us, event | category | flops | bytes accessed | tf_op | source)
XLA Modules:
  0.0 1371.4 jit_solution(6091182122230141165)
XLA Ops:
  11.9 14.2 %all-reduce.6 = (bf16[960]{0:T(1024)(128)(2,1)S(1)}, bf16[960]{0:T(1024)(128)(2,1)}) all-reduce(bf16[960]{0:T(1024)(128)(2,1)S(1)} %dynamic-update-slice, bf16[960]{0:T(1024)(128)(2,1)S(1)} %dynamic-update-slice.1), channel_id=1, replica_groups=mesh['dp'=4,'ctx'=2,'fsdp'=4] {'fsdp'}, use_global_device_ids=true, to_apply=%add | all-reduce | flops 1920 | bytes 7680
  26.1 25.3 %all-gather.4 = bf16[4,240,320]{1,2,0:T(8,128)(2,1)S(1)} all-gather(bf16[1,240,320]{1,2,0:T(8,128)(2,1)S(1)} %bitcast.615), channel_id=1, replica_groups=mesh['dp'=4,'ctx'=2,'fsdp'=4] {'fsdp'}, dimensions={0}, use_global_device_ids=true | all-gather | bytes 768000 | tf_op jit(solution)/shard_map/all_gather | solution.py:115
  55.5 21.1 %all-gather = bf16[768,320]{1,0:T(8,128)(2,1)S(1)} all-gather(bf16[192,320]{1,0:T(8,128)(2,1)S(1)} %add_convert_fusion.3), channel_id=2, replica_groups=mesh['dp'=4,'ctx'=2,'fsdp'=4] {'fsdp'}, dimensions={0}, use_global_device_ids=true | all-gather | bytes 614400 | tf_op jit(solution)/shard_map/all_gather | solution.py:158
  79.1 24.2 %all-gather.5 = bf16[4,240,320]{1,2,0:T(8,128)(2,1)S(1)} all-gather(bf16[1,240,320]{1,2,0:T(8,128)(2,1)S(1)} %bitcast.616), channel_id=1, replica_groups=mesh['dp'=4,'ctx'=2,'fsdp'=4] {'fsdp'}, dimensions={0}, use_global_device_ids=true | all-gather | bytes 768000 | tf_op jit(solution)/shard_map/all_gather | solution.py:116
  104.7 21.8 %all-gather.2 = bf16[768,320]{1,0:T(8,128)(2,1)S(1)} all-gather(bf16[192,320]{1,0:T(8,128)(2,1)S(1)} %convolution_convert_fusion.8), channel_id=4, replica_groups=mesh['dp'=4,'ctx'=2,'fsdp'=4] {'fsdp'}, dimensions={0}, use_global_device_ids=true | all-gather | bytes 614400 | tf_op jit(solution)/shard_map/all_gather | solution.py:159
  127.7 21.7 %all-gather.1 = bf16[1536,320]{1,0:T(8,128)(2,1)} all-gather(bf16[768,320]{1,0:T(8,128)(2,1)S(1)} %all-gather), channel_id=3, replica_groups=mesh['dp'=4,'ctx'=2,'fsdp'=4] {'ctx'}, dimensions={0}, use_global_device_ids=true | all-gather | bytes 1474560 | tf_op jit(solution)/shard_map/all_gather | solution.py:184
  149.4 11.2 all-gather.3
  168.1 35.2 %while.74 = (s32[]{:T(128)}, f32[1,5,3,192]{3,2,1,0:T(4,128)S(1)}, f32[1,5,3,192]{3,2,1,0:T(4,128)S(1)}, f32[1,192,5,3,64]{1,4,3,2,0:T(8,128)}, s32[1,192]{1,0:T...) while((s32[]{:T(128)}, f32[1,5,3,192]{3,2,1,0:T(4,128)S(1)}, ...), condition=%wide.region_6.7_spmd.clone, body=%wide.region_2.6_spmd.clone.sunk | while | flops 397340032 | bytes 51586084 | solution.py:206
  207.9 18.5 %all-gather.16.cloned.1.call-done = bf16[960,2560]{1,0:T(8,128)(2,1)} async-done(((bf16[240,2560]{1,0:T(8,128)(2,1)}), bf16[960,2560]{1,0:T(8,128)(2,1)}) %all-gather.16.cloned.1.call-update) | async-done | bytes 4915216 | tf_op jit(solution)/shard_map/all_gather | solution.py:119
  226.4 4.9 fusion.157
  231.3 87.7 %all-gather.18.cloned.1.call-done = bf16[960,2560]{1,0:T(8,128)(2,1)} async-done(((bf16[240,2560]{1,0:T(8,128)(2,1)}), bf16[960,2560]{1,0:T(8,128)(2,1)}) %all-gather.18.cloned.1.call-update) | async-done | bytes 4915216 | tf_op jit(solution)/shard_map/all_gather | solution.py:120
  318.9 4.9 fusion.158
  323.8 87.7 %all-gather.20.cloned.1.call-done = bf16[2560,960]{0,1:T(8,128)(2,1)} async-done(((bf16[640,960]{0,1:T(8,128)(2,1)}), bf16[2560,960]{0,1:T(8,128)(2,1)}) %all-gather.20.cloned.1.call-update) | async-done | bytes 4915216 | tf_op jit(solution)/shard_map/all_gather | solution.py:121
  411.5 6.1 multiply_convert_fusion
  430.2 36.8 %while.75 = (s32[]{:T(128)}, f32[1,192,5,3,64]{1,4,3,2,0:T(8,128)S(1)}, bf16[1,768,320]{1,2,0:T(8,128)(2,1)}, bf16[1,768,320]{1,2,0:T(8,128)(2,1)}, bf16[1,768,3...) while((s32[]{:T(128)}, ...), condition=%wide.region_12.13_spmd.clone, body=%wide.region_10.12_spmd.clone.sunk | while | flops 481479936 | bytes 30335776 | solution.py:283
  469.6 34.5 %while.73 = (s32[]{:T(128)}, f32[1,192,5,3,64]{1,4,3,2,0:T(8,128)S(1)}, f32[1,768,320]{1,2,0:T(8,128)S(1)}, f32[1,768,320]{1,2,0:T(8,128)}, bf16[1,768,320]{1,2,...) while((s32[]{:T(128)}, ...), condition=%wide.region_15.16_spmd, body=%wide.region_13.15_spmd.sunk | while | flops 481213696 | bytes 31318808 | solution.py:283
  507.3 12.1 collective-permute-done.3
  521.7 7.0 collective-permute-done.4
  530.7 11.3 collective-permute-done.5
  547.5 17.1 %reduce-scatter.30.cloned.1.call-done = bf16[192,320]{1,0:T(8,128)(2,1)} async-done(((bf16[768,320]{1,0:T(8,128)(2,1)}), bf16[192,320]{1,0:T(8,128)(2,1)}) %reduce-scatter.30.cloned.1.call-update) | async-done | bytes 122896
  573.1 4.9 convolution_convert_fusion
  577.9 7.9 copy.104
  586.8 4.9 convolution_convert_fusion.2
  592.1 5.0 convolution_convert_fusion.1
  601.8 5.1 fusion.105
  608.6 9.2 all-reduce.5
  621.2 34.7 %reduce-scatter.20.cloned.1.call-done = bf16[240,960]{1,0:T(8,128)(2,1)} async-done(((bf16[960,960]{1,0:T(8,128)(2,1)}), bf16[240,960]{1,0:T(8,128)(2,1)}) %reduce-scatter.20.cloned.1.call-update) | async-done | bytes 460816 | tf_op jit(solution)/shard_map/reduce_scatter | solution.py:358
  655.9 43.6 %reduce-scatter.22.cloned.1.call-done = bf16[240,960]{1,0:T(8,128)(2,1)} async-done(((bf16[960,960]{1,0:T(8,128)(2,1)}), bf16[240,960]{1,0:T(8,128)(2,1)}) %reduce-scatter.22.cloned.1.call-update) | async-done | bytes 460816 | tf_op jit(solution)/shard_map/reduce_scatter | solution.py:367
  699.5 95.2 %reduce-scatter.36.cloned.1.call-done = bf16[640,960]{1,0:T(8,128)(2,1)} async-done(((bf16[2560,960]{1,0:T(8,128)(2,1)}), bf16[640,960]{1,0:T(8,128)(2,1)}) %reduce-scatter.36.cloned.1.call-update) | async-done | bytes 1228816
  796.8 89.2 %reduce-scatter.24.cloned.1.call-done = bf16[240,2560]{1,0:T(8,128)(2,1)} async-done(((bf16[960,2560]{1,0:T(8,128)(2,1)}), bf16[240,2560]{1,0:T(8,128)(2,1)}) %reduce-scatter.24.cloned.1.call-update) | async-done | bytes 1228816 | tf_op jit(solution)/shard_map/reduce_scatter | solution.py:373
  886.0 91.3 %reduce-scatter.26.cloned.1.call-done = bf16[240,2560]{1,0:T(8,128)(2,1)} async-done(((bf16[960,2560]{1,0:T(8,128)(2,1)}), bf16[240,2560]{1,0:T(8,128)(2,1)}) %reduce-scatter.26.cloned.1.call-update) | async-done | bytes 1228816 | tf_op jit(solution)/shard_map/reduce_scatter | solution.py:376
  977.3 387.3 %all-reduce.8 = (f32[240]{0:T(256)}, f32[240,960]{1,0:T(8,128)}, f32[240,320]{0,1:T(8,128)}, f32[240,320]{0,1:T(8,128)}, f32[240,960]{1,0:T(8,128)}, /*index=5*/...) all-reduce(f32[240]{0:T(256)S(1)} %get-tuple-element.1237, ...), channel_id=1, replica_groups=mesh['dp'=4,'ctx'=2,'fsdp'=4] {'dp','ctx'}, use_global_device_ids=true, to_apply=%region_21.22 | all-reduce | flops 2458080 | bytes 14749440 | tf_op jit(solution)/shard_map/psum | solution.py:383
  (362 shorter events, 178.9 us)
Async XLA Ops:
  7.2 18.9 %copy-start.40 = (bf16[240,320]{0,1:T(8,128)(2,1)S(1)}, bf16[240,320]{0,1:T(8,128)(2,1)}, u32[]{:S(2)}) copy-start(bf16[240,320]{0,1:T(8,128)(2,1)} %param.22) | copy-start | bytes 460804
  7.2 158.1 %all-gather.12.cloned.1.call-start = ((), (), s32[]{:S(2)}) async-start(), calls=%async_computation.9 | async-start | bytes 2457600 | tf_op jit(solution)/shard_map/all_gather | solution.py:114
  8.0 196.7 %all-gather.14.cloned.1.call-start = ((), (), s32[]{:S(2)}) async-start(), calls=%async_computation.10 | async-start | bytes 2457600 | tf_op jit(solution)/shard_map/all_gather | solution.py:117
  8.7 43.8 %copy-start.3 = (bf16[1,192,960]{2,1,0:T(8,128)(2,1)S(1)}, bf16[1,192,960]{2,1,0:T(8,128)(2,1)}, u32[]{:S(2)}) copy-start(bf16[1,192,960]{2,1,0:T(8,128)(2,1)} %param.18) | copy-start | bytes 1105924
  8.7 217.7 %all-gather.16.cloned.1.call-start = ((), (), s32[]{:S(2)}) async-start(), calls=%async_computation.11 | async-start | bytes 6144000 | tf_op jit(solution)/shard_map/all_gather | solution.py:119
  9.4 309.5 %all-gather.18.cloned.1.call-start = ((), (), s32[]{:S(2)}) async-start(), calls=%async_computation.12 | async-start | bytes 6144000 | tf_op jit(solution)/shard_map/all_gather | solution.py:120
  10.0 401.4 %all-gather.20.cloned.1.call-start = ((), (), s32[]{:S(2)}) async-start(), calls=%async_computation.13 | async-start | bytes 6144000 | tf_op jit(solution)/shard_map/all_gather | solution.py:121
  54.0 25.1 %copy-start.41 = (bf16[240,320]{0,1:T(8,128)(2,1)S(1)}, bf16[240,320]{0,1:T(8,128)(2,1)}, u32[]{:S(2)}) copy-start(bf16[240,320]{0,1:T(8,128)(2,1)} %param.23) | copy-start | bytes 460804
  55.0 112.9 %copy-start.17 = (f32[192,64]{0,1:T(8,128)}, f32[192,64]{0,1:T(8,128)S(1)}, u32[]{:S(2)}) copy-start(f32[192,64]{0,1:T(8,128)S(1)} %maximum_bitcast_fusion) | copy-start | bytes 147460
  55.3 23.8 %copy-start.38 = (f32[192,64]{0,1:T(8,128)}, f32[192,64]{0,1:T(8,128)S(1)}, u32[]{:S(2)}) copy-start(f32[192,64]{0,1:T(8,128)S(1)} %maximum_bitcast_fusion.1) | copy-start | bytes 147460
  77.7 390.8 %collective-permute-start = (bf16[1,768,320]{1,2,0:T(8,128)(2,1)}, bf16[1,768,320]{1,2,0:T(8,128)(2,1)}, u32[]{:S(2)}, u32[]{:S(2)}) collective-permute-start(bf16[1,768,320]{1,2,0:T(8,128)(2,1)} %copy.81), channel_id=1, source_target_pairs={{0,4},{4,0},{1,5},{5,1},{2,6},{6,2},{3,7},{7,3},{8,12},{12,8},{9,1... | collective-permute-start | bytes 1474568 | tf_op jit(solution)/shard_map/while/body/eval_jaxpr/ppermute | solution.py:28
  104.3 23.4 %copy-start.24 = (bf16[960,320]{0,1:T(8,128)(2,1)}, bf16[960,320]{0,1:T(8,128)(2,1)S(1)}, u32[]{:S(2)}) copy-start(bf16[960,320]{0,1:T(8,128)(2,1)S(1)} %reshape.1410) | copy-start | bytes 1843204
  127.6 340.9 %collective-permute-start.1 = (bf16[1,768,320]{1,2,0:T(8,128)(2,1)}, bf16[1,768,320]{1,2,0:T(8,128)(2,1)}, u32[]{:S(2)}, u32[]{:S(2)}) collective-permute-start(bf16[1,768,320]{1,2,0:T(8,128)(2,1)} %copy.82), channel_id=1, source_target_pairs={{0,4},{4,0},{1,5},{5,1},{2,6},{6,2},{3,7},{7,3},{8,12},{12,8},{9,1... | collective-permute-start | bytes 1474568 | tf_op jit(solution)/shard_map/while/body/eval_jaxpr/ppermute | solution.py:28
  127.6 35.5 %copy-start.44 = (s32[192]{0:T(256)S(1)}, s32[192]{0:T(256)}, u32[]{:S(2)}) copy-start(s32[192]{0:T(256)} %get-tuple-element.1229) | copy-start | bytes 2308
  127.6 416.7 %reduce-scatter.28.cloned.1.call-start = ((), (), s32[]{:S(2)}) async-start(), calls=%async_computation.18 | async-start | bytes 737280
  207.1 217.6 %copy-start.10 = (f32[192,960]{1,0:T(8,128)}, f32[192,960]{1,0:T(8,128)S(1)}, u32[]{:S(2)}) copy-start(f32[192,960]{1,0:T(8,128)S(1)} %get-tuple-element.1233) | copy-start | bytes 2211844
  207.9 111.0 %copy-start.4 = (bf16[192,960]{1,0:T(8,128)(2,1)}, bf16[192,960]{1,0:T(8,128)(2,1)S(1)}, u32[]{:S(2)}) copy-start(bf16[192,960]{1,0:T(8,128)(2,1)S(1)} %multiply_convert_fusion.3) | copy-start | bytes 1105924
  231.3 180.2 %copy-start.31 = (bf16[1,192,960]{2,1,0:T(8,128)(2,1)S(1)}, bf16[1,192,960]{2,1,0:T(8,128)(2,1)}, u32[]{:S(2)}) copy-start(bf16[1,192,960]{2,1,0:T(8,128)(2,1)} %param.29) | copy-start | bytes 1105924
  466.9 37.1 %collective-permute-start.2 = (bf16[1,768,320]{1,2,0:T(8,128)(2,1)}, bf16[1,768,320]{1,2,0:T(8,128)(2,1)}, u32[]{:S(2)}, u32[]{:S(2)}) collective-permute-start(bf16[1,768,320]{1,2,0:T(8,128)(2,1)} %get-tuple-element.924), channel_id=1, source_target_pairs={{0,4},{4,0},{1,5},{5,1},{2,6},{6,2},{3,7},{7,3},{8,12},{12,8},{9,1... | collective-permute-start | bytes 1474568 | tf_op jit(solution)/shard_map/while/body/eval_jaxpr/ppermute | solution.py:28
  505.2 14.2 %collective-permute-start.3 = (bf16[1,768,320]{1,2,0:T(8,128)(2,1)S(1)}, bf16[1,768,320]{1,2,0:T(8,128)(2,1)S(1)}, u32[]{:S(2)}, u32[]{:S(2)}) collective-permute-start(bf16[1,768,320]{1,2,0:T(8,128)(2,1)S(1)} %add_convert_fusion.2), channel_id=1, source_target_pairs={{0,4},{4,0},{1,5},{5,1},{2,6},{6,2},{3,7},{7,3},{8,12},{12,8},{9,1... | collective-permute-start | bytes 1474568 | tf_op jit(solution)/shard_map/ppermute | solution.py:28
  505.8 22.9 %collective-permute-start.4 = (bf16[1,768,320]{1,2,0:T(8,128)(2,1)}, bf16[1,768,320]{1,2,0:T(8,128)(2,1)}, u32[]{:S(2)}, u32[]{:S(2)}) collective-permute-start(bf16[1,768,320]{1,2,0:T(8,128)(2,1)} %get-tuple-element.926), channel_id=1, source_target_pairs={{0,4},{4,0},{1,5},{5,1},{2,6},{6,2},{3,7},{7,3},{8,12},{12,8},{9,1... | collective-permute-start | bytes 1474568 | tf_op jit(solution)/shard_map/while/body/eval_jaxpr/ppermute | solution.py:28
  521.6 42.9 %reduce-scatter.30.cloned.1.call-start = ((), (), s32[]{:S(2)}) async-start(), calls=%async_computation.19 | async-start | bytes 737280
  530.1 11.9 collective-permute-start.5
  544.3 74.8 %reduce-scatter.32.cloned.1.call-start = ((), (), s32[]{:S(2)}) async-start(), calls=%async_computation.20 | async-start | bytes 921600
  544.3 23.4 %copy-start.28 = (f32[192,64]{0,1:T(8,128)}, f32[192,64]{0,1:T(8,128)S(1)}, u32[]{:S(2)}) copy-start(f32[192,64]{0,1:T(8,128)S(1)} %fusion.141) | copy-start | bytes 147460
  545.8 20.5 %copy-start.20 = (f32[1,192,5,64]{1,3,2,0:T(8,128)}, f32[1,192,5,64]{1,3,2,0:T(8,128)S(1)}, u32[]{:S(2)}) copy-start(f32[1,192,5,64]{1,3,2,0:T(8,128)S(1)} %pad_maximum_fusion.2) | copy-start | bytes 737284
  547.4 72.7 %reduce-scatter.34.cloned.1.call-start = ((), (), s32[]{:S(2)}) async-start(), calls=%async_computation.21 | async-start | bytes 921600
  567.5 88.4 %reduce-scatter.20.cloned.1.call-start = ((), (), s32[]{:S(2)}) async-start(), calls=%async_computation.14 | async-start | bytes 2457600 | tf_op jit(solution)/shard_map/reduce_scatter | solution.py:358
  571.0 128.5 %reduce-scatter.22.cloned.1.call-start = ((), (), s32[]{:S(2)}) async-start(), calls=%async_computation.15 | async-start | bytes 2457600 | tf_op jit(solution)/shard_map/reduce_scatter | solution.py:367
  573.0 221.7 %reduce-scatter.36.cloned.1.call-start = ((), (), s32[]{:S(2)}) async-start(), calls=%async_computation.22 | async-start | bytes 6553600
  585.9 300.1 %reduce-scatter.24.cloned.1.call-start = ((), (), s32[]{:S(2)}) async-start(), calls=%async_computation.16 | async-start | bytes 6144000 | tf_op jit(solution)/shard_map/reduce_scatter | solution.py:373
  591.8 385.5 %reduce-scatter.26.cloned.1.call-start = ((), (), s32[]{:S(2)}) async-start(), calls=%async_computation.17 | async-start | bytes 6144000 | tf_op jit(solution)/shard_map/reduce_scatter | solution.py:376
  (48 other events, 174.6 us)
Sparse Core Ops, SparseCore 0:
  9.6 65.2 all-gather.11
  76.5 57.0 all-gather.13
  135.2 91.1 all-gather.15
  227.8 91.0 all-gather.17
  320.4 91.0 all-gather.19
  521.7 19.4 reduce-scatter.27
  544.4 20.1 reduce-scatter.29
  566.8 21.2 reduce-scatter.31
  590.4 22.1 reduce-scatter.33
  615.4 40.4 reduce-scatter.19
  658.8 40.6 reduce-scatter.21
  701.7 92.9 reduce-scatter.35
  797.0 88.9 reduce-scatter.23
  888.3 88.9 reduce-scatter.25
where the time goes:
time: 1380 us; the launch traced here: 1370 us
  waiting for transfers between devices  598 us (43%)
  blocking collectives  536 us (39%)
  matrix products  134 us (10%)
  local copies, waits for them, and re-layouts  59.3 us (4%)
  other arithmetic  20.1 us (1%)
  between operations  16.5 us (1%)
    psum x1, blocking collectives, on_device(): lax.psum((shares[0], shares[1], shares[2], shares[3], shares[4], shares[5...  387 us
    unnamed x19, waiting for transfers between devices  115 us
    reduce_scatter x1, waiting for transfers between devices, on_device(): lax.psum_scatter(up_weight_grad.astype(jnp.bfloat16), 'fsdp', scatter_dim...  91.3 us
    reduce_scatter x1, waiting for transfers between devices, on_device(): lax.psum_scatter(gate_weight_grad.astype(jnp.bfloat16), 'fsdp', scatter_d...  89.2 us
    all_gather x1, waiting for transfers between devices, on_device(): lax.all_gather(up_weight, 'fsdp', axis=0, tiled=True)  87.7 us
    all_gather x1, waiting for transfers between devices, on_device(): lax.all_gather(down_weight, 'fsdp', axis=0, tiled=True)  87.7 us
    reduce_scatter x1, waiting for transfers between devices, on_device(): lax.psum_scatter(output_weight_grad.astype(jnp.bfloat16), 'fsdp', scatter...  43.6 us
    reduce_scatter x1, waiting for transfers between devices, on_device(): lax.psum_scatter(query_weight_grad.astype(jnp.bfloat16), 'fsdp', scatter_...  34.7 us
  transfers between devices with their start and end apart: 20, of which 12 were waited for; matrix products, arithmetic and copies ran while one was open for 15% of the time, Pallas kernels for 0%

commit v1 on v0

v1 whole, which is shorter than its diff:
```python
import functools
import math

import jax
import jax.numpy as jnp
from jax import lax
from jax.experimental import pallas as pl
from jax.experimental.pallas import tpu as pltpu
from jax.sharding import PartitionSpec as P

HEADS = 15
KV_HEADS = 5
HEAD_DIM = 64
GROUPS = HEADS // KV_HEADS
LANES = 128

EPSILON = 1e-05
ROPE_BASE = 100000.0
MASKED = -1e30

F32 = jnp.float32
BF16 = jnp.bfloat16
VMEM_LIMIT = 56 * 1024 * 1024


def dot_plain(left, right):
    return jnp.dot(left, right, preferred_element_type=F32)


def dot_last(left, right):
    return lax.dot_general(left, right, (((1,), (1,)), ((), ())), preferred_element_type=F32)


def dot_first(left, right):
    return lax.dot_general(left, right, (((0,), (0,)), ((), ())), preferred_element_type=F32)


def swap(x, axis, mask):
    count = lax.axis_size(axis)
    return lax.ppermute(x, axis, [(i, i ^ mask) for i in range(count)])


def swap_plane(x, dp_mask, ctx_mask):
    ctx_count = lax.axis_size("ctx")
    pairs = []
    for d in range(lax.axis_size("dp")):
        for c in range(ctx_count):
            pairs.append((d * ctx_count + c, (d ^ dp_mask) * ctx_count + (c ^ ctx_mask)))
    return lax.ppermute(x, ("dp", "ctx"), pairs)


def swap_core(x):
    return swap_plane(x, 1, 0)


CHIP_MASKS = ((2, 0), (0, 1), (2, 1))


def plane_group_count():
    return lax.axis_size("dp") * 2


def own_and_chips(x):
    return [x] + [swap_plane(x, a, b) for a, b in CHIP_MASKS]


def gather_fsdp(x):
    count = lax.axis_size("fsdp")
    index = lax.axis_index("fsdp")
    out = jnp.zeros((count,) + x.shape, x.dtype)
    for r in range(count):
        piece = x if r == 0 else swap(x, "fsdp", r)
        out = lax.dynamic_update_slice_in_dim(out, piece[None], index ^ r, 0)
    return out


def scatter_fsdp(parts):
    count = lax.axis_size("fsdp")
    index = lax.axis_index("fsdp")
    total = lax.dynamic_index_in_dim(parts, index, 0, keepdims=False).astype(F32)
    for r in range(1, count):
        piece = lax.dynamic_index_in_dim(parts, index ^ r, 0, keepdims=False)
        total = total + swap(piece, "fsdp", r).astype(F32)
    return total


def sum_chips(x):
    own, across, along, diagonal = own_and_chips(x)
    return (own.astype(F32) + across.astype(F32)) + (along.astype(F32) + diagonal.astype(F32))


def sum_far(x):
    count = lax.axis_size("ctx")
    if count == 2:
        return x
    groups = [list(range(0, count, 2)), list(range(1, count, 2))]
    return lax.psum(x.astype(F32), "ctx", axis_index_groups=groups).astype(x.dtype)


def whole(shape, memory_space=pltpu.VMEM):
    return pl.BlockSpec(memory_space=memory_space)


def call(kernel, out_shapes, *args, scratch=(), flops=0, name=None):
    specs = [pl.BlockSpec(memory_space=pltpu.VMEM) for _ in args]
    outs = tuple(jax.ShapeDtypeStruct(s, d) for s, d in out_shapes)
    bytes_all = sum(a.size * a.dtype.itemsize for a in args) + sum(
        math.prod(s) * jnp.dtype(d).itemsize for s, d in out_shapes
    )
    return pl.pallas_call(
        kernel,
        out_shape=outs,
        in_specs=specs,
        out_specs=tuple(pl.BlockSpec(memory_space=pltpu.VMEM) for _ in outs),
        scratch_shapes=list(scratch),
        compiler_params=pltpu.CompilerParams(vmem_limit_bytes=VMEM_LIMIT),
        cost_estimate=pl.CostEstimate(flops=flops, bytes_accessed=bytes_all, transcendentals=0),
        name=name,
    )(*args)


def rope_lanes(values, cosine, sine):
    rows, width = values.shape
    lane = lax.broadcasted_iota(jnp.int32, (rows, LANES), 1)
    first_half = (lane % HEAD_DIM) < (HEAD_DIM // 2)
    out = []
    for start in range(0, width, LANES):
        piece = values[:, start : min(start + LANES, width)]
        size = piece.shape[1]
        if size < LANES:
            piece = jnp.concatenate([piece, jnp.zeros((rows, LANES - size), piece.dtype)], axis=1)
        ahead = pltpu.roll(piece, LANES - HEAD_DIM // 2, 1)
        behind = pltpu.roll(piece, HEAD_DIM // 2, 1)
        partner = jnp.where(first_half, ahead, behind)
        out.append((piece * cosine + partner * sine)[:, :size])
    return jnp.concatenate(out, axis=1)


def heads_of(ref, first, count, rows=None):
    out = []
    for h in range(first, first + count):
        start = (h * HEAD_DIM) // LANES * LANES
        stop = min(start + LANES, ref.shape[-1])
        pair = ref[:, start:stop] if rows is None else ref[rows, start:stop]
        at = h * HEAD_DIM - start
        out.append(pair[:, at : at + HEAD_DIM])
    return out[0] if count == 1 else jnp.concatenate(out, axis=0)


def kv_kernel(normed_ref, mine_ref, other_ref, core_ref, cos_ref, sin_ref, kv_ref):
    normed = normed_ref[...]
    mine = dot_plain(normed, mine_ref[...])
    other = dot_plain(normed, other_ref[...])
    first_core = core_ref[...] == 0
    keys = jnp.where(first_core, mine, other)
    values = jnp.where(first_core, other, mine)
    keys = rope_lanes(keys, cos_ref[...], sin_ref[...])
    kv_ref[...] = jnp.concatenate([keys, values], axis=1).astype(BF16)


def forward_kernel(
    chunk, query_ref, kv_ref, key_pos_ref, query_pos_ref, cos_ref, sin_ref,
    attended_ref, queries_ref, turned_ref, log_ref
):
    key_count = kv_ref.shape[0]
    rows = query_ref.shape[0]
    columns = GROUPS * rows
    roped = rope_lanes(query_ref[...], cos_ref[...], sin_ref[...]).astype(BF16)
    queries_ref[...] = roped * jnp.asarray(1.0 / math.sqrt(HEAD_DIM), BF16)
    query_pos = query_pos_ref[...]
    outs = []
    for kv_head in range(KV_HEADS):
        stacked = heads_of(queries_ref, kv_head * GROUPS, GROUPS)

        def step(j, state, kv_head=kv_head, stacked=stacked):
            largest, total, weighted = state
            at = pl.ds(pl.multiple_of(j * chunk, chunk), chunk)
            keys = heads_of(kv_ref, kv_head, 1, at)
            values = heads_of(kv_ref, KV_HEADS + kv_head, 1, at)
            scores = dot_last(keys, stacked)
            scores = jnp.where(key_pos_ref[at, :] <= query_pos, scores, MASKED)
            new_largest = jnp.maximum(largest, jnp.max(scores, axis=0, keepdims=True))
            weights = jnp.exp(scores - new_largest)
            factor = jnp.exp(largest - new_largest)
            total = total * factor + jnp.sum(weights, axis=0, keepdims=True)
            weighted = weighted * factor + dot_first(values, weights.astype(BF16))
            return new_largest, total, weighted

        start = (
            jnp.full((1, columns), MASKED, F32),
            jnp.zeros((1, columns), F32),
            jnp.zeros((HEAD_DIM, columns), F32),
        )
        largest, total, weighted = lax.fori_loop(0, key_count // chunk, step, start)
        turned = weighted / total
        turned_ref[kv_head] = turned
        log_ref[kv_head : kv_head + 1, :] = largest + jnp.log(total)
        straight = turned.T
        for g in range(GROUPS):
            outs.append(straight[g * rows : (g + 1) * rows, :])
    attended_ref[...] = jnp.concatenate(outs, axis=1).astype(BF16)


def backward_kernel(
    chunk, queries_ref, kv_ref, key_pos_ref, query_pos_ref, cos_ref, sin_ref, turned_ref,
    log_ref, grad_ref, query_grad_ref, kv_grad_ref
):
    key_count = kv_ref.shape[0]
    rows = queries_ref.shape[0]
    columns = GROUPS * rows
    query_pos = query_pos_ref[...]
    outs = []
    for kv_head in range(KV_HEADS):
        stacked = heads_of(queries_ref, kv_head * GROUPS, GROUPS)
        upstream = heads_of(grad_ref, kv_head * GROUPS, GROUPS)
        delta = jnp.sum(
            upstream.astype(F32).T * turned_ref[kv_head], axis=0, keepdims=True
        )
        log_total = log_ref[kv_head : kv_head + 1, :]
        lanes_at = kv_head * HEAD_DIM
        values_at = (KV_HEADS + kv_head) * HEAD_DIM

        def step(j, query_grad, kv_head=kv_head, stacked=stacked, upstream=upstream,
                 delta=delta, log_total=log_total, lanes_at=lanes_at, values_at=values_at):
            at = pl.ds(pl.multiple_of(j * chunk, chunk), chunk)
            keys = heads_of(kv_ref, kv_head, 1, at)
            values = heads_of(kv_ref, KV_HEADS + kv_head, 1, at)
            scores = dot_last(keys, stacked)
            scores = jnp.where(key_pos_ref[at, :] <= query_pos, scores, MASKED)
            weights = jnp.exp(scores - log_total)
            weight_grad = dot_last(values, upstream)
            score_grad = (weights * (weight_grad - delta)).astype(BF16)
            value_grad = dot_plain(weights.astype(BF16), upstream)
            key_grad = dot_plain(score_grad, stacked)
            kv_grad_ref[at, lanes_at : lanes_at + HEAD_DIM] = key_grad.astype(BF16)
            kv_grad_ref[at, values_at : values_at + HEAD_DIM] = value_grad.astype(BF16)
            return query_grad + dot_first(keys, score_grad)

        query_grad = lax.fori_loop(
            0, key_count // chunk, step, jnp.zeros((HEAD_DIM, columns), F32)
        )
        straight = query_grad.T * (1.0 / math.sqrt(HEAD_DIM))
        for g in range(GROUPS):
            outs.append(straight[g * rows : (g + 1) * rows, :])
    query_grad_ref[...] = rope_lanes(
        jnp.concatenate(outs, axis=1), cos_ref[...], -sin_ref[...]
    ).astype(BF16)


def kv_back_kernel(own_ref, one_ref, two_ref, three_ref, cos_ref, sin_ref, out_ref):
    total = (own_ref[...].astype(F32) + one_ref[...].astype(F32)) + (
        two_ref[...].astype(F32) + three_ref[...].astype(F32)
    )
    width = KV_HEADS * HEAD_DIM
    keys = rope_lanes(total[:, :width], cos_ref[...], -sin_ref[...])
    out_ref[...] = jnp.concatenate([keys, total[:, width:]], axis=1).astype(BF16)


def norm_rows(values, gain):
    inverse = lax.rsqrt(jnp.mean(values * values, axis=-1, keepdims=True) + EPSILON)
    return (values * inverse * gain, inverse)


def norm_back(gradient, values, inverse, gain):
    scaled = gradient * gain
    inner_mean = jnp.mean(scaled * values, axis=-1, keepdims=True)
    return inverse * scaled - values * (inverse * inverse * inverse) * inner_mean


def base_of(block_order, stored, block_length):
    which = stored // block_length
    count = block_order.shape[1]
    matches = (which[:, None] == jnp.arange(count, dtype=jnp.int32)[None, :]).astype(jnp.int32)
    return jnp.sum(block_order[0][None, :] * matches, axis=-1) * block_length + stored % block_length


def tables(positions):
    half_dim = HEAD_DIM // 2
    exponent = -(jnp.arange(half_dim, dtype=F32) * 2.0) / HEAD_DIM
    frequency = jnp.power(F32(ROPE_BASE), exponent)
    angles = positions.astype(F32)[:, None] * frequency
    cosine, sine = jnp.cos(angles), jnp.sin(angles)
    return (
        jnp.concatenate([cosine] * 4, axis=-1),
        jnp.concatenate([-sine, sine, -sine, sine], axis=-1),
    )


def on_device(
    tokens,
    block_order,
    attention_gain,
    query_weight,
    key_weight,
    value_weight,
    output_weight,
    feedforward_gain,
    gate_weight,
    up_weight,
    down_weight,
    cotangent,
):
    rows, width = tokens.shape[1], tokens.shape[2]
    shard_count = lax.axis_size("fsdp")
    ctx_count = lax.axis_size("ctx")
    block_length = rows * shard_count * ctx_count // block_order.shape[1]
    shard = lax.axis_index("fsdp")
    ctx = lax.axis_index("ctx")
    dp = lax.axis_index("dp")
    core = dp & 1
    member = dp * 2 + (ctx & 1)
    members = plane_group_count()
    weight_rows = query_weight.shape[0]
    query_width = HEADS * HEAD_DIM
    kv_width = KV_HEADS * HEAD_DIM

    gains = gather_fsdp(jnp.stack([attention_gain, feedforward_gain]))
    gains = jnp.transpose(gains, (1, 0, 2)).reshape(2, width).astype(F32)
    first_gain, second_gain = gains[0], gains[1]
    inputs = tokens[0].astype(F32)
    normed_one, inverse_one = norm_rows(inputs, first_gain)
    normed_one = normed_one.astype(BF16)

    kv_mine = gather_fsdp(jnp.where(core == 0, key_weight, value_weight)).reshape(width, kv_width)
    kv_other = swap_core(kv_mine)

    mine = lax.all_gather(
        jnp.where(core == 0, query_weight, output_weight), "fsdp", axis=0, tiled=True
    )
    other = swap_core(mine)
    query_full = jnp.where(core == 0, mine, other)
    output_full = jnp.where(core == 0, other, mine)

    hidden = gate_weight.shape[1]
    shard_hidden = hidden // shard_count
    piece = shard_hidden // members

    def columns_of(weight):
        grid = weight.reshape(weight_rows, shard_count, members, piece)
        return lax.dynamic_index_in_dim(grid, member, 2, keepdims=False).reshape(
            weight_rows, shard_count * piece
        )

    part_hidden = shard_count * piece
    gate_up = lax.all_gather(
        jnp.concatenate([columns_of(gate_weight), columns_of(up_weight)], axis=1),
        "fsdp", axis=0, tiled=True,
    )
    down_part = lax.all_gather(
        lax.dynamic_slice_in_dim(down_weight, member * piece, piece, 0), "fsdp", axis=0, tiled=True
    )

    my_start = (ctx * shard_count + shard) * rows
    my_base = base_of(block_order, my_start[None], block_length)
    offsets = jnp.arange(rows, dtype=jnp.int32)
    positions = my_base + offsets
    cosine, sine = tables(positions)
    query_pos = jnp.concatenate([positions] * GROUPS)[None, :]
    starts = jnp.stack(
        [((ctx ^ d) * shard_count + (shard ^ r)) * rows
         for d in range(ctx_count) for r in range(shard_count)]
    )
    key_pos = (base_of(block_order, starts, block_length)[:, None] + offsets[None, :]).reshape(-1, 1)

    (kv_own,) = call(
        kv_kernel, [((rows, 2 * kv_width), BF16)], normed_one, kv_mine, kv_other,
        jnp.full((1, kv_width), core, jnp.int32), cosine, sine,
        flops=4 * rows * width * kv_width, name="keys_values",
    )
    near = [kv_own] + [swap(kv_own, "fsdp", r) for r in range(1, shard_count)]
    rest = jnp.concatenate(near[1:], axis=0)
    blocks = list(near)
    for d in range(1, ctx_count):
        blocks += [swap(kv_own, "ctx", d), swap(rest, "ctx", d)]
    kv_all = jnp.concatenate(blocks, axis=0)

    query_raw = dot_plain(normed_one, query_full)
    key_count = kv_all.shape[0]
    chunk = rows * 2
    attention_flops = 2 * HEADS * rows * key_count * HEAD_DIM
    attended_low, queries, attended_turned, log_total = call(
        functools.partial(forward_kernel, chunk),
        [
            ((rows, query_width), BF16),
            ((rows, query_width), BF16),
            ((KV_HEADS, HEAD_DIM, GROUPS * rows), F32),
            ((KV_HEADS, GROUPS * rows), F32),
        ],
        query_raw, kv_all, key_pos, query_pos, cosine, sine,
        flops=8 * attention_flops, name="attention_forward",
    )

    residual = inputs + dot_plain(attended_low, output_full)
    normed_two, inverse_two = norm_rows(residual, second_gain)
    normed_two = normed_two.astype(BF16)

    cot_a = jnp.concatenate(own_and_chips(cotangent[0]), axis=0)
    cot_b = swap_core(cot_a)
    normed_a = jnp.concatenate(own_and_chips(normed_two), axis=0)
    normed_b = swap_core(normed_a)

    def feed_forward(normed, cot):
        gate_value_up = dot_plain(normed, gate_up)
        gate_value, upward = gate_value_up[:, :part_hidden], gate_value_up[:, part_hidden:]
        sigmoid_gate = jax.nn.sigmoid(gate_value)
        activated = (gate_value * sigmoid_gate * upward).astype(BF16)
        act_grad = dot_last(cot, down_part)
        gate_grad = act_grad * upward * sigmoid_gate * (1.0 + gate_value * (1.0 - sigmoid_gate))
        up_grad = act_grad * gate_value * sigmoid_gate
        both = jnp.concatenate([gate_grad.astype(BF16), up_grad.astype(BF16)], axis=1)
        return activated, both

    act_b, both_b = feed_forward(normed_b, cot_b)
    act_a, both_a = feed_forward(normed_a, cot_a)

    def sum_plane(part_b, part_a):
        from_core = swap_core(part_b.astype(BF16))
        chips = (part_a + from_core.astype(F32)).reshape(4, rows, width)
        low = chips.astype(BF16)
        total = chips[0]
        for k, (a, b) in enumerate(CHIP_MASKS):
            total = total + swap_plane(low[k + 1], a, b).astype(F32)
        return total

    normed_two_grad = sum_plane(dot_last(both_b, gate_up), dot_last(both_a, gate_up))
    result = residual + sum_plane(dot_plain(act_b, down_part), dot_plain(act_a, down_part))
    normed_ab = jnp.concatenate([normed_a, normed_b], axis=0)
    both_ab = jnp.concatenate([both_a, both_b], axis=0)
    act_ab = jnp.concatenate([act_a, act_b], axis=0)
    cot_ab = jnp.concatenate([cot_a, cot_b], axis=0)
    gate_up_grad = dot_first(normed_ab, both_ab).astype(BF16)
    down_grad = dot_first(act_ab, cot_ab).astype(BF16)
    gate_up_share = sum_far(lax.psum_scatter(gate_up_grad, "fsdp", scatter_dimension=0, tiled=True))
    down_share = sum_far(lax.psum_scatter(down_grad, "fsdp", scatter_dimension=0, tiled=True))
    group_axes = ("dp", "ctx")
    groups = [
        [d * ctx_count + c for d in range(lax.axis_size("dp")) for c in (first, first + 1)]
        for first in range(0, ctx_count, 2)
    ]
    extra = {} if ctx_count == 2 else {"axis_index_groups": groups}
    gate_up_all = lax.all_gather(gate_up_share, group_axes, axis=0, tiled=False, **extra)
    down_all = lax.all_gather(down_share, group_axes, axis=0, tiled=True, **extra)
    gate_up_all = gate_up_all.reshape(members, weight_rows, 2, shard_count, piece)
    gate_up_all = jnp.transpose(gate_up_all, (2, 1, 3, 0, 4)).reshape(2, weight_rows, hidden)
    gate_weight_grad = gate_up_all[0].astype(F32)
    up_weight_grad = gate_up_all[1].astype(F32)
    down_weight_grad = down_all.astype(F32)

    second_gain_grad = jnp.sum(normed_two_grad * residual * inverse_two, axis=0)
    residual_grad = cotangent[0].astype(F32) + norm_back(
        normed_two_grad, residual, inverse_two, second_gain
    )
    residual_low = residual_grad.astype(BF16)
    attended_grad = dot_last(residual_low, output_full).astype(BF16)
    output_grad = dot_first(attended_low, residual_low).astype(BF16)

    query_low, kv_grad = call(
        functools.partial(backward_kernel, chunk),
        [((rows, query_width), BF16), ((key_count, 2 * kv_width), BF16)],
        queries, kv_all, key_pos, query_pos, cosine, sine, attended_turned, log_total,
        attended_grad,
        flops=20 * attention_flops, name="attention_backward",
    )
    blocks = kv_grad.reshape(ctx_count, shard_count, rows, 2 * kv_width)
    near = blocks[0].astype(F32)
    for d in range(1, ctx_count):
        near = near + swap(blocks[d], "ctx", d).astype(F32)
    near = near.astype(BF16)
    (kv_low,) = call(
        kv_back_kernel, [((rows, 2 * kv_width), BF16)],
        near[0], *[swap(near[r], "fsdp", r) for r in range(1, shard_count)], cosine, sine,
        name="keys_values_back",
    )
    key_low, value_low = kv_low[:, :kv_width], kv_low[:, kv_width:]

    def sum_halves(grad):
        n = grad.shape[1]
        half = weight_rows // 2
        grid = grad.reshape(shard_count, 2, half, n)
        keep = lax.dynamic_index_in_dim(grid, core, 1, keepdims=False)
        send = lax.dynamic_index_in_dim(grid, 1 - core, 1, keepdims=False)
        both = (keep.astype(F32) + swap_core(send).astype(F32)).astype(BF16)
        low = sum_chips(scatter_fsdp(both).astype(BF16))
        low = sum_far(low).astype(BF16)
        away = swap_core(low)
        top = jnp.where(core == 0, low, away)
        bottom = jnp.where(core == 0, away, low)
        return jnp.concatenate([top, bottom], axis=0).astype(F32)

    output_weight_grad = sum_halves(output_grad)
    query_weight_grad = sum_halves(dot_first(normed_one, query_low).astype(BF16))

    kv_low_mine = jnp.where(core == 0, key_low, value_low)
    kv_low_other = jnp.where(core == 0, value_low, key_low)
    normed_one_grad = (
        dot_last(query_low, query_full)
        + dot_last(kv_low_mine, kv_mine)
        + dot_last(kv_low_other, kv_other)
    )
    first_gain_grad = jnp.sum(normed_one_grad * inputs * inverse_one, axis=0)
    input_grad = residual_grad + norm_back(normed_one_grad, inputs, inverse_one, first_gain)

    extra_rows = 8

    def packed(low, gain_grad):
        grid = dot_first(normed_one, low).reshape(shard_count, weight_rows, kv_width)
        gain = gain_grad.reshape(shard_count, 1, weight_rows)
        gain = jnp.pad(gain, ((0, 0), (0, extra_rows - 1), (0, kv_width - weight_rows)))
        return jnp.concatenate([grid.astype(BF16), gain.astype(BF16)], axis=1)

    keep = packed(kv_low_mine, jnp.where(core == 0, first_gain_grad, second_gain_grad))
    send = packed(kv_low_other, jnp.where(core == 0, second_gain_grad, first_gain_grad))
    both = (keep.astype(F32) + swap_core(send).astype(F32)).astype(BF16)
    low = sum_chips(scatter_fsdp(both).astype(BF16))
    low = sum_far(low).astype(BF16)
    away = swap_core(low)
    first = jnp.where(core == 0, low, away).astype(F32)
    second = jnp.where(core == 0, away, low).astype(F32)

    return (
        result[None],
        input_grad[None],
        first[weight_rows, :weight_rows],
        query_weight_grad,
        first[:weight_rows],
        second[:weight_rows],
        output_weight_grad,
        second[weight_rows, :weight_rows],
        gate_weight_grad,
        up_weight_grad,
        down_weight_grad,
    )


def solution(mesh):
    row = P("fsdp", None)
    token = P("dp", ("ctx", "fsdp"), None)
    return jax.shard_map(
        on_device,
        mesh=mesh,
        in_specs=(
            token, P("dp", None), P("fsdp"), row, row, row, row, P("fsdp"), row, row, row, token,
        ),
        out_specs=(
            token, token, P("fsdp"), row, row, row, row, P("fsdp"), row, row, row,
        ),
        check_vma=False,
    )
```

time: 1380 us -> 514 us (0.37)
  blocking collectives: 536 us -> 18 us
  waiting for transfers between devices: 598 us -> 199 us
  matrix products: 134 us -> 47.1 us
  starting transfers between devices: 6.44 us -> 58.6 us
  Pallas kernels: 0 us -> 45.2 us
  local copies, waits for them, and re-layouts: 59.3 us -> 85.7 us
  other arithmetic: 20.1 us -> 37.5 us
    psum x1 -> x0, blocking collectives: 387 us -> none  [on_device(): lax.psum((shares[0], shares[1], shares[2], shares[3], shares[4], shares[5...]
    reduce_scatter x4 -> x2, waiting for transfers between devices: 259 us -> 0.01 us  [the longest x1 0.01 us: on_device(): lax.psum_scatter(down_grad, 'fsdp', scatter_dimension=0, tiled=True)]
    all_gather x5 -> x4, waiting for transfers between devices: 194 us -> 13.1 us  [the longest x1 13.1 us: on_device(): lax.all_gather(jnp.where(core == 0, query_weight, output_weight), 'fsdp',...]
    ppermute x6 -> x57, waiting for transfers between devices: 30.5 us -> 186 us  [the longest x24 132 us: swap(): return lax.ppermute(x, axis, [(i, i ^ mask) for i in range(count)])]
    unnamed x19 -> x6, waiting for transfers between devices: 115 us -> 0.1 us
    all_gather x6 -> x1, blocking collectives: 125 us -> 18 us  [on_device(): lax.all_gather(lax.dynamic_slice_in_dim(down_weight, member * piece, piec...]
    dot_general x43 -> x6, matrix products: 96.7 us -> 14.3 us  [dot_plain(): return jnp.dot(left, right, preferred_element_type=F32)]
    ppermute x6 -> x57, starting transfers between devices: 5.62 us -> 58.4 us  [the longest x24 30.5 us: swap(): return lax.ppermute(x, axis, [(i, i ^ mask) for i in range(count)])]
  transfers between devices with their start and end apart: 20 -> 63, of which waited for: 12 -> 26; matrix products, arithmetic and copies ran while one was open for 15% -> 27% of each run, Pallas kernels for 0% -> 9%
where the time goes in v1:
time: 514 us; the launch traced here: 507 us
  waiting for transfers between devices  199 us (39%)
  local copies, waits for them, and re-layouts  85.7 us (17%)
  starting transfers between devices  58.6 us (11%)
  matrix products  47.1 us (9%)
  Pallas kernels  45.2 us (9%)
  other arithmetic  37.5 us (7%)
  blocking collectives  18 us (4%)
  between operations  16.2 us (3%)
    ppermute x24, waiting for transfers between devices, swap(): return lax.ppermute(x, axis, [(i, i ^ mask) for i in range(count)])  132 us
    ppermute x33, waiting for transfers between devices, swap_plane(): return lax.ppermute(x, ('dp', 'ctx'), pairs)  53.4 us
    pallas_call x4, Pallas kernels, call(): pl.pallas_call(kernel, out_shape=outs, in_specs=specs, out_specs=tuple((p...  45.2 us
    ppermute x24, starting transfers between devices, swap(): return lax.ppermute(x, axis, [(i, i ^ mask) for i in range(count)])  30.5 us
    ppermute x33, starting transfers between devices, swap_plane(): return lax.ppermute(x, ('dp', 'ctx'), pairs)  27.8 us
    dot_general x8, matrix products, dot_last(): lax.dot_general(left, right, (((1,), (1,)), ((), ())), preferred_element_...  21.1 us
    all_gather x1, blocking collectives, on_device(): lax.all_gather(lax.dynamic_slice_in_dim(down_weight, member * piece, piec...  18 us
    unnamed x127, local copies, waits for them, and re-layouts  17.8 us
  transfers between devices with their start and end apart: 63, of which 26 were waited for; matrix products, arithmetic and copies ran while one was open for 27% of the time, Pallas kernels for 9%

profile of v1, /device:TPU:0, one launch (start us, length us, event | category | flops | bytes accessed | tf_op | source)
XLA Modules:
  0.0 507.3 jit_solution(18005156854549621904)
XLA Ops:
  9.4 4.1 collective-permute-start.1
  15.2 3.9 collective-permute-start.6
  34.6 13.2 %collective-permute-done.5 = bf16[240,320]{0,1:T(8,128)(2,1)} collective-permute-done((bf16[240,320]{0,1:T(8,128)(2,1)S(1)}, bf16[240,320]{0,1:T(8,128)(2,1)}, u32[]{:S(2)}, u32[]{:S(2)}) %collective-permute-start.5) | collective-permute-done | bytes 153632 | tf_op jit(solution)/shard_map/ppermute | solution.py:40
  50.4 13.1 %all-gather.6.cloned.1.call-done = bf16[960,960]{1,0:T(8,128)(2,1)} async-done(((bf16[240,960]{1,0:T(8,128)(2,1)}), bf16[960,960]{1,0:T(8,128)(2,1)}) %all-gather.6.cloned.1.call-update) | async-done | bytes 1843216 | tf_op jit(solution)/shard_map/all_gather | solution.py:327
  71.9 10.8 %collective-permute-done.10 = bf16[192,640]{1,0:T(8,128)(2,1)S(1)} collective-permute-done((bf16[192,640]{1,0:T(8,128)(2,1)}, bf16[192,640]{1,0:T(8,128)(2,1)S(1)}, u32[]{:S(2)}, u32[]{:S(2)}) %collective-permute-start.10) | collective-permute-done | bytes 245792 | tf_op jit(solution)/shard_map/ppermute | solution.py:40
  83.9 26.8 %collective-permute-done.9 = bf16[192,640]{1,0:T(8,128)(2,1)S(1)} collective-permute-done((bf16[192,640]{1,0:T(8,128)(2,1)}, bf16[192,640]{1,0:T(8,128)(2,1)S(1)}, u32[]{:S(2)}, u32[]{:S(2)}) %collective-permute-start.9) | collective-permute-done | bytes 245792 | tf_op jit(solution)/shard_map/ppermute | solution.py:40
  113.0 4.9 collective-permute-done.8
  127.6 13.4 %collective-permute-done.11 = bf16[192,640]{1,0:T(8,128)(2,1)S(1)} collective-permute-done((bf16[192,640]{1,0:T(8,128)(2,1)S(1)}, bf16[192,640]{1,0:T(8,128)(2,1)S(1)}, u32[]{:S(2)}, u32[]{:S(2)}) %collective-permute-start.11) | collective-permute-done | bytes 245792 | tf_op jit(solution)/shard_map/ppermute | solution.py:40
  143.9 18.0 %attention_forward.1 = (bf16[192,960]{1,0:T(8,128)(2,1)}, bf16[192,960]{1,0:T(8,128)(2,1)}, f32[5,64,576]{2,1,0:T(8,128)}, f32[5,576]{1,0:T(8,128)}) custom-call(f32[192,960]{1,0:T(8,128)} %fusion.43.query_ref, bf16[1536,640]{1,0:T(8,128)(2,1)} %copy-done.45, s32[1536,1]{1,0:T(8,128)} %add.365.key_pos_ref, s32[1,576]{1,0:T(1,128)} %broadcast_in_dim.69.query_pos_ref, ...), custom_call_target="tpu_custom_call" | custom-call | flops 4529848320 | bytes 4394496 | tf_op jit(solution)/shard_map/attention_forward/pallas_call | solution.py:110
  168.7 9.5 %collective-permute-done.15 = bf16[192,960]{1,0:T(8,128)(2,1)S(1)} collective-permute-done((bf16[192,960]{1,0:T(8,128)(2,1)S(1)}, bf16[192,960]{1,0:T(8,128)(2,1)S(1)}, u32[]{:S(2)}, u32[]{:S(2)}) %collective-permute-start.15) | collective-permute-done | bytes 368672 | tf_op jit(solution)/shard_map/ppermute | solution.py:49
  178.2 6.3 %collective-permute-done.14 = bf16[192,960]{1,0:T(8,128)(2,1)S(1)} collective-permute-done((bf16[192,960]{1,0:T(8,128)(2,1)S(1)}, bf16[192,960]{1,0:T(8,128)(2,1)S(1)}, u32[]{:S(2)}, u32[]{:S(2)}) %collective-permute-start.14) | collective-permute-done | bytes 368672 | tf_op jit(solution)/shard_map/ppermute | solution.py:49
  190.6 18.0 %all_gather.20 = bf16[320,960]{1,0:T(8,128)(2,1)S(1)} all-gather(bf16[80,960]{1,0:T(8,128)(2,1)S(1)} %copy.140), channel_id=1, replica_groups=mesh['dp'=4,'ctx'=2,'fsdp'=4] {'fsdp'}, dimensions={0}, use_global_device_ids=true | all-gather | bytes 768000 | tf_op jit(solution)/shard_map/all_gather | solution.py:349
  214.0 6.6 %concatenate.86 = bf16[1536,960]{0,1:T(8,128)(2,1)} concatenate(bf16[192,960]{0,1:T(8,128)(2,1)S(1)} %copy.131, bf16[192,960]{0,1:T(8,128)(2,1)S(1)} %copy.132, bf16[192,960]{0,1:T(8,128)(2,1)} %copy.133, bf16[192,960]{0,1:T(8,128)(2,1)} %copy.134, bf16[768,960]{0,1:T(8,128)(2,1)} %collective-permute-done.24), dimensions={0} | concatenate | bytes 5898240 | tf_op jit(solution)/shard_map/concatenate | solution.py:430
  229.8 3.4 multiply_convert_fusion.1
  239.4 5.1 %concatenate.83 = bf16[1536,960]{0,1:T(8,128)(2,1)S(1)} concatenate(bf16[192,960]{0,1:T(8,128)(2,1)} %copy.124, bf16[192,960]{0,1:T(8,128)(2,1)} %copy.125, bf16[192,960]{0,1:T(8,128)(2,1)} %copy.126, bf16[192,960]{0,1:T(8,128)(2,1)} %copy.127, bf16[768,960]{0,1:T(8,128)(2,1)} %collective-permute-done.16), dimensions={0} | concatenate | bytes 5898240 | tf_op jit(solution)/shard_map/concatenate | solution.py:427
  244.5 5.0 fusion.11
  249.6 4.1 convolution_convert_fusion.2
  264.6 4.8 fusion.73
  284.3 7.9 %collective-permute-done.28 = bf16[192,960]{1,0:T(8,128)(2,1)} collective-permute-done((bf16[192,960]{1,0:T(8,128)(2,1)}, bf16[192,960]{1,0:T(8,128)(2,1)}, u32[]{:S(2)}, u32[]{:S(2)}) %collective-permute-start.28) | collective-permute-done | bytes 368672 | tf_op jit(solution)/shard_map/ppermute | solution.py:49
  296.6 3.7 collective-permute-done.18
  300.3 9.4 %collective-permute-done.20 = bf16[192,960]{1,0:T(8,128)(2,1)S(1)} collective-permute-done((bf16[192,960]{1,0:T(8,128)(2,1)S(1)}, bf16[192,960]{1,0:T(8,128)(2,1)S(1)}, u32[]{:S(2)}, u32[]{:S(2)}) %collective-permute-start.20) | collective-permute-done | bytes 368672 | tf_op jit(solution)/shard_map/ppermute | solution.py:49
  319.8 21.9 %attention_backward.1 = (bf16[192,960]{1,0:T(8,128)(2,1)}, bf16[1536,640]{1,0:T(8,128)(2,1)}) custom-call(bf16[192,960]{1,0:T(8,128)(2,1)} %get-tuple-element.18.queries_ref, bf16[1536,640]{1,0:T(8,128)(2,1)} %copy-done.45, s32[1536,1]{1,0:T(8,128)} %add.365.key_pos_ref, s32[1,576]{1,0:T(1,128)} %broadcast_in_dim.69.query_pos_ref, ...), custom_call_target="tpu_custom_call" | custom-call | flops 11324620800 | bytes 5991936 | tf_op jit(solution)/shard_map/attention_backward/pallas_call | solution.py:110
  356.8 18.8 %collective-permute-done.29 = bf16[4,192,640]{2,1,0:T(8,128)(2,1)} collective-permute-done((bf16[4,192,640]{2,1,0:T(8,128)(2,1)}, bf16[4,192,640]{2,1,0:T(8,128)(2,1)}, u32[]{:S(2)}, u32[]{:S(2)}) %collective-permute-start.29) | collective-permute-done | bytes 983072 | tf_op jit(solution)/shard_map/ppermute | solution.py:40
  387.7 22.1 %collective-permute-done.43 = bf16[120,960]{1,0:T(8,128)(2,1)S(1)} collective-permute-done((bf16[120,960]{1,0:T(8,128)(2,1)S(1)}, bf16[120,960]{1,0:T(8,128)(2,1)S(1)}, u32[]{:S(2)}, u32[]{:S(2)}) %collective-permute-start.43) | collective-permute-done | bytes 230432 | tf_op jit(solution)/shard_map/ppermute | solution.py:40
  412.7 5.6 %collective-permute-done.31.two_ref = bf16[192,640]{1,0:T(8,128)(2,1)S(1)} collective-permute-done((bf16[192,640]{1,0:T(8,128)(2,1)S(1)}, bf16[192,640]{1,0:T(8,128)(2,1)S(1)}, u32[]{:S(2)}, u32[]{:S(2)}) %collective-permute-start.31) | collective-permute-done | bytes 245792 | tf_op jit(solution)/shard_map/ppermute | solution.py:40
  434.4 5.5 %collective-permute-done.46 = bf16[120,960]{1,0:T(8,128)(2,1)S(1)} collective-permute-done((bf16[120,960]{1,0:T(8,128)(2,1)S(1)}, bf16[120,960]{1,0:T(8,128)(2,1)S(1)}, u32[]{:S(2)}, u32[]{:S(2)}) %collective-permute-start.46) | collective-permute-done | bytes 230432 | tf_op jit(solution)/shard_map/ppermute | solution.py:49
  452.0 4.6 collective-permute-done.36
  456.6 7.2 %collective-permute-done.35 = bf16[248,320]{0,1:T(8,128)(2,1)S(1)} collective-permute-done((bf16[248,320]{0,1:T(8,128)(2,1)S(1)}, bf16[248,320]{0,1:T(8,128)(2,1)S(1)}, u32[]{:S(2)}, u32[]{:S(2)}) %collective-permute-start.35) | collective-permute-done | bytes 158752 | tf_op jit(solution)/shard_map/ppermute | solution.py:40
  467.4 4.5 collective-permute-done.39
  477.9 4.3 copy.128
  482.1 6.1 %reshape.464 = bf16[8,240,2,4,80]{1,0,4,3,2:T(8,128)(2,1)S(1)} reshape(bf16[1920,640]{0,1:T(8,128)(2,1)} %copy.128) | data formatting | bytes 4915200 | tf_op jit(solution)/shard_map/reshape | solution.py:443
  492.9 4.1 copy.129
  (362 shorter events, 194.6 us)
Async XLA Ops:
  7.2 56.3 %all-gather.6.cloned.1.call-start = ((), (), s32[]{:S(2)}) async-start(), calls=%async_computation.2 | async-start | bytes 2457600 | tf_op jit(solution)/shard_map/all_gather | solution.py:327
  9.3 211.3 %all-gather.8.cloned.1.call-start = ((), (), s32[]{:S(2)}) async-start(), calls=%async_computation.3 | async-start | bytes 1536000 | tf_op jit(solution)/shard_map/all_gather | solution.py:345
  15.1 35.1 %collective-permute-start.2 = (bf16[2,240]{1,0:T(2,128)(2,1)S(1)}, bf16[2,240]{1,0:T(2,128)(2,1)S(1)}, u32[]{:S(2)}, u32[]{:S(2)}) collective-permute-start(bf16[2,240]{1,0:T(2,128)(2,1)S(1)} %get-tuple-element.79), channel_id=1, source_target_pairs={{0,3},{1,2},{2,1},{3,0},{4,7},{5,6},{6,5},{7,4},{8,11},{9,10},{10,... | collective-permute-start | bytes 2888 | tf_op jit(solution)/shard_map/ppermute | solution.py:40
  19.0 28.7 %collective-permute-start.5 = (bf16[240,320]{0,1:T(8,128)(2,1)S(1)}, bf16[240,320]{0,1:T(8,128)(2,1)}, u32[]{:S(2)}, u32[]{:S(2)}) collective-permute-start(bf16[240,320]{0,1:T(8,128)(2,1)S(1)} %broadcast_select_fusion.11), channel_id=1, source_target_pairs={{0,2},{1,3},{2,0},{3,1},{4,6},{5,7},{6,4},{7,5},{8,10},{9,11},{10,... | collective-permute-start | bytes 460808 | tf_op jit(solution)/shard_map/ppermute | solution.py:40
  25.1 236.7 %reduce-scatter.5.cloned.1.call-start = ((), (), s32[]{:S(2)}) async-start(), calls=%async_computation.5 | async-start | bytes 819200 | tf_op jit(solution)/shard_map/reduce_scatter | solution.py:434
  30.3 90.1 %collective-permute-start.23 = (bf16[192,960]{1,0:T(8,128)(2,1)S(1)}, bf16[192,960]{1,0:T(8,128)(2,1)}, u32[]{:S(2)}, u32[]{:S(2)}) collective-permute-start(bf16[192,960]{1,0:T(8,128)(2,1)S(1)} %bitcast.150), channel_id=1, source_target_pairs={{0,20},{4,16},{8,28},{12,24},{16,4},{20,0},{24,12},{28,8},{1,21},{... | collective-permute-start | bytes 1105928 | tf_op jit(solution)/shard_map/ppermute | solution.py:49
  33.0 87.4 %collective-permute-start.22 = (bf16[192,960]{1,0:T(8,128)(2,1)S(1)}, bf16[192,960]{1,0:T(8,128)(2,1)}, u32[]{:S(2)}, u32[]{:S(2)}) collective-permute-start(bf16[192,960]{1,0:T(8,128)(2,1)S(1)} %bitcast.151), channel_id=1, source_target_pairs={{0,4},{4,0},{8,12},{12,8},{16,20},{20,16},{24,28},{28,24},{1,5},{5... | collective-permute-start | bytes 1105928 | tf_op jit(solution)/shard_map/ppermute | solution.py:49
  63.5 78.8 %collective-permute-start.3 = (bf16[960,960]{1,0:T(8,128)(2,1)}, bf16[960,960]{1,0:T(8,128)(2,1)}, u32[]{:S(2)}, u32[]{:S(2)}) collective-permute-start(bf16[960,960]{1,0:T(8,128)(2,1)} %all-gather.6.cloned.1.call-done), channel_id=1, source_target_pairs={{0,8},{4,12},{8,0},{12,4},{16,24},{20,28},{24,16},{28,20},{1,9},{5... | collective-permute-start | bytes 5529608 | tf_op jit(solution)/shard_map/ppermute | solution.py:49
  71.8 38.9 %collective-permute-start.9 = (bf16[192,640]{1,0:T(8,128)(2,1)}, bf16[192,640]{1,0:T(8,128)(2,1)S(1)}, u32[]{:S(2)}, u32[]{:S(2)}) collective-permute-start(bf16[192,640]{1,0:T(8,128)(2,1)} %keys_values.1), channel_id=1, source_target_pairs={{0,2},{1,3},{2,0},{3,1},{4,6},{5,7},{6,4},{7,5},{8,10},{9,11},{10,... | collective-permute-start | bytes 737288 | tf_op jit(solution)/shard_map/ppermute | solution.py:40
  82.7 37.7 %collective-permute-start.21 = (bf16[192,960]{1,0:T(8,128)(2,1)S(1)}, bf16[192,960]{1,0:T(8,128)(2,1)}, u32[]{:S(2)}, u32[]{:S(2)}) collective-permute-start(bf16[192,960]{1,0:T(8,128)(2,1)S(1)} %bitcast.152), channel_id=1, source_target_pairs={{0,16},{4,20},{8,24},{12,28},{16,0},{20,4},{24,8},{28,12},{1,17},{... | collective-permute-start | bytes 1105928 | tf_op jit(solution)/shard_map/ppermute | solution.py:49
  118.9 22.2 %collective-permute-start.12 = (bf16[576,640]{1,0:T(8,128)(2,1)}, bf16[576,640]{1,0:T(8,128)(2,1)}, u32[]{:S(2)}, u32[]{:S(2)}) collective-permute-start(bf16[576,640]{1,0:T(8,128)(2,1)} %pad_maximum_fusion.2), channel_id=1, source_target_pairs={{0,4},{4,0},{1,5},{5,1},{2,6},{6,2},{3,7},{7,3},{8,12},{12,8},{9,1... | collective-permute-start | bytes 2211848 | tf_op jit(solution)/shard_map/ppermute | solution.py:40
  124.0 90.0 %collective-permute-start.24 = (bf16[768,960]{0,1:T(8,128)(2,1)}, bf16[768,960]{0,1:T(8,128)(2,1)}, u32[]{:S(2)}, u32[]{:S(2)}) collective-permute-start(bf16[768,960]{0,1:T(8,128)(2,1)} %copy.114), channel_id=1, source_target_pairs={{0,8},{4,12},{8,0},{12,4},{16,24},{20,28},{24,16},{28,20},{1,9},{5... | collective-permute-start | bytes 4423688 | tf_op jit(solution)/shard_map/ppermute | solution.py:49
  190.0 36.9 %collective-permute-start.16 = (bf16[768,960]{0,1:T(8,128)(2,1)}, bf16[768,960]{0,1:T(8,128)(2,1)}, u32[]{:S(2)}, u32[]{:S(2)}) collective-permute-start(bf16[768,960]{0,1:T(8,128)(2,1)} %copy.111), channel_id=1, source_target_pairs={{0,8},{4,12},{8,0},{12,4},{16,24},{20,28},{24,16},{28,20},{1,9},{5... | collective-permute-start | bytes 4423688 | tf_op jit(solution)/shard_map/ppermute | solution.py:49
  235.3 112.5 %reduce-scatter.3.cloned.1.call-start = ((), (), s32[]{:S(2)}) async-start(), calls=%async_computation.4 | async-start | bytes 1536000 | tf_op jit(solution)/shard_map/reduce_scatter | solution.py:433
  249.5 191.6 %all-gather.10.cloned.1.call-start = ((), (), s32[]{:S(2)}) async-start(), calls=%async_computation.6 | async-start | bytes 1474560 | tf_op jit(solution)/shard_map/all_gather | solution.py:442
  261.8 216.1 %all-gather.12.cloned.1.call-start = ((), (), s32[]{:S(2)}) async-start(), calls=%async_computation.7 | async-start | bytes 2764800 | tf_op jit(solution)/shard_map/all_gather | solution.py:441
  280.3 29.5 %collective-permute-start.20 = (bf16[192,960]{1,0:T(8,128)(2,1)S(1)}, bf16[192,960]{1,0:T(8,128)(2,1)S(1)}, u32[]{:S(2)}, u32[]{:S(2)}) collective-permute-start(bf16[192,960]{1,0:T(8,128)(2,1)S(1)} %get-tuple-element.94), channel_id=1, source_target_pairs={{0,20},{4,16},{8,28},{12,24},{16,4},{20,0},{24,12},{28,8},{1,21},{... | collective-permute-start | bytes 1105928 | tf_op jit(solution)/shard_map/ppermute | solution.py:49
  282.8 28.4 %collective-permute-start.19 = (bf16[192,960]{1,0:T(8,128)(2,1)S(1)}, bf16[192,960]{1,0:T(8,128)(2,1)S(1)}, u32[]{:S(2)}, u32[]{:S(2)}) collective-permute-start(bf16[192,960]{1,0:T(8,128)(2,1)S(1)} %get-tuple-element.95), channel_id=1, source_target_pairs={{0,4},{4,0},{8,12},{12,8},{16,20},{20,16},{24,28},{28,24},{1,5},{5... | collective-permute-start | bytes 1105928 | tf_op jit(solution)/shard_map/ppermute | solution.py:49
  316.7 31.1 %collective-permute-start.49 = (bf16[4,120,960]{2,1,0:T(8,128)(2,1)}, bf16[4,120,960]{2,1,0:T(8,128)(2,1)}, u32[]{:S(2)}, u32[]{:S(2)}) collective-permute-start(bf16[4,120,960]{2,1,0:T(8,128)(2,1)} %dynamic-slice_bitcast_fusion), channel_id=1, source_target_pairs={{0,8},{4,12},{8,0},{12,4},{16,24},{20,28},{24,16},{28,20},{1,9},{5... | collective-permute-start | bytes 2764808 | tf_op jit(solution)/shard_map/ppermute | solution.py:49
  346.0 29.5 %collective-permute-start.29 = (bf16[4,192,640]{2,1,0:T(8,128)(2,1)}, bf16[4,192,640]{2,1,0:T(8,128)(2,1)}, u32[]{:S(2)}, u32[]{:S(2)}) collective-permute-start(bf16[4,192,640]{2,1,0:T(8,128)(2,1)} %bitcast.31), channel_id=1, source_target_pairs={{0,4},{4,0},{1,5},{5,1},{2,6},{6,2},{3,7},{7,3},{8,12},{12,8},{9,1... | collective-permute-start | bytes 2949128 | tf_op jit(solution)/shard_map/ppermute | solution.py:40
  349.8 29.8 %collective-permute-start.50 = (bf16[120,960]{1,0:T(8,128)(2,1)S(1)}, bf16[120,960]{1,0:T(8,128)(2,1)S(1)}, u32[]{:S(2)}, u32[]{:S(2)}) collective-permute-start(bf16[120,960]{1,0:T(8,128)(2,1)S(1)} %get-tuple-element.96), channel_id=1, source_target_pairs={{0,1},{1,0},{2,3},{3,2},{4,5},{5,4},{6,7},{7,6},{8,9},{9,8},{10,11... | collective-permute-start | bytes 691208 | tf_op jit(solution)/shard_map/ppermute | solution.py:40
  350.7 28.9 %collective-permute-start.52 = (bf16[120,960]{1,0:T(8,128)(2,1)S(1)}, bf16[120,960]{1,0:T(8,128)(2,1)S(1)}, u32[]{:S(2)}, u32[]{:S(2)}) collective-permute-start(bf16[120,960]{1,0:T(8,128)(2,1)S(1)} %get-tuple-element.97), channel_id=1, source_target_pairs={{0,3},{1,2},{2,1},{3,0},{4,7},{5,6},{6,5},{7,4},{8,11},{9,10},{10,... | collective-permute-start | bytes 691208 | tf_op jit(solution)/shard_map/ppermute | solution.py:40
  352.7 29.0 %collective-permute-start.51 = (bf16[120,960]{1,0:T(8,128)(2,1)S(1)}, bf16[120,960]{1,0:T(8,128)(2,1)S(1)}, u32[]{:S(2)}, u32[]{:S(2)}) collective-permute-start(bf16[120,960]{1,0:T(8,128)(2,1)S(1)} %get-tuple-element.98), channel_id=1, source_target_pairs={{0,2},{1,3},{2,0},{3,1},{4,6},{5,7},{6,4},{7,5},{8,10},{9,11},{10,... | collective-permute-start | bytes 691208 | tf_op jit(solution)/shard_map/ppermute | solution.py:40
  355.0 28.8 %collective-permute-start.42 = (bf16[120,960]{1,0:T(8,128)(2,1)S(1)}, bf16[120,960]{1,0:T(8,128)(2,1)S(1)}, u32[]{:S(2)}, u32[]{:S(2)}) collective-permute-start(bf16[120,960]{1,0:T(8,128)(2,1)S(1)} %get-tuple-element.99), channel_id=1, source_target_pairs={{0,1},{1,0},{2,3},{3,2},{4,5},{5,4},{6,7},{7,6},{8,9},{9,8},{10,11... | collective-permute-start | bytes 691208 | tf_op jit(solution)/shard_map/ppermute | solution.py:40
  379.6 30.2 %collective-permute-start.43 = (bf16[120,960]{1,0:T(8,128)(2,1)S(1)}, bf16[120,960]{1,0:T(8,128)(2,1)S(1)}, u32[]{:S(2)}, u32[]{:S(2)}) collective-permute-start(bf16[120,960]{1,0:T(8,128)(2,1)S(1)} %get-tuple-element.101), channel_id=1, source_target_pairs={{0,2},{1,3},{2,0},{3,1},{4,6},{5,7},{6,4},{7,5},{8,10},{9,11},{10,... | collective-permute-start | bytes 691208 | tf_op jit(solution)/shard_map/ppermute | solution.py:40
  379.6 31.4 %collective-permute-start.32 = (bf16[192,640]{1,0:T(8,128)(2,1)S(1)}, bf16[192,640]{1,0:T(8,128)(2,1)S(1)}, u32[]{:S(2)}, u32[]{:S(2)}) collective-permute-start(bf16[192,640]{1,0:T(8,128)(2,1)S(1)} %get-tuple-element.102), channel_id=1, source_target_pairs={{0,3},{1,2},{2,1},{3,0},{4,7},{5,6},{6,5},{7,4},{8,11},{9,10},{10,... | collective-permute-start | bytes 737288 | tf_op jit(solution)/shard_map/ppermute | solution.py:40
  381.7 36.5 %collective-permute-start.31 = (bf16[192,640]{1,0:T(8,128)(2,1)S(1)}, bf16[192,640]{1,0:T(8,128)(2,1)S(1)}, u32[]{:S(2)}, u32[]{:S(2)}) collective-permute-start(bf16[192,640]{1,0:T(8,128)(2,1)S(1)} %get-tuple-element.103), channel_id=1, source_target_pairs={{0,2},{1,3},{2,0},{3,1},{4,6},{5,7},{6,4},{7,5},{8,10},{9,11},{10,... | collective-permute-start | bytes 737288 | tf_op jit(solution)/shard_map/ppermute | solution.py:40
  383.9 36.4 %collective-permute-start.30 = (bf16[192,640]{1,0:T(8,128)(2,1)S(1)}, bf16[192,640]{1,0:T(8,128)(2,1)S(1)}, u32[]{:S(2)}, u32[]{:S(2)}) collective-permute-start(bf16[192,640]{1,0:T(8,128)(2,1)S(1)} %get-tuple-element.104), channel_id=1, source_target_pairs={{0,1},{1,0},{2,3},{3,2},{4,5},{5,4},{6,7},{7,6},{8,9},{9,8},{10,11... | collective-permute-start | bytes 737288 | tf_op jit(solution)/shard_map/ppermute | solution.py:40
  386.3 45.1 %collective-permute-start.55 = (bf16[120,960]{1,0:T(8,128)(2,1)S(1)}, bf16[120,960]{1,0:T(8,128)(2,1)}, u32[]{:S(2)}, u32[]{:S(2)}) collective-permute-start(bf16[120,960]{1,0:T(8,128)(2,1)S(1)} %fusion.48), channel_id=1, source_target_pairs={{0,20},{4,16},{8,28},{12,24},{16,4},{20,0},{24,12},{28,8},{1,21},{... | collective-permute-start | bytes 691208 | tf_op jit(solution)/shard_map/ppermute | solution.py:49
  409.8 22.2 %collective-permute-start.54 = (bf16[120,960]{1,0:T(8,128)(2,1)S(1)}, bf16[120,960]{1,0:T(8,128)(2,1)}, u32[]{:S(2)}, u32[]{:S(2)}) collective-permute-start(bf16[120,960]{1,0:T(8,128)(2,1)S(1)} %fusion.48), channel_id=1, source_target_pairs={{0,4},{4,0},{8,12},{12,8},{16,20},{20,16},{24,28},{28,24},{1,5},{5... | collective-permute-start | bytes 691208 | tf_op jit(solution)/shard_map/ppermute | solution.py:49
  411.0 22.0 %collective-permute-start.53 = (bf16[120,960]{1,0:T(8,128)(2,1)S(1)}, bf16[120,960]{1,0:T(8,128)(2,1)}, u32[]{:S(2)}, u32[]{:S(2)}) collective-permute-start(bf16[120,960]{1,0:T(8,128)(2,1)S(1)} %fusion.48), channel_id=1, source_target_pairs={{0,16},{4,20},{8,24},{12,28},{16,0},{20,4},{24,8},{28,12},{1,17},{... | collective-permute-start | bytes 691208 | tf_op jit(solution)/shard_map/ppermute | solution.py:49
  441.1 26.3 %collective-permute-start.48 = (bf16[120,960]{1,0:T(8,128)(2,1)S(1)}, bf16[120,960]{1,0:T(8,128)(2,1)S(1)}, u32[]{:S(2)}, u32[]{:S(2)}) collective-permute-start(bf16[120,960]{1,0:T(8,128)(2,1)S(1)} %add_convert_fusion.2), channel_id=1, source_target_pairs={{0,8},{4,12},{8,0},{12,4},{16,24},{20,28},{24,16},{28,20},{1,9},{5... | collective-permute-start | bytes 691208 | tf_op jit(solution)/shard_map/ppermute | solution.py:49
  (89 other events, 1142.5 us)
Sparse Core Ops, SparseCore 0:
  10.2 53.2 all-gather.5
  65.6 47.4 all-gather.7
  235.4 21.5 reduce-scatter.4
  259.2 28.9 reduce-scatter.2
  290.1 32.4 all-gather.9
  347.9 33.9 all-gather.11

commit v2 on v1

v2 whole, which is shorter than its diff:
```python
import functools
import math

import jax
import jax.numpy as jnp
from jax import lax
from jax.experimental import pallas as pl
from jax.experimental.pallas import tpu as pltpu
from jax.sharding import PartitionSpec as P

HEADS = 15
KV_HEADS = 5
HEAD_DIM = 64
GROUPS = HEADS // KV_HEADS
LANES = 128

EPSILON = 1e-05
ROPE_BASE = 100000.0
MASKED = -1e30

F32 = jnp.float32
BF16 = jnp.bfloat16
VMEM_LIMIT = 56 * 1024 * 1024


def dot_plain(left, right):
    return jnp.dot(left, right, preferred_element_type=F32)


def dot_last(left, right):
    return lax.dot_general(left, right, (((1,), (1,)), ((), ())), preferred_element_type=F32)


def dot_first(left, right):
    return lax.dot_general(left, right, (((0,), (0,)), ((), ())), preferred_element_type=F32)


def swap(x, axis, mask):
    count = lax.axis_size(axis)
    return lax.ppermute(x, axis, [(i, i ^ mask) for i in range(count)])


def swap_plane(x, dp_mask, ctx_mask):
    ctx_count = lax.axis_size("ctx")
    pairs = []
    for d in range(lax.axis_size("dp")):
        for c in range(ctx_count):
            pairs.append((d * ctx_count + c, (d ^ dp_mask) * ctx_count + (c ^ ctx_mask)))
    return lax.ppermute(x, ("dp", "ctx"), pairs)


def swap_core(x):
    return swap_plane(x, 1, 0)


CHIP_MASKS = ((2, 0), (0, 1), (2, 1))


def plane_pieces(x):
    mine = [x] + [swap_plane(x, a, b) for a, b in CHIP_MASKS]
    return mine, [swap_core(piece) for piece in mine]


def sum_far(x):
    count = lax.axis_size("ctx")
    if count == 2:
        return x
    groups = [list(range(0, count, 2)), list(range(1, count, 2))]
    return lax.psum(x.astype(F32), "ctx", axis_index_groups=groups).astype(x.dtype)


def call(kernel, spots, args, out_shapes, scratch=(), flops=0, name=None):
    specs = [pl.BlockSpec(memory_space=pltpu.SMEM)]
    specs += [pl.BlockSpec(memory_space=pltpu.VMEM) for _ in args]
    outs = tuple(jax.ShapeDtypeStruct(s, d) for s, d in out_shapes)
    bytes_all = sum(a.size * a.dtype.itemsize for a in args) + sum(
        math.prod(s) * jnp.dtype(d).itemsize for s, d in out_shapes
    )
    return pl.pallas_call(
        kernel,
        out_shape=outs,
        in_specs=specs,
        out_specs=tuple(pl.BlockSpec(memory_space=pltpu.VMEM) for _ in outs),
        scratch_shapes=[pltpu.VMEM(s, d) for s, d in scratch],
        compiler_params=pltpu.CompilerParams(vmem_limit_bytes=VMEM_LIMIT),
        cost_estimate=pl.CostEstimate(flops=flops, bytes_accessed=bytes_all, transcendentals=0),
        name=name,
    )(spots, *args)


def split_refs(refs, *counts):
    out, at = [], 0
    for n in counts:
        out.append(refs[at : at + n])
        at += n
    assert at == len(refs)
    return out


def lane_blocks(values, count):
    size = values.shape[1] // count
    return [values[:, i * size : (i + 1) * size] for i in range(count)]


def join_lanes(ref):
    return jnp.concatenate([ref[i] for i in range(ref.shape[0])], axis=1)


def rope_lanes(values, cosine, sine):
    rows, width = values.shape
    lane = lax.broadcasted_iota(jnp.int32, (rows, LANES), 1)
    first_half = (lane % HEAD_DIM) < (HEAD_DIM // 2)
    out = []
    for start in range(0, width, LANES):
        piece = values[:, start : min(start + LANES, width)]
        size = piece.shape[1]
        if size < LANES:
            piece = jnp.concatenate([piece, jnp.zeros((rows, LANES - size), piece.dtype)], axis=1)
        ahead = pltpu.roll(piece, LANES - HEAD_DIM // 2, 1)
        behind = pltpu.roll(piece, HEAD_DIM // 2, 1)
        partner = jnp.where(first_half, ahead, behind)
        out.append((piece * cosine + partner * sine)[:, :size])
    return jnp.concatenate(out, axis=1)


def heads_of(ref, first, count, rows=None):
    out = []
    for h in range(first, first + count):
        start = (h * HEAD_DIM) // LANES * LANES
        stop = min(start + LANES, ref.shape[-1])
        pair = ref[:, start:stop] if rows is None else ref[rows, start:stop]
        at = h * HEAD_DIM - start
        out.append(pair[:, at : at + HEAD_DIM])
    return out[0] if count == 1 else jnp.concatenate(out, axis=0)


def stack_rows(scratch, pieces):
    rows = pieces[0].shape[0]
    for i, piece in enumerate(pieces):
        scratch[i * rows : (i + 1) * rows, :] = piece[...]


def norm_rows(values, gain):
    inverse = lax.rsqrt(jnp.mean(values * values, axis=-1, keepdims=True) + EPSILON)
    return (values * inverse * gain, inverse)


def norm_back(gradient, values, inverse, gain):
    scaled = gradient * gain
    inner_mean = jnp.mean(scaled * values, axis=-1, keepdims=True)
    return inverse * scaled - values * (inverse * inverse * inverse) * inner_mean


EXTRA_ROWS = 16


def pack_kernel(shards, members, spots, gate_ref, up_ref, down_ref, out_ref):
    member = spots[3]
    span = gate_ref.shape[1] // shards
    piece = span // members
    rows = gate_ref.shape[0]
    pick = (
        lax.broadcasted_iota(jnp.int32, (span, piece), 0)
        == lax.broadcasted_iota(jnp.int32, (span, piece), 1) + member * piece
    ).astype(BF16)
    out = []
    for ref in (gate_ref, up_ref):
        for z in range(shards):
            out.append(dot_plain(ref[:, z * span : (z + 1) * span], pick))
    own = down_ref[pl.ds(pl.multiple_of(member * piece, piece), piece), :]
    folds = rows // piece
    down = jnp.concatenate(lane_blocks(own, folds), axis=0)
    both = jnp.concatenate(out, axis=1).astype(BF16)
    out_ref[...] = jnp.concatenate([both, down], axis=1)


def begin_kernel(shards, spots, *refs):
    ins, outs, scratch = split_refs(refs, 7 + 2 * (shards - 1), 4, 3)
    tokens_ref, gain_one, gain_two, key_ref, value_ref, cos_ref, sin_ref = ins[:7]
    mine, other = split_refs(ins[7:], shards - 1, shards - 1)
    kv_ref, normed_ref, inverse_ref, gains_ref = outs
    blocks, normed_blocks, gain_blocks = scratch
    core, shard = spots[0], spots[1]
    rows = key_ref.shape[0]
    values = tokens_ref[...].astype(F32)
    inverse = lax.rsqrt(jnp.mean(values * values, axis=-1, keepdims=True) + EPSILON)
    inverse_ref[...] = inverse
    for z, block in enumerate(lane_blocks(values * inverse, shards)):
        blocks[z] = block
    sums = []
    for r in range(shards):
        at = shard ^ r
        if r == 0:
            pair = jnp.concatenate([gain_one[...], gain_two[...]], axis=0).astype(F32)
        else:
            pair = mine[r - 1][rows : rows + EXTRA_ROWS, :rows].astype(F32)[0:2, :]
        gain_blocks[at, 0:2, :] = pair
        normed = (blocks[at] * pair[0:1, :]).astype(BF16)
        normed_blocks[at] = normed
        left = key_ref[...] if r == 0 else mine[r - 1][:rows, :]
        right = value_ref[...] if r == 0 else other[r - 1][:rows, :]
        sums.append((dot_plain(normed, left), dot_plain(normed, right)))
    first = sum(s[0] for s in sums[1:])
    second = sum(s[1] for s in sums[1:])
    keys = jnp.where(core == 0, first, second) + sums[0][0]
    vals = jnp.where(core == 0, second, first) + sums[0][1]
    keys = rope_lanes(keys, cos_ref[...], sin_ref[...])
    kv_ref[...] = jnp.concatenate([keys, vals], axis=1).astype(BF16)
    normed_ref[...] = join_lanes(normed_blocks)
    gains_ref[...] = jnp.zeros_like(gains_ref)
    gains_ref[0:2, :] = jnp.concatenate([gain_blocks[z][0:2, :] for z in range(shards)], axis=1)


def attend(chunk, head, kv_ref, key_pos_ref, query_pos, stacked, state):
    def step(j, state):
        largest, total, weighted = state
        at = pl.ds(pl.multiple_of(j * chunk, chunk), chunk)
        keys = heads_of(kv_ref, head, 1, at)
        values = heads_of(kv_ref, KV_HEADS + head, 1, at)
        scores = dot_last(keys, stacked)
        scores = jnp.where(key_pos_ref[at, :] <= query_pos, scores, MASKED)
        new_largest = jnp.maximum(largest, jnp.max(scores, axis=0, keepdims=True))
        weights = jnp.exp(scores - new_largest)
        factor = jnp.exp(largest - new_largest)
        total = total * factor + jnp.sum(weights, axis=0, keepdims=True)
        weighted = weighted * factor + dot_first(values, weights.astype(BF16))
        return new_largest, total, weighted

    return lax.fori_loop(0, kv_ref.shape[0] // chunk, step, state)


def near_kernel(chunk, members, pieces, spots, *refs):
    ins, outs, scratch = split_refs(refs, 5 + members + pieces, 4, 2)
    normed_ref, key_pos_ref, query_pos_ref, cos_ref, sin_ref = ins[:5]
    weights, parts = split_refs(ins[5:], members, pieces)
    queries_ref, largest_ref, total_ref, weighted_ref = outs
    blocks, kv_ref = scratch
    dp = spots[2]
    stack_rows(kv_ref, parts)
    for j in range(members):
        blocks[dp ^ j] = dot_plain(normed_ref[...], weights[j][...])
    roped = rope_lanes(join_lanes(blocks), cos_ref[...], sin_ref[...]).astype(BF16)
    queries_ref[...] = roped * jnp.asarray(1.0 / math.sqrt(HEAD_DIM), BF16)
    columns = GROUPS * queries_ref.shape[0]
    query_pos = query_pos_ref[...]
    for head in range(KV_HEADS):
        stacked = heads_of(queries_ref, head * GROUPS, GROUPS)
        start = (
            jnp.full((1, columns), MASKED, F32),
            jnp.zeros((1, columns), F32),
            jnp.zeros((HEAD_DIM, columns), F32),
        )
        largest, total, weighted = attend(
            chunk, head, kv_ref, key_pos_ref, query_pos, stacked, start
        )
        largest_ref[head : head + 1, :] = largest
        total_ref[head : head + 1, :] = total
        weighted_ref[head] = weighted


def far_kernel(chunk, members, pieces, spots, *refs):
    ins, outs, scratch = split_refs(refs, 8 + members + pieces, 6, 2)
    (queries_ref, key_pos_ref, query_pos_ref, largest_ref, total_ref, weighted_ref, tokens_ref,
     gains_ref) = ins[:8]
    weights, parts = split_refs(ins[8:], members, pieces)
    attended_ref, turned_ref, log_ref, residual_ref, inverse_ref, normed_ref = outs
    blocks, kv_ref = scratch
    dp = spots[2]
    stack_rows(kv_ref, parts)
    rows = queries_ref.shape[0]
    query_pos = query_pos_ref[...]
    heads = []
    for head in range(KV_HEADS):
        stacked = heads_of(queries_ref, head * GROUPS, GROUPS)
        start = (largest_ref[head : head + 1, :], total_ref[head : head + 1, :], weighted_ref[head])
        largest, total, weighted = attend(
            chunk, head, kv_ref, key_pos_ref, query_pos, stacked, start
        )
        turned = weighted / total
        turned_ref[head] = turned
        log_ref[head : head + 1, :] = largest + jnp.log(total)
        straight = turned.T
        heads += [straight[g * rows : (g + 1) * rows, :] for g in range(GROUPS)]
    attended = jnp.concatenate(heads, axis=1).astype(BF16)
    attended_ref[...] = attended
    for j in range(members):
        blocks[dp ^ j] = dot_plain(attended, weights[j][...])
    residual = tokens_ref[...].astype(F32) + join_lanes(blocks)
    residual_ref[...] = residual
    normed, inverse = norm_rows(residual, gains_ref[1:2, :])
    inverse_ref[...] = inverse
    normed_ref[...] = normed.astype(BF16)


def unfold_down(pack_ref, down_ref, shards, part):
    piece = part // shards
    folds = (pack_ref.shape[0] // shards) // piece
    for z in range(shards):
        base = z * folds * piece
        down_ref[z * piece : (z + 1) * piece, :] = jnp.concatenate(
            [pack_ref[base + b * piece : base + (b + 1) * piece, 2 * part :] for b in range(folds)],
            axis=1,
        )


def feed_kernel(shards, pieces, spots, *refs):
    ins, outs, scratch = split_refs(refs, 1 + 2 * pieces, pieces + 2, 3)
    pack_ref = ins[0]
    normed_parts, cot_parts = split_refs(ins[1:], pieces, pieces)
    grads, (act_ref, both_ref) = outs[:pieces], outs[pieces:]
    normed_ref, cot_ref, down_ref = scratch
    part = pack_ref.shape[1] // 3
    rows = normed_parts[0].shape[0]
    stack_rows(normed_ref, normed_parts)
    stack_rows(cot_ref, cot_parts)
    unfold_down(pack_ref, down_ref, shards, part)
    gate_up = dot_plain(normed_ref[...], pack_ref[:, : 2 * part])
    gate, upward = gate_up[:, :part], gate_up[:, part:]
    act_grad = dot_last(cot_ref[...], down_ref[...])
    sigmoid_gate = jax.nn.sigmoid(gate)
    silu = gate * sigmoid_gate
    act_ref[...] = (silu * upward).astype(BF16)
    gate_grad = act_grad * upward * sigmoid_gate * (1.0 + gate * (1.0 - sigmoid_gate))
    both_ref[...] = jnp.concatenate([gate_grad, act_grad * silu], axis=1).astype(BF16)
    grad = dot_last(both_ref[...], pack_ref[:, : 2 * part])
    for i in range(pieces):
        grads[i][...] = grad[i * rows : (i + 1) * rows, :].astype(BF16)


def feed_weights_kernel(shards, pieces, spots, *refs):
    ins, outs, scratch = split_refs(refs, 5 + 2 * pieces, pieces + 1, 5)
    pack_ref, act_a, act_b, both_a, both_b = ins[:5]
    normed_parts, cot_parts = split_refs(ins[5:], pieces, pieces)
    results, grad_ref = outs[:pieces], outs[pieces]
    normed_ref, cot_ref, act_ref, both_ref, down_ref = scratch
    part = pack_ref.shape[1] // 3
    piece = part // shards
    rows = normed_parts[0].shape[0]
    stack_rows(normed_ref, normed_parts)
    stack_rows(cot_ref, cot_parts)
    stack_rows(act_ref, (act_a, act_b))
    stack_rows(both_ref, (both_a, both_b))
    unfold_down(pack_ref, down_ref, shards, part)
    grad_ref[:, : 2 * part] = dot_first(normed_ref[...], both_ref[...]).astype(BF16)
    down_grad = dot_first(act_ref[...], cot_ref[...]).astype(BF16)
    folds = (grad_ref.shape[0] // shards) // piece
    for z in range(shards):
        rows_of = down_grad[z * piece : (z + 1) * piece, :]
        for b, block in enumerate(lane_blocks(rows_of, folds)):
            base = (z * folds + b) * piece
            grad_ref[base : base + piece, 2 * part :] = block
    result = dot_plain(act_ref[...], down_ref[...])
    for i in range(pieces):
        results[i][...] = result[i * rows : (i + 1) * rows, :].astype(BF16)


def middle_kernel(members, spots, *refs):
    ins, outs, scratch = split_refs(refs, 9 + members, 4, 1)
    own_a, own_b, one_ref, two_ref, three_ref, residual_ref, inverse_ref, cot_ref, gains_ref = ins[:9]
    weights = ins[9:]
    residual_grad_ref, low_ref, attended_grad_ref, gain_grad_ref = outs
    (blocks,) = scratch
    dp = spots[2]
    grad = (own_a[...].astype(F32) + own_b[...].astype(F32)) + one_ref[...].astype(F32)
    grad = grad + two_ref[...].astype(F32) + three_ref[...].astype(F32)
    residual, inverse = residual_ref[...], inverse_ref[...]
    gain_grad_ref[...] = jnp.sum(grad * residual * inverse, axis=0, keepdims=True)
    residual_grad = cot_ref[...].astype(F32) + norm_back(grad, residual, inverse, gains_ref[1:2, :])
    residual_grad_ref[...] = residual_grad
    low = residual_grad.astype(BF16)
    low_ref[...] = low
    for i, block in enumerate(lane_blocks(low, members)):
        blocks[i] = block
    attended_grad_ref[...] = sum(
        dot_last(blocks[dp ^ j], weights[j][...]) for j in range(members)
    ).astype(BF16)


def halves_by_core(core, values):
    low, high = lane_blocks(values, 2)
    return jnp.where(core == 0, low, high), jnp.where(core == 0, high, low)


def output_grad_kernel(spots, attended_ref, low_ref, keep_ref, send_ref):
    keep, send = halves_by_core(spots[0], low_ref[...].astype(F32))
    attended = attended_ref[...]
    send_ref[...] = dot_first(attended, send.astype(BF16)).astype(BF16)
    keep_ref[...] = dot_first(attended, keep.astype(BF16)).astype(BF16)


def query_grad_kernel(members, spots, normed_ref, low_ref, *refs):
    weights, (keep_ref, send_ref, back_ref), (blocks,) = split_refs(refs, members, 3, 1)
    dp = spots[2]
    low = low_ref[...]
    keep, send = halves_by_core(spots[0], low.astype(F32))
    normed = normed_ref[...]
    send_ref[...] = dot_first(normed, send.astype(BF16)).astype(BF16)
    keep_ref[...] = dot_first(normed, keep.astype(BF16)).astype(BF16)
    for i, block in enumerate(lane_blocks(low, members)):
        blocks[i] = block
    back_ref[...] = sum(dot_last(blocks[dp ^ j], weights[j][...]) for j in range(members))


def back_kernel(chunk, pieces, first, last, spots, *refs):
    ins, outs, scratch = split_refs(refs, 9 + pieces, pieces + 1, 2)
    (queries_ref, key_pos_ref, query_pos_ref, cos_ref, sin_ref, turned_ref, log_ref, grad_ref,
     start_ref) = ins[:9]
    parts = ins[9:]
    query_grad_ref, kv_grads = outs[0], outs[1:]
    kv_ref, kv_grad_ref = scratch
    stack_rows(kv_ref, parts)
    rows = queries_ref.shape[0]
    columns = GROUPS * rows
    query_pos = query_pos_ref[...]
    heads = []
    for head in range(KV_HEADS):
        stacked = heads_of(queries_ref, head * GROUPS, GROUPS)
        upstream = heads_of(grad_ref, head * GROUPS, GROUPS)
        delta = jnp.sum(upstream.astype(F32).T * turned_ref[head], axis=0, keepdims=True)
        log_total = log_ref[head : head + 1, :]
        keys_at = head * HEAD_DIM
        values_at = (KV_HEADS + head) * HEAD_DIM

        def step(j, query_grad, head=head, stacked=stacked, upstream=upstream,
                 delta=delta, log_total=log_total, keys_at=keys_at, values_at=values_at):
            at = pl.ds(pl.multiple_of(j * chunk, chunk), chunk)
            keys = heads_of(kv_ref, head, 1, at)
            values = heads_of(kv_ref, KV_HEADS + head, 1, at)
            scores = dot_last(keys, stacked)
            scores = jnp.where(key_pos_ref[at, :] <= query_pos, scores, MASKED)
            weights = jnp.exp(scores - log_total)
            weight_grad = dot_last(values, upstream)
            score_grad = (weights * (weight_grad - delta)).astype(BF16)
            value_grad = dot_plain(weights.astype(BF16), upstream)
            key_grad = dot_plain(score_grad, stacked)
            kv_grad_ref[at, keys_at : keys_at + HEAD_DIM] = key_grad.astype(BF16)
            kv_grad_ref[at, values_at : values_at + HEAD_DIM] = value_grad.astype(BF16)
            return query_grad + dot_first(keys, score_grad)

        start = jnp.zeros((HEAD_DIM, columns), F32) if first else start_ref[head]
        query_grad = lax.fori_loop(0, kv_ref.shape[0] // chunk, step, start)
        if not last:
            query_grad_ref[head] = query_grad
        else:
            straight = query_grad.T * (1.0 / math.sqrt(HEAD_DIM))
            heads += [straight[g * rows : (g + 1) * rows, :] for g in range(GROUPS)]
    if last:
        query_grad_ref[...] = rope_lanes(
            jnp.concatenate(heads, axis=1), cos_ref[...], -sin_ref[...]
        ).astype(BF16)
    for i in range(pieces):
        kv_grads[i][...] = kv_grad_ref[i * rows : (i + 1) * rows, :]


def end_kernel(shards, spots, *refs):
    ins, outs, scratch = split_refs(refs, 12 + (shards + 1) + 2 * (shards - 1), 3, 1)
    (cos_ref, sin_ref, normed_ref, tokens_ref, inverse_ref, gains_ref, back_ref, residual_grad_ref,
     key_ref, value_ref, gain_two_ref, _) = ins[:12]
    sums, mine, other = split_refs(ins[12:], shards + 1, shards - 1, shards - 1)
    input_grad_ref, keep_ref, send_ref = outs
    (blocks,) = scratch
    core, shard = spots[0], spots[1]
    rows = key_ref.shape[0]
    width = key_ref.shape[1]
    total = sum(s[...].astype(F32) for s in sums)
    keys = rope_lanes(total[:, :width], cos_ref[...], -sin_ref[...])
    values = total[:, width:]
    keep = jnp.where(core == 0, keys, values).astype(BF16)
    send = jnp.where(core == 0, values, keys).astype(BF16)
    blocks[shard] = dot_last(keys.astype(BF16), key_ref[...]) + dot_last(
        values.astype(BF16), value_ref[...]
    )
    for r in range(1, shards):
        blocks[shard ^ r] = dot_last(keep, mine[r - 1][:rows, :]) + dot_last(
            send, other[r - 1][:rows, :]
        )
    normed_grad = back_ref[...] + join_lanes(blocks)
    inputs, inverse = tokens_ref[...].astype(F32), inverse_ref[...]
    gain_grad = jnp.sum(normed_grad * inputs * inverse, axis=0, keepdims=True)
    input_grad_ref[...] = residual_grad_ref[...] + norm_back(
        normed_grad, inputs, inverse, gains_ref[0:1, :]
    )
    normed = normed_ref[...]
    two = gain_two_ref[...]
    for out_ref, low, gain in (
        (send_ref, send, jnp.where(core == 0, two, gain_grad)),
        (keep_ref, keep, jnp.where(core == 0, gain_grad, two)),
    ):
        grad = dot_first(normed, low).astype(BF16)
        span = rows + EXTRA_ROWS
        for z, block in enumerate(lane_blocks(gain, shards)):
            out_ref[z * span : z * span + rows, :] = grad[z * rows : (z + 1) * rows, :]
            padded = jnp.concatenate([block, jnp.zeros((1, width - rows), F32)], axis=1)
            out_ref[z * span + rows : (z + 1) * span, :] = jnp.broadcast_to(
                padded, (EXTRA_ROWS, width)
            ).astype(BF16)


def spread_kernel(shards, members, spots, *refs):
    parts, outs, (blocks,) = split_refs(refs, members, 3, 1)
    gate_ref, up_ref, down_ref = outs
    member = spots[3]
    part = parts[0].shape[1] // 3
    piece = part // shards
    span = part // shards * members
    folds = parts[0].shape[0] // piece
    for i in range(members):
        at = member ^ i
        blocks[at] = parts[i][:, : 2 * part].astype(F32)
        down = parts[i][:, 2 * part :].astype(F32)
        down_ref[pl.ds(pl.multiple_of(at * piece, piece), piece), :] = jnp.concatenate(
            [down[b * piece : (b + 1) * piece, :] for b in range(folds)], axis=1
        )
    for which, out_ref in enumerate((gate_ref, up_ref)):
        for z in range(shards):
            at = which * part + z * piece
            out_ref[:, z * span : (z + 1) * span] = jnp.concatenate(
                [blocks[p, :, at : at + piece] for p in range(members)], axis=1
            )


def base_of(block_order, stored, block_length):
    which = stored // block_length
    count = block_order.shape[1]
    matches = (which[:, None] == jnp.arange(count, dtype=jnp.int32)[None, :]).astype(jnp.int32)
    return jnp.sum(block_order[0][None, :] * matches, axis=-1) * block_length + stored % block_length


def tables(positions):
    half_dim = HEAD_DIM // 2
    exponent = -(jnp.arange(half_dim, dtype=F32) * 2.0) / HEAD_DIM
    frequency = jnp.power(F32(ROPE_BASE), exponent)
    angles = positions.astype(F32)[:, None] * frequency
    cosine, sine = jnp.cos(angles), jnp.sin(angles)
    return (
        jnp.concatenate([cosine] * 4, axis=-1),
        jnp.concatenate([-sine, sine, -sine, sine], axis=-1),
    )


def after(x, other):
    return lax.optimization_barrier((x, other))[0]


def on_device(
    tokens,
    block_order,
    attention_gain,
    query_weight,
    key_weight,
    value_weight,
    output_weight,
    feedforward_gain,
    gate_weight,
    up_weight,
    down_weight,
    cotangent,
):
    tokens, cotangent = tokens[0], cotangent[0]
    rows, width = tokens.shape
    shards = lax.axis_size("fsdp")
    ctx_count = lax.axis_size("ctx")
    dp_count = lax.axis_size("dp")
    block_length = rows * shards * ctx_count // block_order.shape[1]
    shard = lax.axis_index("fsdp")
    ctx = lax.axis_index("ctx")
    dp = lax.axis_index("dp")
    core = dp & 1
    members = dp_count * 2
    weight_rows = query_weight.shape[0]
    query_width = HEADS * HEAD_DIM
    kv_width = KV_HEADS * HEAD_DIM
    hidden = gate_weight.shape[1]
    part = hidden // members
    spots = jnp.stack([core, shard, dp, dp * 2 + (ctx & 1)]).astype(jnp.int32)

    gain_one, gain_two = attention_gain[None, :], feedforward_gain[None, :]
    kv_pack = jnp.concatenate(
        [
            jnp.where(core == 0, key_weight, value_weight),
            jnp.pad(
                jnp.concatenate([gain_one, gain_two], axis=0),
                ((0, EXTRA_ROWS - 2), (0, kv_width - weight_rows)),
            ),
        ],
        axis=0,
    )
    kv_mine = [swap(kv_pack, "fsdp", r) for r in range(1, shards)]
    kv_other = [swap_core(piece) for piece in kv_mine]

    quarter = width // dp_count

    def spread_columns(weight):
        own = lax.all_gather(
            lax.dynamic_slice_in_dim(weight, dp * quarter, quarter, 1), "fsdp", axis=0, tiled=True
        )
        across = swap_plane(own, 2, 0)
        return [own, swap_core(own), across, swap_core(across)]

    query_parts = spread_columns(query_weight)

    offsets = jnp.arange(rows, dtype=jnp.int32)
    my_start = (ctx * shards + shard) * rows
    positions = base_of(block_order, my_start[None], block_length) + offsets
    cosine, sine = tables(positions)
    query_pos = jnp.concatenate([positions] * GROUPS)[None, :]
    starts = jnp.stack(
        [((ctx ^ d) * shards + (shard ^ r)) * rows for d in range(ctx_count) for r in range(shards)]
    )
    key_pos = (base_of(block_order, starts, block_length)[:, None] + offsets[None, :]).reshape(-1, 1)
    near_count = shards * rows
    near_pos, far_pos = key_pos[:near_count], key_pos[near_count:]
    far_count = far_pos.shape[0]

    (pack,) = call(
        functools.partial(pack_kernel, shards, members), spots,
        [gate_weight, up_weight, down_weight], [((weight_rows, 3 * part), BF16)],
        flops=4 * weight_rows * hidden * part // shards, name="pack_weights",
    )
    kv_own, normed_one, inverse_one, gains = call(
        functools.partial(begin_kernel, shards), spots,
        [tokens, gain_one, gain_two, key_weight, value_weight, cosine, sine, *kv_mine, *kv_other],
        [
            ((rows, 2 * kv_width), BF16), ((rows, width), BF16), ((rows, 1), F32), ((8, width), F32),
        ],
        scratch=[
            ((shards, rows, weight_rows), F32), ((shards, rows, weight_rows), BF16),
            ((shards, 8, weight_rows), F32),
        ],
        flops=4 * rows * width * kv_width, name="norm_keys_values",
    )
    near = [kv_own] + [swap(kv_own, "fsdp", r) for r in range(1, shards)]
    far = [swap(piece, "ctx", d) for d in range(1, ctx_count) for piece in near]

    output_parts = spread_columns(after(output_weight, kv_own))
    pack_all = lax.all_gather(after(pack, kv_own), "fsdp", axis=0, tiled=True)
    cot_a, cot_b = plane_pieces(after(cotangent, kv_own))

    chunk = rows * 2
    unit = 2 * HEADS * rows * near_count * HEAD_DIM
    stat = ((KV_HEADS, GROUPS * rows), F32)
    turned_shape = ((KV_HEADS, HEAD_DIM, GROUPS * rows), F32)
    queries, largest, total, weighted = call(
        functools.partial(near_kernel, chunk, dp_count, shards), spots,
        [normed_one, near_pos, query_pos, cosine, sine, *query_parts, *near],
        [((rows, query_width), BF16), stat, stat, turned_shape],
        scratch=[((dp_count, rows, quarter), F32), ((near_count, 2 * kv_width), BF16)],
        flops=8 * unit, name="attention_near",
    )
    attended, turned, log_total, residual, inverse_two, normed_two = call(
        functools.partial(far_kernel, chunk, dp_count, len(far)), spots,
        [
            queries, far_pos, query_pos, largest, total, weighted, tokens, gains,
            *output_parts, *far,
        ],
        [
            ((rows, query_width), BF16), turned_shape, stat, ((rows, width), F32),
            ((rows, 1), F32), ((rows, width), BF16),
        ],
        scratch=[((dp_count, rows, quarter), F32), ((far_count, 2 * kv_width), BF16)],
        flops=8 * unit * len(far) // shards, name="attention_far",
    )

    normed_a, normed_b = plane_pieces(normed_two)
    token_shape = ((rows, width), BF16)
    half = 4 * rows

    def feed(normed, cot):
        out = call(
            functools.partial(feed_kernel, shards, 4), spots, [pack_all, *normed, *cot],
            [token_shape] * 4 + [((half, part), BF16), ((half, 2 * part), BF16)],
            scratch=[((half, width), BF16), ((half, width), BF16), ((part, width), BF16)],
            flops=10 * half * width * part, name="feed_forward",
        )
        return out[:4], out[4], out[5]

    grad_b, act_b, both_b = feed(normed_b, cot_b)
    from_core = [swap_core(g) for g in grad_b]
    grad_a, act_a, both_a = feed(normed_a, cot_a)

    def send_chips(parts_a, parts_b):
        out = []
        for k, (a, b) in enumerate(CHIP_MASKS):
            both = (parts_a[k + 1].astype(F32) + parts_b[k + 1].astype(F32)).astype(BF16)
            out.append(swap_plane(both, a, b))
        return out

    grad_chips = send_chips(grad_a, from_core)
    out = call(
        functools.partial(feed_weights_kernel, shards, 8), spots,
        [pack_all, act_a, act_b, both_a, both_b, *normed_a, *normed_b, *cot_a, *cot_b],
        [token_shape] * 8 + [((width, 3 * part), BF16)],
        scratch=[
            ((2 * half, width), BF16), ((2 * half, width), BF16), ((2 * half, part), BF16),
            ((2 * half, 2 * part), BF16), ((part, width), BF16),
        ],
        flops=16 * half * width * part, name="feed_forward_weights",
    )
    result_a, result_b, pack_grad = out[:4], out[4:8], out[8]
    pack_share = sum_far(lax.psum_scatter(pack_grad, "fsdp", scatter_dimension=0, tiled=True))

    residual_grad, residual_low, attended_grad, second_gain_grad = call(
        functools.partial(middle_kernel, dp_count), spots,
        [
            grad_a[0], from_core[0], *grad_chips, residual, inverse_two, cotangent, gains,
            *output_parts,
        ],
        [((rows, width), F32), token_shape, ((rows, query_width), BF16), ((1, width), F32)],
        scratch=[((dp_count, rows, quarter), BF16)],
        flops=2 * rows * width * query_width, name="residual_back",
    )

    result_core = [swap_core(after(p, residual_low)) for p in result_b]
    result_chips = send_chips(result_a, result_core)
    result = residual + (
        (result_a[0].astype(F32) + result_core[0].astype(F32)) + result_chips[0].astype(F32)
        + (result_chips[1].astype(F32) + result_chips[2].astype(F32))
    )

    half_shape = ((width, width // 2), BF16)
    output_keep, output_send = call(
        output_grad_kernel, spots, [attended, residual_low], [half_shape, half_shape],
        flops=2 * rows * width * width, name="output_weight_grad",
    )

    def back(first, last, start, pos, pieces):
        count = pos.shape[0]
        shape = ((rows, query_width), BF16) if last else turned_shape
        out = call(
            functools.partial(back_kernel, chunk, len(pieces), first, last), spots,
            [
                queries, pos, query_pos, cosine, sine, turned, log_total, attended_grad, start,
                *pieces,
            ],
            [shape] + [((rows, 2 * kv_width), BF16)] * len(pieces),
            scratch=[((count, 2 * kv_width), BF16), ((count, 2 * kv_width), BF16)],
            flops=20 * unit * len(pieces) // shards,
            name="attention_back_near" if last else "attention_back_far",
        )
        return out[0], out[1:]

    query_partial, far_grads = turned, []
    for d in range(1, ctx_count):
        at = (d - 1) * shards
        query_partial, grads = back(
            d == 1, False, query_partial, far_pos[at * rows : (at + shards) * rows],
            far[at : at + shards],
        )
        far_grads += grads
    home = [
        [swap(far_grads[(d - 1) * shards + r], "ctx", d) for d in range(1, ctx_count)]
        for r in range(shards)
    ]
    query_low, near_grads = back(False, True, query_partial, near_pos, near)
    kv_sums = [
        near_grads[r].astype(F32) + sum(h.astype(F32) for h in home[r]) for r in range(shards)
    ]
    kv_arrived = [swap(kv_sums[r].astype(BF16), "fsdp", r) for r in range(1, shards)]

    def pieces_of(keep, arrived, span):
        out = []
        for r in range(shards):
            at = (shard ^ r) * span
            mine = lax.dynamic_slice_in_dim(keep, at, span, 0).astype(F32)
            theirs = lax.dynamic_slice_in_dim(arrived, at, span, 0).astype(F32)
            out.append((mine + theirs).astype(BF16))
        return out

    def sum_devices(keep, send, span):
        pieces = pieces_of(keep, swap_core(send), span)
        total = pieces[0].astype(F32)
        for r in range(1, shards):
            total = total + swap(pieces[r], "fsdp", r).astype(F32)
        own = total.astype(BF16)
        across, along, diagonal = [swap_plane(own, a, b) for a, b in CHIP_MASKS]
        total = (own.astype(F32) + across.astype(F32)) + (
            along.astype(F32) + diagonal.astype(F32)
        )
        low = sum_far(total.astype(BF16))
        away = swap_core(low)
        return (
            jnp.where(core == 0, low, away).astype(F32), jnp.where(core == 0, away, low).astype(F32)
        )

    output_weight_grad = jnp.concatenate(sum_devices(output_keep, output_send, weight_rows), axis=1)

    query_keep, query_send, query_back = call(
        functools.partial(query_grad_kernel, dp_count), spots,
        [normed_one, query_low, *query_parts],
        [half_shape, half_shape, ((rows, width), F32)],
        scratch=[((dp_count, rows, quarter), BF16)],
        flops=4 * rows * width * width, name="query_weight_grad",
    )
    query_weight_grad = jnp.concatenate(sum_devices(query_keep, query_send, weight_rows), axis=1)

    span = weight_rows + EXTRA_ROWS
    packed_shape = ((shards * span, kv_width), BF16)
    input_grad, kv_keep, kv_send = call(
        functools.partial(end_kernel, shards), spots,
        [
            cosine, sine, normed_one, tokens, inverse_one, gains, query_back, residual_grad,
            key_weight, value_weight, second_gain_grad, gain_one,
            near_grads[0], sum(h.astype(F32) for h in home[0]), *kv_arrived, *kv_mine, *kv_other,
        ],
        [((rows, width), F32), packed_shape, packed_shape],
        scratch=[((shards, rows, weight_rows), F32)],
        flops=8 * rows * width * kv_width, name="keys_values_back",
    )
    first, second = sum_devices(kv_keep, kv_send, span)

    share_a, share_b = plane_pieces(pack_share)
    share_by_mask = [None] * members
    for k, (a, b) in enumerate(((0, 0),) + CHIP_MASKS):
        share_by_mask[2 * a + b] = share_a[k]
        share_by_mask[2 * (a ^ 1) + b] = share_b[k]
    gate_weight_grad, up_weight_grad, down_weight_grad = call(
        functools.partial(spread_kernel, shards, members), spots, share_by_mask,
        [
            ((weight_rows, hidden), F32), ((weight_rows, hidden), F32),
            ((down_weight.shape[0], width), F32),
        ],
        scratch=[((members, weight_rows, 2 * part), F32)],
        name="feed_forward_out",
    )

    return (
        result[None],
        input_grad[None],
        first[weight_rows, :weight_rows],
        query_weight_grad,
        first[:weight_rows],
        second[:weight_rows],
        output_weight_grad,
        second[weight_rows, :weight_rows],
        gate_weight_grad,
        up_weight_grad,
        down_weight_grad,
    )


def solution(mesh):
    row = P("fsdp", None)
    token = P("dp", ("ctx", "fsdp"), None)
    return jax.shard_map(
        on_device,
        mesh=mesh,
        in_specs=(
            token, P("dp", None), P("fsdp"), row, row, row, row, P("fsdp"), row, row, row, token,
        ),
        out_specs=(
            token, token, P("fsdp"), row, row, row, row, P("fsdp"), row, row, row,
        ),
        check_vma=False,
    )
```

time: 514 us -> 480 us (0.934)
  Pallas kernels: 45.2 us -> 113 us
  local copies, waits for them, and re-layouts: 85.7 us -> 26.8 us
  waiting for transfers between devices: 199 us -> 148 us
  blocking collectives: 18 us -> 68.9 us
  matrix products: 47.1 us -> 0 us
  starting transfers between devices: 58.6 us -> 77.5 us
  other arithmetic: 37.5 us -> 25 us
    pallas_call x4 -> x14, Pallas kernels: 45.2 us -> 113 us  [call(): pl.pallas_call(kernel, out_shape=outs, in_specs=specs, out_specs=tuple((p...]
    ppermute x24 -> x26, waiting for transfers between devices: 132 us -> 68.9 us  [swap(): return lax.ppermute(x, axis, [(i, i ^ mask) for i in range(count)])]
    all_gather x1 -> x2, blocking collectives: 18 us -> 68.9 us  [spread_columns(): lax.all_gather(lax.dynamic_slice_in_dim(weight, dp * quarter, quarter, 1)...]
    dot_general x20 -> x0, matrix products: 47.1 us -> none  [the longest x8 21.1 us: dot_last(): lax.dot_general(left, right, (((1,), (1,)), ((), ())), preferred_element_...]
    ppermute x33 -> x59, waiting for transfers between devices: 53.4 us -> 79.1 us  [swap_plane(): return lax.ppermute(x, ('dp', 'ctx'), pairs)]
    concatenate x6 -> x0, local copies, waits for them, and re-layouts: 18.4 us -> none  [the longest x1 6.58 us: on_device(): cot_ab = jnp.concatenate([cot_a, cot_b], axis=0)]
    ppermute x9 -> x0, local copies, waits for them, and re-layouts: 14.9 us -> none  [swap_plane(): return lax.ppermute(x, ('dp', 'ctx'), pairs)]
    all_gather x4 -> x1, waiting for transfers between devices: 13.1 us -> 0.01 us  [on_device(): pack_all = lax.all_gather(after(pack, kv_own), 'fsdp', axis=0, tiled=True)]
  transfers between devices with their start and end apart: 63 -> 87, of which waited for: 26 -> 28; matrix products, arithmetic and copies ran while one was open for 27% -> 9% of each run, Pallas kernels for 9% -> 20%
where the time goes in v2:
time: 480 us; the launch traced here: 475 us
  waiting for transfers between devices  148 us (31%)
  Pallas kernels  113 us (24%)
  starting transfers between devices  77.5 us (16%)
  blocking collectives  68.9 us (14%)
  local copies, waits for them, and re-layouts  26.8 us (6%)
  other arithmetic  25 us (5%)
  between operations  15.9 us (3%)
    pallas_call x14, Pallas kernels, call(): pl.pallas_call(kernel, out_shape=outs, in_specs=specs, out_specs=tuple((p...  113 us
    ppermute x59, waiting for transfers between devices, swap_plane(): return lax.ppermute(x, ('dp', 'ctx'), pairs)  79.1 us
    all_gather x2, blocking collectives, spread_columns(): lax.all_gather(lax.dynamic_slice_in_dim(weight, dp * quarter, quarter, 1)...  68.9 us
    ppermute x26, waiting for transfers between devices, swap(): return lax.ppermute(x, axis, [(i, i ^ mask) for i in range(count)])  68.9 us
    ppermute x26, starting transfers between devices, swap(): return lax.ppermute(x, axis, [(i, i ^ mask) for i in range(count)])  39.7 us
    ppermute x59, starting transfers between devices, swap_plane(): return lax.ppermute(x, ('dp', 'ctx'), pairs)  37.7 us
    unnamed x146, local copies, waits for them, and re-layouts  16 us
  transfers between devices with their start and end apart: 87, of which 28 were waited for; matrix products, arithmetic and copies ran while one was open for 9% of the time, Pallas kernels for 20%

profile of v2, /device:TPU:0, one launch (start us, length us, event | category | flops | bytes accessed | tf_op | source)
XLA Modules:
  0.0 475.3 jit_solution(9840861634178996681)
XLA Ops:
  11.0 5.1 %collective-permute-start.2 = (bf16[256,320]{1,0:T(8,128)(2,1)S(1)}, bf16[256,320]{1,0:T(8,128)(2,1)S(1)}, u32[]{:S(2)}, u32[]{:S(2)}) collective-permute-start(bf16[256,320]{1,0:T(8,128)(2,1)S(1)} %pad_maximum_fusion), channel_id=1, source_target_pairs={{0,3},{1,2},{2,1},{3,0},{4,7},{5,6},{6,5},{7,4},{8,11},{9,10},{10,... | collective-permute-start | bytes 491528 | tf_op jit(solution)/shard_map/ppermute | solution.py:40
  22.0 10.8 %collective-permute-done.1.refs_8_.refs_18_ = bf16[256,320]{1,0:T(8,128)(2,1)S(1)} collective-permute-done((bf16[256,320]{1,0:T(8,128)(2,1)S(1)}, bf16[256,320]{1,0:T(8,128)(2,1)S(1)}, u32[]{:S(2)}, u32[]{:S(2)}) %collective-permute-start.1) | collective-permute-done | bytes 163872 | tf_op jit(solution)/shard_map/ppermute | solution.py:40
  35.9 3.8 pack_weights.1
  41.4 3.6 norm_keys_values.1
  45.3 17.4 %all_gather.9.refs_5_.refs_0_ = bf16[960,240]{1,0:T(8,128)(2,1)S(1)} all-gather(bf16[240,240]{1,0:T(8,128)(2,1)S(1)} %constant_dynamic-slice_fusion.5), channel_id=1, replica_groups=mesh['dp'=4,'ctx'=2,'fsdp'=4] {'fsdp'}, dimensions={0}, use_global_device_ids=true | all-gather | bytes 576000 | tf_op jit(solution)/shard_map/all_gather | solution.py:594
  70.0 51.5 %all_gather.10.refs_8_.refs_9_ = bf16[960,240]{1,0:T(8,128)(2,1)S(1)} all-gather(bf16[240,240]{1,0:T(8,128)(2,1)S(1)} %constant_dynamic-slice_fusion.4), channel_id=1, replica_groups=mesh['dp'=4,'ctx'=2,'fsdp'=4] {'fsdp'}, dimensions={0}, use_global_device_ids=true | all-gather | bytes 576000 | tf_op jit(solution)/shard_map/all_gather | solution.py:594
  128.0 15.8 %collective-permute-done.24.refs_8_.refs_16_ = bf16[192,960]{1,0:T(8,128)(2,1)S(1)} collective-permute-done((bf16[192,960]{1,0:T(8,128)(2,1)}, bf16[192,960]{1,0:T(8,128)(2,1)S(1)}, u32[]{:S(2)}, u32[]{:S(2)}) %collective-permute-start.24) | collective-permute-done | bytes 368672 | tf_op jit(solution)/shard_map/ppermute | solution.py:49
  153.8 11.4 %attention_near.1 = (bf16[192,960]{1,0:T(8,128)(2,1)}, f32[5,576]{1,0:T(8,128)}, f32[5,576]{1,0:T(8,128)}, f32[5,64,576]{2,1,0:T(8,128)}) custom-call(s32[4]{0:T(128)} %pad_add_fusion.1.spots, bf16[192,960]{1,0:T(8,128)(2,1)} %get-tuple-element.78.refs_0_.normed_ref.refs_2_, s32[768,1]{1,0:T(8,128)} %slice.32.refs_1_, s32[1,576]{1,0:T(1,128)} %broadcast_in_dim.29.refs_2_, ...), custom_call_target="tpu_custom_call" | custom-call | flops 2264924160 | bytes 4525824 | tf_op jit(solution)/shard_map/attention_near/pallas_call | solution.py:79
  166.0 13.2 %attention_far.1 = (bf16[192,960]{1,0:T(8,128)(2,1)}, f32[5,64,576]{2,1,0:T(8,128)}, f32[5,576]{1,0:T(8,128)}, f32[192,960]{1,0:T(8,128)}, f32[192,1]{1,0:T(8,128)}, /*index=5*/bf16[192,960]{1,0:T(8,128)(2,1)}) custom-call(s32[4]{0:T(128)} %pad_add_fusion.1.spots, bf16[192,960]{1,0:T(8,128)(2,1)} %get-tuple-element.80.refs_0_, s32[768,1]{1,0:T(8,128)} %slice.33.refs_1_, ...), custom_call_target="tpu_custom_call" | custom-call | flops 2264924160 | bytes 6584064 | tf_op jit(solution)/shard_map/attention_far/pallas_call | solution.py:79
  183.2 9.0 %collective-permute-done.21.refs_4_.refs_8_ = bf16[192,960]{1,0:T(8,128)(2,1)S(1)} collective-permute-done((bf16[192,960]{1,0:T(8,128)(2,1)}, bf16[192,960]{1,0:T(8,128)(2,1)S(1)}, u32[]{:S(2)}, u32[]{:S(2)}) %collective-permute-start.21) | collective-permute-done | bytes 368672 | tf_op jit(solution)/shard_map/ppermute | solution.py:49
  192.2 7.9 %collective-permute-done.20.refs_3_.refs_7_ = bf16[192,960]{1,0:T(8,128)(2,1)S(1)} collective-permute-done((bf16[192,960]{1,0:T(8,128)(2,1)}, bf16[192,960]{1,0:T(8,128)(2,1)S(1)}, u32[]{:S(2)}, u32[]{:S(2)}) %collective-permute-start.20) | collective-permute-done | bytes 368672 | tf_op jit(solution)/shard_map/ppermute | solution.py:49
  202.7 8.5 %feed_forward.3 = (bf16[192,960]{1,0:T(8,128)(2,1)}, bf16[192,960]{1,0:T(8,128)(2,1)}, bf16[192,960]{1,0:T(8,128)(2,1)}, bf16[192,960]{1,0:T(8,128)(2,1)}, bf16[...) custom-call(s32[4]{0:T(128)} %pad_add_fusion.1.spots, bf16[960,960]{1,0:T(8,128)(2,1)} %all-gather.2.cloned.1.call-done.refs_0_, ...), custom_call_target="tpu_custom_call" | custom-call | flops 2359296000 | bytes 7741440 | tf_op jit(solution)/shard_map/feed_forward/pallas_call | solution.py:79
  212.3 8.5 %feed_forward.2 = (bf16[192,960]{1,0:T(8,128)(2,1)}, bf16[192,960]{1,0:T(8,128)(2,1)}, bf16[192,960]{1,0:T(8,128)(2,1)}, bf16[192,960]{1,0:T(8,128)(2,1)}, bf16[...) custom-call(s32[4]{0:T(128)} %pad_add_fusion.1.spots, bf16[960,960]{1,0:T(8,128)(2,1)} %all-gather.2.cloned.1.call-done.refs_0_, ...), custom_call_target="tpu_custom_call" | custom-call | flops 2359296000 | bytes 7741440 | tf_op jit(solution)/shard_map/feed_forward/pallas_call | solution.py:79
  226.9 12.0 %feed_forward_weights.1 = (bf16[192,960]{1,0:T(8,128)(2,1)}, bf16[192,960]{1,0:T(8,128)(2,1)}, bf16[192,960]{1,0:T(8,128)(2,1)}, bf16[192,960]{1,0:T(8,128)(2,1)...) custom-call(s32[4]{0:T(128)} %pad_add_fusion.1.spots, ...), custom_call_target="tpu_custom_call" | custom-call | flops 3774873600 | bytes 15482880 | tf_op jit(solution)/shard_map/feed_forward_weights/pallas_call | solution.py:79
  239.0 4.4 collective-permute-done.37.refs_3_
  244.3 4.8 %residual_back.1 = (f32[192,960]{1,0:T(8,128)}, bf16[192,960]{1,0:T(8,128)(2,1)}, bf16[192,960]{1,0:T(8,128)(2,1)}, f32[1,960]{1,0:T(1,128)}) custom-call(s32[4]{0:T(128)} %pad_add_fusion.1.spots, bf16[192,960]{1,0:T(8,128)(2,1)} %get-tuple-element.96.refs_0_, bf16[192,960]{1,0:T(8,128)(2,1)} %copy-done.32, bf16[192,960]{1,0:T(8,128)(2,1)} %copy-done.33, ...), custom_call_target="tpu_custom_call" | custom-call | flops 353894400 | bytes 6302208 | tf_op jit(solution)/shard_map/residual_back/pallas_call | solution.py:79
  249.8 12.7 %attention_back_far.1 = (f32[5,64,576]{2,1,0:T(8,128)}, bf16[192,640]{1,0:T(8,128)(2,1)}, bf16[192,640]{1,0:T(8,128)(2,1)}, bf16[192,640]{1,0:T(8,128)(2,1)}, bf16[192,640]{1,0:T(8,128)(2,1)}) custom-call(s32[4]{0:T(128)} %pad_add_fusion.1.spots, bf16[192,960]{1,0:T(8,128)(2,1)} %get-tuple-element.80.refs_0_, s32[768,1]{1,0:T(8,128)} %slice.33.refs_1_, ...), custom_call_target="tpu_custom_call" | custom-call | flops 5662310400 | bytes 5128704 | tf_op jit(solution)/shard_map/attention_back_far/pallas_call | solution.py:79
  264.5 13.5 %attention_back_near.1 = (bf16[192,960]{1,0:T(8,128)(2,1)}, bf16[192,640]{1,0:T(8,128)(2,1)}, bf16[192,640]{1,0:T(8,128)(2,1)}, bf16[192,640]{1,0:T(8,128)(2,1)}, bf16[192,640]{1,0:T(8,128)(2,1)}) custom-call(s32[4]{0:T(128)} %pad_add_fusion.1.spots, bf16[192,960]{1,0:T(8,128)(2,1)} %get-tuple-element.80.refs_0_, s32[768,1]{1,0:T(8,128)} %slice.32.refs_1_, ...), custom_call_target="tpu_custom_call" | custom-call | flops 5662310400 | bytes 4760064 | tf_op jit(solution)/shard_map/attention_back_near/pallas_call | solution.py:79
  278.1 4.2 query_weight_grad.1
  282.3 3.1 output_weight_grad.1
  287.0 6.1 %collective-permute-done.52 = bf16[192,640]{1,0:T(8,128)(2,1)S(1)} collective-permute-done((bf16[192,640]{1,0:T(8,128)(2,1)S(1)}, bf16[192,640]{1,0:T(8,128)(2,1)S(1)}, u32[]{:S(2)}, u32[]{:S(2)}) %collective-permute-start.52) | collective-permute-done | bytes 245792 | tf_op jit(solution)/shard_map/ppermute | solution.py:40
  305.9 14.3 %collective-permute-done.51.refs_15_ = bf16[192,640]{1,0:T(8,128)(2,1)S(1)} collective-permute-done((bf16[192,640]{1,0:T(8,128)(2,1)S(1)}, bf16[192,640]{1,0:T(8,128)(2,1)S(1)}, u32[]{:S(2)}, u32[]{:S(2)}) %collective-permute-start.51) | collective-permute-done | bytes 245792 | tf_op jit(solution)/shard_map/ppermute | solution.py:40
  323.8 5.6 %keys_values_back.1 = (f32[192,960]{1,0:T(8,128)}, bf16[1024,320]{1,0:T(8,128)(2,1)}, bf16[1024,320]{1,0:T(8,128)(2,1)}) custom-call(s32[4]{0:T(128)} %pad_add_fusion.1.spots, f32[192,128]{1,0:T(8,128)} %pad_maximum_fusion.1.refs_5_.refs_3_.refs_0_, f32[192,128]{1,0:T(8,128)} %pad_maximum_fusion.2.refs_6_.refs_4_.refs_1_, ...), custom_call_target="tpu_custom_call" | custom-call | flops 471859200 | bytes 7257056 | tf_op jit(solution)/shard_map/keys_values_back/pallas_call | solution.py:79
  331.9 7.2 %collective-permute-done.44 = bf16[192,960]{1,0:T(8,128)(2,1)} collective-permute-done((bf16[192,960]{1,0:T(8,128)(2,1)}, bf16[192,960]{1,0:T(8,128)(2,1)}, u32[]{:S(2)}, u32[]{:S(2)}) %collective-permute-start.44) | collective-permute-done | bytes 368672 | tf_op jit(solution)/shard_map/ppermute | solution.py:49
  359.3 6.5 %collective-permute-start.55 = (bf16[256,320]{1,0:T(8,128)(2,1)S(1)}, bf16[256,320]{1,0:T(8,128)(2,1)S(1)}, u32[]{:S(2)}, u32[]{:S(2)}) collective-permute-start(bf16[256,320]{1,0:T(8,128)(2,1)S(1)} %get-tuple-element.195), channel_id=1, source_target_pairs={{0,1},{1,0},{2,3},{3,2},{4,5},{5,4},{6,7},{7,6},{8,9},{9,8},{10,11... | collective-permute-start | bytes 491528 | tf_op jit(solution)/shard_map/ppermute | solution.py:40
  365.8 16.2 %collective-permute-done.64 = bf16[240,480]{1,0:T(8,128)(2,1)} collective-permute-done((bf16[240,480]{1,0:T(8,128)(2,1)}, bf16[240,480]{1,0:T(8,128)(2,1)}, u32[]{:S(2)}, u32[]{:S(2)}) %collective-permute-start.64) | collective-permute-done | bytes 230432 | tf_op jit(solution)/shard_map/ppermute | solution.py:40
  387.7 12.1 %collective-permute-done.72 = bf16[240,480]{1,0:T(8,128)(2,1)S(1)} collective-permute-done((bf16[240,480]{1,0:T(8,128)(2,1)}, bf16[240,480]{1,0:T(8,128)(2,1)S(1)}, u32[]{:S(2)}, u32[]{:S(2)}) %collective-permute-start.72) | collective-permute-done | bytes 230432 | tf_op jit(solution)/shard_map/ppermute | solution.py:40
  416.8 3.2 collective-permute-done.75
  428.6 11.5 %collective-permute-done.82.refs_5_ = bf16[240,960]{1,0:T(8,128)(2,1)S(1)} collective-permute-done((bf16[240,960]{1,0:T(8,128)(2,1)}, bf16[240,960]{1,0:T(8,128)(2,1)S(1)}, u32[]{:S(2)}, u32[]{:S(2)}) %collective-permute-start.82) | collective-permute-done | bytes 460832 | tf_op jit(solution)/shard_map/ppermute | solution.py:49
  440.1 9.8 %collective-permute-done.81.refs_4_ = bf16[240,960]{1,0:T(8,128)(2,1)S(1)} collective-permute-done((bf16[240,960]{1,0:T(8,128)(2,1)}, bf16[240,960]{1,0:T(8,128)(2,1)S(1)}, u32[]{:S(2)}, u32[]{:S(2)}) %collective-permute-start.81) | collective-permute-done | bytes 460832 | tf_op jit(solution)/shard_map/ppermute | solution.py:49
  456.9 8.2 %feed_forward_out.1 = (f32[240,2560]{1,0:T(8,128)}, f32[240,2560]{1,0:T(8,128)}, f32[640,960]{1,0:T(8,128)}) custom-call(s32[4]{0:T(128)} %pad_add_fusion.1.spots, bf16[240,960]{1,0:T(8,128)(2,1)} %reduce-scatter.2.cloned.1.call-done.refs_0_, bf16[240,960]{1,0:T(8,128)(2,1)} %copy-done.23, bf16[240,960]{1,0:T(8,128)(2,1)} %collective-permute-done.79.refs_2_, ...), custom_call_target="tpu_custom_call" | custom-call | bytes 11059200 | tf_op jit(solution)/shard_map/feed_forward_out/pallas_call | solution.py:79
  465.1 3.2 copy.84
  (361 shorter events, 134.2 us)
Async XLA Ops:
  7.2 195.4 %all-gather.2.cloned.1.call-start = ((), (), s32[]{:S(2)}) async-start(), calls=%async_computation.1 | async-start | bytes 2457600 | tf_op jit(solution)/shard_map/all_gather | solution.py:636
  45.1 379.8 %reduce-scatter.2.cloned.1.call-start = ((), (), s32[]{:S(2)}) async-start(), calls=%async_computation.2 | async-start | bytes 2457600 | tf_op jit(solution)/shard_map/reduce_scatter | solution.py:700
  62.7 58.9 %collective-permute-start.7 = (bf16[960,240]{1,0:T(8,128)(2,1)S(1)}, bf16[960,240]{1,0:T(8,128)(2,1)S(1)}, u32[]{:S(2)}, u32[]{:S(2)}) collective-permute-start(bf16[960,240]{1,0:T(8,128)(2,1)S(1)} %all_gather.9.refs_5_.refs_0_), channel_id=1, source_target_pairs={{0,16},{4,20},{8,24},{12,28},{16,0},{20,4},{24,8},{28,12},{1,17},{... | collective-permute-start | bytes 1382408 | tf_op jit(solution)/shard_map/ppermute | solution.py:49
  64.2 58.3 %collective-permute-start.6 = (bf16[960,240]{1,0:T(8,128)(2,1)S(1)}, bf16[960,240]{1,0:T(8,128)(2,1)S(1)}, u32[]{:S(2)}, u32[]{:S(2)}) collective-permute-start(bf16[960,240]{1,0:T(8,128)(2,1)S(1)} %all_gather.9.refs_5_.refs_0_), channel_id=1, source_target_pairs={{0,8},{4,12},{8,0},{12,4},{16,24},{20,28},{24,16},{28,20},{1,9},{5... | collective-permute-start | bytes 1382408 | tf_op jit(solution)/shard_map/ppermute | solution.py:49
  64.3 59.6 %collective-permute-start.15 = (bf16[192,640]{1,0:T(8,128)(2,1)}, bf16[192,640]{1,0:T(8,128)(2,1)S(1)}, u32[]{:S(2)}, u32[]{:S(2)}) collective-permute-start(bf16[192,640]{1,0:T(8,128)(2,1)} %get-tuple-element.79.refs_9_), channel_id=1, source_target_pairs={{0,4},{4,0},{1,5},{5,1},{2,6},{6,2},{3,7},{7,3},{8,12},{12,8},{9,1... | collective-permute-start | bytes 737288 | tf_op jit(solution)/shard_map/ppermute | solution.py:40
  66.2 57.8 %collective-permute-start.11 = (bf16[192,640]{1,0:T(8,128)(2,1)}, bf16[192,640]{1,0:T(8,128)(2,1)}, u32[]{:S(2)}, u32[]{:S(2)}) collective-permute-start(bf16[192,640]{1,0:T(8,128)(2,1)} %get-tuple-element.79.refs_9_), channel_id=1, source_target_pairs={{0,3},{1,2},{2,1},{3,0},{4,7},{5,6},{6,5},{7,4},{8,11},{9,10},{10,... | collective-permute-start | bytes 737288 | tf_op jit(solution)/shard_map/ppermute | solution.py:40
  69.0 56.5 %collective-permute-start.10 = (bf16[192,640]{1,0:T(8,128)(2,1)}, bf16[192,640]{1,0:T(8,128)(2,1)}, u32[]{:S(2)}, u32[]{:S(2)}) collective-permute-start(bf16[192,640]{1,0:T(8,128)(2,1)} %get-tuple-element.79.refs_9_), channel_id=1, source_target_pairs={{0,2},{1,3},{2,0},{3,1},{4,6},{5,7},{6,4},{7,5},{8,10},{9,11},{10,... | collective-permute-start | bytes 737288 | tf_op jit(solution)/shard_map/ppermute | solution.py:40
  122.5 21.7 %collective-permute-start.13 = (bf16[960,240]{1,0:T(8,128)(2,1)S(1)}, bf16[960,240]{1,0:T(8,128)(2,1)S(1)}, u32[]{:S(2)}, u32[]{:S(2)}) collective-permute-start(bf16[960,240]{1,0:T(8,128)(2,1)S(1)} %all_gather.10.refs_8_.refs_9_), channel_id=1, source_target_pairs={{0,16},{4,20},{8,24},{12,28},{16,0},{20,4},{24,8},{28,12},{1,17},{... | collective-permute-start | bytes 1382408 | tf_op jit(solution)/shard_map/ppermute | solution.py:49
  123.9 23.0 %collective-permute-start.12 = (bf16[960,240]{1,0:T(8,128)(2,1)S(1)}, bf16[960,240]{1,0:T(8,128)(2,1)S(1)}, u32[]{:S(2)}, u32[]{:S(2)}) collective-permute-start(bf16[960,240]{1,0:T(8,128)(2,1)S(1)} %all_gather.10.refs_8_.refs_9_), channel_id=1, source_target_pairs={{0,8},{4,12},{8,0},{12,4},{16,24},{20,28},{24,16},{28,20},{1,9},{5... | collective-permute-start | bytes 1382408 | tf_op jit(solution)/shard_map/ppermute | solution.py:49
  127.9 25.1 %collective-permute-start.8 = (bf16[960,240]{1,0:T(8,128)(2,1)S(1)}, bf16[960,240]{1,0:T(8,128)(2,1)S(1)}, u32[]{:S(2)}, u32[]{:S(2)}) collective-permute-start(bf16[960,240]{1,0:T(8,128)(2,1)S(1)} %collective-permute-done.7.refs_7_.refs_2_), channel_id=1, source_target_pairs={{0,8},{4,12},{8,0},{12,4},{16,24},{20,28},{24,16},{28,20},{1,9},{5... | collective-permute-start | bytes 1382408 | tf_op jit(solution)/shard_map/ppermute | solution.py:49
  144.2 21.8 %collective-permute-start.14 = (bf16[960,240]{1,0:T(8,128)(2,1)S(1)}, bf16[960,240]{1,0:T(8,128)(2,1)}, u32[]{:S(2)}, u32[]{:S(2)}) collective-permute-start(bf16[960,240]{1,0:T(8,128)(2,1)S(1)} %collective-permute-done.13.refs_10_.refs_11_), channel_id=1, source_target_pairs={{0,8},{4,12},{8,0},{12,4},{16,24},{20,28},{24,16},{28,20},{1,9},{5... | collective-permute-start | bytes 1382408 | tf_op jit(solution)/shard_map/ppermute | solution.py:49
  153.0 27.7 %collective-permute-start.29 = (bf16[192,960]{1,0:T(8,128)(2,1)}, bf16[192,960]{1,0:T(8,128)(2,1)S(1)}, u32[]{:S(2)}, u32[]{:S(2)}) collective-permute-start(bf16[192,960]{1,0:T(8,128)(2,1)} %bitcast.17.refs_5_.refs_13_.refs_7_), channel_id=1, source_target_pairs={{0,8},{4,12},{8,0},{12,4},{16,24},{20,28},{24,16},{28,20},{1,9},{5... | collective-permute-start | bytes 1105928 | tf_op jit(solution)/shard_map/ppermute | solution.py:49
  153.0 28.8 %collective-permute-start.22 = (bf16[192,960]{1,0:T(8,128)(2,1)}, bf16[192,960]{1,0:T(8,128)(2,1)S(1)}, u32[]{:S(2)}, u32[]{:S(2)}) collective-permute-start(bf16[192,960]{1,0:T(8,128)(2,1)} %bitcast.17.refs_5_.refs_13_.refs_7_), channel_id=1, source_target_pairs={{0,16},{4,20},{8,24},{12,28},{16,0},{20,4},{24,8},{28,12},{1,17},{... | collective-permute-start | bytes 1105928 | tf_op jit(solution)/shard_map/ppermute | solution.py:49
  211.4 27.6 %collective-permute-start.33 = (bf16[192,960]{1,0:T(8,128)(2,1)}, bf16[192,960]{1,0:T(8,128)(2,1)S(1)}, u32[]{:S(2)}, u32[]{:S(2)}) collective-permute-start(bf16[192,960]{1,0:T(8,128)(2,1)} %get-tuple-element.97), channel_id=1, source_target_pairs={{0,8},{4,12},{8,0},{12,4},{16,24},{20,28},{24,16},{28,20},{1,9},{5... | collective-permute-start | bytes 1105928 | tf_op jit(solution)/shard_map/ppermute | solution.py:49
  249.1 50.8 %collective-permute-start.40 = (bf16[192,960]{1,0:T(8,128)(2,1)S(1)}, bf16[192,960]{1,0:T(8,128)(2,1)S(1)}, u32[]{:S(2)}, u32[]{:S(2)}) collective-permute-start(bf16[192,960]{1,0:T(8,128)(2,1)S(1)} %copy-done.49), channel_id=1, source_target_pairs={{0,8},{4,12},{8,0},{12,4},{16,24},{20,28},{24,16},{28,20},{1,9},{5... | collective-permute-start | bytes 1105928 | tf_op jit(solution)/shard_map/ppermute | solution.py:49
  249.2 45.3 %collective-permute-start.41 = (bf16[192,960]{1,0:T(8,128)(2,1)S(1)}, bf16[192,960]{1,0:T(8,128)(2,1)S(1)}, u32[]{:S(2)}, u32[]{:S(2)}) collective-permute-start(bf16[192,960]{1,0:T(8,128)(2,1)S(1)} %copy-done.55), channel_id=1, source_target_pairs={{0,8},{4,12},{8,0},{12,4},{16,24},{20,28},{24,16},{28,20},{1,9},{5... | collective-permute-start | bytes 1105928 | tf_op jit(solution)/shard_map/ppermute | solution.py:49
  249.7 45.9 %collective-permute-start.43 = (bf16[192,960]{1,0:T(8,128)(2,1)S(1)}, bf16[192,960]{1,0:T(8,128)(2,1)S(1)}, u32[]{:S(2)}, u32[]{:S(2)}) collective-permute-start(bf16[192,960]{1,0:T(8,128)(2,1)S(1)} %copy-done.52), channel_id=1, source_target_pairs={{0,8},{4,12},{8,0},{12,4},{16,24},{20,28},{24,16},{28,20},{1,9},{5... | collective-permute-start | bytes 1105928 | tf_op jit(solution)/shard_map/ppermute | solution.py:49
  262.5 22.9 %collective-permute-start.48 = (bf16[192,640]{1,0:T(8,128)(2,1)}, bf16[192,640]{1,0:T(8,128)(2,1)S(1)}, u32[]{:S(2)}, u32[]{:S(2)}) collective-permute-start(bf16[192,640]{1,0:T(8,128)(2,1)} %get-tuple-element.128), channel_id=1, source_target_pairs={{0,4},{4,0},{1,5},{5,1},{2,6},{6,2},{3,7},{7,3},{8,12},{12,8},{9,1... | collective-permute-start | bytes 737288 | tf_op jit(solution)/shard_map/ppermute | solution.py:40
  263.8 23.1 %collective-permute-start.50 = (bf16[192,640]{1,0:T(8,128)(2,1)}, bf16[192,640]{1,0:T(8,128)(2,1)S(1)}, u32[]{:S(2)}, u32[]{:S(2)}) collective-permute-start(bf16[192,640]{1,0:T(8,128)(2,1)} %get-tuple-element.130), channel_id=1, source_target_pairs={{0,4},{4,0},{1,5},{5,1},{2,6},{6,2},{3,7},{7,3},{8,12},{12,8},{9,1... | collective-permute-start | bytes 737288 | tf_op jit(solution)/shard_map/ppermute | solution.py:40
  294.5 47.2 %collective-permute-start.62 = (bf16[960,480]{1,0:T(8,128)(2,1)}, bf16[960,480]{1,0:T(8,128)(2,1)}, u32[]{:S(2)}, u32[]{:S(2)}) collective-permute-start(bf16[960,480]{1,0:T(8,128)(2,1)} %get-tuple-element.137), channel_id=1, source_target_pairs={{0,8},{4,12},{8,0},{12,4},{16,24},{20,28},{24,16},{28,20},{1,9},{5... | collective-permute-start | bytes 2764808 | tf_op jit(solution)/shard_map/ppermute | solution.py:49
  299.9 47.5 %collective-permute-start.70 = (bf16[960,480]{1,0:T(8,128)(2,1)}, bf16[960,480]{1,0:T(8,128)(2,1)S(1)}, u32[]{:S(2)}, u32[]{:S(2)}) collective-permute-start(bf16[960,480]{1,0:T(8,128)(2,1)} %get-tuple-element.140), channel_id=1, source_target_pairs={{0,8},{4,12},{8,0},{12,4},{16,24},{20,28},{24,16},{28,20},{1,9},{5... | collective-permute-start | bytes 2764808 | tf_op jit(solution)/shard_map/ppermute | solution.py:49
  303.9 27.9 %collective-permute-start.42 = (bf16[192,960]{1,0:T(8,128)(2,1)}, bf16[192,960]{1,0:T(8,128)(2,1)}, u32[]{:S(2)}, u32[]{:S(2)}) collective-permute-start(bf16[192,960]{1,0:T(8,128)(2,1)} %add_convert_fusion.2), channel_id=1, source_target_pairs={{0,16},{4,20},{8,24},{12,28},{16,0},{20,4},{24,8},{28,12},{1,17},{... | collective-permute-start | bytes 1105928 | tf_op jit(solution)/shard_map/ppermute | solution.py:49
  346.7 35.3 %collective-permute-start.64 = (bf16[240,480]{1,0:T(8,128)(2,1)}, bf16[240,480]{1,0:T(8,128)(2,1)}, u32[]{:S(2)}, u32[]{:S(2)}) collective-permute-start(bf16[240,480]{1,0:T(8,128)(2,1)} %get-tuple-element.194), channel_id=1, source_target_pairs={{0,2},{1,3},{2,0},{3,1},{4,6},{5,7},{6,4},{7,5},{8,10},{9,11},{10,... | collective-permute-start | bytes 691208 | tf_op jit(solution)/shard_map/ppermute | solution.py:40
  348.4 37.8 %collective-permute-start.71 = (bf16[240,480]{1,0:T(8,128)(2,1)}, bf16[240,480]{1,0:T(8,128)(2,1)}, u32[]{:S(2)}, u32[]{:S(2)}) collective-permute-start(bf16[240,480]{1,0:T(8,128)(2,1)} %get-tuple-element.189), channel_id=1, source_target_pairs={{0,1},{1,0},{2,3},{3,2},{4,5},{5,4},{6,7},{7,6},{8,9},{9,8},{10,11... | collective-permute-start | bytes 691208 | tf_op jit(solution)/shard_map/ppermute | solution.py:40
  349.3 37.0 %collective-permute-start.73 = (bf16[240,480]{1,0:T(8,128)(2,1)}, bf16[240,480]{1,0:T(8,128)(2,1)}, u32[]{:S(2)}, u32[]{:S(2)}) collective-permute-start(bf16[240,480]{1,0:T(8,128)(2,1)} %get-tuple-element.190), channel_id=1, source_target_pairs={{0,3},{1,2},{2,1},{3,0},{4,7},{5,6},{6,5},{7,4},{8,11},{9,10},{10,... | collective-permute-start | bytes 691208 | tf_op jit(solution)/shard_map/ppermute | solution.py:40
  359.2 40.5 %collective-permute-start.72 = (bf16[240,480]{1,0:T(8,128)(2,1)}, bf16[240,480]{1,0:T(8,128)(2,1)S(1)}, u32[]{:S(2)}, u32[]{:S(2)}) collective-permute-start(bf16[240,480]{1,0:T(8,128)(2,1)} %get-tuple-element.191), channel_id=1, source_target_pairs={{0,2},{1,3},{2,0},{3,1},{4,6},{5,7},{6,4},{7,5},{8,10},{9,11},{10,... | collective-permute-start | bytes 691208 | tf_op jit(solution)/shard_map/ppermute | solution.py:40
  359.3 42.7 %collective-permute-start.55 = (bf16[256,320]{1,0:T(8,128)(2,1)S(1)}, bf16[256,320]{1,0:T(8,128)(2,1)S(1)}, u32[]{:S(2)}, u32[]{:S(2)}) collective-permute-start(bf16[256,320]{1,0:T(8,128)(2,1)S(1)} %get-tuple-element.195), channel_id=1, source_target_pairs={{0,1},{1,0},{2,3},{3,2},{4,5},{5,4},{6,7},{7,6},{8,9},{9,8},{10,11... | collective-permute-start | bytes 491528 | tf_op jit(solution)/shard_map/ppermute | solution.py:40
  386.3 21.8 %collective-permute-start.68 = (bf16[240,480]{1,0:T(8,128)(2,1)S(1)}, bf16[240,480]{1,0:T(8,128)(2,1)S(1)}, u32[]{:S(2)}, u32[]{:S(2)}) collective-permute-start(bf16[240,480]{1,0:T(8,128)(2,1)S(1)} %add_convert_fusion.13), channel_id=1, source_target_pairs={{0,20},{4,16},{8,28},{12,24},{16,4},{20,0},{24,12},{28,8},{1,21},{... | collective-permute-start | bytes 691208 | tf_op jit(solution)/shard_map/ppermute | solution.py:49
  424.7 27.9 %collective-permute-start.61 = (bf16[256,320]{1,0:T(8,128)(2,1)S(1)}, bf16[256,320]{1,0:T(8,128)(2,1)}, u32[]{:S(2)}, u32[]{:S(2)}) collective-permute-start(bf16[256,320]{1,0:T(8,128)(2,1)S(1)} %add_convert_fusion.21), channel_id=1, source_target_pairs={{0,8},{4,12},{8,0},{12,4},{16,24},{20,28},{24,16},{28,20},{1,9},{5... | collective-permute-start | bytes 491528 | tf_op jit(solution)/shard_map/ppermute | solution.py:49
  426.7 23.2 %collective-permute-start.81 = (bf16[240,960]{1,0:T(8,128)(2,1)}, bf16[240,960]{1,0:T(8,128)(2,1)S(1)}, u32[]{:S(2)}, u32[]{:S(2)}) collective-permute-start(bf16[240,960]{1,0:T(8,128)(2,1)} %reduce-scatter.2.cloned.1.call-done.refs_0_), channel_id=1, source_target_pairs={{0,16},{4,20},{8,24},{12,28},{16,0},{20,4},{24,8},{28,12},{1,17},{... | collective-permute-start | bytes 1382408 | tf_op jit(solution)/shard_map/ppermute | solution.py:49
  427.6 22.5 %collective-permute-start.78 = (bf16[240,960]{1,0:T(8,128)(2,1)}, bf16[240,960]{1,0:T(8,128)(2,1)S(1)}, u32[]{:S(2)}, u32[]{:S(2)}) collective-permute-start(bf16[240,960]{1,0:T(8,128)(2,1)} %reduce-scatter.2.cloned.1.call-done.refs_0_), channel_id=1, source_target_pairs={{0,4},{4,0},{8,12},{12,8},{16,20},{20,16},{24,28},{28,24},{1,5},{5... | collective-permute-start | bytes 1382408 | tf_op jit(solution)/shard_map/ppermute | solution.py:49
  428.5 28.1 %collective-permute-start.79 = (bf16[240,960]{1,0:T(8,128)(2,1)S(1)}, bf16[240,960]{1,0:T(8,128)(2,1)}, u32[]{:S(2)}, u32[]{:S(2)}) collective-permute-start(bf16[240,960]{1,0:T(8,128)(2,1)S(1)} %copy-done.17), channel_id=1, source_target_pairs={{0,8},{4,12},{8,0},{12,4},{16,24},{20,28},{24,16},{28,20},{1,9},{5... | collective-permute-start | bytes 1382408 | tf_op jit(solution)/shard_map/ppermute | solution.py:49
  (123 other events, 1775.3 us)
Sparse Core Ops, SparseCore 0:
  45.2 70.0 all-gather.1
  239.1 40.4 reduce-scatter.1

commit v3 on v2

--- a/solution.py
+++ b/solution.py
@@ -167,39 +167,53 @@
     for ref in (gate_ref, up_ref):
         for z in range(shards):
             out.append(dot_plain(ref[:, z * span : (z + 1) * span], pick))
-    own = down_ref[pl.ds(pl.multiple_of(member * piece, piece), piece), :]
-    folds = rows // piece
-    down = jnp.concatenate(lane_blocks(own, folds), axis=0)
-    both = jnp.concatenate(out, axis=1).astype(BF16)
-    out_ref[...] = jnp.concatenate([both, down], axis=1)
+    down = dot_plain(down_ref[...], pick)
+    out += [down[b : b + rows, :] for b in range(0, down_ref.shape[0], rows)]
+    out_ref[...] = jnp.concatenate(out, axis=1).astype(BF16)
+
+
+def quarter_kernel(members, spots, query_ref, output_ref, out_ref):
+    size = query_ref.shape[1] // members
+    for i in range(members):
+
+        @pl.when(spots[2] == i)
+        def _():
+            out_ref[...] = jnp.concatenate(
+                [ref[:, i * size : (i + 1) * size] for ref in (query_ref, output_ref)], axis=1
+            )
+
+
+def stack_kernel(spots, *refs):
+    stack_rows(refs[-1], refs[:-1])
 
 
 def begin_kernel(shards, spots, *refs):
-    ins, outs, scratch = split_refs(refs, 7 + 2 * (shards - 1), 4, 3)
+    ins, outs, scratch = split_refs(refs, 7 + 2 * (shards - 1), 5, 3)
     tokens_ref, gain_one, gain_two, key_ref, value_ref, cos_ref, sin_ref = ins[:7]
     mine, other = split_refs(ins[7:], shards - 1, shards - 1)
-    kv_ref, normed_ref, inverse_ref, gains_ref = outs
+    kv_ref, normed_ref, turned_ref, inverse_ref, gains_ref = outs
     blocks, normed_blocks, gain_blocks = scratch
     core, shard = spots[0], spots[1]
-    rows = key_ref.shape[0]
+    width = key_ref.shape[0]
     values = tokens_ref[...].astype(F32)
     inverse = lax.rsqrt(jnp.mean(values * values, axis=-1, keepdims=True) + EPSILON)
     inverse_ref[...] = inverse
     for z, block in enumerate(lane_blocks(values * inverse, shards)):
         blocks[z] = block
-    sums = []
+    sums, order = [], []
     for r in range(shards):
         at = shard ^ r
         if r == 0:
             pair = jnp.concatenate([gain_one[...], gain_two[...]], axis=0).astype(F32)
         else:
-            pair = mine[r - 1][rows : rows + EXTRA_ROWS, :rows].astype(F32)[0:2, :]
+            pair = mine[r - 1][width : width + EXTRA_ROWS, :].astype(F32)[0:2, :]
         gain_blocks[at, 0:2, :] = pair
         normed = (blocks[at] * pair[0:1, :]).astype(BF16)
         normed_blocks[at] = normed
-        left = key_ref[...] if r == 0 else mine[r - 1][:rows, :]
-        right = value_ref[...] if r == 0 else other[r - 1][:rows, :]
-        sums.append((dot_plain(normed, left), dot_plain(normed, right)))
+        order.append(normed)
+        left = key_ref[...] if r == 0 else mine[r - 1][:width, :]
+        right = value_ref[...] if r == 0 else other[r - 1][:width, :]
+        sums.append((dot_last(normed, left), dot_last(normed, right)))
     first = sum(s[0] for s in sums[1:])
     second = sum(s[1] for s in sums[1:])
     keys = jnp.where(core == 0, first, second) + sums[0][0]
@@ -207,6 +221,7 @@
     keys = rope_lanes(keys, cos_ref[...], sin_ref[...])
     kv_ref[...] = jnp.concatenate([keys, vals], axis=1).astype(BF16)
     normed_ref[...] = join_lanes(normed_blocks)
+    turned_ref[...] = jnp.concatenate(order, axis=1)
     gains_ref[...] = jnp.zeros_like(gains_ref)
     gains_ref[0:2, :] = jnp.concatenate([gain_blocks[z][0:2, :] for z in range(shards)], axis=1)
 
@@ -230,16 +245,20 @@
 
 
 def near_kernel(chunk, members, pieces, spots, *refs):
-    ins, outs, scratch = split_refs(refs, 5 + members + pieces, 4, 2)
-    normed_ref, key_pos_ref, query_pos_ref, cos_ref, sin_ref = ins[:5]
-    weights, parts = split_refs(ins[5:], members, pieces)
+    ins, outs, scratch = split_refs(refs, 6 + members + pieces, 4, 2)
+    normed_ref, key_pos_ref, query_pos_ref, cos_ref, sin_ref, local_ref = ins[:6]
+    weights, parts = split_refs(ins[6:], members, pieces)
     queries_ref, largest_ref, total_ref, weighted_ref = outs
     blocks, kv_ref = scratch
     dp = spots[2]
     stack_rows(kv_ref, parts)
+    own = local_ref.shape[0]
+    size = blocks.shape[-1]
+    away = normed_ref[:, own:]
     for j in range(members):
-        blocks[dp ^ j] = dot_plain(normed_ref[...], weights[j][...])
-    roped = rope_lanes(join_lanes(blocks), cos_ref[...], sin_ref[...]).astype(BF16)
+        blocks[dp ^ j] = dot_plain(away, weights[j][:, :size])
+    raw = join_lanes(blocks) + dot_plain(normed_ref[:, :own], local_ref[...])
+    roped = rope_lanes(raw, cos_ref[...], sin_ref[...]).astype(BF16)
     queries_ref[...] = roped * jnp.asarray(1.0 / math.sqrt(HEAD_DIM), BF16)
     columns = GROUPS * queries_ref.shape[0]
     query_pos = query_pos_ref[...]
@@ -258,14 +277,14 @@
         weighted_ref[head] = weighted
 
 
-def far_kernel(chunk, members, pieces, spots, *refs):
-    ins, outs, scratch = split_refs(refs, 8 + members + pieces, 6, 2)
+def far_kernel(chunk, shards, members, pieces, spots, *refs):
+    ins, outs, scratch = split_refs(refs, 9 + members + pieces, 6, 3)
     (queries_ref, key_pos_ref, query_pos_ref, largest_ref, total_ref, weighted_ref, tokens_ref,
-     gains_ref) = ins[:8]
-    weights, parts = split_refs(ins[8:], members, pieces)
+     gains_ref, local_ref) = ins[:9]
+    weights, parts = split_refs(ins[9:], members, pieces)
     attended_ref, turned_ref, log_ref, residual_ref, inverse_ref, normed_ref = outs
-    blocks, kv_ref = scratch
-    dp = spots[2]
+    blocks, kv_ref, head_blocks = scratch
+    shard, dp = spots[1], spots[2]
     stack_rows(kv_ref, parts)
     rows = queries_ref.shape[0]
     query_pos = query_pos_ref[...]
@@ -283,9 +302,14 @@
         heads += [straight[g * rows : (g + 1) * rows, :] for g in range(GROUPS)]
     attended = jnp.concatenate(heads, axis=1).astype(BF16)
     attended_ref[...] = attended
+    for z, block in enumerate(lane_blocks(attended, shards)):
+        head_blocks[z] = block
+    away = jnp.concatenate([head_blocks[shard ^ r] for r in range(1, shards)], axis=1)
+    size = blocks.shape[-1]
     for j in range(members):
-        blocks[dp ^ j] = dot_plain(attended, weights[j][...])
-    residual = tokens_ref[...].astype(F32) + join_lanes(blocks)
+        blocks[dp ^ j] = dot_plain(away, weights[j][:, size:])
+    added = join_lanes(blocks) + dot_plain(head_blocks[shard], local_ref[...])
+    residual = tokens_ref[...].astype(F32) + added
     residual_ref[...] = residual
     normed, inverse = norm_rows(residual, gains_ref[1:2, :])
     inverse_ref[...] = inverse
@@ -294,74 +318,69 @@
 
 def unfold_down(pack_ref, down_ref, shards, part):
     piece = part // shards
-    folds = (pack_ref.shape[0] // shards) // piece
-    for z in range(shards):
-        base = z * folds * piece
-        down_ref[z * piece : (z + 1) * piece, :] = jnp.concatenate(
-            [pack_ref[base + b * piece : base + (b + 1) * piece, 2 * part :] for b in range(folds)],
-            axis=1,
+    rows = pack_ref.shape[0] // shards
+    for b in range(down_ref.shape[0] // rows):
+        at = 2 * part + b * piece
+        down_ref[b * rows : (b + 1) * rows, :] = jnp.concatenate(
+            [pack_ref[z * rows : (z + 1) * rows, at : at + piece] for z in range(shards)], axis=1
         )
 
 
 def feed_kernel(shards, pieces, spots, *refs):
-    ins, outs, scratch = split_refs(refs, 1 + 2 * pieces, pieces + 2, 3)
+    ins, outs, scratch = split_refs(refs, 1 + 2 * pieces, 3, 3)
     pack_ref = ins[0]
     normed_parts, cot_parts = split_refs(ins[1:], pieces, pieces)
-    grads, (act_ref, both_ref) = outs[:pieces], outs[pieces:]
+    grad_ref, act_ref, both_ref = outs
     normed_ref, cot_ref, down_ref = scratch
     part = pack_ref.shape[1] // 3
-    rows = normed_parts[0].shape[0]
     stack_rows(normed_ref, normed_parts)
     stack_rows(cot_ref, cot_parts)
     unfold_down(pack_ref, down_ref, shards, part)
     gate_up = dot_plain(normed_ref[...], pack_ref[:, : 2 * part])
     gate, upward = gate_up[:, :part], gate_up[:, part:]
-    act_grad = dot_last(cot_ref[...], down_ref[...])
+    act_grad = dot_plain(cot_ref[...], down_ref[...])
     sigmoid_gate = jax.nn.sigmoid(gate)
     silu = gate * sigmoid_gate
     act_ref[...] = (silu * upward).astype(BF16)
     gate_grad = act_grad * upward * sigmoid_gate * (1.0 + gate * (1.0 - sigmoid_gate))
     both_ref[...] = jnp.concatenate([gate_grad, act_grad * silu], axis=1).astype(BF16)
-    grad = dot_last(both_ref[...], pack_ref[:, : 2 * part])
-    for i in range(pieces):
-        grads[i][...] = grad[i * rows : (i + 1) * rows, :].astype(BF16)
+    grad_ref[...] = dot_last(both_ref[...], pack_ref[:, : 2 * part]).astype(BF16)
 
 
 def feed_weights_kernel(shards, pieces, spots, *refs):
-    ins, outs, scratch = split_refs(refs, 5 + 2 * pieces, pieces + 1, 5)
+    ins, outs, scratch = split_refs(refs, 5 + 2 * pieces, 3, 5)
     pack_ref, act_a, act_b, both_a, both_b = ins[:5]
     normed_parts, cot_parts = split_refs(ins[5:], pieces, pieces)
-    results, grad_ref = outs[:pieces], outs[pieces]
+    result_a, result_b, grad_ref = outs
     normed_ref, cot_ref, act_ref, both_ref, down_ref = scratch
     part = pack_ref.shape[1] // 3
     piece = part // shards
-    rows = normed_parts[0].shape[0]
+    rows = grad_ref.shape[0] // shards
     stack_rows(normed_ref, normed_parts)
     stack_rows(cot_ref, cot_parts)
     stack_rows(act_ref, (act_a, act_b))
     stack_rows(both_ref, (both_a, both_b))
     unfold_down(pack_ref, down_ref, shards, part)
     grad_ref[:, : 2 * part] = dot_first(normed_ref[...], both_ref[...]).astype(BF16)
-    down_grad = dot_first(act_ref[...], cot_ref[...]).astype(BF16)
-    folds = (grad_ref.shape[0] // shards) // piece
+    down_grad = dot_first(cot_ref[...], act_ref[...]).astype(BF16)
+    folds = down_grad.shape[0] // rows
     for z in range(shards):
-        rows_of = down_grad[z * piece : (z + 1) * piece, :]
-        for b, block in enumerate(lane_blocks(rows_of, folds)):
-            base = (z * folds + b) * piece
-            grad_ref[base : base + piece, 2 * part :] = block
-    result = dot_plain(act_ref[...], down_ref[...])
-    for i in range(pieces):
-        results[i][...] = result[i * rows : (i + 1) * rows, :].astype(BF16)
-
-
-def middle_kernel(members, spots, *refs):
-    ins, outs, scratch = split_refs(refs, 9 + members, 4, 1)
-    own_a, own_b, one_ref, two_ref, three_ref, residual_ref, inverse_ref, cot_ref, gains_ref = ins[:9]
-    weights = ins[9:]
+        at = z * piece
+        grad_ref[z * rows : (z + 1) * rows, 2 * part :] = jnp.concatenate(
+            [down_grad[b * rows : (b + 1) * rows, at : at + piece] for b in range(folds)], axis=1
+        )
+    result_a[...] = dot_last(act_a[...], down_ref[...]).astype(BF16)
+    result_b[...] = dot_last(act_b[...], down_ref[...]).astype(BF16)
+
+
+def middle_kernel(shards, members, spots, *refs):
+    ins, outs, scratch = split_refs(refs, 10 + members, 4, 2)
+    (own_a, own_b, one_ref, two_ref, three_ref, residual_ref, inverse_ref, cot_ref, gains_ref,
+     local_ref) = ins[:10]
+    weights = ins[10:]
     residual_grad_ref, low_ref, attended_grad_ref, gain_grad_ref = outs
-    (blocks,) = scratch
-    dp = spots[2]
-    grad = (own_a[...].astype(F32) + own_b[...].astype(F32)) + one_ref[...].astype(F32)
+    rows = cot_ref.shape[0]
+    grad = (own_a[:rows, :].astype(F32) + own_b[:rows, :].astype(F32)) + one_ref[...].astype(F32)
     grad = grad + two_ref[...].astype(F32) + three_ref[...].astype(F32)
     residual, inverse = residual_ref[...], inverse_ref[...]
     gain_grad_ref[...] = jnp.sum(grad * residual * inverse, axis=0, keepdims=True)
@@ -369,40 +388,52 @@
     residual_grad_ref[...] = residual_grad
     low = residual_grad.astype(BF16)
     low_ref[...] = low
+    attended_grad_ref[...] = back_through(
+        shards, members, spots, low, weights, local_ref, scratch, 1
+    ).astype(BF16)
+
+
+def back_through(shards, members, spots, low, weights, local_ref, scratch, which):
+    blocks, out_blocks = scratch
+    shard, dp = spots[1], spots[2]
     for i, block in enumerate(lane_blocks(low, members)):
         blocks[i] = block
-    attended_grad_ref[...] = sum(
-        dot_last(blocks[dp ^ j], weights[j][...]) for j in range(members)
-    ).astype(BF16)
-
-
-def halves_by_core(core, values):
-    low, high = lane_blocks(values, 2)
-    return jnp.where(core == 0, low, high), jnp.where(core == 0, high, low)
-
-
-def output_grad_kernel(spots, attended_ref, low_ref, keep_ref, send_ref):
-    keep, send = halves_by_core(spots[0], low_ref[...].astype(F32))
-    attended = attended_ref[...]
-    send_ref[...] = dot_first(attended, send.astype(BF16)).astype(BF16)
-    keep_ref[...] = dot_first(attended, keep.astype(BF16)).astype(BF16)
-
-
-def query_grad_kernel(members, spots, normed_ref, low_ref, *refs):
-    weights, (keep_ref, send_ref, back_ref), (blocks,) = split_refs(refs, members, 3, 1)
+    size = blocks.shape[-1]
+    at = slice(which * size, (which + 1) * size)
+    away = sum(dot_last(blocks[dp ^ j], weights[j][:, at]) for j in range(members))
+    out_blocks[shard] = dot_last(low, local_ref[...])
+    for r, block in enumerate(lane_blocks(away, shards - 1)):
+        out_blocks[shard ^ (r + 1)] = block
+    return join_lanes(out_blocks)
+
+
+def weight_grad_kernel(members, spots, left_ref, low_ref, keep_ref, send_ref, blocks):
     dp = spots[2]
-    low = low_ref[...]
-    keep, send = halves_by_core(spots[0], low.astype(F32))
-    normed = normed_ref[...]
-    send_ref[...] = dot_first(normed, send.astype(BF16)).astype(BF16)
-    keep_ref[...] = dot_first(normed, keep.astype(BF16)).astype(BF16)
-    for i, block in enumerate(lane_blocks(low, members)):
+    for i, block in enumerate(lane_blocks(low_ref[...], members)):
         blocks[i] = block
-    back_ref[...] = sum(dot_last(blocks[dp ^ j], weights[j][...]) for j in range(members))
+    left = left_ref[...]
+    for j in range(members):
+        out_ref = send_ref if j & 1 else keep_ref
+        out_ref[j // 2] = dot_first(left, blocks[dp ^ j]).astype(BF16)
+
+
+def join_kernel(members, spots, pair_ref, other_ref, out_ref, blocks):
+    dp = spots[2]
+    for j in range(members):
+        ref = other_ref if j & 1 else pair_ref
+        blocks[dp ^ j] = ref[j // 2]
+    out_ref[...] = join_lanes(blocks).astype(F32)
+
+
+def query_back_kernel(shards, members, spots, low_ref, local_ref, *refs):
+    weights, (back_ref,), scratch = split_refs(refs, members, 1, 2)
+    back_ref[...] = back_through(
+        shards, members, spots, low_ref[...], weights, local_ref, scratch, 0
+    )
 
 
 def back_kernel(chunk, pieces, first, last, spots, *refs):
-    ins, outs, scratch = split_refs(refs, 9 + pieces, pieces + 1, 2)
+    ins, outs, scratch = split_refs(refs, 9 + pieces, (pieces if last else 2) + 1, 2)
     (queries_ref, key_pos_ref, query_pos_ref, cos_ref, sin_ref, turned_ref, log_ref, grad_ref,
      start_ref) = ins[:9]
     parts = ins[9:]
@@ -448,31 +479,32 @@
         query_grad_ref[...] = rope_lanes(
             jnp.concatenate(heads, axis=1), cos_ref[...], -sin_ref[...]
         ).astype(BF16)
-    for i in range(pieces):
-        kv_grads[i][...] = kv_grad_ref[i * rows : (i + 1) * rows, :]
+    size = kv_ref.shape[0] // len(kv_grads)
+    for i, ref in enumerate(kv_grads):
+        ref[...] = kv_grad_ref[i * size : (i + 1) * size, :]
 
 
 def end_kernel(shards, spots, *refs):
-    ins, outs, scratch = split_refs(refs, 12 + (shards + 1) + 2 * (shards - 1), 3, 1)
+    ins, outs, scratch = split_refs(refs, 11 + (shards + 1) + 2 * (shards - 1), 3, 1)
     (cos_ref, sin_ref, normed_ref, tokens_ref, inverse_ref, gains_ref, back_ref, residual_grad_ref,
-     key_ref, value_ref, gain_two_ref, _) = ins[:12]
-    sums, mine, other = split_refs(ins[12:], shards + 1, shards - 1, shards - 1)
+     key_ref, value_ref, gain_two_ref) = ins[:11]
+    sums, mine, other = split_refs(ins[11:], shards + 1, shards - 1, shards - 1)
     input_grad_ref, keep_ref, send_ref = outs
     (blocks,) = scratch
     core, shard = spots[0], spots[1]
-    rows = key_ref.shape[0]
-    width = key_ref.shape[1]
-    total = sum(s[...].astype(F32) for s in sums)
+    width, span = key_ref.shape
+    rows = tokens_ref.shape[0]
+    total = sum(s[:rows, :].astype(F32) for s in sums)
     keys = rope_lanes(total[:, :width], cos_ref[...], -sin_ref[...])
     values = total[:, width:]
     keep = jnp.where(core == 0, keys, values).astype(BF16)
     send = jnp.where(core == 0, values, keys).astype(BF16)
-    blocks[shard] = dot_last(keys.astype(BF16), key_ref[...]) + dot_last(
+    blocks[shard] = dot_plain(keys.astype(BF16), key_ref[...]) + dot_plain(
         values.astype(BF16), value_ref[...]
     )
     for r in range(1, shards):
-        blocks[shard ^ r] = dot_last(keep, mine[r - 1][:rows, :]) + dot_last(
-            send, other[r - 1][:rows, :]
+        blocks[shard ^ r] = dot_plain(keep, mine[r - 1][:width, :]) + dot_plain(
+            send, other[r - 1][:width, :]
         )
     normed_grad = back_ref[...] + join_lanes(blocks)
     inputs, inverse = tokens_ref[...].astype(F32), inverse_ref[...]
@@ -486,13 +518,13 @@
         (send_ref, send, jnp.where(core == 0, two, gain_grad)),
         (keep_ref, keep, jnp.where(core == 0, gain_grad, two)),
     ):
-        grad = dot_first(normed, low).astype(BF16)
-        span = rows + EXTRA_ROWS
-        for z, block in enumerate(lane_blocks(gain, shards)):
-            out_ref[z * span : z * span + rows, :] = grad[z * rows : (z + 1) * rows, :]
-            padded = jnp.concatenate([block, jnp.zeros((1, width - rows), F32)], axis=1)
-            out_ref[z * span + rows : (z + 1) * span, :] = jnp.broadcast_to(
-                padded, (EXTRA_ROWS, width)
+        grad = dot_first(low, normed).astype(BF16)
+        size = width + EXTRA_ROWS
+        gains = lane_blocks(gain, shards)
+        for z, block in enumerate(lane_blocks(grad, shards)):
+            out_ref[z * size : z * size + width, :] = block
+            out_ref[z * size + width : (z + 1) * size, :] = jnp.broadcast_to(
+                gains[z], (EXTRA_ROWS, span)
             ).astype(BF16)
 
 
@@ -500,23 +532,23 @@
     parts, outs, (blocks,) = split_refs(refs, members, 3, 1)
     gate_ref, up_ref, down_ref = outs
     member = spots[3]
-    part = parts[0].shape[1] // 3
-    piece = part // shards
-    span = part // shards * members
-    folds = parts[0].shape[0] // piece
+    piece = parts[0].shape[1] // 3 // shards
+    rows = parts[0].shape[0]
+    span = piece * members
     for i in range(members):
-        at = member ^ i
-        blocks[at] = parts[i][:, : 2 * part].astype(F32)
-        down = parts[i][:, 2 * part :].astype(F32)
-        down_ref[pl.ds(pl.multiple_of(at * piece, piece), piece), :] = jnp.concatenate(
-            [down[b * piece : (b + 1) * piece, :] for b in range(folds)], axis=1
-        )
-    for which, out_ref in enumerate((gate_ref, up_ref)):
-        for z in range(shards):
-            at = which * part + z * piece
-            out_ref[:, z * span : (z + 1) * span] = jnp.concatenate(
-                [blocks[p, :, at : at + piece] for p in range(members)], axis=1
-            )
+        blocks[member ^ i] = parts[i][...]
+
+    def block(k):
+        at = k * piece
+        return jnp.concatenate(
+            [blocks[p, :, at : at + piece] for p in range(members)], axis=1
+        ).astype(F32)
+
+    for z in range(shards):
+        gate_ref[:, z * span : (z + 1) * span] = block(z)
+        up_ref[:, z * span : (z + 1) * span] = block(shards + z)
+    for b in range(down_ref.shape[0] // rows):
+        down_ref[b * rows : (b + 1) * rows, :] = block(2 * shards + b)
 
 
 def base_of(block_order, stored, block_length):
@@ -575,12 +607,12 @@
     spots = jnp.stack([core, shard, dp, dp * 2 + (ctx & 1)]).astype(jnp.int32)
 
     gain_one, gain_two = attention_gain[None, :], feedforward_gain[None, :]
+    key_turned, value_turned, down_turned = key_weight.T, value_weight.T, down_weight.T
     kv_pack = jnp.concatenate(
         [
-            jnp.where(core == 0, key_weight, value_weight),
+            jnp.where(core == 0, key_turned, value_turned),
             jnp.pad(
-                jnp.concatenate([gain_one, gain_two], axis=0),
-                ((0, EXTRA_ROWS - 2), (0, kv_width - weight_rows)),
+                jnp.concatenate([gain_one, gain_two], axis=0), ((0, EXTRA_ROWS - 2), (0, 0))
             ),
         ],
         axis=0,
@@ -589,15 +621,17 @@
     kv_other = [swap_core(piece) for piece in kv_mine]
 
     quarter = width // dp_count
-
-    def spread_columns(weight):
-        own = lax.all_gather(
-            lax.dynamic_slice_in_dim(weight, dp * quarter, quarter, 1), "fsdp", axis=0, tiled=True
-        )
-        across = swap_plane(own, 2, 0)
-        return [own, swap_core(own), across, swap_core(across)]
-
-    query_parts = spread_columns(query_weight)
+    (quarters,) = call(
+        functools.partial(quarter_kernel, dp_count), spots,
+        [after(query_weight, kv_pack), output_weight],
+        [((weight_rows, 2 * quarter), BF16)], name="quarter_columns",
+    )
+    (stacked,) = call(
+        stack_kernel, spots, [swap(quarters, "fsdp", r) for r in range(1, shards)],
+        [(((shards - 1) * weight_rows, 2 * quarter), BF16)], name="stack_quarters",
+    )
+    across = swap_plane(stacked, 2, 0)
+    stacks = [stacked, swap_core(stacked), across, swap_core(across)]
 
     offsets = jnp.arange(rows, dtype=jnp.int32)
     my_start = (ctx * shards + shard) * rows
@@ -614,14 +648,17 @@
 
     (pack,) = call(
         functools.partial(pack_kernel, shards, members), spots,
-        [gate_weight, up_weight, down_weight], [((weight_rows, 3 * part), BF16)],
+        [gate_weight, up_weight, down_turned], [((weight_rows, 3 * part), BF16)],
         flops=4 * weight_rows * hidden * part // shards, name="pack_weights",
     )
-    kv_own, normed_one, inverse_one, gains = call(
+    kv_own, normed_one, normed_turned, inverse_one, gains = call(
         functools.partial(begin_kernel, shards), spots,
-        [tokens, gain_one, gain_two, key_weight, value_weight, cosine, sine, *kv_mine, *kv_other],
         [
-            ((rows, 2 * kv_width), BF16), ((rows, width), BF16), ((rows, 1), F32), ((8, width), F32),
+            tokens, gain_one, gain_two, key_turned, value_turned, cosine, sine, *kv_mine, *kv_other,
+        ],
+        [
+            ((rows, 2 * kv_width), BF16), ((rows, width), BF16), ((rows, width), BF16),
+            ((rows, 1), F32), ((8, width), F32),
         ],
         scratch=[
             ((shards, rows, weight_rows), F32), ((shards, rows, weight_rows), BF16),
@@ -632,9 +669,8 @@
     near = [kv_own] + [swap(kv_own, "fsdp", r) for r in range(1, shards)]
     far = [swap(piece, "ctx", d) for d in range(1, ctx_count) for piece in near]
 
-    output_parts = spread_columns(after(output_weight, kv_own))
-    pack_all = lax.all_gather(after(pack, kv_own), "fsdp", axis=0, tiled=True)
-    cot_a, cot_b = plane_pieces(after(cotangent, kv_own))
+    pack_all = lax.all_gather(after(pack, near[-1]), "fsdp", axis=0, tiled=True)
+    cot_a, cot_b = plane_pieces(after(cotangent, near[-1]))
 
     chunk = rows * 2
     unit = 2 * HEADS * rows * near_count * HEAD_DIM
@@ -642,86 +678,123 @@
     turned_shape = ((KV_HEADS, HEAD_DIM, GROUPS * rows), F32)
     queries, largest, total, weighted = call(
         functools.partial(near_kernel, chunk, dp_count, shards), spots,
-        [normed_one, near_pos, query_pos, cosine, sine, *query_parts, *near],
+        [normed_turned, near_pos, query_pos, cosine, sine, query_weight, *stacks, *near],
         [((rows, query_width), BF16), stat, stat, turned_shape],
         scratch=[((dp_count, rows, quarter), F32), ((near_count, 2 * kv_width), BF16)],
         flops=8 * unit, name="attention_near",
     )
     attended, turned, log_total, residual, inverse_two, normed_two = call(
-        functools.partial(far_kernel, chunk, dp_count, len(far)), spots,
+        functools.partial(far_kernel, chunk, shards, dp_count, len(far)), spots,
         [
             queries, far_pos, query_pos, largest, total, weighted, tokens, gains,
-            *output_parts, *far,
+            output_weight, *stacks, *far,
         ],
         [
             ((rows, query_width), BF16), turned_shape, stat, ((rows, width), F32),
             ((rows, 1), F32), ((rows, width), BF16),
         ],
-        scratch=[((dp_count, rows, quarter), F32), ((far_count, 2 * kv_width), BF16)],
+        scratch=[
+            ((dp_count, rows, quarter), F32), ((far_count, 2 * kv_width), BF16),
+            ((shards, rows, weight_rows), BF16),
+        ],
         flops=8 * unit * len(far) // shards, name="attention_far",
     )
 
     normed_a, normed_b = plane_pieces(normed_two)
     token_shape = ((rows, width), BF16)
     half = 4 * rows
+    half_shape = ((half, width), BF16)
 
     def feed(normed, cot):
-        out = call(
+        return call(
             functools.partial(feed_kernel, shards, 4), spots, [pack_all, *normed, *cot],
-            [token_shape] * 4 + [((half, part), BF16), ((half, 2 * part), BF16)],
-            scratch=[((half, width), BF16), ((half, width), BF16), ((part, width), BF16)],
+            [half_shape, ((half, part), BF16), ((half, 2 * part), BF16)],
+            scratch=[((half, width), BF16), ((half, width), BF16), ((width, part), BF16)],
             flops=10 * half * width * part, name="feed_forward",
         )
-        return out[:4], out[4], out[5]
 
     grad_b, act_b, both_b = feed(normed_b, cot_b)
-    from_core = [swap_core(g) for g in grad_b]
+    from_core = swap_core(grad_b)
     grad_a, act_a, both_a = feed(normed_a, cot_a)
 
-    def send_chips(parts_a, parts_b):
-        out = []
-        for k, (a, b) in enumerate(CHIP_MASKS):
-            both = (parts_a[k + 1].astype(F32) + parts_b[k + 1].astype(F32)).astype(BF16)
-            out.append(swap_plane(both, a, b))
-        return out
-
-    grad_chips = send_chips(grad_a, from_core)
-    out = call(
+    def chip_sums(parts_a, parts_b):
+        return [
+            (parts_a[k * rows : (k + 1) * rows].astype(F32)
+             + parts_b[k * rows : (k + 1) * rows].astype(F32)).astype(BF16)
+            for k in range(1, 4)
+        ]
+
+    def send_chips(sums):
+        return [swap_plane(x, a, b) for x, (a, b) in zip(sums, CHIP_MASKS)]
+
+    grad_chips = send_chips(chip_sums(grad_a, from_core))
+    result_a, result_b, pack_grad = call(
         functools.partial(feed_weights_kernel, shards, 8), spots,
         [pack_all, act_a, act_b, both_a, both_b, *normed_a, *normed_b, *cot_a, *cot_b],
-        [token_shape] * 8 + [((width, 3 * part), BF16)],
+        [half_shape, half_shape, ((width, 3 * part), BF16)],
         scratch=[
             ((2 * half, width), BF16), ((2 * half, width), BF16), ((2 * half, part), BF16),
-            ((2 * half, 2 * part), BF16), ((part, width), BF16),
+            ((2 * half, 2 * part), BF16), ((width, part), BF16),
         ],
         flops=16 * half * width * part, name="feed_forward_weights",
     )
-    result_a, result_b, pack_grad = out[:4], out[4:8], out[8]
     pack_share = sum_far(lax.psum_scatter(pack_grad, "fsdp", scatter_dimension=0, tiled=True))
 
     residual_grad, residual_low, attended_grad, second_gain_grad = call(
-        functools.partial(middle_kernel, dp_count), spots,
+        functools.partial(middle_kernel, shards, dp_count), spots,
         [
-            grad_a[0], from_core[0], *grad_chips, residual, inverse_two, cotangent, gains,
-            *output_parts,
+            grad_a, from_core, *grad_chips, residual, inverse_two, cotangent, gains, output_weight,
+            *stacks,
         ],
         [((rows, width), F32), token_shape, ((rows, query_width), BF16), ((1, width), F32)],
-        scratch=[((dp_count, rows, quarter), BF16)],
+        scratch=[((dp_count, rows, quarter), BF16), ((shards, rows, weight_rows), F32)],
         flops=2 * rows * width * query_width, name="residual_back",
     )
 
-    result_core = [swap_core(after(p, residual_low)) for p in result_b]
-    result_chips = send_chips(result_a, result_core)
+    result_core = swap_core(result_b)
+    result_sums = chip_sums(after(result_a, residual_low), result_core)
+    result_chips = send_chips(result_sums)
     result = residual + (
-        (result_a[0].astype(F32) + result_core[0].astype(F32)) + result_chips[0].astype(F32)
+        (result_a[:rows].astype(F32) + result_core[:rows].astype(F32))
+        + result_chips[0].astype(F32)
         + (result_chips[1].astype(F32) + result_chips[2].astype(F32))
     )
 
-    half_shape = ((width, width // 2), BF16)
-    output_keep, output_send = call(
-        output_grad_kernel, spots, [attended, residual_low], [half_shape, half_shape],
-        flops=2 * rows * width * width, name="output_weight_grad",
-    )
+    def weight_grad(left, low, name):
+        pair = ((2, width, quarter), BF16)
+        return call(
+            functools.partial(weight_grad_kernel, dp_count), spots, [left, low], [pair, pair],
+            scratch=[((dp_count, rows, quarter), BF16)],
+            flops=2 * rows * width * width, name=name,
+        )
+
+    def sum_quarters(keep, send):
+        away = swap_core(send)
+        sent = (keep[1].astype(F32) + away[1].astype(F32)).astype(BF16)
+        across = swap_plane(sent, 2, 0)
+        pieces = []
+        for r in range(shards):
+            at = (shard ^ r) * weight_rows
+            parts = [
+                lax.dynamic_slice_in_dim(x, at, weight_rows, 0).astype(F32)
+                for x in (keep[0], away[0], across)
+            ]
+            pieces.append((parts[0] + parts[1] + parts[2]).astype(BF16))
+        total = pieces[0].astype(F32)
+        for r in range(1, shards):
+            total = total + swap(pieces[r], "fsdp", r).astype(F32)
+        own = total.astype(BF16)
+        own = sum_far((own.astype(F32) + swap_plane(own, 0, 1).astype(F32)).astype(BF16))
+        pair = jnp.stack([own, swap_plane(own, 2, 0)])
+        (out,) = call(
+            functools.partial(join_kernel, dp_count), spots, [pair, swap_core(pair)],
+            [((weight_rows, width), F32)], scratch=[((dp_count, weight_rows, quarter), BF16)],
+            name="join_columns",
+        )
+        return out
+
+    output_keep, output_send = weight_grad(attended, residual_low, "output_weight_grad")
+    attended_grad, _, _ = lax.optimization_barrier((attended_grad, output_send, result_sums[2]))
 
     def back(first, last, start, pos, pieces):
         count = pos.shape[0]
@@ -732,7 +805,11 @@
                 queries, pos, query_pos, cosine, sine, turned, log_total, attended_grad, start,
                 *pieces,
             ],
-            [shape] + [((rows, 2 * kv_width), BF16)] * len(pieces),
+            [shape]
+            + (
+                [((rows, 2 * kv_width), BF16)] * len(pieces) if last
+                else [((count // 2, 2 * kv_width), BF16)] * 2
+            ),
             scratch=[((count, 2 * kv_width), BF16), ((count, 2 * kv_width), BF16)],
             flops=20 * unit * len(pieces) // shards,
             name="attention_back_near" if last else "attention_back_far",
@@ -746,16 +823,19 @@
             d == 1, False, query_partial, far_pos[at * rows : (at + shards) * rows],
             far[at : at + shards],
         )
-        far_grads += grads
-    home = [
-        [swap(far_grads[(d - 1) * shards + r], "ctx", d) for d in range(1, ctx_count)]
-        for r in range(shards)
-    ]
+        far_grads.append([swap(g, "ctx", d) for g in (grads[1], grads[0])][::-1])
     query_low, near_grads = back(False, True, query_partial, near_pos, near)
-    kv_sums = [
-        near_grads[r].astype(F32) + sum(h.astype(F32) for h in home[r]) for r in range(shards)
-    ]
-    kv_arrived = [swap(kv_sums[r].astype(BF16), "fsdp", r) for r in range(1, shards)]
+    pack_share, *near_grads = lax.optimization_barrier((pack_share, *near_grads))
+
+    def home(r):
+        at = (r % 2) * rows
+        return sum(pair[r // 2][at : at + rows].astype(F32) for pair in far_grads)
+
+    kv_arrived = {
+        r: swap((near_grads[r].astype(F32) + home(r)).astype(BF16), "fsdp", r)
+        for r in reversed(range(1, shards))
+    }
+    share_a, share_b = plane_pieces(pack_share)
 
     def pieces_of(keep, arrived, span):
         out = []
@@ -782,25 +862,25 @@
             jnp.where(core == 0, low, away).astype(F32), jnp.where(core == 0, away, low).astype(F32)
         )
 
-    output_weight_grad = jnp.concatenate(sum_devices(output_keep, output_send, weight_rows), axis=1)
-
-    query_keep, query_send, query_back = call(
-        functools.partial(query_grad_kernel, dp_count), spots,
-        [normed_one, query_low, *query_parts],
-        [half_shape, half_shape, ((rows, width), F32)],
-        scratch=[((dp_count, rows, quarter), BF16)],
-        flops=4 * rows * width * width, name="query_weight_grad",
-    )
-    query_weight_grad = jnp.concatenate(sum_devices(query_keep, query_send, weight_rows), axis=1)
-
-    span = weight_rows + EXTRA_ROWS
-    packed_shape = ((shards * span, kv_width), BF16)
+    query_keep, query_send = weight_grad(normed_one, query_low, "query_weight_grad")
+    (query_back,) = call(
+        functools.partial(query_back_kernel, shards, dp_count), spots,
+        [query_low, query_weight, *stacks], [((rows, width), F32)],
+        scratch=[((dp_count, rows, quarter), BF16), ((shards, rows, weight_rows), F32)],
+        flops=2 * rows * width * width, name="query_back",
+    )
+    output_weight_grad = sum_quarters(output_keep, output_send)
+    query_weight_grad = sum_quarters(query_keep, query_send)
+
+    span = kv_width + EXTRA_ROWS
+    packed_shape = ((shards * span, weight_rows), BF16)
+    home_own = far_grads[0][0] if ctx_count == 2 else home(0)
     input_grad, kv_keep, kv_send = call(
         functools.partial(end_kernel, shards), spots,
         [
             cosine, sine, normed_one, tokens, inverse_one, gains, query_back, residual_grad,
-            key_weight, value_weight, second_gain_grad, gain_one,
-            near_grads[0], sum(h.astype(F32) for h in home[0]), *kv_arrived, *kv_mine, *kv_other,
+            key_turned, value_turned, second_gain_grad, near_grads[0], home_own,
+            *[kv_arrived[r] for r in range(1, shards)], *kv_mine, *kv_other,
         ],
         [((rows, width), F32), packed_shape, packed_shape],
         scratch=[((shards, rows, weight_rows), F32)],
@@ -808,7 +888,6 @@
     )
     first, second = sum_devices(kv_keep, kv_send, span)
 
-    share_a, share_b = plane_pieces(pack_share)
     share_by_mask = [None] * members
     for k, (a, b) in enumerate(((0, 0),) + CHIP_MASKS):
         share_by_mask[2 * a + b] = share_a[k]
@@ -817,24 +896,24 @@
         functools.partial(spread_kernel, shards, members), spots, share_by_mask,
         [
             ((weight_rows, hidden), F32), ((weight_rows, hidden), F32),
-            ((down_weight.shape[0], width), F32),
-        ],
-        scratch=[((members, weight_rows, 2 * part), F32)],
+            ((width, down_weight.shape[0]), F32),
+        ],
+        scratch=[((members, weight_rows, 3 * part), BF16)],
         name="feed_forward_out",
     )
 
     return (
         result[None],
         input_grad[None],
-        first[weight_rows, :weight_rows],
+        first[kv_width],
         query_weight_grad,
-        first[:weight_rows],
-        second[:weight_rows],
+        first[:kv_width].T,
+        second[:kv_width].T,
         output_weight_grad,
-        second[weight_rows, :weight_rows],
+        second[kv_width],
         gate_weight_grad,
         up_weight_grad,
-        down_weight_grad,
+        down_weight_grad.T,
     )
 
 

time: 480 us -> 432 us (0.900)
  blocking collectives: 68.9 us -> 0 us
  Pallas kernels: 113 us -> 127 us
  starting transfers between devices: 77.5 us -> 89.8 us
    all_gather x2 -> x0, blocking collectives: 68.9 us -> none  [spread_columns(): lax.all_gather(lax.dynamic_slice_in_dim(weight, dp * quarter, quarter, 1)...]
    ppermute x59 -> x50, waiting for transfers between devices: 79.1 us -> 60.3 us  [swap_plane(): return lax.ppermute(x, ('dp', 'ctx'), pairs)]
    ppermute x26 -> x27, starting transfers between devices: 39.7 us -> 54.6 us  [swap(): return lax.ppermute(x, axis, [(i, i ^ mask) for i in range(count)])]
    ppermute x26 -> x27, waiting for transfers between devices: 68.9 us -> 83.3 us  [swap(): return lax.ppermute(x, axis, [(i, i ^ mask) for i in range(count)])]
    pallas_call x14 -> x19, Pallas kernels: 113 us -> 127 us  [call(): pl.pallas_call(kernel, out_shape=outs, in_specs=specs, out_specs=tuple((p...]
    unnamed x146 -> x140, local copies, waits for them, and re-layouts: 16 us -> 6.79 us
    convert_element_type x10 -> x12, other arithmetic: 6.13 us -> 13.9 us  [the longest x2 3.88 us: sum_quarters(): sent = (keep[1].astype(F32) + away[1].astype(F32)).astype(BF16)]
    ppermute x59 -> x50, starting transfers between devices: 37.7 us -> 34.9 us  [swap_plane(): return lax.ppermute(x, ('dp', 'ctx'), pairs)]
  transfers between devices with their start and end apart: 87 -> 79, of which waited for: 28 -> 24; matrix products, arithmetic and copies ran while one was open for 9% -> 9% of each run, Pallas kernels for 20% -> 27%
where the time goes in v3:
time: 432 us; the launch traced here: 428 us
  waiting for transfers between devices  144 us (33%)
  Pallas kernels  127 us (29%)
  starting transfers between devices  89.8 us (21%)
  local copies, waits for them, and re-layouts  26.4 us (6%)
  other arithmetic  25.4 us (6%)
  between operations  15.8 us (4%)
    pallas_call x19, Pallas kernels, call(): pl.pallas_call(kernel, out_shape=outs, in_specs=specs, out_specs=tuple((p...  127 us
    ppermute x27, waiting for transfers between devices, swap(): return lax.ppermute(x, axis, [(i, i ^ mask) for i in range(count)])  83.3 us
    ppermute x50, waiting for transfers between devices, swap_plane(): return lax.ppermute(x, ('dp', 'ctx'), pairs)  60.3 us
    ppermute x27, starting transfers between devices, swap(): return lax.ppermute(x, axis, [(i, i ^ mask) for i in range(count)])  54.6 us
    ppermute x50, starting transfers between devices, swap_plane(): return lax.ppermute(x, ('dp', 'ctx'), pairs)  34.9 us
  transfers between devices with their start and end apart: 79, of which 24 were waited for; matrix products, arithmetic and copies ran while one was open for 9% of the time, Pallas kernels for 27%

profile of v3, /device:TPU:0, one launch (start us, length us, event | category | flops | bytes accessed | tf_op | source)
XLA Modules:
  0.0 427.6 jit_solution(17688645726022622169)
XLA Ops:
  9.6 3.1 collective-permute-start
  19.8 8.5 %collective-permute-done.1.refs_8_.refs_17_ = bf16[336,240]{1,0:T(8,128)(2,1)S(1)} collective-permute-done((bf16[336,240]{1,0:T(8,128)(2,1)S(1)}, bf16[336,240]{1,0:T(8,128)(2,1)S(1)}, u32[]{:S(2)}, u32[]{:S(2)}) %collective-permute-start.1) | collective-permute-done | bytes 161312 | tf_op jit(solution)/shard_map/ppermute | solution.py:40
  31.1 3.6 norm_keys_values.1
  43.5 4.1 pack_weights.1
  50.0 27.7 %collective-permute-done.7.refs_1_ = bf16[240,480]{1,0:T(8,128)(2,1)S(1)} collective-permute-done((bf16[240,480]{1,0:T(8,128)(2,1)}, bf16[240,480]{1,0:T(8,128)(2,1)S(1)}, u32[]{:S(2)}, u32[]{:S(2)}) %collective-permute-start.7) | collective-permute-done | bytes 230432 | tf_op jit(solution)/shard_map/ppermute | solution.py:40
  82.8 17.3 %collective-permute-start.12 = (bf16[192,640]{1,0:T(8,128)(2,1)S(1)}, bf16[192,640]{1,0:T(8,128)(2,1)S(1)}, u32[]{:S(2)}, u32[]{:S(2)}) collective-permute-start(bf16[192,640]{1,0:T(8,128)(2,1)S(1)} %copy-done.58), channel_id=1, source_target_pairs={{0,1},{1,0},{2,3},{3,2},{4,5},{5,4},{6,7},{7,6},{8,9},{9,8},{10,11... | collective-permute-start | bytes 737288 | tf_op jit(solution)/shard_map/ppermute | solution.py:40
  103.7 9.5 %collective-permute-done.12.refs_11_.refs_10_ = bf16[192,640]{1,0:T(8,128)(2,1)S(1)} collective-permute-done((bf16[192,640]{1,0:T(8,128)(2,1)S(1)}, bf16[192,640]{1,0:T(8,128)(2,1)S(1)}, u32[]{:S(2)}, u32[]{:S(2)}) %collective-permute-start.12) | collective-permute-done | bytes 245792 | tf_op jit(solution)/shard_map/ppermute | solution.py:40
  116.9 5.0 %collective-permute-done.16.refs_14_.refs_10_ = bf16[192,640]{1,0:T(8,128)(2,1)S(1)} collective-permute-done((bf16[192,640]{1,0:T(8,128)(2,1)S(1)}, bf16[192,640]{1,0:T(8,128)(2,1)S(1)}, u32[]{:S(2)}, u32[]{:S(2)}) %collective-permute-start.16) | collective-permute-done | bytes 245792 | tf_op jit(solution)/shard_map/ppermute | solution.py:40
  123.5 3.7 collective-permute-done.17.refs_15_.refs_11_
  133.9 11.8 %attention_near.1 = (bf16[192,960]{1,0:T(8,128)(2,1)}, f32[5,576]{1,0:T(8,128)}, f32[5,576]{1,0:T(8,128)}, f32[5,64,576]{2,1,0:T(8,128)}) custom-call(s32[4]{0:T(128)} %pad_add_fusion.1.spots, bf16[192,960]{1,0:T(8,128)(2,1)} %get-tuple-element.67.refs_0_, s32[768,1]{1,0:T(8,128)} %slice.144.refs_1_, s32[1,576]{1,0:T(1,128)} %broadcast_in_dim.29.refs_2_, ...), custom_call_target="tpu_custom_call" | custom-call | flops 2264924160 | bytes 5908224 | tf_op jit(solution)/shard_map/attention_near/pallas_call | solution.py:79
  148.5 14.3 %attention_far.1 = (bf16[192,960]{1,0:T(8,128)(2,1)}, f32[5,64,576]{2,1,0:T(8,128)}, f32[5,576]{1,0:T(8,128)}, f32[192,960]{1,0:T(8,128)}, f32[192,1]{1,0:T(8,128)}, /*index=5*/bf16[192,960]{1,0:T(8,128)(2,1)}) custom-call(s32[4]{0:T(128)} %pad_add_fusion.1.spots, bf16[192,960]{1,0:T(8,128)(2,1)} %get-tuple-element.70.refs_0_, s32[768,1]{1,0:T(8,128)} %slice.145.refs_1_, ...), custom_call_target="tpu_custom_call" | custom-call | flops 2264924160 | bytes 7966464 | tf_op jit(solution)/shard_map/attention_far/pallas_call | solution.py:79
  166.9 8.2 %collective-permute-done.19.refs_2_.refs_6_ = bf16[192,960]{1,0:T(8,128)(2,1)S(1)} collective-permute-done((bf16[192,960]{1,0:T(8,128)(2,1)}, bf16[192,960]{1,0:T(8,128)(2,1)S(1)}, u32[]{:S(2)}, u32[]{:S(2)}) %collective-permute-start.19) | collective-permute-done | bytes 368672 | tf_op jit(solution)/shard_map/ppermute | solution.py:49
  175.1 7.8 %collective-permute-done.20.refs_3_.refs_7_ = bf16[192,960]{1,0:T(8,128)(2,1)S(1)} collective-permute-done((bf16[192,960]{1,0:T(8,128)(2,1)}, bf16[192,960]{1,0:T(8,128)(2,1)S(1)}, u32[]{:S(2)}, u32[]{:S(2)}) %collective-permute-start.20) | collective-permute-done | bytes 368672 | tf_op jit(solution)/shard_map/ppermute | solution.py:49
  185.4 8.1 %feed_forward.3 = (bf16[768,960]{1,0:T(8,128)(2,1)}, bf16[768,320]{1,0:T(8,128)(2,1)}, bf16[768,640]{1,0:T(8,128)(2,1)}) custom-call(s32[4]{0:T(128)} %pad_add_fusion.1.spots, bf16[960,960]{1,0:T(8,128)(2,1)} %all-gather.2.cloned.1.call-done.refs_0_, bf16[192,960]{1,0:T(8,128)(2,1)} %copy-done.55, bf16[192,960]{1,0:T(8,128)(2,1)} %copy-done.56, ...), custom_call_target="tpu_custom_call" | custom-call | flops 2359296000 | bytes 7741440 | tf_op jit(solution)/shard_map/feed_forward/pallas_call | solution.py:79
  196.0 8.1 %feed_forward.2 = (bf16[768,960]{1,0:T(8,128)(2,1)}, bf16[768,320]{1,0:T(8,128)(2,1)}, bf16[768,640]{1,0:T(8,128)(2,1)}) custom-call(s32[4]{0:T(128)} %pad_add_fusion.1.spots, bf16[960,960]{1,0:T(8,128)(2,1)} %all-gather.2.cloned.1.call-done.refs_0_, bf16[192,960]{1,0:T(8,128)(2,1)} %get-tuple-element.77.refs_1_.refs_5_, bf16[192,960]{1,0:T(8,128)(2,1)} %copy-done.51, ...), custom_call_target="tpu_custom_call" | custom-call | flops 2359296000 | bytes 7741440 | tf_op jit(solution)/shard_map/feed_forward/pallas_call | solution.py:79
  204.1 12.0 %feed_forward_weights.1 = (bf16[768,960]{1,0:T(8,128)(2,1)}, bf16[768,960]{1,0:T(8,128)(2,1)}, bf16[960,960]{1,0:T(8,128)(2,1)}) custom-call(s32[4]{0:T(128)} %pad_add_fusion.1.spots, bf16[960,960]{1,0:T(8,128)(2,1)} %all-gather.2.cloned.1.call-done.refs_0_, bf16[768,320]{1,0:T(8,128)(2,1)} %get-tuple-element.79.refs_1_, ...), custom_call_target="tpu_custom_call" | custom-call | flops 3774873600 | bytes 15482880 | tf_op jit(solution)/shard_map/feed_forward_weights/pallas_call | solution.py:79
  228.8 6.1 %collective-permute-done.35.refs_2_ = bf16[192,960]{1,0:T(8,128)(2,1)S(1)} collective-permute-done((bf16[192,960]{1,0:T(8,128)(2,1)}, bf16[192,960]{1,0:T(8,128)(2,1)S(1)}, u32[]{:S(2)}, u32[]{:S(2)}) %collective-permute-start.35) | collective-permute-done | bytes 368672 | tf_op jit(solution)/shard_map/ppermute | solution.py:49
  234.9 7.0 %collective-permute-done.36.refs_3_ = bf16[192,960]{1,0:T(8,128)(2,1)S(1)} collective-permute-done((bf16[192,960]{1,0:T(8,128)(2,1)}, bf16[192,960]{1,0:T(8,128)(2,1)S(1)}, u32[]{:S(2)}, u32[]{:S(2)}) %collective-permute-start.36) | collective-permute-done | bytes 368672 | tf_op jit(solution)/shard_map/ppermute | solution.py:49
  243.5 6.4 %residual_back.1 = (f32[192,960]{1,0:T(8,128)}, bf16[192,960]{1,0:T(8,128)(2,1)}, bf16[192,960]{1,0:T(8,128)(2,1)}, f32[1,960]{1,0:T(1,128)}) custom-call(s32[4]{0:T(128)} %pad_add_fusion.1.spots, bf16[768,960]{1,0:T(8,128)(2,1)} %get-tuple-element.85.refs_0_, bf16[768,960]{1,0:T(8,128)(2,1)} %copy-done, bf16[192,960]{1,0:T(8,128)(2,1)} %copy-done.27, ...), custom_call_target="tpu_custom_call" | custom-call | flops 353894400 | bytes 9896448 | tf_op jit(solution)/shard_map/residual_back/pallas_call | solution.py:79
  249.9 3.3 output_weight_grad.1
  254.6 12.6 %attention_back_far.1 = (f32[5,64,576]{2,1,0:T(8,128)}, bf16[384,640]{1,0:T(8,128)(2,1)}, bf16[384,640]{1,0:T(8,128)(2,1)}) custom-call(s32[4]{0:T(128)} %pad_add_fusion.1.spots, bf16[192,960]{1,0:T(8,128)(2,1)} %get-tuple-element.70.refs_0_, s32[768,1]{1,0:T(8,128)} %slice.145.refs_1_, s32[1,576]{1,0:T(1,128)} %broadcast_in_dim.29.refs_2_, ...), custom_call_target="tpu_custom_call" | custom-call | flops 5662310400 | bytes 5128704 | tf_op jit(solution)/shard_map/attention_back_far/pallas_call | solution.py:79
  267.2 13.7 %attention_back_near.1 = (bf16[192,960]{1,0:T(8,128)(2,1)}, bf16[192,640]{1,0:T(8,128)(2,1)}, bf16[192,640]{1,0:T(8,128)(2,1)}, bf16[192,640]{1,0:T(8,128)(2,1)}, bf16[192,640]{1,0:T(8,128)(2,1)}) custom-call(s32[4]{0:T(128)} %pad_add_fusion.1.spots, bf16[192,960]{1,0:T(8,128)(2,1)} %get-tuple-element.70.refs_0_, s32[768,1]{1,0:T(8,128)} %slice.144.refs_1_, ...), custom_call_target="tpu_custom_call" | custom-call | flops 5662310400 | bytes 4760064 | tf_op jit(solution)/shard_map/attention_back_near/pallas_call | solution.py:79
  280.9 3.4 query_weight_grad.1
  292.8 6.3 %collective-permute-done.43 = bf16[384,640]{1,0:T(8,128)(2,1)S(1)} collective-permute-done((bf16[384,640]{1,0:T(8,128)(2,1)}, bf16[384,640]{1,0:T(8,128)(2,1)S(1)}, u32[]{:S(2)}, u32[]{:S(2)}) %collective-permute-start.43) | collective-permute-done | bytes 491552 | tf_op jit(solution)/shard_map/ppermute | solution.py:40
  301.4 7.5 %collective-permute-done.41.refs_12_ = bf16[384,640]{1,0:T(8,128)(2,1)S(1)} collective-permute-done((bf16[384,640]{1,0:T(8,128)(2,1)}, bf16[384,640]{1,0:T(8,128)(2,1)S(1)}, u32[]{:S(2)}, u32[]{:S(2)}) %collective-permute-start.41) | collective-permute-done | bytes 491552 | tf_op jit(solution)/shard_map/ppermute | solution.py:40
  309.0 4.3 query_back.1.refs_6_
  327.0 5.8 %keys_values_back.1 = (f32[192,960]{1,0:T(8,128)}, bf16[1344,240]{1,0:T(8,128)(2,1)}, bf16[1344,240]{1,0:T(8,128)(2,1)}) custom-call(s32[4]{0:T(128)} %pad_add_fusion.1.spots, f32[192,128]{1,0:T(8,128)} %pad_maximum_fusion.3.refs_5_.refs_3_.refs_0_, f32[192,128]{1,0:T(8,128)} %pad_maximum_fusion.4.refs_6_.refs_4_.refs_1_, ...), custom_call_target="tpu_custom_call" | custom-call | flops 471859200 | bytes 7220736 | tf_op jit(solution)/shard_map/keys_values_back/pallas_call | solution.py:79
  339.6 5.7 %collective-permute-done.57 = bf16[240,240]{1,0:T(8,128)(2,1)S(1)} collective-permute-done((bf16[240,240]{1,0:T(8,128)(2,1)}, bf16[240,240]{1,0:T(8,128)(2,1)S(1)}, u32[]{:S(2)}, u32[]{:S(2)}) %collective-permute-start.57) | collective-permute-done | bytes 115232 | tf_op jit(solution)/shard_map/ppermute | solution.py:40
  348.4 9.2 %collective-permute-done.67 = bf16[240,240]{1,0:T(8,128)(2,1)S(1)} collective-permute-done((bf16[240,240]{1,0:T(8,128)(2,1)S(1)}, bf16[240,240]{1,0:T(8,128)(2,1)S(1)}, u32[]{:S(2)}, u32[]{:S(2)}) %collective-permute-start.67) | collective-permute-done | bytes 115232 | tf_op jit(solution)/shard_map/ppermute | solution.py:49
  377.5 13.8 %collective-permute-done.60 = bf16[240,240]{1,0:T(8,128)(2,1)S(1)} collective-permute-done((bf16[240,240]{1,0:T(8,128)(2,1)S(1)}, bf16[240,240]{1,0:T(8,128)(2,1)S(1)}, u32[]{:S(2)}, u32[]{:S(2)}) %collective-permute-start.60) | collective-permute-done | bytes 115232 | tf_op jit(solution)/shard_map/ppermute | solution.py:49
  396.8 3.6 collective-permute-done.51
  411.2 6.7 %feed_forward_out.1 = (f32[240,2560]{1,0:T(8,128)}, f32[240,2560]{1,0:T(8,128)}, f32[960,640]{1,0:T(8,128)}) custom-call(s32[4]{0:T(128)} %pad_add_fusion.1.spots, bf16[240,960]{1,0:T(8,128)(2,1)} %reduce-scatter.2.cloned.1.call-done.refs_0_, bf16[240,960]{1,0:T(8,128)(2,1)} %collective-permute-done.70.refs_1_, bf16[240,960]{1,0:T(8,128)(2,1)} %copy-done.22, ...), custom_call_target="tpu_custom_call" | custom-call | bytes 11059200 | tf_op jit(solution)/shard_map/feed_forward_out/pallas_call | solution.py:79
  (342 shorter events, 143.8 us)
Async XLA Ops:
  7.2 178.1 %all-gather.2.cloned.1.call-start = ((), (), s32[]{:S(2)}) async-start(), calls=%async_computation.1 | async-start | bytes 2457600 | tf_op jit(solution)/shard_map/all_gather | solution.py:672
  40.6 37.1 %collective-permute-start.7 = (bf16[240,480]{1,0:T(8,128)(2,1)}, bf16[240,480]{1,0:T(8,128)(2,1)S(1)}, u32[]{:S(2)}, u32[]{:S(2)}) collective-permute-start(bf16[240,480]{1,0:T(8,128)(2,1)} %quarter_columns.1), channel_id=1, source_target_pairs={{0,2},{1,3},{2,0},{3,1},{4,6},{5,7},{6,4},{7,5},{8,10},{9,11},{10,... | collective-permute-start | bytes 691208 | tf_op jit(solution)/shard_map/ppermute | solution.py:40
  41.1 36.6 %collective-permute-start.8 = (bf16[240,480]{1,0:T(8,128)(2,1)}, bf16[240,480]{1,0:T(8,128)(2,1)S(1)}, u32[]{:S(2)}, u32[]{:S(2)}) collective-permute-start(bf16[240,480]{1,0:T(8,128)(2,1)} %quarter_columns.1), channel_id=1, source_target_pairs={{0,3},{1,2},{2,1},{3,0},{4,7},{5,6},{6,5},{7,4},{8,11},{9,10},{10,... | collective-permute-start | bytes 691208 | tf_op jit(solution)/shard_map/ppermute | solution.py:40
  47.6 245.1 %reduce-scatter.2.cloned.1.call-start = ((), (), s32[]{:S(2)}) async-start(), calls=%async_computation.2 | async-start | bytes 2457600 | tf_op jit(solution)/shard_map/reduce_scatter | solution.py:741
  81.2 33.5 %collective-permute-start.10 = (bf16[720,480]{1,0:T(8,128)(2,1)}, bf16[720,480]{1,0:T(8,128)(2,1)S(1)}, u32[]{:S(2)}, u32[]{:S(2)}) collective-permute-start(bf16[720,480]{1,0:T(8,128)(2,1)} %stack_quarters.1.refs_6_.refs_9_.refs_10_.refs_0_), channel_id=1, source_target_pairs={{0,16},{4,20},{8,24},{12,28},{16,0},{20,4},{24,8},{28,12},{1,17},{... | collective-permute-start | bytes 2073608 | tf_op jit(solution)/shard_map/ppermute | solution.py:49
  82.8 30.3 %collective-permute-start.12 = (bf16[192,640]{1,0:T(8,128)(2,1)S(1)}, bf16[192,640]{1,0:T(8,128)(2,1)S(1)}, u32[]{:S(2)}, u32[]{:S(2)}) collective-permute-start(bf16[192,640]{1,0:T(8,128)(2,1)S(1)} %copy-done.58), channel_id=1, source_target_pairs={{0,1},{1,0},{2,3},{3,2},{4,5},{5,4},{6,7},{7,6},{8,9},{9,8},{10,11... | collective-permute-start | bytes 737288 | tf_op jit(solution)/shard_map/ppermute | solution.py:40
  102.1 29.4 %collective-permute-start.9 = (bf16[720,480]{1,0:T(8,128)(2,1)}, bf16[720,480]{1,0:T(8,128)(2,1)S(1)}, u32[]{:S(2)}, u32[]{:S(2)}) collective-permute-start(bf16[720,480]{1,0:T(8,128)(2,1)} %stack_quarters.1.refs_6_.refs_9_.refs_10_.refs_0_), channel_id=1, source_target_pairs={{0,8},{4,12},{8,0},{12,4},{16,24},{20,28},{24,16},{28,20},{1,9},{5... | collective-permute-start | bytes 2073608 | tf_op jit(solution)/shard_map/ppermute | solution.py:49
  114.6 18.4 %collective-permute-start.11 = (bf16[720,480]{1,0:T(8,128)(2,1)S(1)}, bf16[720,480]{1,0:T(8,128)(2,1)S(1)}, u32[]{:S(2)}, u32[]{:S(2)}) collective-permute-start(bf16[720,480]{1,0:T(8,128)(2,1)S(1)} %collective-permute-done.10.refs_8_.refs_11_.refs_12_.refs_2_), channel_id=1, source_target_pairs={{0,8},{4,12},{8,0},{12,4},{16,24},{20,28},{24,16},{28,20},{1,9},{5... | collective-permute-start | bytes 2073608 | tf_op jit(solution)/shard_map/ppermute | solution.py:49
  115.3 30.3 %collective-permute-start.22 = (bf16[192,960]{1,0:T(8,128)(2,1)S(1)}, bf16[192,960]{1,0:T(8,128)(2,1)S(1)}, u32[]{:S(2)}, u32[]{:S(2)}) collective-permute-start(bf16[192,960]{1,0:T(8,128)(2,1)S(1)} %bitcast.90), channel_id=1, source_target_pairs={{0,16},{4,20},{8,24},{12,28},{16,0},{20,4},{24,8},{28,12},{1,17},{... | collective-permute-start | bytes 1105928 | tf_op jit(solution)/shard_map/ppermute | solution.py:49
  121.9 23.8 %collective-permute-start.23 = (bf16[192,960]{1,0:T(8,128)(2,1)S(1)}, bf16[192,960]{1,0:T(8,128)(2,1)S(1)}, u32[]{:S(2)}, u32[]{:S(2)}) collective-permute-start(bf16[192,960]{1,0:T(8,128)(2,1)S(1)} %bitcast.91), channel_id=1, source_target_pairs={{0,4},{4,0},{8,12},{12,8},{16,20},{20,16},{24,28},{28,24},{1,5},{5... | collective-permute-start | bytes 1105928 | tf_op jit(solution)/shard_map/ppermute | solution.py:49
  127.2 21.3 %collective-permute-start.18 = (bf16[192,640]{1,0:T(8,128)(2,1)}, bf16[192,640]{1,0:T(8,128)(2,1)}, u32[]{:S(2)}, u32[]{:S(2)}) collective-permute-start(bf16[192,640]{1,0:T(8,128)(2,1)} %copy-done.59), channel_id=1, source_target_pairs={{0,4},{4,0},{1,5},{5,1},{2,6},{6,2},{3,7},{7,3},{8,12},{12,8},{9,1... | collective-permute-start | bytes 737288 | tf_op jit(solution)/shard_map/ppermute | solution.py:40
  131.5 32.8 %collective-permute-start.24 = (bf16[192,960]{1,0:T(8,128)(2,1)S(1)}, bf16[192,960]{1,0:T(8,128)(2,1)S(1)}, u32[]{:S(2)}, u32[]{:S(2)}) collective-permute-start(bf16[192,960]{1,0:T(8,128)(2,1)S(1)} %bitcast.92), channel_id=1, source_target_pairs={{0,20},{4,16},{8,28},{12,24},{16,4},{20,0},{24,12},{28,8},{1,21},{... | collective-permute-start | bytes 1105928 | tf_op jit(solution)/shard_map/ppermute | solution.py:49
  133.0 32.8 %collective-permute-start.29 = (bf16[192,960]{1,0:T(8,128)(2,1)S(1)}, bf16[192,960]{1,0:T(8,128)(2,1)S(1)}, u32[]{:S(2)}, u32[]{:S(2)}) collective-permute-start(bf16[192,960]{1,0:T(8,128)(2,1)S(1)} %bitcast.93), channel_id=1, source_target_pairs={{0,8},{4,12},{8,0},{12,4},{16,24},{20,28},{24,16},{28,20},{1,9},{5... | collective-permute-start | bytes 1105928 | tf_op jit(solution)/shard_map/ppermute | solution.py:49
  145.7 20.7 %collective-permute-start.30 = (bf16[192,960]{1,0:T(8,128)(2,1)S(1)}, bf16[192,960]{1,0:T(8,128)(2,1)S(1)}, u32[]{:S(2)}, u32[]{:S(2)}) collective-permute-start(bf16[192,960]{1,0:T(8,128)(2,1)S(1)} %collective-permute-done.22.refs_6_.refs_14_), channel_id=1, source_target_pairs={{0,8},{4,12},{8,0},{12,4},{16,24},{20,28},{24,16},{28,20},{1,9},{5... | collective-permute-start | bytes 1105928 | tf_op jit(solution)/shard_map/ppermute | solution.py:49
  145.8 20.6 %collective-permute-start.31 = (bf16[192,960]{1,0:T(8,128)(2,1)S(1)}, bf16[192,960]{1,0:T(8,128)(2,1)S(1)}, u32[]{:S(2)}, u32[]{:S(2)}) collective-permute-start(bf16[192,960]{1,0:T(8,128)(2,1)S(1)} %collective-permute-done.23.refs_7_.refs_15_), channel_id=1, source_target_pairs={{0,8},{4,12},{8,0},{12,4},{16,24},{20,28},{24,16},{28,20},{1,9},{5... | collective-permute-start | bytes 1105928 | tf_op jit(solution)/shard_map/ppermute | solution.py:49
  164.3 18.6 %collective-permute-start.20 = (bf16[192,960]{1,0:T(8,128)(2,1)}, bf16[192,960]{1,0:T(8,128)(2,1)S(1)}, u32[]{:S(2)}, u32[]{:S(2)}) collective-permute-start(bf16[192,960]{1,0:T(8,128)(2,1)} %get-tuple-element.77.refs_1_.refs_5_), channel_id=1, source_target_pairs={{0,4},{4,0},{8,12},{12,8},{16,20},{20,16},{24,28},{28,24},{1,5},{5... | collective-permute-start | bytes 1105928 | tf_op jit(solution)/shard_map/ppermute | solution.py:49
  195.8 23.4 %collective-permute-start.34 = (bf16[768,960]{0,1:T(8,128)(2,1)S(1)}, bf16[768,960]{0,1:T(8,128)(2,1)}, u32[]{:S(2)}, u32[]{:S(2)}) collective-permute-start(bf16[768,960]{0,1:T(8,128)(2,1)S(1)} %copy.50), channel_id=1, source_target_pairs={{0,8},{4,12},{8,0},{12,4},{16,24},{20,28},{24,16},{28,20},{1,9},{5... | collective-permute-start | bytes 4423688 | tf_op jit(solution)/shard_map/ppermute | solution.py:49
  223.3 18.6 %collective-permute-start.36 = (bf16[192,960]{1,0:T(8,128)(2,1)}, bf16[192,960]{1,0:T(8,128)(2,1)S(1)}, u32[]{:S(2)}, u32[]{:S(2)}) collective-permute-start(bf16[192,960]{1,0:T(8,128)(2,1)} %get-tuple-element.124), channel_id=1, source_target_pairs={{0,4},{4,0},{8,12},{12,8},{16,20},{20,16},{24,28},{28,24},{1,5},{5... | collective-permute-start | bytes 1105928 | tf_op jit(solution)/shard_map/ppermute | solution.py:49
  224.7 18.8 %collective-permute-start.37 = (bf16[192,960]{1,0:T(8,128)(2,1)}, bf16[192,960]{1,0:T(8,128)(2,1)}, u32[]{:S(2)}, u32[]{:S(2)}) collective-permute-start(bf16[192,960]{1,0:T(8,128)(2,1)} %get-tuple-element.123), channel_id=1, source_target_pairs={{0,20},{4,16},{8,28},{12,24},{16,4},{20,0},{24,12},{28,8},{1,21},{... | collective-permute-start | bytes 1105928 | tf_op jit(solution)/shard_map/ppermute | solution.py:49
  253.2 33.7 %collective-permute-start.62 = (bf16[2,960,240]{2,1,0:T(8,128)(2,1)}, bf16[2,960,240]{2,1,0:T(8,128)(2,1)}, u32[]{:S(2)}, u32[]{:S(2)}) collective-permute-start(bf16[2,960,240]{2,1,0:T(8,128)(2,1)} %get-tuple-element.96), channel_id=1, source_target_pairs={{0,8},{4,12},{8,0},{12,4},{16,24},{20,28},{24,16},{28,20},{1,9},{5... | collective-permute-start | bytes 2764808 | tf_op jit(solution)/shard_map/ppermute | solution.py:49
  286.3 22.6 %collective-permute-start.41 = (bf16[384,640]{1,0:T(8,128)(2,1)}, bf16[384,640]{1,0:T(8,128)(2,1)S(1)}, u32[]{:S(2)}, u32[]{:S(2)}) collective-permute-start(bf16[384,640]{1,0:T(8,128)(2,1)} %get-tuple-element.108), channel_id=1, source_target_pairs={{0,4},{4,0},{1,5},{5,1},{2,6},{6,2},{3,7},{7,3},{8,12},{12,8},{9,1... | collective-permute-start | bytes 1474568 | tf_op jit(solution)/shard_map/ppermute | solution.py:40
  288.8 26.7 %collective-permute-start.63 = (bf16[960,240]{1,0:T(8,128)(2,1)}, bf16[960,240]{1,0:T(8,128)(2,1)}, u32[]{:S(2)}, u32[]{:S(2)}) collective-permute-start(bf16[960,240]{1,0:T(8,128)(2,1)} %fusion.1), channel_id=1, source_target_pairs={{0,16},{4,20},{8,24},{12,28},{16,0},{20,4},{24,8},{28,12},{1,17},{... | collective-permute-start | bytes 1382408 | tf_op jit(solution)/shard_map/ppermute | solution.py:49
  292.2 27.0 %collective-permute-start.55 = (bf16[960,240]{1,0:T(8,128)(2,1)}, bf16[960,240]{1,0:T(8,128)(2,1)}, u32[]{:S(2)}, u32[]{:S(2)}) collective-permute-start(bf16[960,240]{1,0:T(8,128)(2,1)} %fusion), channel_id=1, source_target_pairs={{0,16},{4,20},{8,24},{12,28},{16,0},{20,4},{24,8},{28,12},{1,17},{... | collective-permute-start | bytes 1382408 | tf_op jit(solution)/shard_map/ppermute | solution.py:49
  299.2 21.6 %collective-permute-start.44 = (bf16[192,640]{1,0:T(8,128)(2,1)S(1)}, bf16[192,640]{1,0:T(8,128)(2,1)S(1)}, u32[]{:S(2)}, u32[]{:S(2)}) collective-permute-start(bf16[192,640]{1,0:T(8,128)(2,1)S(1)} %get-tuple-element.147), channel_id=1, source_target_pairs={{0,2},{1,3},{2,0},{3,1},{4,6},{5,7},{6,4},{7,5},{8,10},{9,11},{10,... | collective-permute-start | bytes 737288 | tf_op jit(solution)/shard_map/ppermute | solution.py:40
  300.9 22.8 %collective-permute-start.45 = (bf16[192,640]{1,0:T(8,128)(2,1)S(1)}, bf16[192,640]{1,0:T(8,128)(2,1)S(1)}, u32[]{:S(2)}, u32[]{:S(2)}) collective-permute-start(bf16[192,640]{1,0:T(8,128)(2,1)S(1)} %get-tuple-element.146), channel_id=1, source_target_pairs={{0,3},{1,2},{2,1},{3,0},{4,7},{5,6},{6,5},{7,4},{8,11},{9,10},{10,... | collective-permute-start | bytes 737288 | tf_op jit(solution)/shard_map/ppermute | solution.py:40
  319.2 17.6 %collective-permute-start.65 = (bf16[240,240]{1,0:T(8,128)(2,1)}, bf16[240,240]{1,0:T(8,128)(2,1)}, u32[]{:S(2)}, u32[]{:S(2)}) collective-permute-start(bf16[240,240]{1,0:T(8,128)(2,1)} %get-tuple-element.131), channel_id=1, source_target_pairs={{0,2},{1,3},{2,0},{3,1},{4,6},{5,7},{6,4},{7,5},{8,10},{9,11},{10,... | collective-permute-start | bytes 345608 | tf_op jit(solution)/shard_map/ppermute | solution.py:40
  323.7 37.5 %collective-permute-start.40 = (bf16[192,960]{1,0:T(8,128)(2,1)}, bf16[192,960]{1,0:T(8,128)(2,1)}, u32[]{:S(2)}, u32[]{:S(2)}) collective-permute-start(bf16[192,960]{1,0:T(8,128)(2,1)} %get-tuple-element.127), channel_id=1, source_target_pairs={{0,20},{4,16},{8,28},{12,24},{16,4},{20,0},{24,12},{28,8},{1,21},{... | collective-permute-start | bytes 1105928 | tf_op jit(solution)/shard_map/ppermute | solution.py:49
  337.8 19.8 %collective-permute-start.46 = (bf16[1344,240]{0,1:T(8,128)(2,1)S(1)}, bf16[1344,240]{0,1:T(8,128)(2,1)S(1)}, u32[]{:S(2)}, u32[]{:S(2)}) collective-permute-start(bf16[1344,240]{0,1:T(8,128)(2,1)S(1)} %copy.60), channel_id=1, source_target_pairs={{0,8},{4,12},{8,0},{12,4},{16,24},{20,28},{24,16},{28,20},{1,9},{5... | collective-permute-start | bytes 1935368 | tf_op jit(solution)/shard_map/ppermute | solution.py:49
  339.0 19.9 %collective-permute-start.38 = (bf16[192,960]{1,0:T(8,128)(2,1)}, bf16[192,960]{1,0:T(8,128)(2,1)}, u32[]{:S(2)}, u32[]{:S(2)}) collective-permute-start(bf16[192,960]{1,0:T(8,128)(2,1)} %get-tuple-element.126), channel_id=1, source_target_pairs={{0,16},{4,20},{8,24},{12,28},{16,0},{20,4},{24,8},{28,12},{1,17},{... | collective-permute-start | bytes 1105928 | tf_op jit(solution)/shard_map/ppermute | solution.py:49
  359.3 33.7 %collective-permute-start.70 = (bf16[240,960]{1,0:T(8,128)(2,1)S(1)}, bf16[240,960]{1,0:T(8,128)(2,1)}, u32[]{:S(2)}, u32[]{:S(2)}) collective-permute-start(bf16[240,960]{1,0:T(8,128)(2,1)S(1)} %copy-done.21), channel_id=1, source_target_pairs={{0,4},{4,0},{8,12},{12,8},{16,20},{20,16},{24,28},{28,24},{1,5},{5... | collective-permute-start | bytes 1382408 | tf_op jit(solution)/shard_map/ppermute | solution.py:49
  366.8 28.3 %collective-permute-start.73 = (bf16[240,960]{1,0:T(8,128)(2,1)S(1)}, bf16[240,960]{1,0:T(8,128)(2,1)}, u32[]{:S(2)}, u32[]{:S(2)}) collective-permute-start(bf16[240,960]{1,0:T(8,128)(2,1)S(1)} %copy-done.21), channel_id=1, source_target_pairs={{0,16},{4,20},{8,24},{12,28},{16,0},{20,4},{24,8},{28,12},{1,17},{... | collective-permute-start | bytes 1382408 | tf_op jit(solution)/shard_map/ppermute | solution.py:49
  369.3 25.9 %collective-permute-start.74 = (bf16[240,960]{1,0:T(8,128)(2,1)S(1)}, bf16[240,960]{1,0:T(8,128)(2,1)}, u32[]{:S(2)}, u32[]{:S(2)}) collective-permute-start(bf16[240,960]{1,0:T(8,128)(2,1)S(1)} %copy-done.21), channel_id=1, source_target_pairs={{0,20},{4,16},{8,28},{12,24},{16,4},{20,0},{24,12},{28,8},{1,21},{... | collective-permute-start | bytes 1382408 | tf_op jit(solution)/shard_map/ppermute | solution.py:49
  (113 other events, 1231.3 us)
Sparse Core Ops, SparseCore 0:
  47.8 55.3 all-gather.1
  219.3 39.7 reduce-scatter.1

commit v4 on v3

--- a/solution.py
+++ b/solution.py
@@ -21,6 +21,22 @@
 F32 = jnp.float32
 BF16 = jnp.bfloat16
 VMEM_LIMIT = 56 * 1024 * 1024
+FLOPS_PER_US = 1150 * 10**6
+MEASURED_US = {
+    "pack_weights": 4,
+    "norm_keys_values": 4,
+    "attention_near": 12,
+    "attention_far": 14,
+    "feed_forward": 8,
+    "feed_forward_weights": 12,
+    "residual_back": 6,
+    "attention_back_far": 13,
+    "attention_back_near": 14,
+    "query_output_weight_grads": 7,
+    "query_back": 4,
+    "keys_values_back": 6,
+    "feed_forward_out": 7,
+}
 
 
 def dot_plain(left, right):
@@ -53,7 +69,7 @@
     return swap_plane(x, 1, 0)
 
 
-CHIP_MASKS = ((2, 0), (0, 1), (2, 1))
+CHIP_MASKS = ((0, 1), (2, 0), (2, 1))
 
 
 def plane_pieces(x):
@@ -69,13 +85,10 @@
     return lax.psum(x.astype(F32), "ctx", axis_index_groups=groups).astype(x.dtype)
 
 
-def call(kernel, spots, args, out_shapes, scratch=(), flops=0, name=None):
+def call(kernel, spots, args, out_shapes, scratch=(), name=None):
     specs = [pl.BlockSpec(memory_space=pltpu.SMEM)]
     specs += [pl.BlockSpec(memory_space=pltpu.VMEM) for _ in args]
     outs = tuple(jax.ShapeDtypeStruct(s, d) for s, d in out_shapes)
-    bytes_all = sum(a.size * a.dtype.itemsize for a in args) + sum(
-        math.prod(s) * jnp.dtype(d).itemsize for s, d in out_shapes
-    )
     return pl.pallas_call(
         kernel,
         out_shape=outs,
@@ -83,7 +96,9 @@
         out_specs=tuple(pl.BlockSpec(memory_space=pltpu.VMEM) for _ in outs),
         scratch_shapes=[pltpu.VMEM(s, d) for s, d in scratch],
         compiler_params=pltpu.CompilerParams(vmem_limit_bytes=VMEM_LIMIT),
-        cost_estimate=pl.CostEstimate(flops=flops, bytes_accessed=bytes_all, transcendentals=0),
+        cost_estimate=pl.CostEstimate(
+            flops=MEASURED_US.get(name, 2) * FLOPS_PER_US, bytes_accessed=0, transcendentals=0
+        ),
         name=name,
     )(spots, *args)
 
@@ -138,6 +153,12 @@
     rows = pieces[0].shape[0]
     for i, piece in enumerate(pieces):
         scratch[i * rows : (i + 1) * rows, :] = piece[...]
+
+
+def unstack_rows(out_ref, values):
+    count, rows = out_ref.shape[:2]
+    for i in range(count):
+        out_ref[i] = values[i * rows : (i + 1) * rows, :].astype(out_ref.dtype)
 
 
 def norm_rows(values, gain):
@@ -326,10 +347,10 @@
         )
 
 
-def feed_kernel(shards, pieces, spots, *refs):
-    ins, outs, scratch = split_refs(refs, 1 + 2 * pieces, 3, 3)
-    pack_ref = ins[0]
-    normed_parts, cot_parts = split_refs(ins[1:], pieces, pieces)
+def feed_kernel(shards, masks, spots, *refs):
+    ins, outs, scratch = split_refs(refs, 2 + len(masks), 3, 3)
+    pack_ref, cot_all, normed_parts = ins[0], ins[1], ins[2:]
+    cot_parts = [cot_all[spots[3] ^ mask] for mask in masks]
     grad_ref, act_ref, both_ref = outs
     normed_ref, cot_ref, down_ref = scratch
     part = pack_ref.shape[1] // 3
@@ -344,13 +365,14 @@
     act_ref[...] = (silu * upward).astype(BF16)
     gate_grad = act_grad * upward * sigmoid_gate * (1.0 + gate * (1.0 - sigmoid_gate))
     both_ref[...] = jnp.concatenate([gate_grad, act_grad * silu], axis=1).astype(BF16)
-    grad_ref[...] = dot_last(both_ref[...], pack_ref[:, : 2 * part]).astype(BF16)
-
-
-def feed_weights_kernel(shards, pieces, spots, *refs):
-    ins, outs, scratch = split_refs(refs, 5 + 2 * pieces, 3, 5)
-    pack_ref, act_a, act_b, both_a, both_b = ins[:5]
-    normed_parts, cot_parts = split_refs(ins[5:], pieces, pieces)
+    unstack_rows(grad_ref, dot_last(both_ref[...], pack_ref[:, : 2 * part]))
+
+
+def feed_weights_kernel(shards, masks, spots, *refs):
+    ins, outs, scratch = split_refs(refs, 6 + len(masks), 3, 5)
+    pack_ref, act_a, act_b, both_a, both_b, cot_all = ins[:6]
+    normed_parts = ins[6:]
+    cot_parts = [cot_all[spots[3] ^ mask] for mask in masks]
     result_a, result_b, grad_ref = outs
     normed_ref, cot_ref, act_ref, both_ref, down_ref = scratch
     part = pack_ref.shape[1] // 3
@@ -369,8 +391,8 @@
         grad_ref[z * rows : (z + 1) * rows, 2 * part :] = jnp.concatenate(
             [down_grad[b * rows : (b + 1) * rows, at : at + piece] for b in range(folds)], axis=1
         )
-    result_a[...] = dot_last(act_a[...], down_ref[...]).astype(BF16)
-    result_b[...] = dot_last(act_b[...], down_ref[...]).astype(BF16)
+    unstack_rows(result_a, dot_last(act_a[...], down_ref[...]))
+    unstack_rows(result_b, dot_last(act_b[...], down_ref[...]))
 
 
 def middle_kernel(shards, members, spots, *refs):
@@ -380,7 +402,7 @@
     weights = ins[10:]
     residual_grad_ref, low_ref, attended_grad_ref, gain_grad_ref = outs
     rows = cot_ref.shape[0]
-    grad = (own_a[:rows, :].astype(F32) + own_b[:rows, :].astype(F32)) + one_ref[...].astype(F32)
+    grad = (own_a[0].astype(F32) + own_b[0].astype(F32)) + one_ref[...].astype(F32)
     grad = grad + two_ref[...].astype(F32) + three_ref[...].astype(F32)
     residual, inverse = residual_ref[...], inverse_ref[...]
     gain_grad_ref[...] = jnp.sum(grad * residual * inverse, axis=0, keepdims=True)
@@ -407,22 +429,33 @@
     return join_lanes(out_blocks)
 
 
-def weight_grad_kernel(members, spots, left_ref, low_ref, keep_ref, send_ref, blocks):
+def weight_grads_kernel(members, spots, *refs):
+    lefts, lows, (keep_ref, send_ref, blocks) = refs[0:4:2], refs[1:4:2], refs[4:]
     dp = spots[2]
-    for i, block in enumerate(lane_blocks(low_ref[...], members)):
-        blocks[i] = block
-    left = left_ref[...]
-    for j in range(members):
+    for k, (left_ref, low_ref) in enumerate(zip(lefts, lows)):
+        for i, block in enumerate(lane_blocks(low_ref[...], members)):
+            blocks[k * members + i] = block
+    for j in (1, 3, 0, 2):
         out_ref = send_ref if j & 1 else keep_ref
-        out_ref[j // 2] = dot_first(left, blocks[dp ^ j]).astype(BF16)
-
-
-def join_kernel(members, spots, pair_ref, other_ref, out_ref, blocks):
+        out_ref[j // 2] = jnp.concatenate(
+            [
+                dot_first(left_ref[...], blocks[k * members + (dp ^ j)])
+                for k, left_ref in enumerate(lefts)
+            ],
+            axis=1,
+        ).astype(BF16)
+
+
+def join_kernel(members, spots, own_ref, across_ref, core_ref, core_across_ref, *refs):
+    outs, blocks = refs[:2], refs[2]
     dp = spots[2]
-    for j in range(members):
-        ref = other_ref if j & 1 else pair_ref
-        blocks[dp ^ j] = ref[j // 2]
-    out_ref[...] = join_lanes(blocks).astype(F32)
+    for j, ref in enumerate((own_ref, core_ref, across_ref, core_across_ref)):
+        blocks[dp ^ j] = ref[...]
+    size = blocks.shape[-1] // 2
+    for k, out_ref in enumerate(outs):
+        out_ref[...] = jnp.concatenate(
+            [blocks[i][:, k * size : (k + 1) * size] for i in range(members)], axis=1
+        ).astype(F32)
 
 
 def query_back_kernel(shards, members, spots, low_ref, local_ref, *refs):
@@ -433,7 +466,7 @@
 
 
 def back_kernel(chunk, pieces, first, last, spots, *refs):
-    ins, outs, scratch = split_refs(refs, 9 + pieces, (pieces if last else 2) + 1, 2)
+    ins, outs, scratch = split_refs(refs, 9 + pieces, (pieces if last else 1) + 1, 2)
     (queries_ref, key_pos_ref, query_pos_ref, cos_ref, sin_ref, turned_ref, log_ref, grad_ref,
      start_ref) = ins[:9]
     parts = ins[9:]
@@ -479,9 +512,11 @@
         query_grad_ref[...] = rope_lanes(
             jnp.concatenate(heads, axis=1), cos_ref[...], -sin_ref[...]
         ).astype(BF16)
-    size = kv_ref.shape[0] // len(kv_grads)
-    for i, ref in enumerate(kv_grads):
-        ref[...] = kv_grad_ref[i * size : (i + 1) * size, :]
+    if last:
+        for i in range(pieces):
+            kv_grads[i][...] = kv_grad_ref[i * rows : (i + 1) * rows, :]
+    else:
+        unstack_rows(kv_grads[0], kv_grad_ref[...])
 
 
 def end_kernel(shards, spots, *refs):
@@ -494,7 +529,8 @@
     core, shard = spots[0], spots[1]
     width, span = key_ref.shape
     rows = tokens_ref.shape[0]
-    total = sum(s[:rows, :].astype(F32) for s in sums)
+    total = sums[0][...].astype(F32) + sums[1][0].astype(F32)
+    total = total + sum(s[...].astype(F32) for s in sums[2:])
     keys = rope_lanes(total[:, :width], cos_ref[...], -sin_ref[...])
     values = total[:, width:]
     keep = jnp.where(core == 0, keys, values).astype(BF16)
@@ -519,11 +555,10 @@
         (keep_ref, keep, jnp.where(core == 0, gain_grad, two)),
     ):
         grad = dot_first(low, normed).astype(BF16)
-        size = width + EXTRA_ROWS
         gains = lane_blocks(gain, shards)
         for z, block in enumerate(lane_blocks(grad, shards)):
-            out_ref[z * size : z * size + width, :] = block
-            out_ref[z * size + width : (z + 1) * size, :] = jnp.broadcast_to(
+            out_ref[z, :width, :] = block
+            out_ref[z, width:, :] = jnp.broadcast_to(
                 gains[z], (EXTRA_ROWS, span)
             ).astype(BF16)
 
@@ -626,12 +661,16 @@
         [after(query_weight, kv_pack), output_weight],
         [((weight_rows, 2 * quarter), BF16)], name="quarter_columns",
     )
-    (stacked,) = call(
-        stack_kernel, spots, [swap(quarters, "fsdp", r) for r in range(1, shards)],
-        [(((shards - 1) * weight_rows, 2 * quarter), BF16)], name="stack_quarters",
-    )
-    across = swap_plane(stacked, 2, 0)
-    stacks = [stacked, swap_core(stacked), across, swap_core(across)]
+    quarter_pieces = [swap(quarters, "fsdp", r) for r in range(1, shards)]
+
+    group_axes = ("dp", "ctx")
+    extra = {}
+    if ctx_count > 2:
+        extra["axis_index_groups"] = [
+            [d * ctx_count + c for d in range(dp_count) for c in (first, first + 1)]
+            for first in range(0, ctx_count, 2)
+        ]
+    cot_all = lax.all_gather(cotangent, group_axes, axis=0, tiled=False, **extra)
 
     offsets = jnp.arange(rows, dtype=jnp.int32)
     my_start = (ctx * shards + shard) * rows
@@ -649,12 +688,13 @@
     (pack,) = call(
         functools.partial(pack_kernel, shards, members), spots,
         [gate_weight, up_weight, down_turned], [((weight_rows, 3 * part), BF16)],
-        flops=4 * weight_rows * hidden * part // shards, name="pack_weights",
+        name="pack_weights",
     )
     kv_own, normed_one, normed_turned, inverse_one, gains = call(
         functools.partial(begin_kernel, shards), spots,
         [
-            tokens, gain_one, gain_two, key_turned, value_turned, cosine, sine, *kv_mine, *kv_other,
+            lax.optimization_barrier((tokens, quarters, pack))[0], gain_one, gain_two, key_turned, value_turned, cosine, sine,
+            *kv_mine, *kv_other,
         ],
         [
             ((rows, 2 * kv_width), BF16), ((rows, width), BF16), ((rows, width), BF16),
@@ -664,13 +704,19 @@
             ((shards, rows, weight_rows), F32), ((shards, rows, weight_rows), BF16),
             ((shards, 8, weight_rows), F32),
         ],
-        flops=4 * rows * width * kv_width, name="norm_keys_values",
+        name="norm_keys_values",
+    )
+    (stacked,) = call(
+        stack_kernel, spots, lax.optimization_barrier((kv_own, *quarter_pieces))[1:],
+        [(((shards - 1) * weight_rows, 2 * quarter), BF16)], name="stack_quarters",
     )
     near = [kv_own] + [swap(kv_own, "fsdp", r) for r in range(1, shards)]
+    across, *near = lax.optimization_barrier((swap_plane(stacked, 2, 0), *near))
+    stacks = [stacked, swap_core(stacked), across, swap_core(across)]
     far = [swap(piece, "ctx", d) for d in range(1, ctx_count) for piece in near]
 
-    pack_all = lax.all_gather(after(pack, near[-1]), "fsdp", axis=0, tiled=True)
-    cot_a, cot_b = plane_pieces(after(cotangent, near[-1]))
+    pack, cot_all, _ = lax.optimization_barrier((pack, cot_all, near[-1]))
+    pack_all = lax.all_gather(pack, "fsdp", axis=0, tiled=True)
 
     chunk = rows * 2
     unit = 2 * HEADS * rows * near_count * HEAD_DIM
@@ -681,7 +727,7 @@
         [normed_turned, near_pos, query_pos, cosine, sine, query_weight, *stacks, *near],
         [((rows, query_width), BF16), stat, stat, turned_shape],
         scratch=[((dp_count, rows, quarter), F32), ((near_count, 2 * kv_width), BF16)],
-        flops=8 * unit, name="attention_near",
+        name="attention_near",
     )
     attended, turned, log_total, residual, inverse_two, normed_two = call(
         functools.partial(far_kernel, chunk, shards, dp_count, len(far)), spots,
@@ -697,49 +743,54 @@
             ((dp_count, rows, quarter), F32), ((far_count, 2 * kv_width), BF16),
             ((shards, rows, weight_rows), BF16),
         ],
-        flops=8 * unit * len(far) // shards, name="attention_far",
+        name="attention_far",
     )
 
     normed_a, normed_b = plane_pieces(normed_two)
     token_shape = ((rows, width), BF16)
     half = 4 * rows
-    half_shape = ((half, width), BF16)
-
-    def feed(normed, cot):
+    half_shape = ((4, rows, width), BF16)
+
+    masks = [2 * a + b for a, b in ((0, 0),) + CHIP_MASKS]
+    core_masks = [mask ^ 2 for mask in masks]
+
+    def feed(normed, masks):
         return call(
-            functools.partial(feed_kernel, shards, 4), spots, [pack_all, *normed, *cot],
+            functools.partial(feed_kernel, shards, masks), spots, [pack_all, cot_all, *normed],
             [half_shape, ((half, part), BF16), ((half, 2 * part), BF16)],
             scratch=[((half, width), BF16), ((half, width), BF16), ((width, part), BF16)],
-            flops=10 * half * width * part, name="feed_forward",
+        name="feed_forward",
         )
 
-    grad_b, act_b, both_b = feed(normed_b, cot_b)
+    grad_b, act_b, both_b = feed(normed_b, core_masks)
     from_core = swap_core(grad_b)
-    grad_a, act_a, both_a = feed(normed_a, cot_a)
+    grad_a, act_a, both_a = feed(normed_a, masks)
 
     def chip_sums(parts_a, parts_b):
         return [
-            (parts_a[k * rows : (k + 1) * rows].astype(F32)
-             + parts_b[k * rows : (k + 1) * rows].astype(F32)).astype(BF16)
+            (parts_a[k].astype(F32) + parts_b[k].astype(F32)).astype(BF16)
             for k in range(1, 4)
         ]
 
     def send_chips(sums):
         return [swap_plane(x, a, b) for x, (a, b) in zip(sums, CHIP_MASKS)]
 
-    grad_chips = send_chips(chip_sums(grad_a, from_core))
+    grad_sums = chip_sums(grad_a, from_core)
+    grad_chips = send_chips(grad_sums)
+    act_a, *_ = lax.optimization_barrier((act_a, *grad_sums))
     result_a, result_b, pack_grad = call(
-        functools.partial(feed_weights_kernel, shards, 8), spots,
-        [pack_all, act_a, act_b, both_a, both_b, *normed_a, *normed_b, *cot_a, *cot_b],
+        functools.partial(feed_weights_kernel, shards, masks + core_masks), spots,
+        [pack_all, act_a, act_b, both_a, both_b, cot_all, *normed_a, *normed_b],
         [half_shape, half_shape, ((width, 3 * part), BF16)],
         scratch=[
             ((2 * half, width), BF16), ((2 * half, width), BF16), ((2 * half, part), BF16),
             ((2 * half, 2 * part), BF16), ((width, part), BF16),
         ],
-        flops=16 * half * width * part, name="feed_forward_weights",
+        name="feed_forward_weights",
     )
     pack_share = sum_far(lax.psum_scatter(pack_grad, "fsdp", scatter_dimension=0, tiled=True))
 
+    pack_grad, *grad_chips = lax.optimization_barrier((pack_grad, *grad_chips))
     residual_grad, residual_low, attended_grad, second_gain_grad = call(
         functools.partial(middle_kernel, shards, dp_count), spots,
         [
@@ -748,53 +799,48 @@
         ],
         [((rows, width), F32), token_shape, ((rows, query_width), BF16), ((1, width), F32)],
         scratch=[((dp_count, rows, quarter), BF16), ((shards, rows, weight_rows), F32)],
-        flops=2 * rows * width * query_width, name="residual_back",
-    )
-
-    result_core = swap_core(result_b)
-    result_sums = chip_sums(after(result_a, residual_low), result_core)
-    result_chips = send_chips(result_sums)
-    result = residual + (
-        (result_a[:rows].astype(F32) + result_core[:rows].astype(F32))
-        + result_chips[0].astype(F32)
-        + (result_chips[1].astype(F32) + result_chips[2].astype(F32))
-    )
-
-    def weight_grad(left, low, name):
-        pair = ((2, width, quarter), BF16)
-        return call(
-            functools.partial(weight_grad_kernel, dp_count), spots, [left, low], [pair, pair],
-            scratch=[((dp_count, rows, quarter), BF16)],
-            flops=2 * rows * width * width, name=name,
-        )
-
-    def sum_quarters(keep, send):
-        away = swap_core(send)
+        name="residual_back",
+    )
+
+    result_core = swap_core(after(result_b, residual_low))
+    attended_grad, result_a = lax.optimization_barrier((attended_grad, result_a))
+
+    def sum_x(keep, away):
         sent = (keep[1].astype(F32) + away[1].astype(F32)).astype(BF16)
-        across = swap_plane(sent, 2, 0)
-        pieces = []
+        return sent, (keep[0], away[0], swap_plane(sent, 2, 0))
+
+    def pieces_z(terms):
+        out = []
         for r in range(shards):
             at = (shard ^ r) * weight_rows
             parts = [
-                lax.dynamic_slice_in_dim(x, at, weight_rows, 0).astype(F32)
-                for x in (keep[0], away[0], across)
+                lax.dynamic_slice_in_dim(x, at, weight_rows, 0).astype(F32) for x in terms
             ]
-            pieces.append((parts[0] + parts[1] + parts[2]).astype(BF16))
+            out.append((parts[0] + parts[1] + parts[2]).astype(BF16))
+        return out
+
+    def sum_z(pieces):
         total = pieces[0].astype(F32)
         for r in range(1, shards):
             total = total + swap(pieces[r], "fsdp", r).astype(F32)
-        own = total.astype(BF16)
-        own = sum_far((own.astype(F32) + swap_plane(own, 0, 1).astype(F32)).astype(BF16))
-        pair = jnp.stack([own, swap_plane(own, 2, 0)])
-        (out,) = call(
-            functools.partial(join_kernel, dp_count), spots, [pair, swap_core(pair)],
-            [((weight_rows, width), F32)], scratch=[((dp_count, weight_rows, quarter), BF16)],
-            name="join_columns",
+        return total.astype(BF16)
+
+    def sum_y(own):
+        return sum_far((own.astype(F32) + swap_plane(own, 0, 1).astype(F32)).astype(BF16))
+
+    def finish_quarters(own):
+        across = swap_plane(own, 2, 0)
+        return call(
+            functools.partial(join_kernel, dp_count), spots,
+            [own, across, swap_core(own), swap_core(across)],
+            [((weight_rows, width), F32)] * 2,
+            scratch=[((dp_count, weight_rows, 2 * quarter), BF16)], name="join_columns",
         )
-        return out
-
-    output_keep, output_send = weight_grad(attended, residual_low, "output_weight_grad")
-    attended_grad, _, _ = lax.optimization_barrier((attended_grad, output_send, result_sums[2]))
+
+    def sum_chips(own):
+        for a, b in ((2, 0), (0, 1)):
+            own = (own.astype(F32) + swap_plane(own, a, b).astype(F32)).astype(BF16)
+        return sum_far(own)
 
     def back(first, last, start, pos, pieces):
         count = pos.shape[0]
@@ -808,10 +854,9 @@
             [shape]
             + (
                 [((rows, 2 * kv_width), BF16)] * len(pieces) if last
-                else [((count // 2, 2 * kv_width), BF16)] * 2
+                else [((shards, rows, 2 * kv_width), BF16)]
             ),
             scratch=[((count, 2 * kv_width), BF16), ((count, 2 * kv_width), BF16)],
-            flops=20 * unit * len(pieces) // shards,
             name="attention_back_near" if last else "attention_back_far",
         )
         return out[0], out[1:]
@@ -823,70 +868,79 @@
             d == 1, False, query_partial, far_pos[at * rows : (at + shards) * rows],
             far[at : at + shards],
         )
-        far_grads.append([swap(g, "ctx", d) for g in (grads[1], grads[0])][::-1])
+        far_grads.append(swap(grads[0], "ctx", d))
+    result_sent = (result_a[2:].astype(F32) + result_core[2:].astype(F32)).astype(BF16)
+    query_partial, result_sent = lax.optimization_barrier((query_partial, result_sent))
+    result_across = swap_plane(result_sent, 2, 0)
     query_low, near_grads = back(False, True, query_partial, near_pos, near)
-    pack_share, *near_grads = lax.optimization_barrier((pack_share, *near_grads))
+    query_low, pack_share = lax.optimization_barrier((query_low, pack_share))
+    result_across = after(result_across, query_low)
+    result_own, result_along = [
+        (result_a[k].astype(F32) + result_core[k].astype(F32)) + result_across[k].astype(F32)
+        for k in (0, 1)
+    ]
+    result_along = result_along.astype(BF16)
+    share_across = swap_plane(pack_share, 2, 0)
+    query_low, result_along, far_grads[-1] = lax.optimization_barrier(
+        (query_low, result_along, far_grads[-1])
+    )
 
     def home(r):
-        at = (r % 2) * rows
-        return sum(pair[r // 2][at : at + rows].astype(F32) for pair in far_grads)
+        return sum(grads[r].astype(F32) for grads in far_grads)
 
     kv_arrived = {
         r: swap((near_grads[r].astype(F32) + home(r)).astype(BF16), "fsdp", r)
         for r in reversed(range(1, shards))
     }
-    share_a, share_b = plane_pieces(pack_share)
-
-    def pieces_of(keep, arrived, span):
-        out = []
-        for r in range(shards):
-            at = (shard ^ r) * span
-            mine = lax.dynamic_slice_in_dim(keep, at, span, 0).astype(F32)
-            theirs = lax.dynamic_slice_in_dim(arrived, at, span, 0).astype(F32)
-            out.append((mine + theirs).astype(BF16))
-        return out
-
-    def sum_devices(keep, send, span):
-        pieces = pieces_of(keep, swap_core(send), span)
-        total = pieces[0].astype(F32)
-        for r in range(1, shards):
-            total = total + swap(pieces[r], "fsdp", r).astype(F32)
-        own = total.astype(BF16)
-        across, along, diagonal = [swap_plane(own, a, b) for a, b in CHIP_MASKS]
-        total = (own.astype(F32) + across.astype(F32)) + (
-            along.astype(F32) + diagonal.astype(F32)
-        )
-        low = sum_far(total.astype(BF16))
-        away = swap_core(low)
-        return (
-            jnp.where(core == 0, low, away).astype(F32), jnp.where(core == 0, away, low).astype(F32)
-        )
-
-    query_keep, query_send = weight_grad(normed_one, query_low, "query_weight_grad")
+    share_own, share_across, _ = lax.optimization_barrier(
+        (pack_share, share_across, far_grads[-1])
+    )
+    share_a = [share_own, swap_plane(share_own, 0, 1), share_across, swap_plane(share_across, 0, 1)]
+
+    pair_shape = ((2, width, 2 * quarter), BF16)
+    weights_keep, weights_send = call(
+        functools.partial(weight_grads_kernel, dp_count), spots,
+        [attended, residual_low, normed_one, query_low], [pair_shape, pair_shape],
+        scratch=[((2 * dp_count, rows, quarter), BF16)], name="query_output_weight_grads",
+    )
+    weights_away = swap_core(weights_send)
+    query_turn = after(query_low, weights_send)
     (query_back,) = call(
         functools.partial(query_back_kernel, shards, dp_count), spots,
-        [query_low, query_weight, *stacks], [((rows, width), F32)],
+        [query_turn, query_weight, *stacks], [((rows, width), F32)],
         scratch=[((dp_count, rows, quarter), BF16), ((shards, rows, weight_rows), F32)],
-        flops=2 * rows * width * width, name="query_back",
-    )
-    output_weight_grad = sum_quarters(output_keep, output_send)
-    query_weight_grad = sum_quarters(query_keep, query_send)
-
+        name="query_back",
+    )
+    _, weights_terms = sum_x(weights_keep, weights_away)
+    weights_pieces = pieces_z(weights_terms)
+    query_back, *weights_pieces = lax.optimization_barrier((query_back, *weights_pieces))
     span = kv_width + EXTRA_ROWS
-    packed_shape = ((shards * span, weight_rows), BF16)
-    home_own = far_grads[0][0] if ctx_count == 2 else home(0)
+    packed_shape = ((shards, span, weight_rows), BF16)
+    home_all = far_grads[0]
+    if ctx_count > 2:
+        home_all = sum(grads.astype(F32) for grads in far_grads)
     input_grad, kv_keep, kv_send = call(
         functools.partial(end_kernel, shards), spots,
         [
             cosine, sine, normed_one, tokens, inverse_one, gains, query_back, residual_grad,
-            key_turned, value_turned, second_gain_grad, near_grads[0], home_own,
+            key_turned, value_turned, second_gain_grad, near_grads[0], home_all,
             *[kv_arrived[r] for r in range(1, shards)], *kv_mine, *kv_other,
         ],
         [((rows, width), F32), packed_shape, packed_shape],
         scratch=[((shards, rows, weight_rows), F32)],
-        flops=8 * rows * width * kv_width, name="keys_values_back",
-    )
-    first, second = sum_devices(kv_keep, kv_send, span)
+        name="keys_values_back",
+    )
+    kv_away = swap_core(kv_send)
+    pieces = [
+        (lax.dynamic_index_in_dim(kv_keep, shard ^ r, 0, keepdims=False).astype(F32)
+         + lax.dynamic_index_in_dim(kv_away, shard ^ r, 0, keepdims=False).astype(F32)).astype(BF16)
+        for r in range(shards)
+    ]
+    share_b = [swap_core(piece) for piece in share_a]
+    kv_share = pieces[0].astype(F32)
+    for r in range(1, shards):
+        kv_share = kv_share + swap(pieces[r], "fsdp", r).astype(F32)
+    kv_share = kv_share.astype(BF16)
 
     share_by_mask = [None] * members
     for k, (a, b) in enumerate(((0, 0),) + CHIP_MASKS):
@@ -901,6 +955,17 @@
         scratch=[((members, weight_rows, 3 * part), BF16)],
         name="feed_forward_out",
     )
+    weights_own = sum_y(sum_z(weights_pieces))
+    kv_share, weights_own, result_along, *big = lax.optimization_barrier(
+        (kv_share, weights_own, result_along, gate_weight_grad, up_weight_grad, down_weight_grad)
+    )
+    gate_weight_grad, up_weight_grad, down_weight_grad = big
+    result = residual + (result_own + swap_plane(result_along, 0, 1).astype(F32))
+    output_weight_grad, query_weight_grad = finish_quarters(weights_own)
+    low = sum_chips(kv_share)
+    away = swap_core(low)
+    first = jnp.where(core == 0, low, away).astype(F32)
+    second = jnp.where(core == 0, away, low).astype(F32)
 
     return (
         result[None],

time: 432 us -> 393 us (0.910)
  starting transfers between devices: 89.8 us -> 64.3 us
  local copies, waits for them, and re-layouts: 26.4 us -> 14.6 us
  other arithmetic: 25.4 us -> 19.5 us
  waiting for transfers between devices: 144 us -> 149 us
    ppermute x50 -> x37, waiting for transfers between devices: 60.3 us -> 79.6 us  [swap_plane(): return lax.ppermute(x, ('dp', 'ctx'), pairs)]
    ppermute x27 -> x23, waiting for transfers between devices: 83.3 us -> 67.3 us  [swap(): return lax.ppermute(x, axis, [(i, i ^ mask) for i in range(count)])]
    ppermute x50 -> x37, starting transfers between devices: 34.9 us -> 20.5 us  [swap_plane(): return lax.ppermute(x, ('dp', 'ctx'), pairs)]
    ppermute x27 -> x23, starting transfers between devices: 54.6 us -> 43.2 us  [swap(): return lax.ppermute(x, axis, [(i, i ^ mask) for i in range(count)])]
    pallas_call x3 -> x0, local copies, waits for them, and re-layouts: 6.43 us -> none  [call(): pl.pallas_call(kernel, out_shape=outs, in_specs=specs, out_specs=tuple((p...]
    convert_element_type x14 -> x12, other arithmetic: 16.4 us -> 10.3 us  [the longest x1 2.41 us: sum_x(): sent = (keep[1].astype(F32) + away[1].astype(F32)).astype(BF16)]
    pallas_call x19 -> x17, Pallas kernels: 127 us -> 125 us  [call(): pl.pallas_call(kernel, out_shape=outs, in_specs=specs, out_specs=tuple((p...]
  transfers between devices with their start and end apart: 79 -> 63, of which waited for: 24 -> 23; matrix products, arithmetic and copies ran while one was open for 9% -> 5% of each run, Pallas kernels for 27% -> 29%
where the time goes in v4:
time: 393 us; the launch traced here: 387 us
  waiting for transfers between devices  149 us (38%)
  Pallas kernels  125 us (32%)
  starting transfers between devices  64.3 us (16%)
  other arithmetic  19.5 us (5%)
  between operations  15.2 us (4%)
  local copies, waits for them, and re-layouts  14.6 us (4%)
    pallas_call x17, Pallas kernels, call(): pl.pallas_call(kernel, out_shape=outs, in_specs=specs, out_specs=tuple((p...  125 us
    ppermute x37, waiting for transfers between devices, swap_plane(): return lax.ppermute(x, ('dp', 'ctx'), pairs)  79.6 us
    ppermute x23, waiting for transfers between devices, swap(): return lax.ppermute(x, axis, [(i, i ^ mask) for i in range(count)])  67.3 us
    ppermute x23, starting transfers between devices, swap(): return lax.ppermute(x, axis, [(i, i ^ mask) for i in range(count)])  43.2 us
    ppermute x37, starting transfers between devices, swap_plane(): return lax.ppermute(x, ('dp', 'ctx'), pairs)  20.5 us
  transfers between devices with their start and end apart: 63, of which 23 were waited for; matrix products, arithmetic and copies ran while one was open for 5% of the time, Pallas kernels for 29%

profile of v4, /device:TPU:0, one launch (start us, length us, event | category | flops | bytes accessed | tf_op | source)
XLA Modules:
  0.0 387.4 jit_solution(12921943702201572863)
XLA Ops:
  24.4 4.2 %pack_weights.1 = bf16[240,960]{1,0:T(8,128)(2,1)} custom-call(s32[4]{0:T(128)} %pad_add_fusion.1.spots, bf16[240,2560]{1,0:T(8,128)(2,1)} %gate_ref.1, bf16[240,2560]{1,0:T(8,128)(2,1)} %up_ref.1, bf16[960,640]{1,0:T(8,128)(2,1)} %bitcast.92), custom_call_target="tpu_custom_call" | custom-call | flops 4600000000 | tf_op jit(solution)/shard_map/pack_weights/pallas_call | solution.py:92
  38.0 9.1 %collective-permute-done.7.refs_1_ = bf16[240,480]{1,0:T(8,128)(2,1)S(1)} collective-permute-done((bf16[240,480]{1,0:T(8,128)(2,1)}, bf16[240,480]{1,0:T(8,128)(2,1)S(1)}, u32[]{:S(2)}, u32[]{:S(2)}) %collective-permute-start.7) | collective-permute-done | bytes 230432 | tf_op jit(solution)/shard_map/ppermute | solution.py:56
  51.6 6.5 %collective-permute-start.11 = (bf16[192,640]{1,0:T(8,128)(2,1)S(1)}, bf16[192,640]{1,0:T(8,128)(2,1)S(1)}, u32[]{:S(2)}, u32[]{:S(2)}) collective-permute-start(bf16[192,640]{1,0:T(8,128)(2,1)S(1)} %copy-done.28), channel_id=1, source_target_pairs={{0,1},{1,0},{2,3},{3,2},{4,5},{5,4},{6,7},{7,6},{8,9},{9,8},{10,11... | collective-permute-start | bytes 737288 | tf_op jit(solution)/shard_map/ppermute | solution.py:56
  60.8 7.4 %collective-permute-done.11.refs_11_.refs_10_ = bf16[192,640]{1,0:T(8,128)(2,1)S(1)} collective-permute-done((bf16[192,640]{1,0:T(8,128)(2,1)S(1)}, bf16[192,640]{1,0:T(8,128)(2,1)S(1)}, u32[]{:S(2)}, u32[]{:S(2)}) %collective-permute-start.11) | collective-permute-done | bytes 245792 | tf_op jit(solution)/shard_map/ppermute | solution.py:56
  68.2 10.2 %collective-permute-done.12.refs_12_.refs_11_ = bf16[192,640]{1,0:T(8,128)(2,1)S(1)} collective-permute-done((bf16[192,640]{1,0:T(8,128)(2,1)S(1)}, bf16[192,640]{1,0:T(8,128)(2,1)S(1)}, u32[]{:S(2)}, u32[]{:S(2)}) %collective-permute-start.12) | collective-permute-done | bytes 245792 | tf_op jit(solution)/shard_map/ppermute | solution.py:56
  86.9 11.8 %attention_near.1 = (bf16[192,960]{1,0:T(8,128)(2,1)}, f32[5,576]{1,0:T(8,128)}, f32[5,576]{1,0:T(8,128)}, f32[5,64,576]{2,1,0:T(8,128)}) custom-call(s32[4]{0:T(128)} %pad_add_fusion.1.spots, bf16[192,960]{1,0:T(8,128)(2,1)} %get-tuple-element.99.refs_0_, s32[768,1]{1,0:T(8,128)} %slice.116.refs_1_, s32[1,576]{1,0:T(1,128)} %broadcast_in_dim.29.refs_2_, ...), custom_call_target="tpu_custom_call" | custom-call | flops 13799999488 | tf_op jit(solution)/shard_map/attention_near/pallas_call | solution.py:92
  98.7 6.8 %collective-permute-done.17.refs_15_.refs_11_ = bf16[192,640]{1,0:T(8,128)(2,1)S(1)} collective-permute-done((bf16[192,640]{1,0:T(8,128)(2,1)S(1)}, bf16[192,640]{1,0:T(8,128)(2,1)S(1)}, u32[]{:S(2)}, u32[]{:S(2)}) %collective-permute-start.17) | collective-permute-done | bytes 245792 | tf_op jit(solution)/shard_map/ppermute | solution.py:56
  106.2 14.3 %attention_far.1 = (bf16[192,960]{1,0:T(8,128)(2,1)}, f32[5,64,576]{2,1,0:T(8,128)}, f32[5,576]{1,0:T(8,128)}, f32[192,960]{1,0:T(8,128)}, f32[192,1]{1,0:T(8,128)}, /*index=5*/bf16[192,960]{1,0:T(8,128)(2,1)}) custom-call(s32[4]{0:T(128)} %pad_add_fusion.1.spots, bf16[192,960]{1,0:T(8,128)(2,1)} %get-tuple-element.109.refs_0_, s32[768,1]{1,0:T(8,128)} %slice.117.refs_1_, ...), custom_call_target="tpu_custom_call" | custom-call | flops 16099999744 | tf_op jit(solution)/shard_map/attention_far/pallas_call | solution.py:92
  124.0 7.9 %collective-permute-done.19.refs_3_.refs_7_ = bf16[192,960]{1,0:T(8,128)(2,1)S(1)} collective-permute-done((bf16[192,960]{1,0:T(8,128)(2,1)}, bf16[192,960]{1,0:T(8,128)(2,1)S(1)}, u32[]{:S(2)}, u32[]{:S(2)}) %collective-permute-start.19) | collective-permute-done | bytes 368672 | tf_op jit(solution)/shard_map/ppermute | solution.py:65
  134.3 6.9 %collective-permute-done.21.refs_5_.refs_9_ = bf16[192,960]{1,0:T(8,128)(2,1)S(1)} collective-permute-done((bf16[192,960]{1,0:T(8,128)(2,1)}, bf16[192,960]{1,0:T(8,128)(2,1)S(1)}, u32[]{:S(2)}, u32[]{:S(2)}) %collective-permute-start.21) | collective-permute-done | bytes 368672 | tf_op jit(solution)/shard_map/ppermute | solution.py:65
  143.6 8.5 %feed_forward.3 = (bf16[4,192,960]{2,1,0:T(8,128)(2,1)}, bf16[768,320]{1,0:T(8,128)(2,1)}, bf16[768,640]{1,0:T(8,128)(2,1)}) custom-call(s32[4]{0:T(128)} %pad_add_fusion.1.spots, bf16[960,960]{1,0:T(8,128)(2,1)} %all-gather.5.cloned.1.call-done.refs_0_, bf16[8,192,960]{2,1,0:T(8,128)(2,1)} %all-gather.3.cloned.1.call-done.refs_1_.refs_5_, ...), custom_call_target="tpu_custom_call" | custom-call | flops 9200000000 | tf_op jit(solution)/shard_map/feed_forward/pallas_call | solution.py:92
  152.4 8.5 %feed_forward.2 = (bf16[4,192,960]{2,1,0:T(8,128)(2,1)}, bf16[768,320]{1,0:T(8,128)(2,1)}, bf16[768,640]{1,0:T(8,128)(2,1)}) custom-call(s32[4]{0:T(128)} %pad_add_fusion.1.spots, bf16[960,960]{1,0:T(8,128)(2,1)} %all-gather.5.cloned.1.call-done.refs_0_, bf16[8,192,960]{2,1,0:T(8,128)(2,1)} %all-gather.3.cloned.1.call-done.refs_1_.refs_5_, ...), custom_call_target="tpu_custom_call" | custom-call | flops 9200000000 | tf_op jit(solution)/shard_map/feed_forward/pallas_call | solution.py:92
  166.8 12.4 %feed_forward_weights.1 = (bf16[4,192,960]{2,1,0:T(8,128)(2,1)}, bf16[4,192,960]{2,1,0:T(8,128)(2,1)}, bf16[960,960]{1,0:T(8,128)(2,1)}) custom-call(s32[4]{0:T(128)} %pad_add_fusion.1.spots, bf16[960,960]{1,0:T(8,128)(2,1)} %all-gather.5.cloned.1.call-done.refs_0_, bf16[768,320]{1,0:T(8,128)(2,1)} %get-tuple-element.121.refs_1_, ...), custom_call_target="tpu_custom_call" | custom-call | flops 13799999488 | tf_op jit(solution)/shard_map/feed_forward_weights/pallas_call | solution.py:92
  179.2 5.1 %collective-permute-done.29.refs_4_ = bf16[192,960]{1,0:T(8,128)(2,1)S(1)} collective-permute-done((bf16[192,960]{1,0:T(8,128)(2,1)S(1)}, bf16[192,960]{1,0:T(8,128)(2,1)S(1)}, u32[]{:S(2)}, u32[]{:S(2)}) %collective-permute-start.29) | collective-permute-done | bytes 368672 | tf_op jit(solution)/shard_map/ppermute | solution.py:65
  185.0 6.7 %residual_back.1 = (f32[192,960]{1,0:T(8,128)}, bf16[192,960]{1,0:T(8,128)(2,1)}, bf16[192,960]{1,0:T(8,128)(2,1)}, f32[1,960]{1,0:T(1,128)}) custom-call(s32[4]{0:T(128)} %pad_add_fusion.1.spots, bf16[4,192,960]{2,1,0:T(8,128)(2,1)} %get-tuple-element.118.refs_0_, bf16[4,192,960]{2,1,0:T(8,128)(2,1)} %copy-done.3, bf16[192,960]{1,0:T(8,128)(2,1)} %copy-done.25, ...), custom_call_target="tpu_custom_call" | custom-call | flops 6899999744 | tf_op jit(solution)/shard_map/residual_back/pallas_call | solution.py:92
  191.8 12.7 %attention_back_far.1 = (f32[5,64,576]{2,1,0:T(8,128)}, bf16[4,192,640]{2,1,0:T(8,128)(2,1)}) custom-call(s32[4]{0:T(128)} %pad_add_fusion.1.spots, bf16[192,960]{1,0:T(8,128)(2,1)} %get-tuple-element.109.refs_0_, s32[768,1]{1,0:T(8,128)} %slice.117.refs_1_, s32[1,576]{1,0:T(1,128)} %broadcast_in_dim.29.refs_2_, ...), custom_call_target="tpu_custom_call" | custom-call | flops 14949999616 | tf_op jit(solution)/shard_map/attention_back_far/pallas_call | solution.py:92
  207.9 13.6 %attention_back_near.1 = (bf16[192,960]{1,0:T(8,128)(2,1)}, bf16[192,640]{1,0:T(8,128)(2,1)}, bf16[192,640]{1,0:T(8,128)(2,1)}, bf16[192,640]{1,0:T(8,128)(2,1)}, bf16[192,640]{1,0:T(8,128)(2,1)}) custom-call(s32[4]{0:T(128)} %pad_add_fusion.1.spots, bf16[192,960]{1,0:T(8,128)(2,1)} %get-tuple-element.109.refs_0_, s32[768,1]{1,0:T(8,128)} %slice.116.refs_1_, ...), custom_call_target="tpu_custom_call" | custom-call | flops 16099999744 | tf_op jit(solution)/shard_map/attention_back_near/pallas_call | solution.py:92
  222.6 4.9 %collective-permute-done.31 = bf16[2,192,960]{2,1,0:T(8,128)(2,1)} collective-permute-done((bf16[2,192,960]{2,1,0:T(8,128)(2,1)}, bf16[2,192,960]{2,1,0:T(8,128)(2,1)}, u32[]{:S(2)}, u32[]{:S(2)}) %collective-permute-start.31) | collective-permute-done | bytes 737312 | tf_op jit(solution)/shard_map/ppermute | solution.py:65
  229.5 5.0 %query_output_weight_grads.1 = (bf16[2,960,480]{2,1,0:T(8,128)(2,1)}, bf16[2,960,480]{2,1,0:T(8,128)(2,1)}) custom-call(s32[4]{0:T(128)} %pad_add_fusion.1.spots, bf16[192,960]{1,0:T(8,128)(2,1)} %get-tuple-element.149.refs_0_, bf16[192,960]{1,0:T(8,128)(2,1)} %get-tuple-element.134.refs_1_, bf16[192,960]{1,0:T(8,128)(2,1)} %get-tuple-element.145.refs_2_, ...), custom_call_target="tpu_custom_call" | custom-call | flops 8049999872 | tf_op jit(solution)/shard_map/query_output_weight_grads/pallas_call | solution.py:92
  234.5 4.2 %collective-permute-done.33 = bf16[2,960,480]{2,1,0:T(8,128)(2,1)S(1)} collective-permute-done((bf16[2,960,480]{2,1,0:T(8,128)(2,1)}, bf16[2,960,480]{2,1,0:T(8,128)(2,1)S(1)}, u32[]{:S(2)}, u32[]{:S(2)}) %collective-permute-start.33) | collective-permute-done | bytes 1843232 | tf_op jit(solution)/shard_map/ppermute | solution.py:65
  245.4 3.8 collective-permute-start.35
  250.1 25.6 %collective-permute-done.46.refs_4_ = bf16[240,960]{1,0:T(8,128)(2,1)} collective-permute-done((bf16[240,960]{1,0:T(8,128)(2,1)}, bf16[240,960]{1,0:T(8,128)(2,1)}, u32[]{:S(2)}, u32[]{:S(2)}) %collective-permute-start.46) | collective-permute-done | bytes 460832 | tf_op jit(solution)/shard_map/ppermute | solution.py:65
  277.7 4.1 %query_back.1.refs_6_ = f32[192,960]{1,0:T(8,128)} custom-call(s32[4]{0:T(128)} %pad_add_fusion.1.spots, bf16[192,960]{1,0:T(8,128)(2,1)} %get-tuple-element.151.refs_3_.low_ref, bf16[240,960]{1,0:T(8,128)(2,1)} %local_ref.1, bf16[720,480]{1,0:T(8,128)(2,1)} %stack_quarters.1.refs_6_.refs_9_.refs_10_.refs_0_, bf16[720,480]{1,0:T(8,128)(2,1)} %copy-done.12, ...), custom_call_target="tpu_custom_call" | custom-call | flops 4600000000 | tf_op jit(solution)/shard_map/query_back/pallas_call | solution.py:92
  292.7 6.3 %collective-permute-done.50.refs_5_ = bf16[240,960]{1,0:T(8,128)(2,1)} collective-permute-done((bf16[240,960]{1,0:T(8,128)(2,1)}, bf16[240,960]{1,0:T(8,128)(2,1)}, u32[]{:S(2)}, u32[]{:S(2)}) %collective-permute-start.50) | collective-permute-done | bytes 460832 | tf_op jit(solution)/shard_map/ppermute | solution.py:65
  299.5 17.5 %collective-permute-done.43 = bf16[240,480]{1,0:T(8,128)(2,1)S(1)} collective-permute-done((bf16[240,480]{1,0:T(8,128)(2,1)S(1)}, bf16[240,480]{1,0:T(8,128)(2,1)S(1)}, u32[]{:S(2)}, u32[]{:S(2)}) %collective-permute-start.43) | collective-permute-done | bytes 230432 | tf_op jit(solution)/shard_map/ppermute | solution.py:56
  317.0 6.0 %keys_values_back.1 = (f32[192,960]{1,0:T(8,128)}, bf16[4,336,240]{2,1,0:T(8,128)(2,1)}, bf16[4,336,240]{2,1,0:T(8,128)(2,1)}) custom-call(s32[4]{0:T(128)} %pad_add_fusion.1.spots, f32[192,128]{1,0:T(8,128)} %pad_maximum_fusion.1.refs_5_.refs_3_.refs_0_, f32[192,128]{1,0:T(8,128)} %pad_maximum_fusion.2.refs_6_.refs_4_.refs_1_, ...), custom_call_target="tpu_custom_call" | custom-call | flops 6899999744 | tf_op jit(solution)/shard_map/keys_values_back/pallas_call | solution.py:92
  328.0 6.7 %feed_forward_out.1 = (f32[240,2560]{1,0:T(8,128)}, f32[240,2560]{1,0:T(8,128)}, f32[960,640]{1,0:T(8,128)}) custom-call(s32[4]{0:T(128)} %pad_add_fusion.1.spots, bf16[240,960]{1,0:T(8,128)(2,1)} %reduce-scatter.2.cloned.1.call-done.refs_0_, bf16[240,960]{1,0:T(8,128)(2,1)} %collective-permute-done.47.refs_1_, bf16[240,960]{1,0:T(8,128)(2,1)} %copy-done.14, ...), custom_call_target="tpu_custom_call" | custom-call | flops 8049999872 | tf_op jit(solution)/shard_map/feed_forward_out/pallas_call | solution.py:92
  339.5 4.7 %collective-permute-done.41 = bf16[336,240]{1,0:T(8,128)(2,1)S(1)} collective-permute-done((bf16[336,240]{1,0:T(8,128)(2,1)S(1)}, bf16[336,240]{1,0:T(8,128)(2,1)S(1)}, u32[]{:S(2)}, u32[]{:S(2)}) %collective-permute-start.41) | collective-permute-done | bytes 161312 | tf_op jit(solution)/shard_map/ppermute | solution.py:56
  344.2 8.1 %collective-permute-done.40 = bf16[336,240]{1,0:T(8,128)(2,1)S(1)} collective-permute-done((bf16[336,240]{1,0:T(8,128)(2,1)S(1)}, bf16[336,240]{1,0:T(8,128)(2,1)S(1)}, u32[]{:S(2)}, u32[]{:S(2)}) %collective-permute-start.40) | collective-permute-done | bytes 161312 | tf_op jit(solution)/shard_map/ppermute | solution.py:56
  354.5 5.3 %collective-permute-done.54 = bf16[336,240]{1,0:T(8,128)(2,1)S(1)} collective-permute-done((bf16[336,240]{1,0:T(8,128)(2,1)S(1)}, bf16[336,240]{1,0:T(8,128)(2,1)S(1)}, u32[]{:S(2)}, u32[]{:S(2)}) %collective-permute-start.54) | collective-permute-done | bytes 161312 | tf_op jit(solution)/shard_map/ppermute | solution.py:65
  363.5 3.8 collective-permute-done.55
  367.4 4.1 %collective-permute-done.53 = bf16[192,960]{1,0:T(8,128)(2,1)S(1)} collective-permute-done((bf16[192,960]{1,0:T(8,128)(2,1)S(1)}, bf16[192,960]{1,0:T(8,128)(2,1)S(1)}, u32[]{:S(2)}, u32[]{:S(2)}) %collective-permute-start.53) | collective-permute-done | bytes 368672 | tf_op jit(solution)/shard_map/ppermute | solution.py:65
  (254 shorter events, 109.7 us)
Async XLA Ops:
  7.2 77.7 %all-gather.3.cloned.1.call-start = ((), (), s32[]{:S(2)}) async-start(), calls=%async_computation.1 | async-start | bytes 3538944 | tf_op jit(solution)/shard_map/all_gather | solution.py:673
  7.9 134.9 %all-gather.5.cloned.1.call-start = ((), (), s32[]{:S(2)}) async-start(), calls=%async_computation.2 | async-start | bytes 2457600 | tf_op jit(solution)/shard_map/all_gather | solution.py:719
  10.4 18.6 %collective-permute-start = (bf16[336,240]{1,0:T(8,128)(2,1)S(1)}, bf16[336,240]{1,0:T(8,128)(2,1)S(1)}, u32[]{:S(2)}, u32[]{:S(2)}) collective-permute-start(bf16[336,240]{1,0:T(8,128)(2,1)S(1)} %pad_maximum_fusion), channel_id=1, source_target_pairs={{0,1},{1,0},{2,3},{3,2},{4,5},{5,4},{6,7},{7,6},{8,9},{9,8},{10,11... | collective-permute-start | bytes 483848 | tf_op jit(solution)/shard_map/ppermute | solution.py:56
  18.7 19.3 %collective-permute-start.6 = (bf16[240,480]{1,0:T(8,128)(2,1)}, bf16[240,480]{1,0:T(8,128)(2,1)S(1)}, u32[]{:S(2)}, u32[]{:S(2)}) collective-permute-start(bf16[240,480]{1,0:T(8,128)(2,1)} %quarter_columns.1), channel_id=1, source_target_pairs={{0,1},{1,0},{2,3},{3,2},{4,5},{5,4},{6,7},{7,6},{8,9},{9,8},{10,11... | collective-permute-start | bytes 691208 | tf_op jit(solution)/shard_map/ppermute | solution.py:56
  19.6 27.6 %collective-permute-start.7 = (bf16[240,480]{1,0:T(8,128)(2,1)}, bf16[240,480]{1,0:T(8,128)(2,1)S(1)}, u32[]{:S(2)}, u32[]{:S(2)}) collective-permute-start(bf16[240,480]{1,0:T(8,128)(2,1)} %quarter_columns.1), channel_id=1, source_target_pairs={{0,2},{1,3},{2,0},{3,1},{4,6},{5,7},{6,4},{7,5},{8,10},{9,11},{10,... | collective-permute-start | bytes 691208 | tf_op jit(solution)/shard_map/ppermute | solution.py:56
  31.3 15.9 %collective-permute-start.8 = (bf16[240,480]{1,0:T(8,128)(2,1)S(1)}, bf16[240,480]{1,0:T(8,128)(2,1)S(1)}, u32[]{:S(2)}, u32[]{:S(2)}) collective-permute-start(bf16[240,480]{1,0:T(8,128)(2,1)S(1)} %copy-done.36), channel_id=1, source_target_pairs={{0,3},{1,2},{2,1},{3,0},{4,7},{5,6},{6,5},{7,4},{8,11},{9,10},{10,... | collective-permute-start | bytes 691208 | tf_op jit(solution)/shard_map/ppermute | solution.py:56
  50.0 28.4 %collective-permute-start.10 = (bf16[720,480]{1,0:T(8,128)(2,1)}, bf16[720,480]{1,0:T(8,128)(2,1)S(1)}, u32[]{:S(2)}, u32[]{:S(2)}) collective-permute-start(bf16[720,480]{1,0:T(8,128)(2,1)} %stack_quarters.1.refs_6_.refs_9_.refs_10_.refs_0_), channel_id=1, source_target_pairs={{0,16},{4,20},{8,24},{12,28},{16,0},{20,4},{24,8},{28,12},{1,17},{... | collective-permute-start | bytes 2073608 | tf_op jit(solution)/shard_map/ppermute | solution.py:65
  51.6 16.6 %collective-permute-start.11 = (bf16[192,640]{1,0:T(8,128)(2,1)S(1)}, bf16[192,640]{1,0:T(8,128)(2,1)S(1)}, u32[]{:S(2)}, u32[]{:S(2)}) collective-permute-start(bf16[192,640]{1,0:T(8,128)(2,1)S(1)} %copy-done.28), channel_id=1, source_target_pairs={{0,1},{1,0},{2,3},{3,2},{4,5},{5,4},{6,7},{7,6},{8,9},{9,8},{10,11... | collective-permute-start | bytes 737288 | tf_op jit(solution)/shard_map/ppermute | solution.py:56
  58.1 20.3 %collective-permute-start.12 = (bf16[192,640]{1,0:T(8,128)(2,1)S(1)}, bf16[192,640]{1,0:T(8,128)(2,1)S(1)}, u32[]{:S(2)}, u32[]{:S(2)}) collective-permute-start(bf16[192,640]{1,0:T(8,128)(2,1)S(1)} %copy-done.28), channel_id=1, source_target_pairs={{0,2},{1,3},{2,0},{3,1},{4,6},{5,7},{6,4},{7,5},{8,10},{9,11},{10,... | collective-permute-start | bytes 737288 | tf_op jit(solution)/shard_map/ppermute | solution.py:56
  59.3 19.1 %collective-permute-start.13 = (bf16[192,640]{1,0:T(8,128)(2,1)S(1)}, bf16[192,640]{1,0:T(8,128)(2,1)S(1)}, u32[]{:S(2)}, u32[]{:S(2)}) collective-permute-start(bf16[192,640]{1,0:T(8,128)(2,1)S(1)} %copy-done.28), channel_id=1, source_target_pairs={{0,3},{1,2},{2,1},{3,0},{4,7},{5,6},{6,5},{7,4},{8,11},{9,10},{10,... | collective-permute-start | bytes 737288 | tf_op jit(solution)/shard_map/ppermute | solution.py:56
  60.8 24.6 %collective-permute-start.9 = (bf16[720,480]{1,0:T(8,128)(2,1)}, bf16[720,480]{1,0:T(8,128)(2,1)S(1)}, u32[]{:S(2)}, u32[]{:S(2)}) collective-permute-start(bf16[720,480]{1,0:T(8,128)(2,1)} %stack_quarters.1.refs_6_.refs_9_.refs_10_.refs_0_), channel_id=1, source_target_pairs={{0,8},{4,12},{8,0},{12,4},{16,24},{20,28},{24,16},{28,20},{1,9},{5... | collective-permute-start | bytes 2073608 | tf_op jit(solution)/shard_map/ppermute | solution.py:65
  81.4 17.3 %collective-permute-start.15 = (bf16[192,640]{1,0:T(8,128)(2,1)S(1)}, bf16[192,640]{1,0:T(8,128)(2,1)}, u32[]{:S(2)}, u32[]{:S(2)}) collective-permute-start(bf16[192,640]{1,0:T(8,128)(2,1)S(1)} %copy-done.28), channel_id=1, source_target_pairs={{0,4},{4,0},{1,5},{5,1},{2,6},{6,2},{3,7},{7,3},{8,12},{12,8},{9,1... | collective-permute-start | bytes 737288 | tf_op jit(solution)/shard_map/ppermute | solution.py:56
  83.4 22.1 %collective-permute-start.18 = (bf16[192,640]{1,0:T(8,128)(2,1)S(1)}, bf16[192,640]{1,0:T(8,128)(2,1)}, u32[]{:S(2)}, u32[]{:S(2)}) collective-permute-start(bf16[192,640]{1,0:T(8,128)(2,1)S(1)} %collective-permute-done.13.refs_13_.refs_12_), channel_id=1, source_target_pairs={{0,4},{4,0},{1,5},{5,1},{2,6},{6,2},{3,7},{7,3},{8,12},{12,8},{9,1... | collective-permute-start | bytes 737288 | tf_op jit(solution)/shard_map/ppermute | solution.py:56
  84.9 137.7 %reduce-scatter.2.cloned.1.call-start = ((), (), s32[]{:S(2)}) async-start(), calls=%async_computation.3 | async-start | bytes 2457600 | tf_op jit(solution)/shard_map/reduce_scatter | solution.py:791
  85.5 20.0 %collective-permute-start.17 = (bf16[192,640]{1,0:T(8,128)(2,1)S(1)}, bf16[192,640]{1,0:T(8,128)(2,1)S(1)}, u32[]{:S(2)}, u32[]{:S(2)}) collective-permute-start(bf16[192,640]{1,0:T(8,128)(2,1)S(1)} %collective-permute-done.12.refs_12_.refs_11_), channel_id=1, source_target_pairs={{0,4},{4,0},{1,5},{5,1},{2,6},{6,2},{3,7},{7,3},{8,12},{12,8},{9,1... | collective-permute-start | bytes 737288 | tf_op jit(solution)/shard_map/ppermute | solution.py:56
  122.5 18.6 %collective-permute-start.21 = (bf16[192,960]{1,0:T(8,128)(2,1)}, bf16[192,960]{1,0:T(8,128)(2,1)S(1)}, u32[]{:S(2)}, u32[]{:S(2)}) collective-permute-start(bf16[192,960]{1,0:T(8,128)(2,1)} %get-tuple-element.117.refs_2_.refs_6_), channel_id=1, source_target_pairs={{0,20},{4,16},{8,28},{12,24},{16,4},{20,0},{24,12},{28,8},{1,21},{... | collective-permute-start | bytes 1105928 | tf_op jit(solution)/shard_map/ppermute | solution.py:65
  124.0 17.2 %collective-permute-start.22 = (bf16[192,960]{1,0:T(8,128)(2,1)}, bf16[192,960]{1,0:T(8,128)(2,1)S(1)}, u32[]{:S(2)}, u32[]{:S(2)}) collective-permute-start(bf16[192,960]{1,0:T(8,128)(2,1)} %get-tuple-element.117.refs_2_.refs_6_), channel_id=1, source_target_pairs={{0,8},{4,12},{8,0},{12,4},{16,24},{20,28},{24,16},{28,20},{1,9},{5... | collective-permute-start | bytes 1105928 | tf_op jit(solution)/shard_map/ppermute | solution.py:65
  163.2 16.0 %collective-permute-start.27 = (bf16[192,960]{1,0:T(8,128)(2,1)S(1)}, bf16[192,960]{1,0:T(8,128)(2,1)S(1)}, u32[]{:S(2)}, u32[]{:S(2)}) collective-permute-start(bf16[192,960]{1,0:T(8,128)(2,1)S(1)} %get-tuple-element.185), channel_id=1, source_target_pairs={{0,4},{4,0},{8,12},{12,8},{16,20},{20,16},{24,28},{28,24},{1,5},{5... | collective-permute-start | bytes 1105928 | tf_op jit(solution)/shard_map/ppermute | solution.py:65
  165.4 18.9 %collective-permute-start.29 = (bf16[192,960]{1,0:T(8,128)(2,1)S(1)}, bf16[192,960]{1,0:T(8,128)(2,1)S(1)}, u32[]{:S(2)}, u32[]{:S(2)}) collective-permute-start(bf16[192,960]{1,0:T(8,128)(2,1)S(1)} %get-tuple-element.183), channel_id=1, source_target_pairs={{0,20},{4,16},{8,28},{12,24},{16,4},{20,0},{24,12},{28,8},{1,21},{... | collective-permute-start | bytes 1105928 | tf_op jit(solution)/shard_map/ppermute | solution.py:65
  204.6 24.9 %collective-permute-start.32 = (bf16[4,192,640]{2,1,0:T(8,128)(2,1)}, bf16[4,192,640]{2,1,0:T(8,128)(2,1)}, u32[]{:S(2)}, u32[]{:S(2)}) collective-permute-start(bf16[4,192,640]{2,1,0:T(8,128)(2,1)} %get-tuple-element.147), channel_id=1, source_target_pairs={{0,4},{4,0},{1,5},{5,1},{2,6},{6,2},{3,7},{7,3},{8,12},{12,8},{9,1... | collective-permute-start | bytes 2949128 | tf_op jit(solution)/shard_map/ppermute | solution.py:56
  207.5 20.0 %collective-permute-start.31 = (bf16[2,192,960]{2,1,0:T(8,128)(2,1)}, bf16[2,192,960]{2,1,0:T(8,128)(2,1)}, u32[]{:S(2)}, u32[]{:S(2)}) collective-permute-start(bf16[2,192,960]{2,1,0:T(8,128)(2,1)} %add_convert_fusion.1), channel_id=1, source_target_pairs={{0,16},{4,20},{8,24},{12,28},{16,0},{20,4},{24,8},{28,12},{1,17},{... | collective-permute-start | bytes 2211848 | tf_op jit(solution)/shard_map/ppermute | solution.py:65
  241.1 40.9 %collective-permute-start.34 = (bf16[960,480]{1,0:T(8,128)(2,1)}, bf16[960,480]{1,0:T(8,128)(2,1)}, u32[]{:S(2)}, u32[]{:S(2)}) collective-permute-start(bf16[960,480]{1,0:T(8,128)(2,1)} %fusion), channel_id=1, source_target_pairs={{0,16},{4,20},{8,24},{12,28},{16,0},{20,4},{24,8},{28,12},{1,17},{... | collective-permute-start | bytes 2764808 | tf_op jit(solution)/shard_map/ppermute | solution.py:65
  241.5 34.3 %collective-permute-start.46 = (bf16[240,960]{1,0:T(8,128)(2,1)}, bf16[240,960]{1,0:T(8,128)(2,1)}, u32[]{:S(2)}, u32[]{:S(2)}) collective-permute-start(bf16[240,960]{1,0:T(8,128)(2,1)} %reduce-scatter.2.cloned.1.call-done.refs_0_), channel_id=1, source_target_pairs={{0,16},{4,20},{8,24},{12,28},{16,0},{20,4},{24,8},{28,12},{1,17},{... | collective-permute-start | bytes 1382408 | tf_op jit(solution)/shard_map/ppermute | solution.py:65
  245.4 40.9 %collective-permute-start.35 = (bf16[192,640]{1,0:T(8,128)(2,1)S(1)}, bf16[192,640]{1,0:T(8,128)(2,1)S(1)}, u32[]{:S(2)}, u32[]{:S(2)}) collective-permute-start(bf16[192,640]{1,0:T(8,128)(2,1)S(1)} %get-tuple-element.195), channel_id=1, source_target_pairs={{0,1},{1,0},{2,3},{3,2},{4,5},{5,4},{6,7},{7,6},{8,9},{9,8},{10,11... | collective-permute-start | bytes 737288 | tf_op jit(solution)/shard_map/ppermute | solution.py:56
  249.3 38.4 %collective-permute-start.36 = (bf16[192,640]{1,0:T(8,128)(2,1)S(1)}, bf16[192,640]{1,0:T(8,128)(2,1)}, u32[]{:S(2)}, u32[]{:S(2)}) collective-permute-start(bf16[192,640]{1,0:T(8,128)(2,1)S(1)} %get-tuple-element.194), channel_id=1, source_target_pairs={{0,2},{1,3},{2,0},{3,1},{4,6},{5,7},{6,4},{7,5},{8,10},{9,11},{10,... | collective-permute-start | bytes 737288 | tf_op jit(solution)/shard_map/ppermute | solution.py:56
  275.7 16.4 %collective-permute-start.47 = (bf16[240,960]{1,0:T(8,128)(2,1)}, bf16[240,960]{1,0:T(8,128)(2,1)}, u32[]{:S(2)}, u32[]{:S(2)}) collective-permute-start(bf16[240,960]{1,0:T(8,128)(2,1)} %reduce-scatter.2.cloned.1.call-done.refs_0_), channel_id=1, source_target_pairs={{0,4},{4,0},{8,12},{12,8},{16,20},{20,16},{24,28},{28,24},{1,5},{5... | collective-permute-start | bytes 1382408 | tf_op jit(solution)/shard_map/ppermute | solution.py:65
  276.8 22.2 %collective-permute-start.50 = (bf16[240,960]{1,0:T(8,128)(2,1)}, bf16[240,960]{1,0:T(8,128)(2,1)}, u32[]{:S(2)}, u32[]{:S(2)}) collective-permute-start(bf16[240,960]{1,0:T(8,128)(2,1)} %collective-permute-done.46.refs_4_), channel_id=1, source_target_pairs={{0,4},{4,0},{8,12},{12,8},{16,20},{20,16},{24,28},{28,24},{1,5},{5... | collective-permute-start | bytes 1382408 | tf_op jit(solution)/shard_map/ppermute | solution.py:65
  287.7 29.3 %collective-permute-start.43 = (bf16[240,480]{1,0:T(8,128)(2,1)S(1)}, bf16[240,480]{1,0:T(8,128)(2,1)S(1)}, u32[]{:S(2)}, u32[]{:S(2)}) collective-permute-start(bf16[240,480]{1,0:T(8,128)(2,1)S(1)} %get-tuple-element.165), channel_id=1, source_target_pairs={{0,2},{1,3},{2,0},{3,1},{4,6},{5,7},{6,4},{7,5},{8,10},{9,11},{10,... | collective-permute-start | bytes 691208 | tf_op jit(solution)/shard_map/ppermute | solution.py:56
  292.2 32.9 %collective-permute-start.48 = (bf16[240,960]{1,0:T(8,128)(2,1)}, bf16[240,960]{1,0:T(8,128)(2,1)S(1)}, u32[]{:S(2)}, u32[]{:S(2)}) collective-permute-start(bf16[240,960]{1,0:T(8,128)(2,1)} %reduce-scatter.2.cloned.1.call-done.refs_0_), channel_id=1, source_target_pairs={{0,8},{4,12},{8,0},{12,4},{16,24},{20,28},{24,16},{28,20},{1,9},{5... | collective-permute-start | bytes 1382408 | tf_op jit(solution)/shard_map/ppermute | solution.py:65
  292.2 34.1 %collective-permute-start.51 = (bf16[240,960]{1,0:T(8,128)(2,1)}, bf16[240,960]{1,0:T(8,128)(2,1)S(1)}, u32[]{:S(2)}, u32[]{:S(2)}) collective-permute-start(bf16[240,960]{1,0:T(8,128)(2,1)} %collective-permute-done.46.refs_4_), channel_id=1, source_target_pairs={{0,8},{4,12},{8,0},{12,4},{16,24},{20,28},{24,16},{28,20},{1,9},{5... | collective-permute-start | bytes 1382408 | tf_op jit(solution)/shard_map/ppermute | solution.py:65
  299.0 27.3 %collective-permute-start.49 = (bf16[240,960]{1,0:T(8,128)(2,1)}, bf16[240,960]{1,0:T(8,128)(2,1)S(1)}, u32[]{:S(2)}, u32[]{:S(2)}) collective-permute-start(bf16[240,960]{1,0:T(8,128)(2,1)} %collective-permute-done.47.refs_1_), channel_id=1, source_target_pairs={{0,8},{4,12},{8,0},{12,4},{16,24},{20,28},{24,16},{28,20},{1,9},{5... | collective-permute-start | bytes 1382408 | tf_op jit(solution)/shard_map/ppermute | solution.py:65
  299.0 27.3 %collective-permute-start.52 = (bf16[240,960]{1,0:T(8,128)(2,1)}, bf16[240,960]{1,0:T(8,128)(2,1)S(1)}, u32[]{:S(2)}, u32[]{:S(2)}) collective-permute-start(bf16[240,960]{1,0:T(8,128)(2,1)} %collective-permute-done.50.refs_5_), channel_id=1, source_target_pairs={{0,8},{4,12},{8,0},{12,4},{16,24},{20,28},{24,16},{28,20},{1,9},{5... | collective-permute-start | bytes 1382408 | tf_op jit(solution)/shard_map/ppermute | solution.py:65
  (80 other events, 708.2 us)
Sparse Core Ops, SparseCore 0:
  9.9 35.0 all-gather.2
  85.1 44.4 all-gather.4
  179.3 43.2 reduce-scatter.1

commit v5 on v4

--- a/solution.py
+++ b/solution.py
@@ -32,8 +32,10 @@
     "residual_back": 6,
     "attention_back_far": 13,
     "attention_back_near": 14,
-    "query_output_weight_grads": 7,
-    "query_back": 4,
+    "query_output_weight_grads": 0,
+    "query_back": 0,
+    "stack_quarters": 0,
+    "quarter_columns": 0,
     "keys_values_back": 6,
     "feed_forward_out": 7,
 }
@@ -63,6 +65,14 @@
         for c in range(ctx_count):
             pairs.append((d * ctx_count + c, (d ^ dp_mask) * ctx_count + (c ^ ctx_mask)))
     return lax.ppermute(x, ("dp", "ctx"), pairs)
+
+
+def swaps_fsdp(x):
+    pieces = {0: x}
+    for r in range(1, lax.axis_size("fsdp")):
+        top = 1 << (r.bit_length() - 1)
+        pieces[r] = swap(pieces[r - top], "fsdp", top)
+    return [pieces[r] for r in range(1, lax.axis_size("fsdp"))]
 
 
 def swap_core(x):
@@ -652,7 +662,7 @@
         ],
         axis=0,
     )
-    kv_mine = [swap(kv_pack, "fsdp", r) for r in range(1, shards)]
+    kv_mine = swaps_fsdp(kv_pack)
     kv_other = [swap_core(piece) for piece in kv_mine]
 
     quarter = width // dp_count
@@ -661,7 +671,7 @@
         [after(query_weight, kv_pack), output_weight],
         [((weight_rows, 2 * quarter), BF16)], name="quarter_columns",
     )
-    quarter_pieces = [swap(quarters, "fsdp", r) for r in range(1, shards)]
+    quarter_pieces = swaps_fsdp(quarters)
 
     group_axes = ("dp", "ctx")
     extra = {}
@@ -706,11 +716,12 @@
         ],
         name="norm_keys_values",
     )
+    near = [kv_own] + swaps_fsdp(kv_own)
+    quarter_pieces = lax.optimization_barrier((kv_own, *quarter_pieces))[1:]
     (stacked,) = call(
-        stack_kernel, spots, lax.optimization_barrier((kv_own, *quarter_pieces))[1:],
+        stack_kernel, spots, quarter_pieces,
         [(((shards - 1) * weight_rows, 2 * quarter), BF16)], name="stack_quarters",
     )
-    near = [kv_own] + [swap(kv_own, "fsdp", r) for r in range(1, shards)]
     across, *near = lax.optimization_barrier((swap_plane(stacked, 2, 0), *near))
     stacks = [stacked, swap_core(stacked), across, swap_core(across)]
     far = [swap(piece, "ctx", d) for d in range(1, ctx_count) for piece in near]
@@ -820,10 +831,20 @@
         return out
 
     def sum_z(pieces):
-        total = pieces[0].astype(F32)
-        for r in range(1, shards):
-            total = total + swap(pieces[r], "fsdp", r).astype(F32)
-        return total.astype(BF16)
+        arrived = {r: swap(pieces[r], "fsdp", r) for r in reversed(range(1, shards))}
+        return sum(
+            (arrived[r].astype(F32) for r in range(1, shards)), pieces[0].astype(F32)
+        ).astype(BF16)
+
+    def relay_z(terms):
+        span = shards
+        pieces = {r: piece.astype(F32) for r, piece in enumerate(pieces_z(terms))}
+        while span > 1:
+            span //= 2
+            sent = jnp.stack([pieces[r].astype(BF16) for r in range(span, 2 * span)])
+            arrived = swap(sent, "fsdp", span)
+            pieces = {r: pieces[r] + arrived[r].astype(F32) for r in range(span)}
+        return pieces[0].astype(BF16)
 
     def sum_y(own):
         return sum_far((own.astype(F32) + swap_plane(own, 0, 1).astype(F32)).astype(BF16))
@@ -873,47 +894,42 @@
     query_partial, result_sent = lax.optimization_barrier((query_partial, result_sent))
     result_across = swap_plane(result_sent, 2, 0)
     query_low, near_grads = back(False, True, query_partial, near_pos, near)
-    query_low, pack_share = lax.optimization_barrier((query_low, pack_share))
-    result_across = after(result_across, query_low)
+    pair_shape = ((2, width, 2 * quarter), BF16)
+    weights_keep, weights_send = call(
+        functools.partial(weight_grads_kernel, dp_count), spots,
+        [attended, residual_low, normed_one, query_low], [pair_shape, pair_shape],
+        scratch=[((2 * dp_count, rows, quarter), BF16)], name="query_output_weight_grads",
+    )
+    weights_send, pack_share, result_across, far_grads[-1] = lax.optimization_barrier(
+        (weights_send, pack_share, result_across, far_grads[-1])
+    )
+
+    def home(r):
+        return sum(grads[r].astype(F32) for grads in far_grads)
+
+    kv_sums = {
+        r: (near_grads[r].astype(F32) + home(r)).astype(BF16) for r in range(1, shards)
+    }
+    kv_arrived = {r: swap(kv_sums[r], "fsdp", r) for r in reversed(range(1, shards))}
+    query_low, result_across, *_ = lax.optimization_barrier(
+        (query_low, result_across, *kv_sums.values())
+    )
     result_own, result_along = [
         (result_a[k].astype(F32) + result_core[k].astype(F32)) + result_across[k].astype(F32)
         for k in (0, 1)
     ]
     result_along = result_along.astype(BF16)
-    share_across = swap_plane(pack_share, 2, 0)
-    query_low, result_along, far_grads[-1] = lax.optimization_barrier(
-        (query_low, result_along, far_grads[-1])
-    )
-
-    def home(r):
-        return sum(grads[r].astype(F32) for grads in far_grads)
-
-    kv_arrived = {
-        r: swap((near_grads[r].astype(F32) + home(r)).astype(BF16), "fsdp", r)
-        for r in reversed(range(1, shards))
-    }
-    share_own, share_across, _ = lax.optimization_barrier(
-        (pack_share, share_across, far_grads[-1])
-    )
-    share_a = [share_own, swap_plane(share_own, 0, 1), share_across, swap_plane(share_across, 0, 1)]
-
-    pair_shape = ((2, width, 2 * quarter), BF16)
-    weights_keep, weights_send = call(
-        functools.partial(weight_grads_kernel, dp_count), spots,
-        [attended, residual_low, normed_one, query_low], [pair_shape, pair_shape],
-        scratch=[((2 * dp_count, rows, quarter), BF16)], name="query_output_weight_grads",
-    )
+
     weights_away = swap_core(weights_send)
-    query_turn = after(query_low, weights_send)
+    query_turn = query_low
     (query_back,) = call(
         functools.partial(query_back_kernel, shards, dp_count), spots,
         [query_turn, query_weight, *stacks], [((rows, width), F32)],
         scratch=[((dp_count, rows, quarter), BF16), ((shards, rows, weight_rows), F32)],
         name="query_back",
     )
-    _, weights_terms = sum_x(weights_keep, weights_away)
-    weights_pieces = pieces_z(weights_terms)
-    query_back, *weights_pieces = lax.optimization_barrier((query_back, *weights_pieces))
+    weights_sent, weights_terms = sum_x(weights_keep, weights_away)
+    query_back, weights_sent = lax.optimization_barrier((query_back, weights_sent))
     span = kv_width + EXTRA_ROWS
     packed_shape = ((shards, span, weight_rows), BF16)
     home_all = far_grads[0]
@@ -930,17 +946,22 @@
         scratch=[((shards, rows, weight_rows), F32)],
         name="keys_values_back",
     )
+    pack_share = after(pack_share, kv_send)
+    share_across = swap_plane(pack_share, 2, 0)
+    share_along = swap_plane(pack_share, 0, 1)
     kv_away = swap_core(kv_send)
     pieces = [
         (lax.dynamic_index_in_dim(kv_keep, shard ^ r, 0, keepdims=False).astype(F32)
          + lax.dynamic_index_in_dim(kv_away, shard ^ r, 0, keepdims=False).astype(F32)).astype(BF16)
         for r in range(shards)
     ]
+    weights_terms, *pieces = lax.optimization_barrier((weights_terms, *pieces))
+    kv_share = sum_z(pieces)
+    kv_share, share_across, share_along = lax.optimization_barrier(
+        (kv_share, share_across, share_along)
+    )
+    share_a = [pack_share, share_along, share_across, swap_plane(share_across, 0, 1)]
     share_b = [swap_core(piece) for piece in share_a]
-    kv_share = pieces[0].astype(F32)
-    for r in range(1, shards):
-        kv_share = kv_share + swap(pieces[r], "fsdp", r).astype(F32)
-    kv_share = kv_share.astype(BF16)
 
     share_by_mask = [None] * members
     for k, (a, b) in enumerate(((0, 0),) + CHIP_MASKS):
@@ -955,11 +976,8 @@
         scratch=[((members, weight_rows, 3 * part), BF16)],
         name="feed_forward_out",
     )
-    weights_own = sum_y(sum_z(weights_pieces))
-    kv_share, weights_own, result_along, *big = lax.optimization_barrier(
-        (kv_share, weights_own, result_along, gate_weight_grad, up_weight_grad, down_weight_grad)
-    )
-    gate_weight_grad, up_weight_grad, down_weight_grad = big
+    kv_share, result_along = lax.optimization_barrier((kv_share, result_along))
+    weights_own = sum_y(relay_z(weights_terms))
     result = residual + (result_own + swap_plane(result_along, 0, 1).astype(F32))
     output_weight_grad, query_weight_grad = finish_quarters(weights_own)
     low = sum_chips(kv_share)

time: 393 us -> 385 us (0.980)
  starting transfers between devices: 64.3 us -> 50.2 us
    ppermute x23 -> x22, waiting for transfers between devices: 67.3 us -> 94.1 us  [swap(): return lax.ppermute(x, axis, [(i, i ^ mask) for i in range(count)])]
    ppermute x37, waiting for transfers between devices: 79.6 us -> 56.3 us  [swap_plane(): return lax.ppermute(x, ('dp', 'ctx'), pairs)]
    ppermute x23 -> x22, starting transfers between devices: 43.2 us -> 31.8 us  [swap(): return lax.ppermute(x, axis, [(i, i ^ mask) for i in range(count)])]
    unnamed x98 -> x112, local copies, waits for them, and re-layouts: 7.8 us -> 10.1 us
  transfers between devices with their start and end apart: 63 -> 62, of which waited for: 23 -> 23; matrix products, arithmetic and copies ran while one was open for 5% -> 7% of each run, Pallas kernels for 29% -> 30%
where the time goes in v5:
time: 385 us; the launch traced here: 380 us
  waiting for transfers between devices  151 us (39%)
  Pallas kernels  125 us (32%)
  starting transfers between devices  50.2 us (13%)
  other arithmetic  21.4 us (6%)
  local copies, waits for them, and re-layouts  17 us (4%)
  between operations  15.3 us (4%)
    pallas_call x17, Pallas kernels, call(): pl.pallas_call(kernel, out_shape=outs, in_specs=specs, out_specs=tuple((p...  125 us
    ppermute x22, waiting for transfers between devices, swap(): return lax.ppermute(x, axis, [(i, i ^ mask) for i in range(count)])  94.1 us
    ppermute x37, waiting for transfers between devices, swap_plane(): return lax.ppermute(x, ('dp', 'ctx'), pairs)  56.3 us
    ppermute x22, starting transfers between devices, swap(): return lax.ppermute(x, axis, [(i, i ^ mask) for i in range(count)])  31.8 us
    ppermute x37, starting transfers between devices, swap_plane(): return lax.ppermute(x, ('dp', 'ctx'), pairs)  17.8 us
    unnamed x112, local copies, waits for them, and re-layouts  10.1 us
  transfers between devices with their start and end apart: 62, of which 23 were waited for; matrix products, arithmetic and copies ran while one was open for 7% of the time, Pallas kernels for 30%

profile of v5, /device:TPU:0, one launch (start us, length us, event | category | flops | bytes accessed | tf_op | source)
XLA Modules:
  0.0 379.9 jit_solution(13419688558700722060)
XLA Ops:
  19.7 4.3 %pack_weights.1 = bf16[240,960]{1,0:T(8,128)(2,1)} custom-call(s32[4]{0:T(128)} %pad_add_fusion.1.spots, bf16[240,2560]{1,0:T(8,128)(2,1)} %gate_ref.1, bf16[240,2560]{1,0:T(8,128)(2,1)} %up_ref.1, bf16[960,640]{1,0:T(8,128)(2,1)} %bitcast.96), custom_call_target="tpu_custom_call" | custom-call | flops 4600000000 | tf_op jit(solution)/shard_map/pack_weights/pallas_call | solution.py:102
  28.7 13.2 %collective-permute-done.2.refs_9_.refs_18_ = bf16[336,240]{1,0:T(8,128)(2,1)S(1)} collective-permute-done((bf16[336,240]{1,0:T(8,128)(2,1)S(1)}, bf16[336,240]{1,0:T(8,128)(2,1)S(1)}, u32[]{:S(2)}, u32[]{:S(2)}) %collective-permute-start.2) | collective-permute-done | bytes 161312 | tf_op jit(solution)/shard_map/ppermute | solution.py:58
  44.3 3.6 norm_keys_values.1
  48.0 9.9 %collective-permute-done.8.refs_2_ = bf16[240,480]{1,0:T(8,128)(2,1)S(1)} collective-permute-done((bf16[240,480]{1,0:T(8,128)(2,1)S(1)}, bf16[240,480]{1,0:T(8,128)(2,1)S(1)}, u32[]{:S(2)}, u32[]{:S(2)}) %collective-permute-start.8) | collective-permute-done | bytes 230432 | tf_op jit(solution)/shard_map/ppermute | solution.py:58
  64.1 9.8 %collective-permute-done.11.refs_11_.refs_10_ = bf16[192,640]{1,0:T(8,128)(2,1)S(1)} collective-permute-done((bf16[192,640]{1,0:T(8,128)(2,1)}, bf16[192,640]{1,0:T(8,128)(2,1)S(1)}, u32[]{:S(2)}, u32[]{:S(2)}) %collective-permute-start.11) | collective-permute-done | bytes 245792 | tf_op jit(solution)/shard_map/ppermute | solution.py:58
  74.6 7.0 %collective-permute-done.12.refs_12_.refs_11_ = bf16[192,640]{1,0:T(8,128)(2,1)S(1)} collective-permute-done((bf16[192,640]{1,0:T(8,128)(2,1)}, bf16[192,640]{1,0:T(8,128)(2,1)S(1)}, u32[]{:S(2)}, u32[]{:S(2)}) %collective-permute-start.12) | collective-permute-done | bytes 245792 | tf_op jit(solution)/shard_map/ppermute | solution.py:58
  81.6 5.2 %collective-permute-done.13.refs_13_.refs_12_ = bf16[192,640]{1,0:T(8,128)(2,1)S(1)} collective-permute-done((bf16[192,640]{1,0:T(8,128)(2,1)S(1)}, bf16[192,640]{1,0:T(8,128)(2,1)S(1)}, u32[]{:S(2)}, u32[]{:S(2)}) %collective-permute-start.13) | collective-permute-done | bytes 245792 | tf_op jit(solution)/shard_map/ppermute | solution.py:58
  95.4 11.9 %attention_near.1 = (bf16[192,960]{1,0:T(8,128)(2,1)}, f32[5,576]{1,0:T(8,128)}, f32[5,576]{1,0:T(8,128)}, f32[5,64,576]{2,1,0:T(8,128)}) custom-call(s32[4]{0:T(128)} %pad_add_fusion.1.spots, bf16[192,960]{1,0:T(8,128)(2,1)} %get-tuple-element.99.refs_0_, s32[768,1]{1,0:T(8,128)} %slice.124.refs_1_, s32[1,576]{1,0:T(1,128)} %broadcast_in_dim.29.refs_2_, ...), custom_call_target="tpu_custom_call" | custom-call | flops 13799999488 | tf_op jit(solution)/shard_map/attention_near/pallas_call | solution.py:102
  107.3 6.6 %collective-permute-done.17.refs_15_.refs_11_ = bf16[192,640]{1,0:T(8,128)(2,1)S(1)} collective-permute-done((bf16[192,640]{1,0:T(8,128)(2,1)S(1)}, bf16[192,640]{1,0:T(8,128)(2,1)S(1)}, u32[]{:S(2)}, u32[]{:S(2)}) %collective-permute-start.17) | collective-permute-done | bytes 245792 | tf_op jit(solution)/shard_map/ppermute | solution.py:58
  114.6 14.2 %attention_far.1 = (bf16[192,960]{1,0:T(8,128)(2,1)}, f32[5,64,576]{2,1,0:T(8,128)}, f32[5,576]{1,0:T(8,128)}, f32[192,960]{1,0:T(8,128)}, f32[192,1]{1,0:T(8,128)}, /*index=5*/bf16[192,960]{1,0:T(8,128)(2,1)}) custom-call(s32[4]{0:T(128)} %pad_add_fusion.1.spots, bf16[192,960]{1,0:T(8,128)(2,1)} %get-tuple-element.109.refs_0_, s32[768,1]{1,0:T(8,128)} %slice.125.refs_1_, ...), custom_call_target="tpu_custom_call" | custom-call | flops 16099999744 | tf_op jit(solution)/shard_map/attention_far/pallas_call | solution.py:102
  132.3 7.9 %collective-permute-done.19.refs_3_.refs_7_ = bf16[192,960]{1,0:T(8,128)(2,1)S(1)} collective-permute-done((bf16[192,960]{1,0:T(8,128)(2,1)}, bf16[192,960]{1,0:T(8,128)(2,1)S(1)}, u32[]{:S(2)}, u32[]{:S(2)}) %collective-permute-start.19) | collective-permute-done | bytes 368672 | tf_op jit(solution)/shard_map/ppermute | solution.py:67
  142.6 6.8 %collective-permute-done.21.refs_5_.refs_9_ = bf16[192,960]{1,0:T(8,128)(2,1)S(1)} collective-permute-done((bf16[192,960]{1,0:T(8,128)(2,1)}, bf16[192,960]{1,0:T(8,128)(2,1)S(1)}, u32[]{:S(2)}, u32[]{:S(2)}) %collective-permute-start.21) | collective-permute-done | bytes 368672 | tf_op jit(solution)/shard_map/ppermute | solution.py:67
  151.9 8.5 %feed_forward.3 = (bf16[4,192,960]{2,1,0:T(8,128)(2,1)}, bf16[768,320]{1,0:T(8,128)(2,1)}, bf16[768,640]{1,0:T(8,128)(2,1)}) custom-call(s32[4]{0:T(128)} %pad_add_fusion.1.spots, bf16[960,960]{1,0:T(8,128)(2,1)} %all-gather.5.cloned.1.call-done.refs_0_, bf16[8,192,960]{2,1,0:T(8,128)(2,1)} %all-gather.3.cloned.1.call-done.refs_1_.refs_5_, ...), custom_call_target="tpu_custom_call" | custom-call | flops 9200000000 | tf_op jit(solution)/shard_map/feed_forward/pallas_call | solution.py:102
  160.7 8.5 %feed_forward.2 = (bf16[4,192,960]{2,1,0:T(8,128)(2,1)}, bf16[768,320]{1,0:T(8,128)(2,1)}, bf16[768,640]{1,0:T(8,128)(2,1)}) custom-call(s32[4]{0:T(128)} %pad_add_fusion.1.spots, bf16[960,960]{1,0:T(8,128)(2,1)} %all-gather.5.cloned.1.call-done.refs_0_, bf16[8,192,960]{2,1,0:T(8,128)(2,1)} %all-gather.3.cloned.1.call-done.refs_1_.refs_5_, ...), custom_call_target="tpu_custom_call" | custom-call | flops 9200000000 | tf_op jit(solution)/shard_map/feed_forward/pallas_call | solution.py:102
  175.1 12.4 %feed_forward_weights.1 = (bf16[4,192,960]{2,1,0:T(8,128)(2,1)}, bf16[4,192,960]{2,1,0:T(8,128)(2,1)}, bf16[960,960]{1,0:T(8,128)(2,1)}) custom-call(s32[4]{0:T(128)} %pad_add_fusion.1.spots, bf16[960,960]{1,0:T(8,128)(2,1)} %all-gather.5.cloned.1.call-done.refs_0_, bf16[768,320]{1,0:T(8,128)(2,1)} %get-tuple-element.121.refs_1_, ...), custom_call_target="tpu_custom_call" | custom-call | flops 13799999488 | tf_op jit(solution)/shard_map/feed_forward_weights/pallas_call | solution.py:102
  187.5 5.0 %collective-permute-done.29.refs_4_ = bf16[192,960]{1,0:T(8,128)(2,1)S(1)} collective-permute-done((bf16[192,960]{1,0:T(8,128)(2,1)S(1)}, bf16[192,960]{1,0:T(8,128)(2,1)S(1)}, u32[]{:S(2)}, u32[]{:S(2)}) %collective-permute-start.29) | collective-permute-done | bytes 368672 | tf_op jit(solution)/shard_map/ppermute | solution.py:67
  193.3 6.4 %residual_back.1 = (f32[192,960]{1,0:T(8,128)}, bf16[192,960]{1,0:T(8,128)(2,1)}, bf16[192,960]{1,0:T(8,128)(2,1)}, f32[1,960]{1,0:T(1,128)}) custom-call(s32[4]{0:T(128)} %pad_add_fusion.1.spots, bf16[4,192,960]{2,1,0:T(8,128)(2,1)} %get-tuple-element.118.refs_0_, bf16[4,192,960]{2,1,0:T(8,128)(2,1)} %copy-done.5, bf16[192,960]{1,0:T(8,128)(2,1)} %copy-done.34, ...), custom_call_target="tpu_custom_call" | custom-call | flops 6899999744 | tf_op jit(solution)/shard_map/residual_back/pallas_call | solution.py:102
  199.8 12.8 %attention_back_far.1 = (f32[5,64,576]{2,1,0:T(8,128)}, bf16[4,192,640]{2,1,0:T(8,128)(2,1)}) custom-call(s32[4]{0:T(128)} %pad_add_fusion.1.spots, bf16[192,960]{1,0:T(8,128)(2,1)} %get-tuple-element.109.refs_0_, s32[768,1]{1,0:T(8,128)} %slice.125.refs_1_, s32[1,576]{1,0:T(1,128)} %broadcast_in_dim.29.refs_2_, ...), custom_call_target="tpu_custom_call" | custom-call | flops 14949999616 | tf_op jit(solution)/shard_map/attention_back_far/pallas_call | solution.py:102
  214.9 13.6 %attention_back_near.1 = (bf16[192,960]{1,0:T(8,128)(2,1)}, bf16[192,640]{1,0:T(8,128)(2,1)}, bf16[192,640]{1,0:T(8,128)(2,1)}, bf16[192,640]{1,0:T(8,128)(2,1)}, bf16[192,640]{1,0:T(8,128)(2,1)}) custom-call(s32[4]{0:T(128)} %pad_add_fusion.1.spots, bf16[192,960]{1,0:T(8,128)(2,1)} %get-tuple-element.109.refs_0_, s32[768,1]{1,0:T(8,128)} %slice.124.refs_1_, ...), custom_call_target="tpu_custom_call" | custom-call | flops 16099999744 | tf_op jit(solution)/shard_map/attention_back_near/pallas_call | solution.py:102
  228.5 5.0 %query_output_weight_grads.1 = (bf16[2,960,480]{2,1,0:T(8,128)(2,1)}, bf16[2,960,480]{2,1,0:T(8,128)(2,1)}) custom-call(s32[4]{0:T(128)} %pad_add_fusion.1.spots, bf16[192,960]{1,0:T(8,128)(2,1)} %get-tuple-element.142.refs_0_, bf16[192,960]{1,0:T(8,128)(2,1)} %get-tuple-element.134.refs_1_, bf16[192,960]{1,0:T(8,128)(2,1)} %get-tuple-element.143.refs_2_, ...), custom_call_target="tpu_custom_call" | custom-call | tf_op jit(solution)/shard_map/query_output_weight_grads/pallas_call | solution.py:102
  233.5 3.4 collective-permute-done.32.refs_12_
  243.1 4.1 %query_back.1.refs_6_ = f32[192,960]{1,0:T(8,128)} custom-call(s32[4]{0:T(128)} %pad_add_fusion.1.spots, bf16[192,960]{1,0:T(8,128)(2,1)} %get-tuple-element.156.refs_3_.low_ref, bf16[240,960]{1,0:T(8,128)(2,1)} %local_ref.1, bf16[720,480]{1,0:T(8,128)(2,1)} %stack_quarters.1.refs_6_.refs_9_.refs_10_.refs_0_, bf16[720,480]{1,0:T(8,128)(2,1)} %copy-done.8, ...), custom_call_target="tpu_custom_call" | custom-call | tf_op jit(solution)/shard_map/query_back/pallas_call | solution.py:102
  251.3 7.8 %collective-permute-done.36.refs_14_ = bf16[192,640]{1,0:T(8,128)(2,1)S(1)} collective-permute-done((bf16[192,640]{1,0:T(8,128)(2,1)S(1)}, bf16[192,640]{1,0:T(8,128)(2,1)S(1)}, u32[]{:S(2)}, u32[]{:S(2)}) %collective-permute-start.36) | collective-permute-done | bytes 245792 | tf_op jit(solution)/shard_map/ppermute | solution.py:58
  259.8 6.0 %keys_values_back.1 = (f32[192,960]{1,0:T(8,128)}, bf16[4,336,240]{2,1,0:T(8,128)(2,1)}, bf16[4,336,240]{2,1,0:T(8,128)(2,1)}) custom-call(s32[4]{0:T(128)} %pad_add_fusion.1.spots, f32[192,128]{1,0:T(8,128)} %pad_maximum_fusion.2.refs_5_.refs_3_.refs_0_, f32[192,128]{1,0:T(8,128)} %pad_maximum_fusion.3.refs_6_.refs_4_.refs_1_, ...), custom_call_target="tpu_custom_call" | custom-call | flops 6899999744 | tf_op jit(solution)/shard_map/keys_values_back/pallas_call | solution.py:102
  283.5 18.5 %collective-permute-done.40 = bf16[336,240]{1,0:T(8,128)(2,1)S(1)} collective-permute-done((bf16[336,240]{1,0:T(8,128)(2,1)S(1)}, bf16[336,240]{1,0:T(8,128)(2,1)S(1)}, u32[]{:S(2)}, u32[]{:S(2)}) %collective-permute-start.40) | collective-permute-done | bytes 161312 | tf_op jit(solution)/shard_map/ppermute | solution.py:58
  306.6 3.5 collective-permute-done.45
  316.7 15.1 %collective-permute-done.46 = bf16[336,240]{1,0:T(8,128)(2,1)S(1)} collective-permute-done((bf16[336,240]{1,0:T(8,128)(2,1)S(1)}, bf16[336,240]{1,0:T(8,128)(2,1)S(1)}, u32[]{:S(2)}, u32[]{:S(2)}) %collective-permute-start.46) | collective-permute-done | bytes 161312 | tf_op jit(solution)/shard_map/ppermute | solution.py:67
  334.8 4.2 %collective-permute-start.49 = (bf16[1,240,480]{2,1,0:T(8,128)(2,1)S(1)}, bf16[1,240,480]{2,1,0:T(8,128)(2,1)S(1)}, u32[]{:S(2)}, u32[]{:S(2)}) collective-permute-start(bf16[1,240,480]{2,1,0:T(8,128)(2,1)S(1)} %fusion.14), channel_id=1, source_target_pairs={{0,1},{1,0},{2,3},{3,2},{4,5},{5,4},{6,7},{7,6},{8,9},{9,8},{10,11... | collective-permute-start | bytes 691208 | tf_op jit(solution)/shard_map/ppermute | solution.py:58
  340.2 4.9 %collective-permute-done.49 = bf16[1,240,480]{2,1,0:T(8,128)(2,1)S(1)} collective-permute-done((bf16[1,240,480]{2,1,0:T(8,128)(2,1)S(1)}, bf16[1,240,480]{2,1,0:T(8,128)(2,1)S(1)}, u32[]{:S(2)}, u32[]{:S(2)}) %collective-permute-start.49) | collective-permute-done | bytes 230432 | tf_op jit(solution)/shard_map/ppermute | solution.py:58
  347.7 6.1 %collective-permute-done.50 = bf16[240,480]{1,0:T(8,128)(2,1)S(1)} collective-permute-done((bf16[240,480]{1,0:T(8,128)(2,1)S(1)}, bf16[240,480]{1,0:T(8,128)(2,1)S(1)}, u32[]{:S(2)}, u32[]{:S(2)}) %collective-permute-start.50) | collective-permute-done | bytes 230432 | tf_op jit(solution)/shard_map/ppermute | solution.py:67
  355.3 5.1 %collective-permute-done.51.across_ref = bf16[240,480]{1,0:T(8,128)(2,1)S(1)} collective-permute-done((bf16[240,480]{1,0:T(8,128)(2,1)S(1)}, bf16[240,480]{1,0:T(8,128)(2,1)S(1)}, u32[]{:S(2)}, u32[]{:S(2)}) %collective-permute-start.51) | collective-permute-done | bytes 230432 | tf_op jit(solution)/shard_map/ppermute | solution.py:67
  362.2 6.7 %feed_forward_out.1 = (f32[240,2560]{1,0:T(8,128)}, f32[240,2560]{1,0:T(8,128)}, f32[960,640]{1,0:T(8,128)}) custom-call(s32[4]{0:T(128)} %pad_add_fusion.1.spots, bf16[240,960]{1,0:T(8,128)(2,1)} %reduce-scatter.2.cloned.1.call-done.refs_0_, bf16[240,960]{1,0:T(8,128)(2,1)} %copy-done.20, bf16[240,960]{1,0:T(8,128)(2,1)} %copy-done.22, ...), custom_call_target="tpu_custom_call" | custom-call | flops 8049999872 | tf_op jit(solution)/shard_map/feed_forward_out/pallas_call | solution.py:102
  (268 shorter events, 106.4 us)
Async XLA Ops:
  7.2 86.1 %all-gather.3.cloned.1.call-start = ((), (), s32[]{:S(2)}) async-start(), calls=%async_computation.1 | async-start | bytes 3538944 | tf_op jit(solution)/shard_map/all_gather | solution.py:683
  7.9 143.2 %all-gather.5.cloned.1.call-start = ((), (), s32[]{:S(2)}) async-start(), calls=%async_computation.2 | async-start | bytes 2457600 | tf_op jit(solution)/shard_map/all_gather | solution.py:730
  18.6 24.8 %collective-permute-start.6 = (bf16[240,480]{1,0:T(8,128)(2,1)}, bf16[240,480]{1,0:T(8,128)(2,1)S(1)}, u32[]{:S(2)}, u32[]{:S(2)}) collective-permute-start(bf16[240,480]{1,0:T(8,128)(2,1)} %quarter_columns.1), channel_id=1, source_target_pairs={{0,1},{1,0},{2,3},{3,2},{4,5},{5,4},{6,7},{7,6},{8,9},{9,8},{10,11... | collective-permute-start | bytes 691208 | tf_op jit(solution)/shard_map/ppermute | solution.py:58
  19.1 28.9 %collective-permute-start.7 = (bf16[240,480]{1,0:T(8,128)(2,1)}, bf16[240,480]{1,0:T(8,128)(2,1)S(1)}, u32[]{:S(2)}, u32[]{:S(2)}) collective-permute-start(bf16[240,480]{1,0:T(8,128)(2,1)} %quarter_columns.1), channel_id=1, source_target_pairs={{0,2},{1,3},{2,0},{3,1},{4,6},{5,7},{6,4},{7,5},{8,10},{9,11},{10,... | collective-permute-start | bytes 691208 | tf_op jit(solution)/shard_map/ppermute | solution.py:58
  24.7 17.2 %collective-permute-start.2 = (bf16[336,240]{1,0:T(8,128)(2,1)S(1)}, bf16[336,240]{1,0:T(8,128)(2,1)S(1)}, u32[]{:S(2)}, u32[]{:S(2)}) collective-permute-start(bf16[336,240]{1,0:T(8,128)(2,1)S(1)} %collective-permute-done.refs_7_.refs_16_), channel_id=1, source_target_pairs={{0,2},{1,3},{2,0},{3,1},{4,6},{5,7},{6,4},{7,5},{8,10},{9,11},{10,... | collective-permute-start | bytes 483848 | tf_op jit(solution)/shard_map/ppermute | solution.py:58
  60.6 26.2 %collective-permute-start.10 = (bf16[720,480]{1,0:T(8,128)(2,1)}, bf16[720,480]{1,0:T(8,128)(2,1)S(1)}, u32[]{:S(2)}, u32[]{:S(2)}) collective-permute-start(bf16[720,480]{1,0:T(8,128)(2,1)} %stack_quarters.1.refs_6_.refs_9_.refs_10_.refs_0_), channel_id=1, source_target_pairs={{0,16},{4,20},{8,24},{12,28},{16,0},{20,4},{24,8},{28,12},{1,17},{... | collective-permute-start | bytes 2073608 | tf_op jit(solution)/shard_map/ppermute | solution.py:67
  62.2 19.4 %collective-permute-start.12 = (bf16[192,640]{1,0:T(8,128)(2,1)}, bf16[192,640]{1,0:T(8,128)(2,1)S(1)}, u32[]{:S(2)}, u32[]{:S(2)}) collective-permute-start(bf16[192,640]{1,0:T(8,128)(2,1)} %get-tuple-element.105.refs_10_.refs_9_), channel_id=1, source_target_pairs={{0,2},{1,3},{2,0},{3,1},{4,6},{5,7},{6,4},{7,5},{8,10},{9,11},{10,... | collective-permute-start | bytes 737288 | tf_op jit(solution)/shard_map/ppermute | solution.py:58
  74.5 19.3 %collective-permute-start.9 = (bf16[720,480]{1,0:T(8,128)(2,1)}, bf16[720,480]{1,0:T(8,128)(2,1)S(1)}, u32[]{:S(2)}, u32[]{:S(2)}) collective-permute-start(bf16[720,480]{1,0:T(8,128)(2,1)} %stack_quarters.1.refs_6_.refs_9_.refs_10_.refs_0_), channel_id=1, source_target_pairs={{0,8},{4,12},{8,0},{12,4},{16,24},{20,28},{24,16},{28,20},{1,9},{5... | collective-permute-start | bytes 2073608 | tf_op jit(solution)/shard_map/ppermute | solution.py:67
  89.7 17.5 %collective-permute-start.15 = (bf16[192,640]{1,0:T(8,128)(2,1)S(1)}, bf16[192,640]{1,0:T(8,128)(2,1)S(1)}, u32[]{:S(2)}, u32[]{:S(2)}) collective-permute-start(bf16[192,640]{1,0:T(8,128)(2,1)S(1)} %copy-done.37), channel_id=1, source_target_pairs={{0,4},{4,0},{1,5},{5,1},{2,6},{6,2},{3,7},{7,3},{8,12},{12,8},{9,1... | collective-permute-start | bytes 737288 | tf_op jit(solution)/shard_map/ppermute | solution.py:58
  91.8 22.1 %collective-permute-start.18 = (bf16[192,640]{1,0:T(8,128)(2,1)S(1)}, bf16[192,640]{1,0:T(8,128)(2,1)}, u32[]{:S(2)}, u32[]{:S(2)}) collective-permute-start(bf16[192,640]{1,0:T(8,128)(2,1)S(1)} %collective-permute-done.13.refs_13_.refs_12_), channel_id=1, source_target_pairs={{0,4},{4,0},{1,5},{5,1},{2,6},{6,2},{3,7},{7,3},{8,12},{12,8},{9,1... | collective-permute-start | bytes 737288 | tf_op jit(solution)/shard_map/ppermute | solution.py:58
  93.3 143.7 %reduce-scatter.2.cloned.1.call-start = ((), (), s32[]{:S(2)}) async-start(), calls=%async_computation.3 | async-start | bytes 2457600 | tf_op jit(solution)/shard_map/reduce_scatter | solution.py:802
  93.9 20.0 %collective-permute-start.17 = (bf16[192,640]{1,0:T(8,128)(2,1)S(1)}, bf16[192,640]{1,0:T(8,128)(2,1)S(1)}, u32[]{:S(2)}, u32[]{:S(2)}) collective-permute-start(bf16[192,640]{1,0:T(8,128)(2,1)S(1)} %collective-permute-done.12.refs_12_.refs_11_), channel_id=1, source_target_pairs={{0,4},{4,0},{1,5},{5,1},{2,6},{6,2},{3,7},{7,3},{8,12},{12,8},{9,1... | collective-permute-start | bytes 737288 | tf_op jit(solution)/shard_map/ppermute | solution.py:58
  130.9 18.6 %collective-permute-start.21 = (bf16[192,960]{1,0:T(8,128)(2,1)}, bf16[192,960]{1,0:T(8,128)(2,1)S(1)}, u32[]{:S(2)}, u32[]{:S(2)}) collective-permute-start(bf16[192,960]{1,0:T(8,128)(2,1)} %get-tuple-element.117.refs_2_.refs_6_), channel_id=1, source_target_pairs={{0,20},{4,16},{8,28},{12,24},{16,4},{20,0},{24,12},{28,8},{1,21},{... | collective-permute-start | bytes 1105928 | tf_op jit(solution)/shard_map/ppermute | solution.py:67
  132.3 17.1 %collective-permute-start.22 = (bf16[192,960]{1,0:T(8,128)(2,1)}, bf16[192,960]{1,0:T(8,128)(2,1)S(1)}, u32[]{:S(2)}, u32[]{:S(2)}) collective-permute-start(bf16[192,960]{1,0:T(8,128)(2,1)} %get-tuple-element.117.refs_2_.refs_6_), channel_id=1, source_target_pairs={{0,8},{4,12},{8,0},{12,4},{16,24},{20,28},{24,16},{28,20},{1,9},{5... | collective-permute-start | bytes 1105928 | tf_op jit(solution)/shard_map/ppermute | solution.py:67
  173.6 18.9 %collective-permute-start.29 = (bf16[192,960]{1,0:T(8,128)(2,1)S(1)}, bf16[192,960]{1,0:T(8,128)(2,1)S(1)}, u32[]{:S(2)}, u32[]{:S(2)}) collective-permute-start(bf16[192,960]{1,0:T(8,128)(2,1)S(1)} %get-tuple-element.183), channel_id=1, source_target_pairs={{0,20},{4,16},{8,28},{12,24},{16,4},{20,0},{24,12},{28,8},{1,21},{... | collective-permute-start | bytes 1105928 | tf_op jit(solution)/shard_map/ppermute | solution.py:67
  212.5 24.4 %collective-permute-start.32 = (bf16[4,192,640]{2,1,0:T(8,128)(2,1)}, bf16[4,192,640]{2,1,0:T(8,128)(2,1)}, u32[]{:S(2)}, u32[]{:S(2)}) collective-permute-start(bf16[4,192,640]{2,1,0:T(8,128)(2,1)} %get-tuple-element.146), channel_id=1, source_target_pairs={{0,4},{4,0},{1,5},{5,1},{2,6},{6,2},{3,7},{7,3},{8,12},{12,8},{9,1... | collective-permute-start | bytes 2949128 | tf_op jit(solution)/shard_map/ppermute | solution.py:58
  214.4 22.6 %collective-permute-start.31 = (bf16[2,192,960]{2,1,0:T(8,128)(2,1)S(1)}, bf16[2,192,960]{2,1,0:T(8,128)(2,1)}, u32[]{:S(2)}, u32[]{:S(2)}) collective-permute-start(bf16[2,192,960]{2,1,0:T(8,128)(2,1)S(1)} %add_convert_fusion.1), channel_id=1, source_target_pairs={{0,16},{4,20},{8,24},{12,28},{16,0},{20,4},{24,8},{28,12},{1,17},{... | collective-permute-start | bytes 2211848 | tf_op jit(solution)/shard_map/ppermute | solution.py:67
  238.7 20.3 %collective-permute-start.36 = (bf16[192,640]{1,0:T(8,128)(2,1)S(1)}, bf16[192,640]{1,0:T(8,128)(2,1)S(1)}, u32[]{:S(2)}, u32[]{:S(2)}) collective-permute-start(bf16[192,640]{1,0:T(8,128)(2,1)S(1)} %get-tuple-element.193), channel_id=1, source_target_pairs={{0,2},{1,3},{2,0},{3,1},{4,6},{5,7},{6,4},{7,5},{8,10},{9,11},{10,... | collective-permute-start | bytes 737288 | tf_op jit(solution)/shard_map/ppermute | solution.py:58
  240.9 18.1 %collective-permute-start.37 = (bf16[192,640]{1,0:T(8,128)(2,1)S(1)}, bf16[192,640]{1,0:T(8,128)(2,1)S(1)}, u32[]{:S(2)}, u32[]{:S(2)}) collective-permute-start(bf16[192,640]{1,0:T(8,128)(2,1)S(1)} %get-tuple-element.192), channel_id=1, source_target_pairs={{0,3},{1,2},{2,1},{3,0},{4,7},{5,6},{6,5},{7,4},{8,11},{9,10},{10,... | collective-permute-start | bytes 737288 | tf_op jit(solution)/shard_map/ppermute | solution.py:58
  248.7 24.5 %collective-permute-start.34 = (bf16[960,480]{1,0:T(8,128)(2,1)}, bf16[960,480]{1,0:T(8,128)(2,1)}, u32[]{:S(2)}, u32[]{:S(2)}) collective-permute-start(bf16[960,480]{1,0:T(8,128)(2,1)} %fusion), channel_id=1, source_target_pairs={{0,16},{4,20},{8,24},{12,28},{16,0},{20,4},{24,8},{28,12},{1,17},{... | collective-permute-start | bytes 2764808 | tf_op jit(solution)/shard_map/ppermute | solution.py:67
  268.2 34.7 %collective-permute-start.42 = (bf16[240,960]{1,0:T(8,128)(2,1)S(1)}, bf16[240,960]{1,0:T(8,128)(2,1)S(1)}, u32[]{:S(2)}, u32[]{:S(2)}) collective-permute-start(bf16[240,960]{1,0:T(8,128)(2,1)S(1)} %copy-done.18), channel_id=1, source_target_pairs={{0,16},{4,20},{8,24},{12,28},{16,0},{20,4},{24,8},{28,12},{1,17},{... | collective-permute-start | bytes 1382408 | tf_op jit(solution)/shard_map/ppermute | solution.py:67
  268.8 34.1 %collective-permute-start.43 = (bf16[240,960]{1,0:T(8,128)(2,1)S(1)}, bf16[240,960]{1,0:T(8,128)(2,1)S(1)}, u32[]{:S(2)}, u32[]{:S(2)}) collective-permute-start(bf16[240,960]{1,0:T(8,128)(2,1)S(1)} %copy-done.18), channel_id=1, source_target_pairs={{0,4},{4,0},{8,12},{12,8},{16,20},{20,16},{24,28},{28,24},{1,5},{5... | collective-permute-start | bytes 1382408 | tf_op jit(solution)/shard_map/ppermute | solution.py:67
  276.0 26.1 %collective-permute-start.40 = (bf16[336,240]{1,0:T(8,128)(2,1)S(1)}, bf16[336,240]{1,0:T(8,128)(2,1)S(1)}, u32[]{:S(2)}, u32[]{:S(2)}) collective-permute-start(bf16[336,240]{1,0:T(8,128)(2,1)S(1)} %get-tuple-element.165), channel_id=1, source_target_pairs={{0,2},{1,3},{2,0},{3,1},{4,6},{5,7},{6,4},{7,5},{8,10},{9,11},{10,... | collective-permute-start | bytes 483848 | tf_op jit(solution)/shard_map/ppermute | solution.py:58
  276.4 25.7 %collective-permute-start.41 = (bf16[336,240]{1,0:T(8,128)(2,1)S(1)}, bf16[336,240]{1,0:T(8,128)(2,1)S(1)}, u32[]{:S(2)}, u32[]{:S(2)}) collective-permute-start(bf16[336,240]{1,0:T(8,128)(2,1)S(1)} %get-tuple-element.166), channel_id=1, source_target_pairs={{0,3},{1,2},{2,1},{3,0},{4,7},{5,6},{6,5},{7,4},{8,11},{9,10},{10,... | collective-permute-start | bytes 483848 | tf_op jit(solution)/shard_map/ppermute | solution.py:58
  282.9 32.1 %collective-permute-start.48 = (bf16[2,240,480]{2,1,0:T(8,128)(2,1)}, bf16[2,240,480]{2,1,0:T(8,128)(2,1)}, u32[]{:S(2)}, u32[]{:S(2)}) collective-permute-start(bf16[2,240,480]{2,1,0:T(8,128)(2,1)} %pad_maximum_fusion), channel_id=1, source_target_pairs={{0,2},{1,3},{2,0},{3,1},{4,6},{5,7},{6,4},{7,5},{8,10},{9,11},{10,... | collective-permute-start | bytes 1382408 | tf_op jit(solution)/shard_map/ppermute | solution.py:58
  305.9 49.4 %collective-permute-start.54 = (bf16[240,960]{1,0:T(8,128)(2,1)}, bf16[240,960]{1,0:T(8,128)(2,1)S(1)}, u32[]{:S(2)}, u32[]{:S(2)}) collective-permute-start(bf16[240,960]{1,0:T(8,128)(2,1)} %reduce-scatter.2.cloned.1.call-done.refs_0_), channel_id=1, source_target_pairs={{0,8},{4,12},{8,0},{12,4},{16,24},{20,28},{24,16},{28,20},{1,9},{5... | collective-permute-start | bytes 1382408 | tf_op jit(solution)/shard_map/ppermute | solution.py:67
  305.9 28.9 %collective-permute-start.56 = (bf16[240,960]{1,0:T(8,128)(2,1)}, bf16[240,960]{1,0:T(8,128)(2,1)S(1)}, u32[]{:S(2)}, u32[]{:S(2)}) collective-permute-start(bf16[240,960]{1,0:T(8,128)(2,1)} %copy-done.19), channel_id=1, source_target_pairs={{0,4},{4,0},{8,12},{12,8},{16,20},{20,16},{24,28},{28,24},{1,5},{5... | collective-permute-start | bytes 1382408 | tf_op jit(solution)/shard_map/ppermute | solution.py:67
  306.4 54.0 %collective-permute-start.57 = (bf16[240,960]{1,0:T(8,128)(2,1)}, bf16[240,960]{1,0:T(8,128)(2,1)S(1)}, u32[]{:S(2)}, u32[]{:S(2)}) collective-permute-start(bf16[240,960]{1,0:T(8,128)(2,1)} %copy-done.19), channel_id=1, source_target_pairs={{0,8},{4,12},{8,0},{12,4},{16,24},{20,28},{24,16},{28,20},{1,9},{5... | collective-permute-start | bytes 1382408 | tf_op jit(solution)/shard_map/ppermute | solution.py:67
  310.1 21.8 %collective-permute-start.44 = (bf16[192,960]{1,0:T(8,128)(2,1)}, bf16[192,960]{1,0:T(8,128)(2,1)S(1)}, u32[]{:S(2)}, u32[]{:S(2)}) collective-permute-start(bf16[192,960]{1,0:T(8,128)(2,1)} %fusion.11), channel_id=1, source_target_pairs={{0,4},{4,0},{8,12},{12,8},{16,20},{20,16},{24,28},{28,24},{1,5},{5... | collective-permute-start | bytes 1105928 | tf_op jit(solution)/shard_map/ppermute | solution.py:67
  315.0 16.8 %collective-permute-start.46 = (bf16[336,240]{1,0:T(8,128)(2,1)S(1)}, bf16[336,240]{1,0:T(8,128)(2,1)S(1)}, u32[]{:S(2)}, u32[]{:S(2)}) collective-permute-start(bf16[336,240]{1,0:T(8,128)(2,1)S(1)} %add_convert_fusion.12), channel_id=1, source_target_pairs={{0,4},{4,0},{8,12},{12,8},{16,20},{20,16},{24,28},{28,24},{1,5},{5... | collective-permute-start | bytes 483848 | tf_op jit(solution)/shard_map/ppermute | solution.py:67
  331.8 28.5 %collective-permute-start.55 = (bf16[240,960]{1,0:T(8,128)(2,1)S(1)}, bf16[240,960]{1,0:T(8,128)(2,1)S(1)}, u32[]{:S(2)}, u32[]{:S(2)}) collective-permute-start(bf16[240,960]{1,0:T(8,128)(2,1)S(1)} %copy-done.21), channel_id=1, source_target_pairs={{0,8},{4,12},{8,0},{12,4},{16,24},{20,28},{24,16},{28,20},{1,9},{5... | collective-permute-start | bytes 1382408 | tf_op jit(solution)/shard_map/ppermute | solution.py:67
  339.0 21.4 %collective-permute-start.58 = (bf16[240,960]{1,0:T(8,128)(2,1)S(1)}, bf16[240,960]{1,0:T(8,128)(2,1)S(1)}, u32[]{:S(2)}, u32[]{:S(2)}) collective-permute-start(bf16[240,960]{1,0:T(8,128)(2,1)S(1)} %collective-permute-done.56.refs_5_), channel_id=1, source_target_pairs={{0,8},{4,12},{8,0},{12,4},{16,24},{20,28},{24,16},{28,20},{1,9},{5... | collective-permute-start | bytes 1382408 | tf_op jit(solution)/shard_map/ppermute | solution.py:67
  (86 other events, 758.9 us)
Sparse Core Ops, SparseCore 0:
  9.9 35.0 all-gather.2
  93.4 40.9 all-gather.4
  187.6 39.5 reduce-scatter.1

commit v6 on v5

--- a/solution.py
+++ b/solution.py
@@ -73,6 +73,10 @@
         top = 1 << (r.bit_length() - 1)
         pieces[r] = swap(pieces[r - top], "fsdp", top)
     return [pieces[r] for r in range(1, lax.axis_size("fsdp"))]
+
+
+def direct_fsdp(x):
+    return [swap(x, "fsdp", r) for r in range(1, lax.axis_size("fsdp"))]
 
 
 def swap_core(x):
@@ -662,8 +666,7 @@
         ],
         axis=0,
     )
-    kv_mine = swaps_fsdp(kv_pack)
-    kv_other = [swap_core(piece) for piece in kv_mine]
+    kv_mine = direct_fsdp(kv_pack)
 
     quarter = width // dp_count
     (quarters,) = call(
@@ -672,6 +675,8 @@
         [((weight_rows, 2 * quarter), BF16)], name="quarter_columns",
     )
     quarter_pieces = swaps_fsdp(quarters)
+    quarter_pieces[0], *kv_mine = lax.optimization_barrier((quarter_pieces[0], *kv_mine))
+    kv_other = [swap_core(piece) for piece in kv_mine]
 
     group_axes = ("dp", "ctx")
     extra = {}
@@ -703,7 +708,7 @@
     kv_own, normed_one, normed_turned, inverse_one, gains = call(
         functools.partial(begin_kernel, shards), spots,
         [
-            lax.optimization_barrier((tokens, quarters, pack))[0], gain_one, gain_two, key_turned, value_turned, cosine, sine,
+            lax.optimization_barrier((tokens, quarter_pieces[1], pack))[0], gain_one, gain_two, key_turned, value_turned, cosine, sine,
             *kv_mine, *kv_other,
         ],
         [
@@ -716,8 +721,8 @@
         ],
         name="norm_keys_values",
     )
-    near = [kv_own] + swaps_fsdp(kv_own)
-    quarter_pieces = lax.optimization_barrier((kv_own, *quarter_pieces))[1:]
+    near = [kv_own] + direct_fsdp(kv_own)
+    near[1], *quarter_pieces = lax.optimization_barrier((near[1], *quarter_pieces))
     (stacked,) = call(
         stack_kernel, spots, quarter_pieces,
         [(((shards - 1) * weight_rows, 2 * quarter), BF16)], name="stack_quarters",
@@ -728,6 +733,8 @@
 
     pack, cot_all, _ = lax.optimization_barrier((pack, cot_all, near[-1]))
     pack_all = lax.all_gather(pack, "fsdp", axis=0, tiled=True)
+
+    normed_turned, far[0], far[1] = lax.optimization_barrier((normed_turned, far[0], far[1]))
 
     chunk = rows * 2
     unit = 2 * HEADS * rows * near_count * HEAD_DIM
@@ -894,15 +901,21 @@
     query_partial, result_sent = lax.optimization_barrier((query_partial, result_sent))
     result_across = swap_plane(result_sent, 2, 0)
     query_low, near_grads = back(False, True, query_partial, near_pos, near)
+    query_low, result_across = lax.optimization_barrier((query_low, result_across))
+    result_own, result_along = [
+        (result_a[k].astype(F32) + result_core[k].astype(F32)) + result_across[k].astype(F32)
+        for k in (0, 1)
+    ]
+    result_along = swap_plane(result_along.astype(BF16), 0, 1)
     pair_shape = ((2, width, 2 * quarter), BF16)
     weights_keep, weights_send = call(
         functools.partial(weight_grads_kernel, dp_count), spots,
         [attended, residual_low, normed_one, query_low], [pair_shape, pair_shape],
         scratch=[((2 * dp_count, rows, quarter), BF16)], name="query_output_weight_grads",
     )
-    weights_send, pack_share, result_across, far_grads[-1] = lax.optimization_barrier(
-        (weights_send, pack_share, result_across, far_grads[-1])
-    )
+    pack_share, query_low = lax.optimization_barrier((pack_share, query_low))
+    share_across = swap_plane(pack_share, 2, 0)
+    weights_send, far_grads[-1] = lax.optimization_barrier((weights_send, far_grads[-1]))
 
     def home(r):
         return sum(grads[r].astype(F32) for grads in far_grads)
@@ -911,25 +924,21 @@
         r: (near_grads[r].astype(F32) + home(r)).astype(BF16) for r in range(1, shards)
     }
     kv_arrived = {r: swap(kv_sums[r], "fsdp", r) for r in reversed(range(1, shards))}
-    query_low, result_across, *_ = lax.optimization_barrier(
-        (query_low, result_across, *kv_sums.values())
-    )
-    result_own, result_along = [
-        (result_a[k].astype(F32) + result_core[k].astype(F32)) + result_across[k].astype(F32)
-        for k in (0, 1)
-    ]
-    result_along = result_along.astype(BF16)
+    query_low, *_ = lax.optimization_barrier((query_low, *kv_sums.values()))
 
     weights_away = swap_core(weights_send)
-    query_turn = query_low
+    weights_sent, weights_terms = sum_x(weights_keep, weights_away)
+    query_turn = after(query_low, weights_sent)
     (query_back,) = call(
         functools.partial(query_back_kernel, shards, dp_count), spots,
         [query_turn, query_weight, *stacks], [((rows, width), F32)],
         scratch=[((dp_count, rows, quarter), BF16), ((shards, rows, weight_rows), F32)],
         name="query_back",
     )
-    weights_sent, weights_terms = sum_x(weights_keep, weights_away)
-    query_back, weights_sent = lax.optimization_barrier((query_back, weights_sent))
+    query_back, share_across = lax.optimization_barrier((query_back, share_across))
+    share_a = [
+        pack_share, swap_plane(pack_share, 0, 1), share_across, swap_plane(share_across, 0, 1)
+    ]
     span = kv_width + EXTRA_ROWS
     packed_shape = ((shards, span, weight_rows), BF16)
     home_all = far_grads[0]
@@ -946,21 +955,17 @@
         scratch=[((shards, rows, weight_rows), F32)],
         name="keys_values_back",
     )
-    pack_share = after(pack_share, kv_send)
-    share_across = swap_plane(pack_share, 2, 0)
-    share_along = swap_plane(pack_share, 0, 1)
     kv_away = swap_core(kv_send)
     pieces = [
         (lax.dynamic_index_in_dim(kv_keep, shard ^ r, 0, keepdims=False).astype(F32)
          + lax.dynamic_index_in_dim(kv_away, shard ^ r, 0, keepdims=False).astype(F32)).astype(BF16)
         for r in range(shards)
     ]
-    weights_terms, *pieces = lax.optimization_barrier((weights_terms, *pieces))
+    weights_terms, result_along, *pieces = lax.optimization_barrier(
+        (weights_terms, result_along, *pieces)
+    )
     kv_share = sum_z(pieces)
-    kv_share, share_across, share_along = lax.optimization_barrier(
-        (kv_share, share_across, share_along)
-    )
-    share_a = [pack_share, share_along, share_across, swap_plane(share_across, 0, 1)]
+    kv_share, *share_a = lax.optimization_barrier((kv_share, *share_a))
     share_b = [swap_core(piece) for piece in share_a]
 
     share_by_mask = [None] * members
@@ -976,9 +981,8 @@
         scratch=[((members, weight_rows, 3 * part), BF16)],
         name="feed_forward_out",
     )
-    kv_share, result_along = lax.optimization_barrier((kv_share, result_along))
     weights_own = sum_y(relay_z(weights_terms))
-    result = residual + (result_own + swap_plane(result_along, 0, 1).astype(F32))
+    result = residual + (result_own + result_along.astype(F32))
     output_weight_grad, query_weight_grad = finish_quarters(weights_own)
     low = sum_chips(kv_share)
     away = swap_core(low)

time: 385 us -> 379 us (0.984)
  starting transfers between devices: 50.2 us -> 63.7 us
  waiting for transfers between devices: 151 us -> 140 us
  other arithmetic: 21.4 us -> 13.7 us
    ppermute x22, waiting for transfers between devices: 94.1 us -> 79.5 us  [swap(): return lax.ppermute(x, axis, [(i, i ^ mask) for i in range(count)])]
    ppermute x22, starting transfers between devices: 31.8 us -> 42.2 us  [swap(): return lax.ppermute(x, axis, [(i, i ^ mask) for i in range(count)])]
    reduce_scatter x1, waiting for transfers between devices: 0.01 us -> 4.6 us  [on_device(): lax.psum_scatter(pack_grad, 'fsdp', scatter_dimension=0, tiled=True)]
    unnamed x112 -> x110, local copies, waits for them, and re-layouts: 10.1 us -> 8.25 us
  transfers between devices with their start and end apart: 62 -> 62, of which waited for: 23 -> 25; matrix products, arithmetic and copies ran while one was open for 7% -> 5% of each run, Pallas kernels for 30% -> 29%
where the time goes in v6:
time: 379 us; the launch traced here: 374 us
  waiting for transfers between devices  140 us (37%)
  Pallas kernels  125 us (33%)
  starting transfers between devices  63.7 us (17%)
  local copies, waits for them, and re-layouts  16.3 us (4%)
  between operations  15.4 us (4%)
  other arithmetic  13.7 us (4%)
    pallas_call x17, Pallas kernels, call(): pl.pallas_call(kernel, out_shape=outs, in_specs=specs, out_specs=tuple((p...  125 us
    ppermute x22, waiting for transfers between devices, swap(): return lax.ppermute(x, axis, [(i, i ^ mask) for i in range(count)])  79.5 us
    ppermute x37, waiting for transfers between devices, swap_plane(): return lax.ppermute(x, ('dp', 'ctx'), pairs)  55 us
    ppermute x22, starting transfers between devices, swap(): return lax.ppermute(x, axis, [(i, i ^ mask) for i in range(count)])  42.2 us
    ppermute x37, starting transfers between devices, swap_plane(): return lax.ppermute(x, ('dp', 'ctx'), pairs)  21 us
    unnamed x110, local copies, waits for them, and re-layouts  8.25 us
  transfers between devices with their start and end apart: 62, of which 25 were waited for; matrix products, arithmetic and copies ran while one was open for 5% of the time, Pallas kernels for 29%

profile of v6, /device:TPU:0, one launch (start us, length us, event | category | flops | bytes accessed | tf_op | source)
XLA Modules:
  0.0 373.8 jit_solution(11823681602664493823)
XLA Ops:
  13.0 4.0 %collective-permute-start = (bf16[240,480]{1,0:T(8,128)(2,1)}, bf16[240,480]{1,0:T(8,128)(2,1)S(1)}, u32[]{:S(2)}, u32[]{:S(2)}) collective-permute-start(bf16[240,480]{1,0:T(8,128)(2,1)} %quarter_columns.1), channel_id=1, source_target_pairs={{0,2},{1,3},{2,0},{3,1},{4,6},{5,7},{6,4},{7,5},{8,10},{9,11},{10,... | collective-permute-start | bytes 691208 | tf_op jit(solution)/shard_map/ppermute | solution.py:58
  19.1 3.9 %collective-permute-start.4 = (bf16[336,240]{1,0:T(8,128)(2,1)S(1)}, bf16[336,240]{1,0:T(8,128)(2,1)S(1)}, u32[]{:S(2)}, u32[]{:S(2)}) collective-permute-start(bf16[336,240]{1,0:T(8,128)(2,1)S(1)} %pad_maximum_fusion.1), channel_id=1, source_target_pairs={{0,3},{1,2},{2,1},{3,0},{4,7},{5,6},{6,5},{7,4},{8,11},{9,10},{10,... | collective-permute-start | bytes 483848 | tf_op jit(solution)/shard_map/ppermute | solution.py:58
  24.3 4.1 %pack_weights.1 = bf16[240,960]{1,0:T(8,128)(2,1)} custom-call(s32[4]{0:T(128)} %pad_add_fusion.1.spots, bf16[240,2560]{1,0:T(8,128)(2,1)} %gate_ref.1, bf16[240,2560]{1,0:T(8,128)(2,1)} %up_ref.1, bf16[960,640]{1,0:T(8,128)(2,1)} %bitcast.96), custom_call_target="tpu_custom_call" | custom-call | flops 4600000000 | tf_op jit(solution)/shard_map/pack_weights/pallas_call | solution.py:106
  28.9 7.4 %collective-permute-done.2.refs_7_.refs_16_ = bf16[336,240]{1,0:T(8,128)(2,1)S(1)} collective-permute-done((bf16[336,240]{1,0:T(8,128)(2,1)S(1)}, bf16[336,240]{1,0:T(8,128)(2,1)S(1)}, u32[]{:S(2)}, u32[]{:S(2)}) %collective-permute-start.2) | collective-permute-done | bytes 161312 | tf_op jit(solution)/shard_map/ppermute | solution.py:58
  36.4 4.4 %collective-permute-done.4.refs_9_.refs_18_ = bf16[336,240]{1,0:T(8,128)(2,1)S(1)} collective-permute-done((bf16[336,240]{1,0:T(8,128)(2,1)S(1)}, bf16[336,240]{1,0:T(8,128)(2,1)S(1)}, u32[]{:S(2)}, u32[]{:S(2)}) %collective-permute-start.4) | collective-permute-done | bytes 161312 | tf_op jit(solution)/shard_map/ppermute | solution.py:58
  52.9 9.2 %collective-permute-done.9.refs_2_ = bf16[240,480]{1,0:T(8,128)(2,1)S(1)} collective-permute-done((bf16[240,480]{1,0:T(8,128)(2,1)S(1)}, bf16[240,480]{1,0:T(8,128)(2,1)S(1)}, u32[]{:S(2)}, u32[]{:S(2)}) %collective-permute-start.9) | collective-permute-done | bytes 230432 | tf_op jit(solution)/shard_map/ppermute | solution.py:58
  73.5 14.1 %collective-permute-done.11.refs_12_.refs_11_ = bf16[192,640]{1,0:T(8,128)(2,1)S(1)} collective-permute-done((bf16[192,640]{1,0:T(8,128)(2,1)}, bf16[192,640]{1,0:T(8,128)(2,1)S(1)}, u32[]{:S(2)}, u32[]{:S(2)}) %collective-permute-start.11) | collective-permute-done | bytes 245792 | tf_op jit(solution)/shard_map/ppermute | solution.py:58
  98.3 3.8 %collective-permute-done.14.refs_14_.refs_10_ = bf16[192,640]{1,0:T(8,128)(2,1)} collective-permute-done((bf16[192,640]{1,0:T(8,128)(2,1)S(1)}, bf16[192,640]{1,0:T(8,128)(2,1)}, u32[]{:S(2)}, u32[]{:S(2)}) %collective-permute-start.14) | collective-permute-done | bytes 245792 | tf_op jit(solution)/shard_map/ppermute | solution.py:58
  104.5 11.8 %attention_near.1 = (bf16[192,960]{1,0:T(8,128)(2,1)}, f32[5,576]{1,0:T(8,128)}, f32[5,576]{1,0:T(8,128)}, f32[5,64,576]{2,1,0:T(8,128)}) custom-call(s32[4]{0:T(128)} %pad_add_fusion.1.spots, bf16[192,960]{1,0:T(8,128)(2,1)} %get-tuple-element.122.refs_0_, s32[768,1]{1,0:T(8,128)} %slice.124.refs_1_, s32[1,576]{1,0:T(1,128)} %broadcast_in_dim.29.refs_2_, ...), custom_call_target="tpu_custom_call" | custom-call | flops 13799999488 | tf_op jit(solution)/shard_map/attention_near/pallas_call | solution.py:106
  116.3 14.2 %attention_far.1 = (bf16[192,960]{1,0:T(8,128)(2,1)}, f32[5,64,576]{2,1,0:T(8,128)}, f32[5,576]{1,0:T(8,128)}, f32[192,960]{1,0:T(8,128)}, f32[192,1]{1,0:T(8,128)}, /*index=5*/bf16[192,960]{1,0:T(8,128)(2,1)}) custom-call(s32[4]{0:T(128)} %pad_add_fusion.1.spots, bf16[192,960]{1,0:T(8,128)(2,1)} %get-tuple-element.126.refs_0_, s32[768,1]{1,0:T(8,128)} %slice.125.refs_1_, ...), custom_call_target="tpu_custom_call" | custom-call | flops 16099999744 | tf_op jit(solution)/shard_map/attention_far/pallas_call | solution.py:106
  134.0 7.9 %collective-permute-done.19.refs_3_.refs_7_ = bf16[192,960]{1,0:T(8,128)(2,1)S(1)} collective-permute-done((bf16[192,960]{1,0:T(8,128)(2,1)}, bf16[192,960]{1,0:T(8,128)(2,1)S(1)}, u32[]{:S(2)}, u32[]{:S(2)}) %collective-permute-start.19) | collective-permute-done | bytes 368672 | tf_op jit(solution)/shard_map/ppermute | solution.py:67
  144.3 6.4 %collective-permute-done.21.refs_5_.refs_9_ = bf16[192,960]{1,0:T(8,128)(2,1)S(1)} collective-permute-done((bf16[192,960]{1,0:T(8,128)(2,1)}, bf16[192,960]{1,0:T(8,128)(2,1)S(1)}, u32[]{:S(2)}, u32[]{:S(2)}) %collective-permute-start.21) | collective-permute-done | bytes 368672 | tf_op jit(solution)/shard_map/ppermute | solution.py:67
  153.2 8.5 %feed_forward.3 = (bf16[4,192,960]{2,1,0:T(8,128)(2,1)}, bf16[768,320]{1,0:T(8,128)(2,1)}, bf16[768,640]{1,0:T(8,128)(2,1)}) custom-call(s32[4]{0:T(128)} %pad_add_fusion.1.spots, bf16[960,960]{1,0:T(8,128)(2,1)} %all-gather.5.cloned.1.call-done.refs_0_, bf16[8,192,960]{2,1,0:T(8,128)(2,1)} %all-gather.3.cloned.1.call-done.refs_1_.refs_5_, ...), custom_call_target="tpu_custom_call" | custom-call | flops 9200000000 | tf_op jit(solution)/shard_map/feed_forward/pallas_call | solution.py:106
  161.9 8.5 %feed_forward.2 = (bf16[4,192,960]{2,1,0:T(8,128)(2,1)}, bf16[768,320]{1,0:T(8,128)(2,1)}, bf16[768,640]{1,0:T(8,128)(2,1)}) custom-call(s32[4]{0:T(128)} %pad_add_fusion.1.spots, bf16[960,960]{1,0:T(8,128)(2,1)} %all-gather.5.cloned.1.call-done.refs_0_, bf16[8,192,960]{2,1,0:T(8,128)(2,1)} %all-gather.3.cloned.1.call-done.refs_1_.refs_5_, ...), custom_call_target="tpu_custom_call" | custom-call | flops 9200000000 | tf_op jit(solution)/shard_map/feed_forward/pallas_call | solution.py:106
  176.4 12.4 %feed_forward_weights.1 = (bf16[4,192,960]{2,1,0:T(8,128)(2,1)}, bf16[4,192,960]{2,1,0:T(8,128)(2,1)}, bf16[960,960]{1,0:T(8,128)(2,1)}) custom-call(s32[4]{0:T(128)} %pad_add_fusion.1.spots, bf16[960,960]{1,0:T(8,128)(2,1)} %all-gather.5.cloned.1.call-done.refs_0_, bf16[768,320]{1,0:T(8,128)(2,1)} %get-tuple-element.140.refs_1_, ...), custom_call_target="tpu_custom_call" | custom-call | flops 13799999488 | tf_op jit(solution)/shard_map/feed_forward_weights/pallas_call | solution.py:106
  188.8 5.1 %collective-permute-done.29.refs_4_ = bf16[192,960]{1,0:T(8,128)(2,1)S(1)} collective-permute-done((bf16[192,960]{1,0:T(8,128)(2,1)S(1)}, bf16[192,960]{1,0:T(8,128)(2,1)S(1)}, u32[]{:S(2)}, u32[]{:S(2)}) %collective-permute-start.29) | collective-permute-done | bytes 368672 | tf_op jit(solution)/shard_map/ppermute | solution.py:67
  194.6 6.3 %residual_back.1 = (f32[192,960]{1,0:T(8,128)}, bf16[192,960]{1,0:T(8,128)(2,1)}, bf16[192,960]{1,0:T(8,128)(2,1)}, f32[1,960]{1,0:T(1,128)}) custom-call(s32[4]{0:T(128)} %pad_add_fusion.1.spots, bf16[4,192,960]{2,1,0:T(8,128)(2,1)} %get-tuple-element.137.refs_0_, bf16[4,192,960]{2,1,0:T(8,128)(2,1)} %copy-done.4, bf16[192,960]{1,0:T(8,128)(2,1)} %copy-done.35, ...), custom_call_target="tpu_custom_call" | custom-call | flops 6899999744 | tf_op jit(solution)/shard_map/residual_back/pallas_call | solution.py:106
  200.9 12.7 %attention_back_far.1 = (f32[5,64,576]{2,1,0:T(8,128)}, bf16[4,192,640]{2,1,0:T(8,128)(2,1)}) custom-call(s32[4]{0:T(128)} %pad_add_fusion.1.spots, bf16[192,960]{1,0:T(8,128)(2,1)} %get-tuple-element.126.refs_0_, s32[768,1]{1,0:T(8,128)} %slice.125.refs_1_, s32[1,576]{1,0:T(1,128)} %broadcast_in_dim.29.refs_2_, ...), custom_call_target="tpu_custom_call" | custom-call | flops 14949999616 | tf_op jit(solution)/shard_map/attention_back_far/pallas_call | solution.py:106
  216.1 13.7 %attention_back_near.1 = (bf16[192,960]{1,0:T(8,128)(2,1)}, bf16[192,640]{1,0:T(8,128)(2,1)}, bf16[192,640]{1,0:T(8,128)(2,1)}, bf16[192,640]{1,0:T(8,128)(2,1)}, bf16[192,640]{1,0:T(8,128)(2,1)}) custom-call(s32[4]{0:T(128)} %pad_add_fusion.1.spots, bf16[192,960]{1,0:T(8,128)(2,1)} %get-tuple-element.126.refs_0_, s32[768,1]{1,0:T(8,128)} %slice.124.refs_1_, ...), custom_call_target="tpu_custom_call" | custom-call | flops 16099999744 | tf_op jit(solution)/shard_map/attention_back_near/pallas_call | solution.py:106
  229.8 5.5 %collective-permute-done.31 = bf16[2,192,960]{2,1,0:T(8,128)(2,1)S(1)} collective-permute-done((bf16[2,192,960]{2,1,0:T(8,128)(2,1)S(1)}, bf16[2,192,960]{2,1,0:T(8,128)(2,1)S(1)}, u32[]{:S(2)}, u32[]{:S(2)}) %collective-permute-start.31) | collective-permute-done | bytes 737312 | tf_op jit(solution)/shard_map/ppermute | solution.py:67
  236.1 5.0 %query_output_weight_grads.1 = (bf16[2,960,480]{2,1,0:T(8,128)(2,1)}, bf16[2,960,480]{2,1,0:T(8,128)(2,1)}) custom-call(s32[4]{0:T(128)} %pad_add_fusion.1.spots, bf16[192,960]{1,0:T(8,128)(2,1)} %get-tuple-element.163.refs_0_, bf16[192,960]{1,0:T(8,128)(2,1)} %get-tuple-element.153.refs_1_, bf16[192,960]{1,0:T(8,128)(2,1)} %get-tuple-element.164.refs_2_, ...), custom_call_target="tpu_custom_call" | custom-call | tf_op jit(solution)/shard_map/query_output_weight_grads/pallas_call | solution.py:106
  241.3 4.6 %reduce-scatter.2.cloned.1.call-done.refs_0_ = bf16[240,960]{1,0:T(8,128)(2,1)} async-done(((bf16[960,960]{1,0:T(8,128)(2,1)}), bf16[240,960]{1,0:T(8,128)(2,1)}) %reduce-scatter.2.cloned.1.call-update) | async-done | bytes 460816 | tf_op jit(solution)/shard_map/reduce_scatter | solution.py:809
  256.4 4.1 %query_back.1.refs_6_ = f32[192,960]{1,0:T(8,128)} custom-call(s32[4]{0:T(128)} %pad_add_fusion.1.spots, bf16[192,960]{1,0:T(8,128)(2,1)} %get-tuple-element.177.refs_3_.low_ref, bf16[240,960]{1,0:T(8,128)(2,1)} %local_ref.1, bf16[720,480]{1,0:T(8,128)(2,1)} %stack_quarters.1.refs_6_.refs_9_.refs_10_.refs_0_, bf16[720,480]{1,0:T(8,128)(2,1)} %copy-done.10, ...), custom_call_target="tpu_custom_call" | custom-call | tf_op jit(solution)/shard_map/query_back/pallas_call | solution.py:106
  260.6 9.4 %collective-permute-done.38.refs_14_ = bf16[192,640]{1,0:T(8,128)(2,1)S(1)} collective-permute-done((bf16[192,640]{1,0:T(8,128)(2,1)S(1)}, bf16[192,640]{1,0:T(8,128)(2,1)S(1)}, u32[]{:S(2)}, u32[]{:S(2)}) %collective-permute-start.38) | collective-permute-done | bytes 245792 | tf_op jit(solution)/shard_map/ppermute | solution.py:58
  270.8 6.1 %keys_values_back.1 = (f32[192,960]{1,0:T(8,128)}, bf16[4,336,240]{2,1,0:T(8,128)(2,1)}, bf16[4,336,240]{2,1,0:T(8,128)(2,1)}) custom-call(s32[4]{0:T(128)} %pad_add_fusion.1.spots, f32[192,128]{1,0:T(8,128)} %pad_maximum_fusion.2.refs_5_.refs_3_.refs_0_, f32[192,128]{1,0:T(8,128)} %pad_maximum_fusion.3.refs_6_.refs_4_.refs_1_, ...), custom_call_target="tpu_custom_call" | custom-call | flops 6899999744 | tf_op jit(solution)/shard_map/keys_values_back/pallas_call | solution.py:106
  282.5 6.8 %collective-permute-done.35 = bf16[192,960]{1,0:T(8,128)(2,1)S(1)} collective-permute-done((bf16[192,960]{1,0:T(8,128)(2,1)S(1)}, bf16[192,960]{1,0:T(8,128)(2,1)S(1)}, u32[]{:S(2)}, u32[]{:S(2)}) %collective-permute-start.35) | collective-permute-done | bytes 368672 | tf_op jit(solution)/shard_map/ppermute | solution.py:67
  289.3 4.0 %collective-permute-start.41 = (bf16[336,240]{1,0:T(8,128)(2,1)S(1)}, bf16[336,240]{1,0:T(8,128)(2,1)S(1)}, u32[]{:S(2)}, u32[]{:S(2)}) collective-permute-start(bf16[336,240]{1,0:T(8,128)(2,1)S(1)} %get-tuple-element.188), channel_id=1, source_target_pairs={{0,1},{1,0},{2,3},{3,2},{4,5},{5,4},{6,7},{7,6},{8,9},{9,8},{10,11... | collective-permute-start | bytes 483848 | tf_op jit(solution)/shard_map/ppermute | solution.py:58
  301.7 17.7 %collective-permute-done.42 = bf16[336,240]{1,0:T(8,128)(2,1)S(1)} collective-permute-done((bf16[336,240]{1,0:T(8,128)(2,1)S(1)}, bf16[336,240]{1,0:T(8,128)(2,1)S(1)}, u32[]{:S(2)}, u32[]{:S(2)}) %collective-permute-start.42) | collective-permute-done | bytes 161312 | tf_op jit(solution)/shard_map/ppermute | solution.py:58
  325.0 6.6 %collective-permute-done.49 = bf16[2,240,480]{2,1,0:T(8,128)(2,1)S(1)} collective-permute-done((bf16[2,240,480]{2,1,0:T(8,128)(2,1)S(1)}, bf16[2,240,480]{2,1,0:T(8,128)(2,1)S(1)}, u32[]{:S(2)}, u32[]{:S(2)}) %collective-permute-start.49) | collective-permute-done | bytes 460832 | tf_op jit(solution)/shard_map/ppermute | solution.py:58
  339.0 6.7 %feed_forward_out.1 = (f32[240,2560]{1,0:T(8,128)}, f32[240,2560]{1,0:T(8,128)}, f32[960,640]{1,0:T(8,128)}) custom-call(s32[4]{0:T(128)} %pad_add_fusion.1.spots, bf16[240,960]{1,0:T(8,128)(2,1)} %reduce-scatter.2.cloned.1.call-done.refs_0_, bf16[240,960]{1,0:T(8,128)(2,1)} %copy-done.22, bf16[240,960]{1,0:T(8,128)(2,1)} %copy-done.24, ...), custom_call_target="tpu_custom_call" | custom-call | flops 8049999872 | tf_op jit(solution)/shard_map/feed_forward_out/pallas_call | solution.py:106
  348.7 5.6 %collective-permute-done.51 = bf16[240,480]{1,0:T(8,128)(2,1)S(1)} collective-permute-done((bf16[240,480]{1,0:T(8,128)(2,1)S(1)}, bf16[240,480]{1,0:T(8,128)(2,1)S(1)}, u32[]{:S(2)}, u32[]{:S(2)}) %collective-permute-start.51) | collective-permute-done | bytes 230432 | tf_op jit(solution)/shard_map/ppermute | solution.py:67
  356.1 5.9 %collective-permute-done.52.across_ref = bf16[240,480]{1,0:T(8,128)(2,1)S(1)} collective-permute-done((bf16[240,480]{1,0:T(8,128)(2,1)S(1)}, bf16[240,480]{1,0:T(8,128)(2,1)S(1)}, u32[]{:S(2)}, u32[]{:S(2)}) %collective-permute-start.52) | collective-permute-done | bytes 230432 | tf_op jit(solution)/shard_map/ppermute | solution.py:67
  (266 shorter events, 111.7 us)
Async XLA Ops:
  7.2 95.0 %all-gather.3.cloned.1.call-start = ((), (), s32[]{:S(2)}) async-start(), calls=%async_computation.1 | async-start | bytes 3538944 | tf_op jit(solution)/shard_map/all_gather | solution.py:688
  7.9 144.5 %all-gather.5.cloned.1.call-start = ((), (), s32[]{:S(2)}) async-start(), calls=%async_computation.2 | async-start | bytes 2457600 | tf_op jit(solution)/shard_map/all_gather | solution.py:735
  13.0 30.0 %collective-permute-start = (bf16[240,480]{1,0:T(8,128)(2,1)}, bf16[240,480]{1,0:T(8,128)(2,1)S(1)}, u32[]{:S(2)}, u32[]{:S(2)}) collective-permute-start(bf16[240,480]{1,0:T(8,128)(2,1)} %quarter_columns.1), channel_id=1, source_target_pairs={{0,2},{1,3},{2,0},{3,1},{4,6},{5,7},{6,4},{7,5},{8,10},{9,11},{10,... | collective-permute-start | bytes 691208 | tf_op jit(solution)/shard_map/ppermute | solution.py:58
  17.1 23.7 %collective-permute-start.1 = (bf16[240,480]{1,0:T(8,128)(2,1)}, bf16[240,480]{1,0:T(8,128)(2,1)S(1)}, u32[]{:S(2)}, u32[]{:S(2)}) collective-permute-start(bf16[240,480]{1,0:T(8,128)(2,1)} %quarter_columns.1), channel_id=1, source_target_pairs={{0,1},{1,0},{2,3},{3,2},{4,5},{5,4},{6,7},{7,6},{8,9},{9,8},{10,11... | collective-permute-start | bytes 691208 | tf_op jit(solution)/shard_map/ppermute | solution.py:58
  18.6 17.7 %collective-permute-start.2 = (bf16[336,240]{1,0:T(8,128)(2,1)S(1)}, bf16[336,240]{1,0:T(8,128)(2,1)S(1)}, u32[]{:S(2)}, u32[]{:S(2)}) collective-permute-start(bf16[336,240]{1,0:T(8,128)(2,1)S(1)} %pad_maximum_fusion.1), channel_id=1, source_target_pairs={{0,1},{1,0},{2,3},{3,2},{4,5},{5,4},{6,7},{7,6},{8,9},{9,8},{10,11... | collective-permute-start | bytes 483848 | tf_op jit(solution)/shard_map/ppermute | solution.py:58
  19.1 17.3 %collective-permute-start.3 = (bf16[336,240]{1,0:T(8,128)(2,1)S(1)}, bf16[336,240]{1,0:T(8,128)(2,1)S(1)}, u32[]{:S(2)}, u32[]{:S(2)}) collective-permute-start(bf16[336,240]{1,0:T(8,128)(2,1)S(1)} %pad_maximum_fusion.1), channel_id=1, source_target_pairs={{0,2},{1,3},{2,0},{3,1},{4,6},{5,7},{6,4},{7,5},{8,10},{9,11},{10,... | collective-permute-start | bytes 483848 | tf_op jit(solution)/shard_map/ppermute | solution.py:58
  19.1 21.7 %collective-permute-start.4 = (bf16[336,240]{1,0:T(8,128)(2,1)S(1)}, bf16[336,240]{1,0:T(8,128)(2,1)S(1)}, u32[]{:S(2)}, u32[]{:S(2)}) collective-permute-start(bf16[336,240]{1,0:T(8,128)(2,1)S(1)} %pad_maximum_fusion.1), channel_id=1, source_target_pairs={{0,3},{1,2},{2,1},{3,0},{4,7},{5,6},{6,5},{7,4},{8,11},{9,10},{10,... | collective-permute-start | bytes 483848 | tf_op jit(solution)/shard_map/ppermute | solution.py:58
  47.5 15.3 %collective-permute-start.8 = (bf16[192,640]{1,0:T(8,128)(2,1)}, bf16[192,640]{1,0:T(8,128)(2,1)S(1)}, u32[]{:S(2)}, u32[]{:S(2)}) collective-permute-start(bf16[192,640]{1,0:T(8,128)(2,1)} %get-tuple-element.120.refs_10_.refs_9_), channel_id=1, source_target_pairs={{0,1},{1,0},{2,3},{3,2},{4,5},{5,4},{6,7},{7,6},{8,9},{9,8},{10,11... | collective-permute-start | bytes 737288 | tf_op jit(solution)/shard_map/ppermute | solution.py:58
  65.0 22.7 %collective-permute-start.10 = (bf16[720,480]{1,0:T(8,128)(2,1)}, bf16[720,480]{1,0:T(8,128)(2,1)S(1)}, u32[]{:S(2)}, u32[]{:S(2)}) collective-permute-start(bf16[720,480]{1,0:T(8,128)(2,1)} %stack_quarters.1.refs_6_.refs_9_.refs_10_.refs_0_), channel_id=1, source_target_pairs={{0,16},{4,20},{8,24},{12,28},{16,0},{20,4},{24,8},{28,12},{1,17},{... | collective-permute-start | bytes 2073608 | tf_op jit(solution)/shard_map/ppermute | solution.py:67
  66.6 21.0 %collective-permute-start.11 = (bf16[192,640]{1,0:T(8,128)(2,1)}, bf16[192,640]{1,0:T(8,128)(2,1)S(1)}, u32[]{:S(2)}, u32[]{:S(2)}) collective-permute-start(bf16[192,640]{1,0:T(8,128)(2,1)} %get-tuple-element.120.refs_10_.refs_9_), channel_id=1, source_target_pairs={{0,2},{1,3},{2,0},{3,1},{4,6},{5,7},{6,4},{7,5},{8,10},{9,11},{10,... | collective-permute-start | bytes 737288 | tf_op jit(solution)/shard_map/ppermute | solution.py:58
  70.0 17.6 %collective-permute-start.12 = (bf16[192,640]{1,0:T(8,128)(2,1)}, bf16[192,640]{1,0:T(8,128)(2,1)S(1)}, u32[]{:S(2)}, u32[]{:S(2)}) collective-permute-start(bf16[192,640]{1,0:T(8,128)(2,1)} %get-tuple-element.120.refs_10_.refs_9_), channel_id=1, source_target_pairs={{0,3},{1,2},{2,1},{3,0},{4,7},{5,6},{6,5},{7,4},{8,11},{9,10},{10,... | collective-permute-start | bytes 737288 | tf_op jit(solution)/shard_map/ppermute | solution.py:58
  73.5 29.2 %collective-permute-start.15 = (bf16[720,480]{1,0:T(8,128)(2,1)}, bf16[720,480]{1,0:T(8,128)(2,1)S(1)}, u32[]{:S(2)}, u32[]{:S(2)}) collective-permute-start(bf16[720,480]{1,0:T(8,128)(2,1)} %stack_quarters.1.refs_6_.refs_9_.refs_10_.refs_0_), channel_id=1, source_target_pairs={{0,8},{4,12},{8,0},{12,4},{16,24},{20,28},{24,16},{28,20},{1,9},{5... | collective-permute-start | bytes 2073608 | tf_op jit(solution)/shard_map/ppermute | solution.py:67
  92.6 23.7 %collective-permute-start.17 = (bf16[192,640]{1,0:T(8,128)(2,1)S(1)}, bf16[192,640]{1,0:T(8,128)(2,1)}, u32[]{:S(2)}, u32[]{:S(2)}) collective-permute-start(bf16[192,640]{1,0:T(8,128)(2,1)S(1)} %collective-permute-done.11.refs_12_.refs_11_), channel_id=1, source_target_pairs={{0,4},{4,0},{1,5},{5,1},{2,6},{6,2},{3,7},{7,3},{8,12},{12,8},{9,1... | collective-permute-start | bytes 737288 | tf_op jit(solution)/shard_map/ppermute | solution.py:58
  96.8 19.5 %collective-permute-start.18 = (bf16[192,640]{1,0:T(8,128)(2,1)S(1)}, bf16[192,640]{1,0:T(8,128)(2,1)}, u32[]{:S(2)}, u32[]{:S(2)}) collective-permute-start(bf16[192,640]{1,0:T(8,128)(2,1)S(1)} %collective-permute-done.12.refs_13_.refs_12_), channel_id=1, source_target_pairs={{0,4},{4,0},{1,5},{5,1},{2,6},{6,2},{3,7},{7,3},{8,12},{12,8},{9,1... | collective-permute-start | bytes 737288 | tf_op jit(solution)/shard_map/ppermute | solution.py:58
  102.2 143.7 %reduce-scatter.2.cloned.1.call-start = ((), (), s32[]{:S(2)}) async-start(), calls=%async_computation.3 | async-start | bytes 2457600 | tf_op jit(solution)/shard_map/reduce_scatter | solution.py:809
  132.5 18.1 %collective-permute-start.21 = (bf16[192,960]{1,0:T(8,128)(2,1)}, bf16[192,960]{1,0:T(8,128)(2,1)S(1)}, u32[]{:S(2)}, u32[]{:S(2)}) collective-permute-start(bf16[192,960]{1,0:T(8,128)(2,1)} %get-tuple-element.136.refs_2_.refs_6_), channel_id=1, source_target_pairs={{0,20},{4,16},{8,28},{12,24},{16,4},{20,0},{24,12},{28,8},{1,21},{... | collective-permute-start | bytes 1105928 | tf_op jit(solution)/shard_map/ppermute | solution.py:67
  134.0 16.7 %collective-permute-start.22 = (bf16[192,960]{1,0:T(8,128)(2,1)}, bf16[192,960]{1,0:T(8,128)(2,1)S(1)}, u32[]{:S(2)}, u32[]{:S(2)}) collective-permute-start(bf16[192,960]{1,0:T(8,128)(2,1)} %get-tuple-element.136.refs_2_.refs_6_), channel_id=1, source_target_pairs={{0,8},{4,12},{8,0},{12,4},{16,24},{20,28},{24,16},{28,20},{1,9},{5... | collective-permute-start | bytes 1105928 | tf_op jit(solution)/shard_map/ppermute | solution.py:67
  172.8 15.9 %collective-permute-start.27 = (bf16[192,960]{1,0:T(8,128)(2,1)S(1)}, bf16[192,960]{1,0:T(8,128)(2,1)S(1)}, u32[]{:S(2)}, u32[]{:S(2)}) collective-permute-start(bf16[192,960]{1,0:T(8,128)(2,1)S(1)} %get-tuple-element.207), channel_id=1, source_target_pairs={{0,4},{4,0},{8,12},{12,8},{16,20},{20,16},{24,28},{28,24},{1,5},{5... | collective-permute-start | bytes 1105928 | tf_op jit(solution)/shard_map/ppermute | solution.py:67
  174.9 19.0 %collective-permute-start.29 = (bf16[192,960]{1,0:T(8,128)(2,1)S(1)}, bf16[192,960]{1,0:T(8,128)(2,1)S(1)}, u32[]{:S(2)}, u32[]{:S(2)}) collective-permute-start(bf16[192,960]{1,0:T(8,128)(2,1)S(1)} %get-tuple-element.205), channel_id=1, source_target_pairs={{0,20},{4,16},{8,28},{12,24},{16,4},{20,0},{24,12},{28,8},{1,21},{... | collective-permute-start | bytes 1105928 | tf_op jit(solution)/shard_map/ppermute | solution.py:67
  213.7 27.5 %collective-permute-start.32 = (bf16[4,192,640]{2,1,0:T(8,128)(2,1)}, bf16[4,192,640]{2,1,0:T(8,128)(2,1)}, u32[]{:S(2)}, u32[]{:S(2)}) collective-permute-start(bf16[4,192,640]{2,1,0:T(8,128)(2,1)} %get-tuple-element.168), channel_id=1, source_target_pairs={{0,4},{4,0},{1,5},{5,1},{2,6},{6,2},{3,7},{7,3},{8,12},{12,8},{9,1... | collective-permute-start | bytes 2949128 | tf_op jit(solution)/shard_map/ppermute | solution.py:58
  215.5 19.7 %collective-permute-start.31 = (bf16[2,192,960]{2,1,0:T(8,128)(2,1)S(1)}, bf16[2,192,960]{2,1,0:T(8,128)(2,1)S(1)}, u32[]{:S(2)}, u32[]{:S(2)}) collective-permute-start(bf16[2,192,960]{2,1,0:T(8,128)(2,1)S(1)} %add_convert_fusion.1), channel_id=1, source_target_pairs={{0,16},{4,20},{8,24},{12,28},{16,0},{20,4},{24,8},{28,12},{1,17},{... | collective-permute-start | bytes 2211848 | tf_op jit(solution)/shard_map/ppermute | solution.py:67
  249.8 20.3 %collective-permute-start.38 = (bf16[192,640]{1,0:T(8,128)(2,1)S(1)}, bf16[192,640]{1,0:T(8,128)(2,1)S(1)}, u32[]{:S(2)}, u32[]{:S(2)}) collective-permute-start(bf16[192,640]{1,0:T(8,128)(2,1)S(1)} %get-tuple-element.215), channel_id=1, source_target_pairs={{0,2},{1,3},{2,0},{3,1},{4,6},{5,7},{6,4},{7,5},{8,10},{9,11},{10,... | collective-permute-start | bytes 737288 | tf_op jit(solution)/shard_map/ppermute | solution.py:58
  251.2 18.9 %collective-permute-start.39 = (bf16[192,640]{1,0:T(8,128)(2,1)S(1)}, bf16[192,640]{1,0:T(8,128)(2,1)S(1)}, u32[]{:S(2)}, u32[]{:S(2)}) collective-permute-start(bf16[192,640]{1,0:T(8,128)(2,1)S(1)} %get-tuple-element.214), channel_id=1, source_target_pairs={{0,3},{1,2},{2,1},{3,0},{4,7},{5,6},{6,5},{7,4},{8,11},{9,10},{10,... | collective-permute-start | bytes 737288 | tf_op jit(solution)/shard_map/ppermute | solution.py:58
  255.9 33.4 %collective-permute-start.34 = (bf16[960,480]{1,0:T(8,128)(2,1)}, bf16[960,480]{1,0:T(8,128)(2,1)S(1)}, u32[]{:S(2)}, u32[]{:S(2)}) collective-permute-start(bf16[960,480]{1,0:T(8,128)(2,1)} %fusion), channel_id=1, source_target_pairs={{0,16},{4,20},{8,24},{12,28},{16,0},{20,4},{24,8},{28,12},{1,17},{... | collective-permute-start | bytes 2764808 | tf_op jit(solution)/shard_map/ppermute | solution.py:67
  278.9 40.6 %collective-permute-start.44 = (bf16[240,960]{1,0:T(8,128)(2,1)S(1)}, bf16[240,960]{1,0:T(8,128)(2,1)S(1)}, u32[]{:S(2)}, u32[]{:S(2)}) collective-permute-start(bf16[240,960]{1,0:T(8,128)(2,1)S(1)} %copy-done.21), channel_id=1, source_target_pairs={{0,4},{4,0},{8,12},{12,8},{16,20},{20,16},{24,28},{28,24},{1,5},{5... | collective-permute-start | bytes 1382408 | tf_op jit(solution)/shard_map/ppermute | solution.py:67
  279.5 40.0 %collective-permute-start.45 = (bf16[240,960]{1,0:T(8,128)(2,1)}, bf16[240,960]{1,0:T(8,128)(2,1)S(1)}, u32[]{:S(2)}, u32[]{:S(2)}) collective-permute-start(bf16[240,960]{1,0:T(8,128)(2,1)} %collective-permute-done.36.refs_4_), channel_id=1, source_target_pairs={{0,4},{4,0},{8,12},{12,8},{16,20},{20,16},{24,28},{28,24},{1,5},{5... | collective-permute-start | bytes 1382408 | tf_op jit(solution)/shard_map/ppermute | solution.py:67
  293.3 26.0 %collective-permute-start.42 = (bf16[336,240]{1,0:T(8,128)(2,1)S(1)}, bf16[336,240]{1,0:T(8,128)(2,1)S(1)}, u32[]{:S(2)}, u32[]{:S(2)}) collective-permute-start(bf16[336,240]{1,0:T(8,128)(2,1)S(1)} %get-tuple-element.189), channel_id=1, source_target_pairs={{0,2},{1,3},{2,0},{3,1},{4,6},{5,7},{6,4},{7,5},{8,10},{9,11},{10,... | collective-permute-start | bytes 483848 | tf_op jit(solution)/shard_map/ppermute | solution.py:58
  294.4 24.9 %collective-permute-start.43 = (bf16[336,240]{1,0:T(8,128)(2,1)S(1)}, bf16[336,240]{1,0:T(8,128)(2,1)S(1)}, u32[]{:S(2)}, u32[]{:S(2)}) collective-permute-start(bf16[336,240]{1,0:T(8,128)(2,1)S(1)} %get-tuple-element.190), channel_id=1, source_target_pairs={{0,3},{1,2},{2,1},{3,0},{4,7},{5,6},{6,5},{7,4},{8,11},{9,10},{10,... | collective-permute-start | bytes 483848 | tf_op jit(solution)/shard_map/ppermute | solution.py:58
  299.3 32.3 %collective-permute-start.49 = (bf16[2,240,480]{2,1,0:T(8,128)(2,1)S(1)}, bf16[2,240,480]{2,1,0:T(8,128)(2,1)S(1)}, u32[]{:S(2)}, u32[]{:S(2)}) collective-permute-start(bf16[2,240,480]{2,1,0:T(8,128)(2,1)S(1)} %pad_maximum_fusion), channel_id=1, source_target_pairs={{0,2},{1,3},{2,0},{3,1},{4,6},{5,7},{6,4},{7,5},{8,10},{9,11},{10,... | collective-permute-start | bytes 1382408 | tf_op jit(solution)/shard_map/ppermute | solution.py:58
  321.2 16.0 %collective-permute-start.55 = (bf16[240,960]{1,0:T(8,128)(2,1)S(1)}, bf16[240,960]{1,0:T(8,128)(2,1)S(1)}, u32[]{:S(2)}, u32[]{:S(2)}) collective-permute-start(bf16[240,960]{1,0:T(8,128)(2,1)S(1)} %copy-done.21), channel_id=1, source_target_pairs={{0,8},{4,12},{8,0},{12,4},{16,24},{20,28},{24,16},{28,20},{1,9},{5... | collective-permute-start | bytes 1382408 | tf_op jit(solution)/shard_map/ppermute | solution.py:67
  321.2 16.1 %collective-permute-start.56 = (bf16[240,960]{1,0:T(8,128)(2,1)S(1)}, bf16[240,960]{1,0:T(8,128)(2,1)S(1)}, u32[]{:S(2)}, u32[]{:S(2)}) collective-permute-start(bf16[240,960]{1,0:T(8,128)(2,1)S(1)} %collective-permute-done.44.refs_1_), channel_id=1, source_target_pairs={{0,8},{4,12},{8,0},{12,4},{16,24},{20,28},{24,16},{28,20},{1,9},{5... | collective-permute-start | bytes 1382408 | tf_op jit(solution)/shard_map/ppermute | solution.py:67
  321.7 15.6 %collective-permute-start.57 = (bf16[240,960]{1,0:T(8,128)(2,1)}, bf16[240,960]{1,0:T(8,128)(2,1)S(1)}, u32[]{:S(2)}, u32[]{:S(2)}) collective-permute-start(bf16[240,960]{1,0:T(8,128)(2,1)} %collective-permute-done.36.refs_4_), channel_id=1, source_target_pairs={{0,8},{4,12},{8,0},{12,4},{16,24},{20,28},{24,16},{28,20},{1,9},{5... | collective-permute-start | bytes 1382408 | tf_op jit(solution)/shard_map/ppermute | solution.py:67
  (85 other events, 697.1 us)
Sparse Core Ops, SparseCore 0:
  9.9 35.0 all-gather.2
  102.3 46.7 all-gather.4
  201.1 44.7 reduce-scatter.1

commit v7 on v6

--- a/solution.py
+++ b/solution.py
@@ -26,7 +26,7 @@
     "pack_weights": 4,
     "norm_keys_values": 4,
     "attention_near": 12,
-    "attention_far": 14,
+    "attention_far": 12,
     "feed_forward": 8,
     "feed_forward_weights": 12,
     "residual_back": 6,
@@ -164,9 +164,10 @@
 
 
 def stack_rows(scratch, pieces):
-    rows = pieces[0].shape[0]
-    for i, piece in enumerate(pieces):
-        scratch[i * rows : (i + 1) * rows, :] = piece[...]
+    at = 0
+    for piece in pieces:
+        scratch[at : at + piece.shape[0], :] = piece[...]
+        at += piece.shape[0]
 
 
 def unstack_rows(out_ref, values):
@@ -207,15 +208,14 @@
     out_ref[...] = jnp.concatenate(out, axis=1).astype(BF16)
 
 
-def quarter_kernel(members, spots, query_ref, output_ref, out_ref):
+def quarter_kernel(members, spots, query_ref, output_ref, *outs):
     size = query_ref.shape[1] // members
     for i in range(members):
 
         @pl.when(spots[2] == i)
         def _():
-            out_ref[...] = jnp.concatenate(
-                [ref[:, i * size : (i + 1) * size] for ref in (query_ref, output_ref)], axis=1
-            )
+            for ref, out_ref in zip((query_ref, output_ref), outs):
+                out_ref[...] = ref[:, i * size : (i + 1) * size]
 
 
 def stack_kernel(spots, *refs):
@@ -288,10 +288,9 @@
     dp = spots[2]
     stack_rows(kv_ref, parts)
     own = local_ref.shape[0]
-    size = blocks.shape[-1]
     away = normed_ref[:, own:]
     for j in range(members):
-        blocks[dp ^ j] = dot_plain(away, weights[j][:, :size])
+        blocks[dp ^ j] = dot_plain(away, weights[j][...])
     raw = join_lanes(blocks) + dot_plain(normed_ref[:, :own], local_ref[...])
     roped = rope_lanes(raw, cos_ref[...], sin_ref[...]).astype(BF16)
     queries_ref[...] = roped * jnp.asarray(1.0 / math.sqrt(HEAD_DIM), BF16)
@@ -312,14 +311,11 @@
         weighted_ref[head] = weighted
 
 
-def far_kernel(chunk, shards, members, pieces, spots, *refs):
-    ins, outs, scratch = split_refs(refs, 9 + members + pieces, 6, 3)
-    (queries_ref, key_pos_ref, query_pos_ref, largest_ref, total_ref, weighted_ref, tokens_ref,
-     gains_ref, local_ref) = ins[:9]
-    weights, parts = split_refs(ins[9:], members, pieces)
-    attended_ref, turned_ref, log_ref, residual_ref, inverse_ref, normed_ref = outs
-    blocks, kv_ref, head_blocks = scratch
-    shard, dp = spots[1], spots[2]
+def far_kernel(chunk, pieces, spots, *refs):
+    ins, outs, (kv_ref,) = split_refs(refs, 6 + pieces, 3, 1)
+    queries_ref, key_pos_ref, query_pos_ref, largest_ref, total_ref, weighted_ref = ins[:6]
+    parts = ins[6:]
+    attended_ref, turned_ref, log_ref = outs
     stack_rows(kv_ref, parts)
     rows = queries_ref.shape[0]
     query_pos = query_pos_ref[...]
@@ -335,14 +331,20 @@
         log_ref[head : head + 1, :] = largest + jnp.log(total)
         straight = turned.T
         heads += [straight[g * rows : (g + 1) * rows, :] for g in range(GROUPS)]
-    attended = jnp.concatenate(heads, axis=1).astype(BF16)
-    attended_ref[...] = attended
-    for z, block in enumerate(lane_blocks(attended, shards)):
+    attended_ref[...] = jnp.concatenate(heads, axis=1).astype(BF16)
+
+
+def project_kernel(shards, members, spots, *refs):
+    ins, outs, (blocks, head_blocks) = split_refs(refs, 4 + members, 3, 2)
+    attended_ref, tokens_ref, gains_ref, local_ref = ins[:4]
+    weights = ins[4:]
+    residual_ref, inverse_ref, normed_ref = outs
+    shard, dp = spots[1], spots[2]
+    for z, block in enumerate(lane_blocks(attended_ref[...], shards)):
         head_blocks[z] = block
     away = jnp.concatenate([head_blocks[shard ^ r] for r in range(1, shards)], axis=1)
-    size = blocks.shape[-1]
     for j in range(members):
-        blocks[dp ^ j] = dot_plain(away, weights[j][:, size:])
+        blocks[dp ^ j] = dot_plain(away, weights[j][...])
     added = join_lanes(blocks) + dot_plain(head_blocks[shard], local_ref[...])
     residual = tokens_ref[...].astype(F32) + added
     residual_ref[...] = residual
@@ -425,18 +427,16 @@
     low = residual_grad.astype(BF16)
     low_ref[...] = low
     attended_grad_ref[...] = back_through(
-        shards, members, spots, low, weights, local_ref, scratch, 1
+        shards, members, spots, low, weights, local_ref, scratch
     ).astype(BF16)
 
 
-def back_through(shards, members, spots, low, weights, local_ref, scratch, which):
+def back_through(shards, members, spots, low, weights, local_ref, scratch):
     blocks, out_blocks = scratch
     shard, dp = spots[1], spots[2]
     for i, block in enumerate(lane_blocks(low, members)):
         blocks[i] = block
-    size = blocks.shape[-1]
-    at = slice(which * size, (which + 1) * size)
-    away = sum(dot_last(blocks[dp ^ j], weights[j][:, at]) for j in range(members))
+    away = sum(dot_last(blocks[dp ^ j], weights[j][...]) for j in range(members))
     out_blocks[shard] = dot_last(low, local_ref[...])
     for r, block in enumerate(lane_blocks(away, shards - 1)):
         out_blocks[shard ^ (r + 1)] = block
@@ -475,7 +475,7 @@
 def query_back_kernel(shards, members, spots, low_ref, local_ref, *refs):
     weights, (back_ref,), scratch = split_refs(refs, members, 1, 2)
     back_ref[...] = back_through(
-        shards, members, spots, low_ref[...], weights, local_ref, scratch, 0
+        shards, members, spots, low_ref[...], weights, local_ref, scratch
     )
 
 
@@ -669,14 +669,23 @@
     kv_mine = direct_fsdp(kv_pack)
 
     quarter = width // dp_count
-    (quarters,) = call(
+    query_quarter, output_quarter = call(
         functools.partial(quarter_kernel, dp_count), spots,
         [after(query_weight, kv_pack), output_weight],
-        [((weight_rows, 2 * quarter), BF16)], name="quarter_columns",
-    )
-    quarter_pieces = swaps_fsdp(quarters)
-    quarter_pieces[0], *kv_mine = lax.optimization_barrier((quarter_pieces[0], *kv_mine))
+        [((weight_rows, quarter), BF16)] * 2, name="quarter_columns",
+    )
+    query_pieces = direct_fsdp(query_quarter)
     kv_other = [swap_core(piece) for piece in kv_mine]
+
+    def stack(pieces):
+        (stacked,) = call(
+            stack_kernel, spots, pieces, [(((shards - 1) * weight_rows, quarter), BF16)],
+            name="stack_quarters",
+        )
+        return stacked, swap_plane(stacked, 2, 0)
+
+    def four(stacked, across):
+        return [stacked, swap_core(stacked), across, swap_core(across)]
 
     group_axes = ("dp", "ctx")
     extra = {}
@@ -708,7 +717,7 @@
     kv_own, normed_one, normed_turned, inverse_one, gains = call(
         functools.partial(begin_kernel, shards), spots,
         [
-            lax.optimization_barrier((tokens, quarter_pieces[1], pack))[0], gain_one, gain_two, key_turned, value_turned, cosine, sine,
+            lax.optimization_barrier((tokens, query_quarter, pack))[0], gain_one, gain_two, key_turned, value_turned, cosine, sine,
             *kv_mine, *kv_other,
         ],
         [
@@ -722,19 +731,21 @@
         name="norm_keys_values",
     )
     near = [kv_own] + direct_fsdp(kv_own)
-    near[1], *quarter_pieces = lax.optimization_barrier((near[1], *quarter_pieces))
-    (stacked,) = call(
-        stack_kernel, spots, quarter_pieces,
-        [(((shards - 1) * weight_rows, 2 * quarter), BF16)], name="stack_quarters",
-    )
-    across, *near = lax.optimization_barrier((swap_plane(stacked, 2, 0), *near))
-    stacks = [stacked, swap_core(stacked), across, swap_core(across)]
-    far = [swap(piece, "ctx", d) for d in range(1, ctx_count) for piece in near]
+    query_pieces = lax.optimization_barrier((kv_own, *query_pieces))[1:]
+    stacked, across = stack(query_pieces)
+    across, *near = lax.optimization_barrier((across, *near))
+    query_stacks = four(stacked, across)
+    output_quarter, near[-1] = lax.optimization_barrier((output_quarter, near[-1]))
+    output_pieces = direct_fsdp(output_quarter)
+    (near_all,) = call(
+        stack_kernel, spots, near, [((near_count, 2 * kv_width), BF16)],
+        name="stack_keys_values",
+    )
+    far = [swap(near_all, "ctx", d) for d in range(1, ctx_count)]
 
     pack, cot_all, _ = lax.optimization_barrier((pack, cot_all, near[-1]))
     pack_all = lax.all_gather(pack, "fsdp", axis=0, tiled=True)
 
-    normed_turned, far[0], far[1] = lax.optimization_barrier((normed_turned, far[0], far[1]))
 
     chunk = rows * 2
     unit = 2 * HEADS * rows * near_count * HEAD_DIM
@@ -742,26 +753,25 @@
     turned_shape = ((KV_HEADS, HEAD_DIM, GROUPS * rows), F32)
     queries, largest, total, weighted = call(
         functools.partial(near_kernel, chunk, dp_count, shards), spots,
-        [normed_turned, near_pos, query_pos, cosine, sine, query_weight, *stacks, *near],
+        [normed_turned, near_pos, query_pos, cosine, sine, query_weight, *query_stacks, *near],
         [((rows, query_width), BF16), stat, stat, turned_shape],
         scratch=[((dp_count, rows, quarter), F32), ((near_count, 2 * kv_width), BF16)],
         name="attention_near",
     )
-    attended, turned, log_total, residual, inverse_two, normed_two = call(
-        functools.partial(far_kernel, chunk, shards, dp_count, len(far)), spots,
-        [
-            queries, far_pos, query_pos, largest, total, weighted, tokens, gains,
-            output_weight, *stacks, *far,
-        ],
-        [
-            ((rows, query_width), BF16), turned_shape, stat, ((rows, width), F32),
-            ((rows, 1), F32), ((rows, width), BF16),
-        ],
-        scratch=[
-            ((dp_count, rows, quarter), F32), ((far_count, 2 * kv_width), BF16),
-            ((shards, rows, weight_rows), BF16),
-        ],
-        name="attention_far",
+    attended, turned, log_total = call(
+        functools.partial(far_kernel, chunk, len(far)), spots,
+        [queries, far_pos, query_pos, largest, total, weighted, *far],
+        [((rows, query_width), BF16), turned_shape, stat],
+        scratch=[((far_count, 2 * kv_width), BF16)], name="attention_far",
+    )
+    output_pieces = lax.optimization_barrier((queries, *output_pieces))[1:]
+    output_stacks = four(*stack(output_pieces))
+    residual, inverse_two, normed_two = call(
+        functools.partial(project_kernel, shards, dp_count), spots,
+        [attended, tokens, gains, output_weight, *output_stacks],
+        [((rows, width), F32), ((rows, 1), F32), ((rows, width), BF16)],
+        scratch=[((dp_count, rows, quarter), F32), ((shards, rows, weight_rows), BF16)],
+        name="project_residual",
     )
 
     normed_a, normed_b = plane_pieces(normed_two)
@@ -813,7 +823,7 @@
         functools.partial(middle_kernel, shards, dp_count), spots,
         [
             grad_a, from_core, *grad_chips, residual, inverse_two, cotangent, gains, output_weight,
-            *stacks,
+            *output_stacks,
         ],
         [((rows, width), F32), token_shape, ((rows, query_width), BF16), ((1, width), F32)],
         scratch=[((dp_count, rows, quarter), BF16), ((shards, rows, weight_rows), F32)],
@@ -843,18 +853,16 @@
             (arrived[r].astype(F32) for r in range(1, shards)), pieces[0].astype(F32)
         ).astype(BF16)
 
-    def relay_z(terms):
-        span = shards
-        pieces = {r: piece.astype(F32) for r, piece in enumerate(pieces_z(terms))}
-        while span > 1:
-            span //= 2
-            sent = jnp.stack([pieces[r].astype(BF16) for r in range(span, 2 * span)])
-            arrived = swap(sent, "fsdp", span)
-            pieces = {r: pieces[r] + arrived[r].astype(F32) for r in range(span)}
-        return pieces[0].astype(BF16)
+    def halve_z(pieces, span):
+        sent = jnp.stack([piece.astype(BF16) for piece in pieces[span:]])
+        arrived = swap(sent, "fsdp", span)
+        return [pieces[r].astype(F32) + arrived[r].astype(F32) for r in range(span)]
+
+    def sum_swap(own, dp_mask, ctx_mask):
+        return (own.astype(F32) + swap_plane(own, dp_mask, ctx_mask).astype(F32)).astype(BF16)
 
     def sum_y(own):
-        return sum_far((own.astype(F32) + swap_plane(own, 0, 1).astype(F32)).astype(BF16))
+        return sum_far(sum_swap(own, 0, 1))
 
     def finish_quarters(own):
         across = swap_plane(own, 2, 0)
@@ -864,11 +872,6 @@
             [((weight_rows, width), F32)] * 2,
             scratch=[((dp_count, weight_rows, 2 * quarter), BF16)], name="join_columns",
         )
-
-    def sum_chips(own):
-        for a, b in ((2, 0), (0, 1)):
-            own = (own.astype(F32) + swap_plane(own, a, b).astype(F32)).astype(BF16)
-        return sum_far(own)
 
     def back(first, last, start, pos, pieces):
         count = pos.shape[0]
@@ -891,31 +894,29 @@
 
     query_partial, far_grads = turned, []
     for d in range(1, ctx_count):
-        at = (d - 1) * shards
+        at = (d - 1) * near_count
         query_partial, grads = back(
-            d == 1, False, query_partial, far_pos[at * rows : (at + shards) * rows],
-            far[at : at + shards],
+            d == 1, False, query_partial, far_pos[at : at + near_count], far[d - 1 : d]
         )
         far_grads.append(swap(grads[0], "ctx", d))
     result_sent = (result_a[2:].astype(F32) + result_core[2:].astype(F32)).astype(BF16)
     query_partial, result_sent = lax.optimization_barrier((query_partial, result_sent))
     result_across = swap_plane(result_sent, 2, 0)
     query_low, near_grads = back(False, True, query_partial, near_pos, near)
-    query_low, result_across = lax.optimization_barrier((query_low, result_across))
+    pair_shape = ((2, width, 2 * quarter), BF16)
+    weights_keep, weights_send = call(
+        functools.partial(weight_grads_kernel, dp_count), spots,
+        [attended, residual_low, normed_one, query_low], [pair_shape, pair_shape],
+        scratch=[((2 * dp_count, rows, quarter), BF16)], name="query_output_weight_grads",
+    )
+    weights_send, far_grads[-1], result_across = lax.optimization_barrier(
+        (weights_send, far_grads[-1], result_across)
+    )
     result_own, result_along = [
         (result_a[k].astype(F32) + result_core[k].astype(F32)) + result_across[k].astype(F32)
         for k in (0, 1)
     ]
     result_along = swap_plane(result_along.astype(BF16), 0, 1)
-    pair_shape = ((2, width, 2 * quarter), BF16)
-    weights_keep, weights_send = call(
-        functools.partial(weight_grads_kernel, dp_count), spots,
-        [attended, residual_low, normed_one, query_low], [pair_shape, pair_shape],
-        scratch=[((2 * dp_count, rows, quarter), BF16)], name="query_output_weight_grads",
-    )
-    pack_share, query_low = lax.optimization_barrier((pack_share, query_low))
-    share_across = swap_plane(pack_share, 2, 0)
-    weights_send, far_grads[-1] = lax.optimization_barrier((weights_send, far_grads[-1]))
 
     def home(r):
         return sum(grads[r].astype(F32) for grads in far_grads)
@@ -924,21 +925,22 @@
         r: (near_grads[r].astype(F32) + home(r)).astype(BF16) for r in range(1, shards)
     }
     kv_arrived = {r: swap(kv_sums[r], "fsdp", r) for r in reversed(range(1, shards))}
-    query_low, *_ = lax.optimization_barrier((query_low, *kv_sums.values()))
+    query_low, pack_share, *_ = lax.optimization_barrier(
+        (query_low, pack_share, *kv_sums.values())
+    )
+    share_across = swap_plane(pack_share, 2, 0)
 
     weights_away = swap_core(weights_send)
     weights_sent, weights_terms = sum_x(weights_keep, weights_away)
     query_turn = after(query_low, weights_sent)
     (query_back,) = call(
         functools.partial(query_back_kernel, shards, dp_count), spots,
-        [query_turn, query_weight, *stacks], [((rows, width), F32)],
+        [query_turn, query_weight, *query_stacks], [((rows, width), F32)],
         scratch=[((dp_count, rows, quarter), BF16), ((shards, rows, weight_rows), F32)],
         name="query_back",
     )
-    query_back, share_across = lax.optimization_barrier((query_back, share_across))
-    share_a = [
-        pack_share, swap_plane(pack_share, 0, 1), share_across, swap_plane(share_across, 0, 1)
-    ]
+    share_along = swap_plane(pack_share, 0, 1)
+    share_diagonal = swap_plane(share_across, 0, 1)
     span = kv_width + EXTRA_ROWS
     packed_shape = ((shards, span, weight_rows), BF16)
     home_all = far_grads[0]
@@ -956,16 +958,24 @@
         name="keys_values_back",
     )
     kv_away = swap_core(kv_send)
+    kv_keep, *weights_terms = lax.optimization_barrier((kv_keep, *weights_terms))
+    weights_pieces = pieces_z(weights_terms)
     pieces = [
         (lax.dynamic_index_in_dim(kv_keep, shard ^ r, 0, keepdims=False).astype(F32)
          + lax.dynamic_index_in_dim(kv_away, shard ^ r, 0, keepdims=False).astype(F32)).astype(BF16)
         for r in range(shards)
     ]
-    weights_terms, result_along, *pieces = lax.optimization_barrier(
-        (weights_terms, result_along, *pieces)
-    )
+    weights_pieces, *pieces = lax.optimization_barrier((weights_pieces, *pieces))
     kv_share = sum_z(pieces)
-    kv_share, *share_a = lax.optimization_barrier((kv_share, *share_a))
+    weights_half = halve_z(weights_pieces, shards // 2)
+    kv_share, weights_half, share_across = lax.optimization_barrier(
+        (kv_share, weights_half, share_across)
+    )
+    kv_share = sum_swap(kv_share, 2, 0)
+    kv_share, share_along, share_diagonal, result_along = lax.optimization_barrier(
+        (kv_share, share_along, share_diagonal, result_along)
+    )
+    share_a = [pack_share, share_along, share_across, share_diagonal]
     share_b = [swap_core(piece) for piece in share_a]
 
     share_by_mask = [None] * members
@@ -981,10 +991,14 @@
         scratch=[((members, weight_rows, 3 * part), BF16)],
         name="feed_forward_out",
     )
-    weights_own = sum_y(relay_z(weights_terms))
+    span = shards // 2
+    while span > 1:
+        span //= 2
+        weights_half = halve_z(weights_half, span)
+    weights_own = sum_y(weights_half[0].astype(BF16))
     result = residual + (result_own + result_along.astype(F32))
     output_weight_grad, query_weight_grad = finish_quarters(weights_own)
-    low = sum_chips(kv_share)
+    low = sum_far(sum_swap(kv_share, 0, 1))
     away = swap_core(low)
     first = jnp.where(core == 0, low, away).astype(F32)
     second = jnp.where(core == 0, away, low).astype(F32)

time: 379 us -> 368 us (0.971)
  the two profiles are of different devices: /device:TPU:0 before, /device:TPU:17 now
where the time goes in v7:
time: 368 us; the launch traced here: 363 us
  Pallas kernels  128 us (35%)
  waiting for transfers between devices  119 us (32%)
  starting transfers between devices  64.8 us (18%)
  local copies, waits for them, and re-layouts  19.6 us (5%)
  other arithmetic  15.6 us (4%)
  between operations  15.2 us (4%)
    pallas_call x20, Pallas kernels, call(): pl.pallas_call(kernel, out_shape=outs, in_specs=specs, out_specs=tuple((p...  128 us
    ppermute x22, waiting for transfers between devices, swap(): return lax.ppermute(x, axis, [(i, i ^ mask) for i in range(count)])  65.3 us
    ppermute x40, waiting for transfers between devices, swap_plane(): return lax.ppermute(x, ('dp', 'ctx'), pairs)  53.2 us
    ppermute x40, starting transfers between devices, swap_plane(): return lax.ppermute(x, ('dp', 'ctx'), pairs)  42.2 us
    ppermute x22, starting transfers between devices, swap(): return lax.ppermute(x, axis, [(i, i ^ mask) for i in range(count)])  22 us
    unnamed x114, local copies, waits for them, and re-layouts  11.6 us
  transfers between devices with their start and end apart: 65, of which 21 were waited for; matrix products, arithmetic and copies ran while one was open for 6% of the time, Pallas kernels for 31%

profile of v7, /device:TPU:17, one launch (start us, length us, event | category | flops | bytes accessed | tf_op | source)
XLA Modules:
  0.0 362.7 jit_solution(7883269177757878012)
XLA Ops:
  19.8 4.2 %pack_weights.1 = bf16[240,960]{1,0:T(8,128)(2,1)} custom-call(s32[4]{0:T(128)} %pad_add_fusion.1.spots, bf16[240,2560]{1,0:T(8,128)(2,1)} %gate_ref.1, bf16[240,2560]{1,0:T(8,128)(2,1)} %up_ref.1, bf16[960,640]{1,0:T(8,128)(2,1)} %bitcast.98), custom_call_target="tpu_custom_call" | custom-call | flops 4600000000 | tf_op jit(solution)/shard_map/pack_weights/pallas_call | solution.py:106
  26.6 3.9 %collective-permute-done.2.refs_9_.refs_18_ = bf16[336,240]{1,0:T(8,128)(2,1)S(1)} collective-permute-done((bf16[336,240]{1,0:T(8,128)(2,1)S(1)}, bf16[336,240]{1,0:T(8,128)(2,1)S(1)}, u32[]{:S(2)}, u32[]{:S(2)}) %collective-permute-start.2) | collective-permute-done | bytes 161312 | tf_op jit(solution)/shard_map/ppermute | solution.py:58
  35.3 3.7 %norm_keys_values.1 = (bf16[192,640]{1,0:T(8,128)(2,1)}, bf16[192,960]{1,0:T(8,128)(2,1)}, bf16[192,960]{1,0:T(8,128)(2,1)}, f32[192,1]{1,0:T(8,128)}, f32[8,960]{1,0:T(8,128)}) custom-call(s32[4]{0:T(128)} %pad_add_fusion.1.spots, bf16[192,960]{1,0:T(8,128)(2,1)} %bitcast.99, bf16[1,240]{1,0:T(2,128)(2,1)} %copy-done.19, bf16[1,240]{1,0:T(2,128)(2,1)} %copy-done.18, ...), custom_call_target="tpu_custom_call" | custom-call | flops 4600000000 | tf_op jit(solution)/shard_map/norm_keys_values/pallas_call | solution.py:106
  49.5 3.3 collective-permute-done.12.refs_12_.refs_2_.refs_11_
  52.9 10.4 %collective-permute-done.13.refs_13_.refs_3_.refs_12_ = bf16[192,640]{1,0:T(8,128)(2,1)S(1)} collective-permute-done((bf16[192,640]{1,0:T(8,128)(2,1)}, bf16[192,640]{1,0:T(8,128)(2,1)S(1)}, u32[]{:S(2)}, u32[]{:S(2)}) %collective-permute-start.13) | collective-permute-done | bytes 245792 | tf_op jit(solution)/shard_map/ppermute | solution.py:58
  74.1 11.3 %attention_near.1 = (bf16[192,960]{1,0:T(8,128)(2,1)}, f32[5,576]{1,0:T(8,128)}, f32[5,576]{1,0:T(8,128)}, f32[5,64,576]{2,1,0:T(8,128)}) custom-call(s32[4]{0:T(128)} %pad_add_fusion.1.spots, bf16[192,960]{1,0:T(8,128)(2,1)} %get-tuple-element.113.refs_0_, s32[768,1]{1,0:T(8,128)} %slice.124.refs_1_, s32[1,576]{1,0:T(1,128)} %broadcast_in_dim.29.refs_2_, ...), custom_call_target="tpu_custom_call" | custom-call | flops 13799999488 | tf_op jit(solution)/shard_map/attention_near/pallas_call | solution.py:106
  91.6 5.5 %collective-permute-done.20.refs_6_.refs_12_ = bf16[720,240]{1,0:T(8,128)(2,1)S(1)} collective-permute-done((bf16[720,240]{1,0:T(8,128)(2,1)}, bf16[720,240]{1,0:T(8,128)(2,1)S(1)}, u32[]{:S(2)}, u32[]{:S(2)}) %collective-permute-start.20) | collective-permute-done | bytes 345632 | tf_op jit(solution)/shard_map/ppermute | solution.py:67
  100.1 11.6 %attention_far.1 = (bf16[192,960]{1,0:T(8,128)(2,1)}, f32[5,64,576]{2,1,0:T(8,128)}, f32[5,576]{1,0:T(8,128)}) custom-call(s32[4]{0:T(128)} %pad_add_fusion.1.spots, bf16[192,960]{1,0:T(8,128)(2,1)} %get-tuple-element.125.refs_0_, s32[768,1]{1,0:T(8,128)} %slice.125.refs_1_, s32[1,576]{1,0:T(1,128)} %broadcast_in_dim.29.refs_2_, ...), custom_call_target="tpu_custom_call" | custom-call | flops 13799999488 | tf_op jit(solution)/shard_map/attention_far/pallas_call | solution.py:106
  112.6 3.8 %project_residual.1 = (f32[192,960]{1,0:T(8,128)}, f32[192,1]{1,0:T(8,128)}, bf16[192,960]{1,0:T(8,128)(2,1)}) custom-call(s32[4]{0:T(128)} %pad_add_fusion.1.spots, bf16[192,960]{1,0:T(8,128)(2,1)} %get-tuple-element.129.refs_0_, bf16[192,960]{1,0:T(8,128)(2,1)} %bitcast.100, f32[8,960]{1,0:T(8,128)} %get-tuple-element.130.refs_2_.refs_8_.refs_5_, ...), custom_call_target="tpu_custom_call" | custom-call | flops 2300000000 | tf_op jit(solution)/shard_map/project_residual/pallas_call | solution.py:106
  120.0 7.3 %collective-permute-done.22.refs_3_.refs_7_ = bf16[192,960]{1,0:T(8,128)(2,1)S(1)} collective-permute-done((bf16[192,960]{1,0:T(8,128)(2,1)}, bf16[192,960]{1,0:T(8,128)(2,1)S(1)}, u32[]{:S(2)}, u32[]{:S(2)}) %collective-permute-start.22) | collective-permute-done | bytes 368672 | tf_op jit(solution)/shard_map/ppermute | solution.py:67
  129.1 7.5 %collective-permute-done.24.refs_5_.refs_9_ = bf16[192,960]{1,0:T(8,128)(2,1)S(1)} collective-permute-done((bf16[192,960]{1,0:T(8,128)(2,1)}, bf16[192,960]{1,0:T(8,128)(2,1)S(1)}, u32[]{:S(2)}, u32[]{:S(2)}) %collective-permute-start.24) | collective-permute-done | bytes 368672 | tf_op jit(solution)/shard_map/ppermute | solution.py:67
  139.9 8.5 %feed_forward.3 = (bf16[4,192,960]{2,1,0:T(8,128)(2,1)}, bf16[768,320]{1,0:T(8,128)(2,1)}, bf16[768,640]{1,0:T(8,128)(2,1)}) custom-call(s32[4]{0:T(128)} %pad_add_fusion.1.spots, bf16[960,960]{1,0:T(8,128)(2,1)} %all-gather.5.cloned.1.call-done.refs_0_, bf16[8,192,960]{2,1,0:T(8,128)(2,1)} %all-gather.3.cloned.1.call-done.refs_1_.refs_5_, ...), custom_call_target="tpu_custom_call" | custom-call | flops 9200000000 | tf_op jit(solution)/shard_map/feed_forward/pallas_call | solution.py:106
  148.9 8.5 %feed_forward.2 = (bf16[4,192,960]{2,1,0:T(8,128)(2,1)}, bf16[768,320]{1,0:T(8,128)(2,1)}, bf16[768,640]{1,0:T(8,128)(2,1)}) custom-call(s32[4]{0:T(128)} %pad_add_fusion.1.spots, bf16[960,960]{1,0:T(8,128)(2,1)} %all-gather.5.cloned.1.call-done.refs_0_, bf16[8,192,960]{2,1,0:T(8,128)(2,1)} %all-gather.3.cloned.1.call-done.refs_1_.refs_5_, ...), custom_call_target="tpu_custom_call" | custom-call | flops 9200000000 | tf_op jit(solution)/shard_map/feed_forward/pallas_call | solution.py:106
  162.4 12.4 %feed_forward_weights.1 = (bf16[4,192,960]{2,1,0:T(8,128)(2,1)}, bf16[4,192,960]{2,1,0:T(8,128)(2,1)}, bf16[960,960]{1,0:T(8,128)(2,1)}) custom-call(s32[4]{0:T(128)} %pad_add_fusion.1.spots, bf16[960,960]{1,0:T(8,128)(2,1)} %all-gather.5.cloned.1.call-done.refs_0_, bf16[768,320]{1,0:T(8,128)(2,1)} %get-tuple-element.142.refs_1_, ...), custom_call_target="tpu_custom_call" | custom-call | flops 13799999488 | tf_op jit(solution)/shard_map/feed_forward_weights/pallas_call | solution.py:106
  174.8 4.8 %collective-permute-done.32.refs_4_ = bf16[192,960]{1,0:T(8,128)(2,1)S(1)} collective-permute-done((bf16[192,960]{1,0:T(8,128)(2,1)S(1)}, bf16[192,960]{1,0:T(8,128)(2,1)S(1)}, u32[]{:S(2)}, u32[]{:S(2)}) %collective-permute-start.32) | collective-permute-done | bytes 368672 | tf_op jit(solution)/shard_map/ppermute | solution.py:67
  180.4 5.7 %residual_back.1 = (f32[192,960]{1,0:T(8,128)}, bf16[192,960]{1,0:T(8,128)(2,1)}, bf16[192,960]{1,0:T(8,128)(2,1)}, f32[1,960]{1,0:T(1,128)}) custom-call(s32[4]{0:T(128)} %pad_add_fusion.1.spots, bf16[4,192,960]{2,1,0:T(8,128)(2,1)} %get-tuple-element.139.refs_0_, bf16[4,192,960]{2,1,0:T(8,128)(2,1)} %copy-done.4, bf16[192,960]{1,0:T(8,128)(2,1)} %copy-done.36, ...), custom_call_target="tpu_custom_call" | custom-call | flops 6899999744 | tf_op jit(solution)/shard_map/residual_back/pallas_call | solution.py:106
  187.4 12.8 %attention_back_far.1 = (f32[5,64,576]{2,1,0:T(8,128)}, bf16[4,192,640]{2,1,0:T(8,128)(2,1)}) custom-call(s32[4]{0:T(128)} %pad_add_fusion.1.spots, bf16[192,960]{1,0:T(8,128)(2,1)} %get-tuple-element.125.refs_0_, s32[768,1]{1,0:T(8,128)} %slice.125.refs_1_, s32[1,576]{1,0:T(1,128)} %broadcast_in_dim.29.refs_2_, ...), custom_call_target="tpu_custom_call" | custom-call | flops 14949999616 | tf_op jit(solution)/shard_map/attention_back_far/pallas_call | solution.py:106
  202.0 13.6 %attention_back_near.1 = (bf16[192,960]{1,0:T(8,128)(2,1)}, bf16[192,640]{1,0:T(8,128)(2,1)}, bf16[192,640]{1,0:T(8,128)(2,1)}, bf16[192,640]{1,0:T(8,128)(2,1)}, bf16[192,640]{1,0:T(8,128)(2,1)}) custom-call(s32[4]{0:T(128)} %pad_add_fusion.1.spots, bf16[192,960]{1,0:T(8,128)(2,1)} %get-tuple-element.125.refs_0_, s32[768,1]{1,0:T(8,128)} %slice.124.refs_1_, ...), custom_call_target="tpu_custom_call" | custom-call | flops 16099999744 | tf_op jit(solution)/shard_map/attention_back_near/pallas_call | solution.py:106
  215.6 5.0 %query_output_weight_grads.1 = (bf16[2,960,480]{2,1,0:T(8,128)(2,1)}, bf16[2,960,480]{2,1,0:T(8,128)(2,1)}) custom-call(s32[4]{0:T(128)} %pad_add_fusion.1.spots, bf16[192,960]{1,0:T(8,128)(2,1)} %get-tuple-element.129.refs_0_, bf16[192,960]{1,0:T(8,128)(2,1)} %get-tuple-element.155.refs_1_, bf16[192,960]{1,0:T(8,128)(2,1)} %get-tuple-element.157.refs_2_, ...), custom_call_target="tpu_custom_call" | custom-call | tf_op jit(solution)/shard_map/query_output_weight_grads/pallas_call | solution.py:106
  220.6 3.2 collective-permute-done.34.refs_12_
  233.3 3.6 query_back.1.refs_6_
  239.5 6.8 %collective-permute-done.38.refs_14_ = bf16[192,640]{1,0:T(8,128)(2,1)} collective-permute-done((bf16[192,640]{1,0:T(8,128)(2,1)}, bf16[192,640]{1,0:T(8,128)(2,1)}, u32[]{:S(2)}, u32[]{:S(2)}) %collective-permute-start.38) | collective-permute-done | bytes 245792 | tf_op jit(solution)/shard_map/ppermute | solution.py:58
  246.3 6.2 %collective-permute-done.39.refs_15_ = bf16[192,640]{1,0:T(8,128)(2,1)} collective-permute-done((bf16[192,640]{1,0:T(8,128)(2,1)}, bf16[192,640]{1,0:T(8,128)(2,1)}, u32[]{:S(2)}, u32[]{:S(2)}) %collective-permute-start.39) | collective-permute-done | bytes 245792 | tf_op jit(solution)/shard_map/ppermute | solution.py:58
  252.5 6.0 %keys_values_back.1 = (f32[192,960]{1,0:T(8,128)}, bf16[4,336,240]{2,1,0:T(8,128)(2,1)}, bf16[4,336,240]{2,1,0:T(8,128)(2,1)}) custom-call(s32[4]{0:T(128)} %pad_add_fusion.1.spots, f32[192,128]{1,0:T(8,128)} %pad_maximum_fusion.2.refs_5_.refs_3_.refs_0_, f32[192,128]{1,0:T(8,128)} %pad_maximum_fusion.3.refs_6_.refs_4_.refs_1_, ...), custom_call_target="tpu_custom_call" | custom-call | flops 6899999744 | tf_op jit(solution)/shard_map/keys_values_back/pallas_call | solution.py:106
  268.4 3.3 collective-permute-done.46.refs_4_
  271.9 25.4 %collective-permute-done.44 = bf16[336,240]{1,0:T(8,128)(2,1)S(1)} collective-permute-done((bf16[336,240]{1,0:T(8,128)(2,1)S(1)}, bf16[336,240]{1,0:T(8,128)(2,1)S(1)}, u32[]{:S(2)}, u32[]{:S(2)}) %collective-permute-start.44) | collective-permute-done | bytes 161312 | tf_op jit(solution)/shard_map/ppermute | solution.py:58
  300.8 3.3 collective-permute-start.58
  306.9 9.0 %collective-permute-done.50 = bf16[192,960]{1,0:T(8,128)(2,1)S(1)} collective-permute-done((bf16[192,960]{1,0:T(8,128)(2,1)S(1)}, bf16[192,960]{1,0:T(8,128)(2,1)S(1)}, u32[]{:S(2)}, u32[]{:S(2)}) %collective-permute-start.50) | collective-permute-done | bytes 368672 | tf_op jit(solution)/shard_map/ppermute | solution.py:67
  315.9 3.5 collective-permute-start.60
  325.6 6.6 %collective-permute-done.54 = bf16[240,480]{1,0:T(8,128)(2,1)S(1)} collective-permute-done((bf16[240,480]{1,0:T(8,128)(2,1)S(1)}, bf16[240,480]{1,0:T(8,128)(2,1)S(1)}, u32[]{:S(2)}, u32[]{:S(2)}) %collective-permute-start.54) | collective-permute-done | bytes 230432 | tf_op jit(solution)/shard_map/ppermute | solution.py:67
  338.4 3.7 %collective-permute-done.55.across_ref = bf16[240,480]{1,0:T(8,128)(2,1)S(1)} collective-permute-done((bf16[240,480]{1,0:T(8,128)(2,1)S(1)}, bf16[240,480]{1,0:T(8,128)(2,1)S(1)}, u32[]{:S(2)}, u32[]{:S(2)}) %collective-permute-start.55) | collective-permute-done | bytes 230432 | tf_op jit(solution)/shard_map/ppermute | solution.py:67
  345.1 6.7 %feed_forward_out.1 = (f32[240,2560]{1,0:T(8,128)}, f32[240,2560]{1,0:T(8,128)}, f32[960,640]{1,0:T(8,128)}) custom-call(s32[4]{0:T(128)} %pad_add_fusion.1.spots, bf16[240,960]{1,0:T(8,128)(2,1)} %reduce-scatter.2.cloned.1.call-done.refs_0_, bf16[240,960]{1,0:T(8,128)(2,1)} %copy-done.23, bf16[240,960]{1,0:T(8,128)(2,1)} %copy-done.25, ...), custom_call_target="tpu_custom_call" | custom-call | flops 8049999872 | tf_op jit(solution)/shard_map/feed_forward_out/pallas_call | solution.py:106
  (280 shorter events, 116.2 us)
Async XLA Ops:
  7.2 64.2 %all-gather.3.cloned.1.call-start = ((), (), s32[]{:S(2)}) async-start(), calls=%async_computation.1 | async-start | bytes 3538944 | tf_op jit(solution)/shard_map/all_gather | solution.py:697
  7.9 131.2 %all-gather.5.cloned.1.call-start = ((), (), s32[]{:S(2)}) async-start(), calls=%async_computation.2 | async-start | bytes 2457600 | tf_op jit(solution)/shard_map/all_gather | solution.py:747
  11.8 18.7 %collective-permute-start.2 = (bf16[336,240]{1,0:T(8,128)(2,1)S(1)}, bf16[336,240]{1,0:T(8,128)(2,1)S(1)}, u32[]{:S(2)}, u32[]{:S(2)}) collective-permute-start(bf16[336,240]{1,0:T(8,128)(2,1)S(1)} %pad_maximum_fusion.1), channel_id=1, source_target_pairs={{0,3},{1,2},{2,1},{3,0},{4,7},{5,6},{6,5},{7,4},{8,11},{9,10},{10,... | collective-permute-start | bytes 483848 | tf_op jit(solution)/shard_map/ppermute | solution.py:58
  15.8 25.7 %collective-permute-start.6 = (bf16[240,240]{1,0:T(8,128)(2,1)}, bf16[240,240]{1,0:T(8,128)(2,1)S(1)}, u32[]{:S(2)}, u32[]{:S(2)}) collective-permute-start(bf16[240,240]{1,0:T(8,128)(2,1)} %get-tuple-element.111), channel_id=1, source_target_pairs={{0,1},{1,0},{2,3},{3,2},{4,5},{5,4},{6,7},{7,6},{8,9},{9,8},{10,11... | collective-permute-start | bytes 345608 | tf_op jit(solution)/shard_map/ppermute | solution.py:58
  18.0 23.7 %collective-permute-start.7 = (bf16[240,240]{1,0:T(8,128)(2,1)}, bf16[240,240]{1,0:T(8,128)(2,1)S(1)}, u32[]{:S(2)}, u32[]{:S(2)}) collective-permute-start(bf16[240,240]{1,0:T(8,128)(2,1)} %get-tuple-element.111), channel_id=1, source_target_pairs={{0,2},{1,3},{2,0},{3,1},{4,6},{5,7},{6,4},{7,5},{8,10},{9,11},{10,... | collective-permute-start | bytes 345608 | tf_op jit(solution)/shard_map/ppermute | solution.py:58
  41.5 21.8 %collective-permute-start.13 = (bf16[192,640]{1,0:T(8,128)(2,1)}, bf16[192,640]{1,0:T(8,128)(2,1)S(1)}, u32[]{:S(2)}, u32[]{:S(2)}) collective-permute-start(bf16[192,640]{1,0:T(8,128)(2,1)} %get-tuple-element.119.refs_10_.refs_0_.refs_9_), channel_id=1, source_target_pairs={{0,3},{1,2},{2,1},{3,0},{4,7},{5,6},{6,5},{7,4},{8,11},{9,10},{10,... | collective-permute-start | bytes 737288 | tf_op jit(solution)/shard_map/ppermute | solution.py:58
  44.8 18.5 %collective-permute-start.10 = (bf16[720,240]{1,0:T(8,128)(2,1)}, bf16[720,240]{1,0:T(8,128)(2,1)S(1)}, u32[]{:S(2)}, u32[]{:S(2)}) collective-permute-start(bf16[720,240]{1,0:T(8,128)(2,1)} %stack_quarters.2.refs_6_.refs_0_), channel_id=1, source_target_pairs={{0,16},{4,20},{8,24},{12,28},{16,0},{20,4},{24,8},{28,12},{1,17},{... | collective-permute-start | bytes 1036808 | tf_op jit(solution)/shard_map/ppermute | solution.py:67
  46.1 25.8 %collective-permute-start.9 = (bf16[720,240]{1,0:T(8,128)(2,1)}, bf16[720,240]{1,0:T(8,128)(2,1)S(1)}, u32[]{:S(2)}, u32[]{:S(2)}) collective-permute-start(bf16[720,240]{1,0:T(8,128)(2,1)} %stack_quarters.2.refs_6_.refs_0_), channel_id=1, source_target_pairs={{0,8},{4,12},{8,0},{12,4},{16,24},{20,28},{24,16},{28,20},{1,9},{5... | collective-permute-start | bytes 1036808 | tf_op jit(solution)/shard_map/ppermute | solution.py:67
  66.4 19.0 %collective-permute-start.16 = (bf16[240,240]{1,0:T(8,128)(2,1)S(1)}, bf16[240,240]{1,0:T(8,128)(2,1)S(1)}, u32[]{:S(2)}, u32[]{:S(2)}) collective-permute-start(bf16[240,240]{1,0:T(8,128)(2,1)S(1)} %copy-done.54), channel_id=1, source_target_pairs={{0,1},{1,0},{2,3},{3,2},{4,5},{5,4},{6,7},{7,6},{8,9},{9,8},{10,11... | collective-permute-start | bytes 345608 | tf_op jit(solution)/shard_map/ppermute | solution.py:58
  66.4 19.0 %collective-permute-start.17 = (bf16[240,240]{1,0:T(8,128)(2,1)S(1)}, bf16[240,240]{1,0:T(8,128)(2,1)S(1)}, u32[]{:S(2)}, u32[]{:S(2)}) collective-permute-start(bf16[240,240]{1,0:T(8,128)(2,1)S(1)} %copy-done.54), channel_id=1, source_target_pairs={{0,2},{1,3},{2,0},{3,1},{4,6},{5,7},{6,4},{7,5},{8,10},{9,11},{10,... | collective-permute-start | bytes 345608 | tf_op jit(solution)/shard_map/ppermute | solution.py:58
  71.5 159.1 %reduce-scatter.2.cloned.1.call-start = ((), (), s32[]{:S(2)}) async-start(), calls=%async_computation.3 | async-start | bytes 2457600 | tf_op jit(solution)/shard_map/reduce_scatter | solution.py:819
  72.0 27.2 %collective-permute-start.15 = (bf16[768,640]{1,0:T(8,128)(2,1)}, bf16[768,640]{1,0:T(8,128)(2,1)S(1)}, u32[]{:S(2)}, u32[]{:S(2)}) collective-permute-start(bf16[768,640]{1,0:T(8,128)(2,1)} %stack_keys_values.1), channel_id=1, source_target_pairs={{0,4},{4,0},{1,5},{5,1},{2,6},{6,2},{3,7},{7,3},{8,12},{12,8},{9,1... | collective-permute-start | bytes 2949128 | tf_op jit(solution)/shard_map/ppermute | solution.py:58
  90.2 21.6 %collective-permute-start.19 = (bf16[720,240]{1,0:T(8,128)(2,1)}, bf16[720,240]{1,0:T(8,128)(2,1)S(1)}, u32[]{:S(2)}, u32[]{:S(2)}) collective-permute-start(bf16[720,240]{1,0:T(8,128)(2,1)} %stack_quarters.3.refs_4_.refs_10_), channel_id=1, source_target_pairs={{0,8},{4,12},{8,0},{12,4},{16,24},{20,28},{24,16},{28,20},{1,9},{5... | collective-permute-start | bytes 1036808 | tf_op jit(solution)/shard_map/ppermute | solution.py:67
  117.9 18.7 %collective-permute-start.24 = (bf16[192,960]{1,0:T(8,128)(2,1)}, bf16[192,960]{1,0:T(8,128)(2,1)S(1)}, u32[]{:S(2)}, u32[]{:S(2)}) collective-permute-start(bf16[192,960]{1,0:T(8,128)(2,1)} %get-tuple-element.138.refs_2_.refs_6_), channel_id=1, source_target_pairs={{0,20},{4,16},{8,28},{12,24},{16,4},{20,0},{24,12},{28,8},{1,21},{... | collective-permute-start | bytes 1105928 | tf_op jit(solution)/shard_map/ppermute | solution.py:67
  119.1 18.7 %collective-permute-start.25 = (bf16[192,960]{1,0:T(8,128)(2,1)}, bf16[192,960]{1,0:T(8,128)(2,1)S(1)}, u32[]{:S(2)}, u32[]{:S(2)}) collective-permute-start(bf16[192,960]{1,0:T(8,128)(2,1)} %get-tuple-element.138.refs_2_.refs_6_), channel_id=1, source_target_pairs={{0,8},{4,12},{8,0},{12,4},{16,24},{20,28},{24,16},{28,20},{1,9},{5... | collective-permute-start | bytes 1105928 | tf_op jit(solution)/shard_map/ppermute | solution.py:67
  161.2 18.4 %collective-permute-start.32 = (bf16[192,960]{1,0:T(8,128)(2,1)S(1)}, bf16[192,960]{1,0:T(8,128)(2,1)S(1)}, u32[]{:S(2)}, u32[]{:S(2)}) collective-permute-start(bf16[192,960]{1,0:T(8,128)(2,1)S(1)} %get-tuple-element.209), channel_id=1, source_target_pairs={{0,20},{4,16},{8,28},{12,24},{16,4},{20,0},{24,12},{28,8},{1,21},{... | collective-permute-start | bytes 1105928 | tf_op jit(solution)/shard_map/ppermute | solution.py:67
  200.1 23.7 %collective-permute-start.34 = (bf16[4,192,640]{2,1,0:T(8,128)(2,1)}, bf16[4,192,640]{2,1,0:T(8,128)(2,1)S(1)}, u32[]{:S(2)}, u32[]{:S(2)}) collective-permute-start(bf16[4,192,640]{2,1,0:T(8,128)(2,1)} %get-tuple-element.165), channel_id=1, source_target_pairs={{0,4},{4,0},{1,5},{5,1},{2,6},{6,2},{3,7},{7,3},{8,12},{12,8},{9,1... | collective-permute-start | bytes 2949128 | tf_op jit(solution)/shard_map/ppermute | solution.py:58
  200.7 23.2 %collective-permute-start.35 = (bf16[2,192,960]{2,1,0:T(8,128)(2,1)S(1)}, bf16[2,192,960]{2,1,0:T(8,128)(2,1)}, u32[]{:S(2)}, u32[]{:S(2)}) collective-permute-start(bf16[2,192,960]{2,1,0:T(8,128)(2,1)S(1)} %add_convert_fusion.1), channel_id=1, source_target_pairs={{0,16},{4,20},{8,24},{12,28},{16,0},{20,4},{24,8},{28,12},{1,17},{... | collective-permute-start | bytes 2211848 | tf_op jit(solution)/shard_map/ppermute | solution.py:67
  228.9 17.4 %collective-permute-start.38 = (bf16[192,640]{1,0:T(8,128)(2,1)}, bf16[192,640]{1,0:T(8,128)(2,1)}, u32[]{:S(2)}, u32[]{:S(2)}) collective-permute-start(bf16[192,640]{1,0:T(8,128)(2,1)} %get-tuple-element.221), channel_id=1, source_target_pairs={{0,2},{1,3},{2,0},{3,1},{4,6},{5,7},{6,4},{7,5},{8,10},{9,11},{10,... | collective-permute-start | bytes 737288 | tf_op jit(solution)/shard_map/ppermute | solution.py:58
  230.4 22.1 %collective-permute-start.39 = (bf16[192,640]{1,0:T(8,128)(2,1)}, bf16[192,640]{1,0:T(8,128)(2,1)}, u32[]{:S(2)}, u32[]{:S(2)}) collective-permute-start(bf16[192,640]{1,0:T(8,128)(2,1)} %get-tuple-element.220), channel_id=1, source_target_pairs={{0,3},{1,2},{2,1},{3,0},{4,7},{5,6},{6,5},{7,4},{8,11},{9,10},{10,... | collective-permute-start | bytes 737288 | tf_op jit(solution)/shard_map/ppermute | solution.py:58
  232.0 30.2 %collective-permute-start.40 = (bf16[960,480]{1,0:T(8,128)(2,1)S(1)}, bf16[960,480]{1,0:T(8,128)(2,1)S(1)}, u32[]{:S(2)}, u32[]{:S(2)}) collective-permute-start(bf16[960,480]{1,0:T(8,128)(2,1)S(1)} %fusion), channel_id=1, source_target_pairs={{0,16},{4,20},{8,24},{12,28},{16,0},{20,4},{24,8},{28,12},{1,17},{... | collective-permute-start | bytes 2764808 | tf_op jit(solution)/shard_map/ppermute | solution.py:67
  263.6 35.2 %collective-permute-start.45 = (bf16[2,240,480]{2,1,0:T(8,128)(2,1)S(1)}, bf16[2,240,480]{2,1,0:T(8,128)(2,1)S(1)}, u32[]{:S(2)}, u32[]{:S(2)}) collective-permute-start(bf16[2,240,480]{2,1,0:T(8,128)(2,1)S(1)} %pad_maximum_fusion), channel_id=1, source_target_pairs={{0,2},{1,3},{2,0},{3,1},{4,6},{5,7},{6,4},{7,5},{8,10},{9,11},{10,... | collective-permute-start | bytes 1382408 | tf_op jit(solution)/shard_map/ppermute | solution.py:58
  263.7 33.7 %collective-permute-start.44 = (bf16[336,240]{1,0:T(8,128)(2,1)S(1)}, bf16[336,240]{1,0:T(8,128)(2,1)S(1)}, u32[]{:S(2)}, u32[]{:S(2)}) collective-permute-start(bf16[336,240]{1,0:T(8,128)(2,1)S(1)} %get-tuple-element.189), channel_id=1, source_target_pairs={{0,3},{1,2},{2,1},{3,0},{4,7},{5,6},{6,5},{7,4},{8,11},{9,10},{10,... | collective-permute-start | bytes 483848 | tf_op jit(solution)/shard_map/ppermute | solution.py:58
  265.2 33.5 %collective-permute-start.43 = (bf16[336,240]{1,0:T(8,128)(2,1)S(1)}, bf16[336,240]{1,0:T(8,128)(2,1)S(1)}, u32[]{:S(2)}, u32[]{:S(2)}) collective-permute-start(bf16[336,240]{1,0:T(8,128)(2,1)S(1)} %get-tuple-element.188), channel_id=1, source_target_pairs={{0,2},{1,3},{2,0},{3,1},{4,6},{5,7},{6,4},{7,5},{8,10},{9,11},{10,... | collective-permute-start | bytes 483848 | tf_op jit(solution)/shard_map/ppermute | solution.py:58
  268.4 30.3 %collective-permute-start.42 = (bf16[336,240]{1,0:T(8,128)(2,1)S(1)}, bf16[336,240]{1,0:T(8,128)(2,1)S(1)}, u32[]{:S(2)}, u32[]{:S(2)}) collective-permute-start(bf16[336,240]{1,0:T(8,128)(2,1)S(1)} %get-tuple-element.187), channel_id=1, source_target_pairs={{0,1},{1,0},{2,3},{3,2},{4,5},{5,4},{6,7},{7,6},{8,9},{9,8},{10,11... | collective-permute-start | bytes 483848 | tf_op jit(solution)/shard_map/ppermute | solution.py:58
  271.7 47.8 %collective-permute-start.48 = (bf16[240,960]{1,0:T(8,128)(2,1)S(1)}, bf16[240,960]{1,0:T(8,128)(2,1)S(1)}, u32[]{:S(2)}, u32[]{:S(2)}) collective-permute-start(bf16[240,960]{1,0:T(8,128)(2,1)S(1)} %copy-done.21), channel_id=1, source_target_pairs={{0,4},{4,0},{8,12},{12,8},{16,20},{20,16},{24,28},{28,24},{1,5},{5... | collective-permute-start | bytes 1382408 | tf_op jit(solution)/shard_map/ppermute | solution.py:67
  297.4 22.1 %collective-permute-start.49 = (bf16[240,960]{1,0:T(8,128)(2,1)S(1)}, bf16[240,960]{1,0:T(8,128)(2,1)S(1)}, u32[]{:S(2)}, u32[]{:S(2)}) collective-permute-start(bf16[240,960]{1,0:T(8,128)(2,1)S(1)} %collective-permute-done.46.refs_4_), channel_id=1, source_target_pairs={{0,4},{4,0},{8,12},{12,8},{16,20},{20,16},{24,28},{28,24},{1,5},{5... | collective-permute-start | bytes 1382408 | tf_op jit(solution)/shard_map/ppermute | solution.py:67
  300.8 37.0 %collective-permute-start.58 = (bf16[240,960]{1,0:T(8,128)(2,1)S(1)}, bf16[240,960]{1,0:T(8,128)(2,1)S(1)}, u32[]{:S(2)}, u32[]{:S(2)}) collective-permute-start(bf16[240,960]{1,0:T(8,128)(2,1)S(1)} %copy-done.21), channel_id=1, source_target_pairs={{0,8},{4,12},{8,0},{12,4},{16,24},{20,28},{24,16},{28,20},{1,9},{5... | collective-permute-start | bytes 1382408 | tf_op jit(solution)/shard_map/ppermute | solution.py:67
  304.1 17.9 %collective-permute-start.53 = (bf16[1,240,480]{2,1,0:T(8,128)(2,1)S(1)}, bf16[1,240,480]{2,1,0:T(8,128)(2,1)S(1)}, u32[]{:S(2)}, u32[]{:S(2)}) collective-permute-start(bf16[1,240,480]{2,1,0:T(8,128)(2,1)S(1)} %bitcast.91), channel_id=1, source_target_pairs={{0,1},{1,0},{2,3},{3,2},{4,5},{5,4},{6,7},{7,6},{8,9},{9,8},{10,11... | collective-permute-start | bytes 691208 | tf_op jit(solution)/shard_map/ppermute | solution.py:58
  315.9 27.4 %collective-permute-start.60 = (bf16[240,960]{1,0:T(8,128)(2,1)S(1)}, bf16[240,960]{1,0:T(8,128)(2,1)S(1)}, u32[]{:S(2)}, u32[]{:S(2)}) collective-permute-start(bf16[240,960]{1,0:T(8,128)(2,1)S(1)} %collective-permute-done.46.refs_4_), channel_id=1, source_target_pairs={{0,8},{4,12},{8,0},{12,4},{16,24},{20,28},{24,16},{28,20},{1,9},{5... | collective-permute-start | bytes 1382408 | tf_op jit(solution)/shard_map/ppermute | solution.py:67
  319.5 23.8 %collective-permute-start.59 = (bf16[240,960]{1,0:T(8,128)(2,1)S(1)}, bf16[240,960]{1,0:T(8,128)(2,1)S(1)}, u32[]{:S(2)}, u32[]{:S(2)}) collective-permute-start(bf16[240,960]{1,0:T(8,128)(2,1)S(1)} %collective-permute-done.48.refs_1_), channel_id=1, source_target_pairs={{0,8},{4,12},{8,0},{12,4},{16,24},{20,28},{24,16},{28,20},{1,9},{5... | collective-permute-start | bytes 1382408 | tf_op jit(solution)/shard_map/ppermute | solution.py:67
  322.0 21.3 %collective-permute-start.61 = (bf16[240,960]{1,0:T(8,128)(2,1)S(1)}, bf16[240,960]{1,0:T(8,128)(2,1)S(1)}, u32[]{:S(2)}, u32[]{:S(2)}) collective-permute-start(bf16[240,960]{1,0:T(8,128)(2,1)S(1)} %collective-permute-done.49.refs_5_), channel_id=1, source_target_pairs={{0,8},{4,12},{8,0},{12,4},{16,24},{20,28},{24,16},{28,20},{1,9},{5... | collective-permute-start | bytes 1382408 | tf_op jit(solution)/shard_map/ppermute | solution.py:67
  (90 other events, 770.6 us)
Sparse Core Ops, SparseCore 0:
  9.9 33.7 all-gather.2
  71.6 43.1 all-gather.4
  187.5 40.0 reduce-scatter.1

commit v8 on v7

--- a/solution.py
+++ b/solution.py
@@ -261,10 +261,24 @@
     gains_ref[0:2, :] = jnp.concatenate([gain_blocks[z][0:2, :] for z in range(shards)], axis=1)
 
 
+def repeat(count, step, state):
+    if count > 2:
+        return lax.fori_loop(0, count, step, state)
+    for j in range(count):
+        state = step(j, state)
+    return state
+
+
+def rows_at(j, chunk):
+    if isinstance(j, int):
+        return slice(j * chunk, (j + 1) * chunk)
+    return pl.ds(pl.multiple_of(j * chunk, chunk), chunk)
+
+
 def attend(chunk, head, kv_ref, key_pos_ref, query_pos, stacked, state):
     def step(j, state):
         largest, total, weighted = state
-        at = pl.ds(pl.multiple_of(j * chunk, chunk), chunk)
+        at = rows_at(j, chunk)
         keys = heads_of(kv_ref, head, 1, at)
         values = heads_of(kv_ref, KV_HEADS + head, 1, at)
         scores = dot_last(keys, stacked)
@@ -276,7 +290,7 @@
         weighted = weighted * factor + dot_first(values, weights.astype(BF16))
         return new_largest, total, weighted
 
-    return lax.fori_loop(0, kv_ref.shape[0] // chunk, step, state)
+    return repeat(kv_ref.shape[0] // chunk, step, state)
 
 
 def near_kernel(chunk, members, pieces, spots, *refs):
@@ -501,7 +515,7 @@
 
         def step(j, query_grad, head=head, stacked=stacked, upstream=upstream,
                  delta=delta, log_total=log_total, keys_at=keys_at, values_at=values_at):
-            at = pl.ds(pl.multiple_of(j * chunk, chunk), chunk)
+            at = rows_at(j, chunk)
             keys = heads_of(kv_ref, head, 1, at)
             values = heads_of(kv_ref, KV_HEADS + head, 1, at)
             scores = dot_last(keys, stacked)
@@ -516,7 +530,7 @@
             return query_grad + dot_first(keys, score_grad)
 
         start = jnp.zeros((HEAD_DIM, columns), F32) if first else start_ref[head]
-        query_grad = lax.fori_loop(0, kv_ref.shape[0] // chunk, step, start)
+        query_grad = repeat(kv_ref.shape[0] // chunk, step, start)
         if not last:
             query_grad_ref[head] = query_grad
         else:
@@ -733,9 +747,9 @@
     near = [kv_own] + direct_fsdp(kv_own)
     query_pieces = lax.optimization_barrier((kv_own, *query_pieces))[1:]
     stacked, across = stack(query_pieces)
+    output_quarter = after(output_quarter, near[1])
     across, *near = lax.optimization_barrier((across, *near))
     query_stacks = four(stacked, across)
-    output_quarter, near[-1] = lax.optimization_barrier((output_quarter, near[-1]))
     output_pieces = direct_fsdp(output_quarter)
     (near_all,) = call(
         stack_kernel, spots, near, [((near_count, 2 * kv_width), BF16)],
@@ -928,7 +942,6 @@
     query_low, pack_share, *_ = lax.optimization_barrier(
         (query_low, pack_share, *kv_sums.values())
     )
-    share_across = swap_plane(pack_share, 2, 0)
 
     weights_away = swap_core(weights_send)
     weights_sent, weights_terms = sum_x(weights_keep, weights_away)
@@ -939,8 +952,10 @@
         scratch=[((dp_count, rows, quarter), BF16), ((shards, rows, weight_rows), F32)],
         name="query_back",
     )
-    share_along = swap_plane(pack_share, 0, 1)
-    share_diagonal = swap_plane(share_across, 0, 1)
+    query_back, share_along = lax.optimization_barrier(
+        (query_back, swap_plane(pack_share, 0, 1))
+    )
+    share_across = swap_plane(after(pack_share, weights_sent), 2, 0)
     span = kv_width + EXTRA_ROWS
     packed_shape = ((shards, span, weight_rows), BF16)
     home_all = far_grads[0]
@@ -966,18 +981,11 @@
         for r in range(shards)
     ]
     weights_pieces, *pieces = lax.optimization_barrier((weights_pieces, *pieces))
+    share_across = lax.optimization_barrier((share_across, *pieces))[0]
+    share_a = [pack_share, share_along, share_across, swap_plane(share_across, 0, 1)]
+    share_b = [swap_core(piece) for piece in share_a]
     kv_share = sum_z(pieces)
     weights_half = halve_z(weights_pieces, shards // 2)
-    kv_share, weights_half, share_across = lax.optimization_barrier(
-        (kv_share, weights_half, share_across)
-    )
-    kv_share = sum_swap(kv_share, 2, 0)
-    kv_share, share_along, share_diagonal, result_along = lax.optimization_barrier(
-        (kv_share, share_along, share_diagonal, result_along)
-    )
-    share_a = [pack_share, share_along, share_across, share_diagonal]
-    share_b = [swap_core(piece) for piece in share_a]
-
     share_by_mask = [None] * members
     for k, (a, b) in enumerate(((0, 0),) + CHIP_MASKS):
         share_by_mask[2 * a + b] = share_a[k]
@@ -991,6 +999,12 @@
         scratch=[((members, weight_rows, 3 * part), BF16)],
         name="feed_forward_out",
     )
+    kv_share, weights_half = lax.optimization_barrier((kv_share, weights_half))
+    kv_share, result_along, *big = lax.optimization_barrier(
+        (sum_swap(kv_share, 2, 0), result_along, gate_weight_grad, up_weight_grad,
+         down_weight_grad)
+    )
+    gate_weight_grad, up_weight_grad, down_weight_grad = big
     span = shards // 2
     while span > 1:
         span //= 2

time: 368 us -> 355 us (0.965)
  the two profiles are of different devices: /device:TPU:17 before, /device:TPU:0 now
where the time goes in v8:
time: 355 us; the launch traced here: 349 us
  Pallas kernels  118 us (33%)
  waiting for transfers between devices  115 us (32%)
  starting transfers between devices  66.7 us (19%)
  local copies, waits for them, and re-layouts  20.5 us (6%)
  between operations  15.6 us (4%)
  other arithmetic  14.2 us (4%)
    pallas_call x20, Pallas kernels, call(): pl.pallas_call(kernel, out_shape=outs, in_specs=specs, out_specs=tuple((p...  118 us
    ppermute x22, waiting for transfers between devices, swap(): return lax.ppermute(x, axis, [(i, i ^ mask) for i in range(count)])  65.7 us
    ppermute x40, waiting for transfers between devices, swap_plane(): return lax.ppermute(x, ('dp', 'ctx'), pairs)  44.9 us
    ppermute x22, starting transfers between devices, swap(): return lax.ppermute(x, axis, [(i, i ^ mask) for i in range(count)])  42.8 us
    ppermute x40, starting transfers between devices, swap_plane(): return lax.ppermute(x, ('dp', 'ctx'), pairs)  23.6 us
    unnamed x122, local copies, waits for them, and re-layouts  12.5 us
  transfers between devices with their start and end apart: 65, of which 21 were waited for; matrix products, arithmetic and copies ran while one was open for 6% of the time, Pallas kernels for 29%

profile of v8, /device:TPU:0, one launch (start us, length us, event | category | flops | bytes accessed | tf_op | source)
XLA Modules:
  0.0 349.5 jit_solution(7292013731268292570)
XLA Ops:
  19.5 3.5 collective-permute-start.7
  24.9 4.2 %pack_weights.1 = bf16[240,960]{1,0:T(8,128)(2,1)} custom-call(s32[4]{0:T(128)} %pad_add_fusion.1.spots, bf16[240,2560]{1,0:T(8,128)(2,1)} %gate_ref.1, bf16[240,2560]{1,0:T(8,128)(2,1)} %up_ref.1, bf16[960,640]{1,0:T(8,128)(2,1)} %bitcast.98), custom_call_target="tpu_custom_call" | custom-call | flops 4600000000 | tf_op jit(solution)/shard_map/pack_weights/pallas_call | solution.py:106
  31.3 4.2 %collective-permute-start.8 = (bf16[240,240]{1,0:T(8,128)(2,1)S(1)}, bf16[240,240]{1,0:T(8,128)(2,1)S(1)}, u32[]{:S(2)}, u32[]{:S(2)}) collective-permute-start(bf16[240,240]{1,0:T(8,128)(2,1)S(1)} %copy-done.59), channel_id=1, source_target_pairs={{0,3},{1,2},{2,1},{3,0},{4,7},{5,6},{6,5},{7,4},{8,11},{9,10},{10,... | collective-permute-start | bytes 345608 | tf_op jit(solution)/shard_map/ppermute | solution.py:58
  36.3 3.7 %norm_keys_values.1 = (bf16[192,640]{1,0:T(8,128)(2,1)}, bf16[192,960]{1,0:T(8,128)(2,1)}, bf16[192,960]{1,0:T(8,128)(2,1)}, f32[192,1]{1,0:T(8,128)}, f32[8,960]{1,0:T(8,128)}) custom-call(s32[4]{0:T(128)} %pad_add_fusion.1.spots, bf16[192,960]{1,0:T(8,128)(2,1)} %bitcast.99, bf16[1,240]{1,0:T(2,128)(2,1)} %copy-done.22, bf16[1,240]{1,0:T(2,128)(2,1)} %copy-done.21, ...), custom_call_target="tpu_custom_call" | custom-call | flops 4600000000 | tf_op jit(solution)/shard_map/norm_keys_values/pallas_call | solution.py:106
  49.9 3.5 collective-permute-done.11.refs_11_.refs_1_.refs_10_
  53.4 9.9 %collective-permute-done.12.refs_12_.refs_2_.refs_11_ = bf16[192,640]{1,0:T(8,128)(2,1)S(1)} collective-permute-done((bf16[192,640]{1,0:T(8,128)(2,1)}, bf16[192,640]{1,0:T(8,128)(2,1)S(1)}, u32[]{:S(2)}, u32[]{:S(2)}) %collective-permute-start.12) | collective-permute-done | bytes 245792 | tf_op jit(solution)/shard_map/ppermute | solution.py:58
  65.1 4.8 %collective-permute-start.16 = (bf16[240,240]{1,0:T(8,128)(2,1)S(1)}, bf16[240,240]{1,0:T(8,128)(2,1)S(1)}, u32[]{:S(2)}, u32[]{:S(2)}) collective-permute-start(bf16[240,240]{1,0:T(8,128)(2,1)S(1)} %copy-done.58), channel_id=1, source_target_pairs={{0,1},{1,0},{2,3},{3,2},{4,5},{5,4},{6,7},{7,6},{8,9},{9,8},{10,11... | collective-permute-start | bytes 345608 | tf_op jit(solution)/shard_map/ppermute | solution.py:58
  77.3 8.8 %attention_near.1 = (bf16[192,960]{1,0:T(8,128)(2,1)}, f32[5,576]{1,0:T(8,128)}, f32[5,576]{1,0:T(8,128)}, f32[5,64,576]{2,1,0:T(8,128)}) custom-call(s32[4]{0:T(128)} %pad_add_fusion.1.spots, bf16[192,960]{1,0:T(8,128)(2,1)} %get-tuple-element.116.refs_0_, s32[768,1]{1,0:T(8,128)} %slice.124.refs_1_, s32[1,576]{1,0:T(1,128)} %broadcast_in_dim.29.refs_2_, ...), custom_call_target="tpu_custom_call" | custom-call | flops 13799999488 | tf_op jit(solution)/shard_map/attention_near/pallas_call | solution.py:106
  91.1 7.8 %collective-permute-done.20.refs_6_.refs_12_ = bf16[720,240]{1,0:T(8,128)(2,1)S(1)} collective-permute-done((bf16[720,240]{1,0:T(8,128)(2,1)}, bf16[720,240]{1,0:T(8,128)(2,1)S(1)}, u32[]{:S(2)}, u32[]{:S(2)}) %collective-permute-start.20) | collective-permute-done | bytes 345632 | tf_op jit(solution)/shard_map/ppermute | solution.py:67
  99.9 9.0 %attention_far.1 = (bf16[192,960]{1,0:T(8,128)(2,1)}, f32[5,64,576]{2,1,0:T(8,128)}, f32[5,576]{1,0:T(8,128)}) custom-call(s32[4]{0:T(128)} %pad_add_fusion.1.spots, bf16[192,960]{1,0:T(8,128)(2,1)} %get-tuple-element.126.refs_0_, s32[768,1]{1,0:T(8,128)} %slice.125.refs_1_, s32[1,576]{1,0:T(1,128)} %broadcast_in_dim.29.refs_2_, ...), custom_call_target="tpu_custom_call" | custom-call | flops 13799999488 | tf_op jit(solution)/shard_map/attention_far/pallas_call | solution.py:106
  109.8 4.2 %project_residual.1 = (f32[192,960]{1,0:T(8,128)}, f32[192,1]{1,0:T(8,128)}, bf16[192,960]{1,0:T(8,128)(2,1)}) custom-call(s32[4]{0:T(128)} %pad_add_fusion.1.spots, bf16[192,960]{1,0:T(8,128)(2,1)} %get-tuple-element.130.refs_0_, bf16[192,960]{1,0:T(8,128)(2,1)} %bitcast.100, f32[8,960]{1,0:T(8,128)} %get-tuple-element.131.refs_2_.refs_8_.refs_5_, ...), custom_call_target="tpu_custom_call" | custom-call | flops 2300000000 | tf_op jit(solution)/shard_map/project_residual/pallas_call | solution.py:106
  117.5 8.2 %collective-permute-done.22.refs_3_.refs_7_ = bf16[192,960]{1,0:T(8,128)(2,1)S(1)} collective-permute-done((bf16[192,960]{1,0:T(8,128)(2,1)}, bf16[192,960]{1,0:T(8,128)(2,1)S(1)}, u32[]{:S(2)}, u32[]{:S(2)}) %collective-permute-start.22) | collective-permute-done | bytes 368672 | tf_op jit(solution)/shard_map/ppermute | solution.py:67
  127.7 7.6 %collective-permute-done.24.refs_5_.refs_9_ = bf16[192,960]{1,0:T(8,128)(2,1)S(1)} collective-permute-done((bf16[192,960]{1,0:T(8,128)(2,1)}, bf16[192,960]{1,0:T(8,128)(2,1)S(1)}, u32[]{:S(2)}, u32[]{:S(2)}) %collective-permute-start.24) | collective-permute-done | bytes 368672 | tf_op jit(solution)/shard_map/ppermute | solution.py:67
  137.8 8.5 %feed_forward.3 = (bf16[4,192,960]{2,1,0:T(8,128)(2,1)}, bf16[768,320]{1,0:T(8,128)(2,1)}, bf16[768,640]{1,0:T(8,128)(2,1)}) custom-call(s32[4]{0:T(128)} %pad_add_fusion.1.spots, bf16[960,960]{1,0:T(8,128)(2,1)} %all-gather.5.cloned.1.call-done.refs_0_, bf16[8,192,960]{2,1,0:T(8,128)(2,1)} %all-gather.3.cloned.1.call-done.refs_1_.refs_5_, ...), custom_call_target="tpu_custom_call" | custom-call | flops 9200000000 | tf_op jit(solution)/shard_map/feed_forward/pallas_call | solution.py:106
  146.5 8.5 %feed_forward.2 = (bf16[4,192,960]{2,1,0:T(8,128)(2,1)}, bf16[768,320]{1,0:T(8,128)(2,1)}, bf16[768,640]{1,0:T(8,128)(2,1)}) custom-call(s32[4]{0:T(128)} %pad_add_fusion.1.spots, bf16[960,960]{1,0:T(8,128)(2,1)} %all-gather.5.cloned.1.call-done.refs_0_, bf16[8,192,960]{2,1,0:T(8,128)(2,1)} %all-gather.3.cloned.1.call-done.refs_1_.refs_5_, ...), custom_call_target="tpu_custom_call" | custom-call | flops 9200000000 | tf_op jit(solution)/shard_map/feed_forward/pallas_call | solution.py:106
  160.9 12.1 %feed_forward_weights.1 = (bf16[4,192,960]{2,1,0:T(8,128)(2,1)}, bf16[4,192,960]{2,1,0:T(8,128)(2,1)}, bf16[960,960]{1,0:T(8,128)(2,1)}) custom-call(s32[4]{0:T(128)} %pad_add_fusion.1.spots, bf16[960,960]{1,0:T(8,128)(2,1)} %all-gather.5.cloned.1.call-done.refs_0_, bf16[768,320]{1,0:T(8,128)(2,1)} %get-tuple-element.144.refs_1_, ...), custom_call_target="tpu_custom_call" | custom-call | flops 13799999488 | tf_op jit(solution)/shard_map/feed_forward_weights/pallas_call | solution.py:106
  173.1 5.3 %collective-permute-done.32.refs_4_ = bf16[192,960]{1,0:T(8,128)(2,1)S(1)} collective-permute-done((bf16[192,960]{1,0:T(8,128)(2,1)S(1)}, bf16[192,960]{1,0:T(8,128)(2,1)S(1)}, u32[]{:S(2)}, u32[]{:S(2)}) %collective-permute-start.32) | collective-permute-done | bytes 368672 | tf_op jit(solution)/shard_map/ppermute | solution.py:67
  179.2 5.7 %residual_back.1 = (f32[192,960]{1,0:T(8,128)}, bf16[192,960]{1,0:T(8,128)(2,1)}, bf16[192,960]{1,0:T(8,128)(2,1)}, f32[1,960]{1,0:T(1,128)}) custom-call(s32[4]{0:T(128)} %pad_add_fusion.1.spots, bf16[4,192,960]{2,1,0:T(8,128)(2,1)} %get-tuple-element.141.refs_0_, bf16[4,192,960]{2,1,0:T(8,128)(2,1)} %copy-done.4, bf16[192,960]{1,0:T(8,128)(2,1)} %copy-done.37, ...), custom_call_target="tpu_custom_call" | custom-call | flops 6899999744 | tf_op jit(solution)/shard_map/residual_back/pallas_call | solution.py:106
  184.9 10.3 %attention_back_far.1 = (f32[5,64,576]{2,1,0:T(8,128)}, bf16[4,192,640]{2,1,0:T(8,128)(2,1)}) custom-call(s32[4]{0:T(128)} %pad_add_fusion.1.spots, bf16[192,960]{1,0:T(8,128)(2,1)} %get-tuple-element.126.refs_0_, s32[768,1]{1,0:T(8,128)} %slice.125.refs_1_, s32[1,576]{1,0:T(1,128)} %broadcast_in_dim.29.refs_2_, ...), custom_call_target="tpu_custom_call" | custom-call | flops 14949999616 | tf_op jit(solution)/shard_map/attention_back_far/pallas_call | solution.py:106
  197.6 10.5 %attention_back_near.1 = (bf16[192,960]{1,0:T(8,128)(2,1)}, bf16[192,640]{1,0:T(8,128)(2,1)}, bf16[192,640]{1,0:T(8,128)(2,1)}, bf16[192,640]{1,0:T(8,128)(2,1)}, bf16[192,640]{1,0:T(8,128)(2,1)}) custom-call(s32[4]{0:T(128)} %pad_add_fusion.1.spots, bf16[192,960]{1,0:T(8,128)(2,1)} %get-tuple-element.126.refs_0_, s32[768,1]{1,0:T(8,128)} %slice.124.refs_1_, ...), custom_call_target="tpu_custom_call" | custom-call | flops 16099999744 | tf_op jit(solution)/shard_map/attention_back_near/pallas_call | solution.py:106
  208.1 5.1 %query_output_weight_grads.1 = (bf16[2,960,480]{2,1,0:T(8,128)(2,1)}, bf16[2,960,480]{2,1,0:T(8,128)(2,1)}) custom-call(s32[4]{0:T(128)} %pad_add_fusion.1.spots, bf16[192,960]{1,0:T(8,128)(2,1)} %get-tuple-element.130.refs_0_, bf16[192,960]{1,0:T(8,128)(2,1)} %get-tuple-element.157.refs_1_, bf16[192,960]{1,0:T(8,128)(2,1)} %get-tuple-element.159.refs_2_, ...), custom_call_target="tpu_custom_call" | custom-call | tf_op jit(solution)/shard_map/query_output_weight_grads/pallas_call | solution.py:106
  213.2 6.3 %collective-permute-done.34.refs_12_ = bf16[4,192,640]{2,1,0:T(8,128)(2,1)S(1)} collective-permute-done((bf16[4,192,640]{2,1,0:T(8,128)(2,1)}, bf16[4,192,640]{2,1,0:T(8,128)(2,1)S(1)}, u32[]{:S(2)}, u32[]{:S(2)}) %collective-permute-start.34) | collective-permute-done | bytes 983072 | tf_op jit(solution)/shard_map/ppermute | solution.py:58
  221.5 3.3 reduce-scatter.2.cloned.1.call-done.refs_0_
  233.7 3.6 %query_back.1.refs_6_ = f32[192,960]{1,0:T(8,128)} custom-call(s32[4]{0:T(128)} %pad_add_fusion.1.spots, bf16[192,960]{1,0:T(8,128)(2,1)} %get-tuple-element.178.refs_3_.low_ref, bf16[240,960]{1,0:T(8,128)(2,1)} %local_ref.1, bf16[720,240]{1,0:T(8,128)(2,1)} %stack_quarters.2.refs_6_.refs_0_, bf16[720,240]{1,0:T(8,128)(2,1)} %copy-done.9, ...), custom_call_target="tpu_custom_call" | custom-call | tf_op jit(solution)/shard_map/query_back/pallas_call | solution.py:106
  238.1 9.4 %collective-permute-done.39.refs_14_ = bf16[192,640]{1,0:T(8,128)(2,1)S(1)} collective-permute-done((bf16[192,640]{1,0:T(8,128)(2,1)}, bf16[192,640]{1,0:T(8,128)(2,1)S(1)}, u32[]{:S(2)}, u32[]{:S(2)}) %collective-permute-start.39) | collective-permute-done | bytes 245792 | tf_op jit(solution)/shard_map/ppermute | solution.py:58
  248.3 6.2 %keys_values_back.1 = (f32[192,960]{1,0:T(8,128)}, bf16[4,336,240]{2,1,0:T(8,128)(2,1)}, bf16[4,336,240]{2,1,0:T(8,128)(2,1)}) custom-call(s32[4]{0:T(128)} %pad_add_fusion.1.spots, f32[192,128]{1,0:T(8,128)} %pad_maximum_fusion.2.refs_5_.refs_3_.refs_0_, f32[192,128]{1,0:T(8,128)} %pad_maximum_fusion.3.refs_6_.refs_4_.refs_1_, ...), custom_call_target="tpu_custom_call" | custom-call | flops 6899999744 | tf_op jit(solution)/shard_map/keys_values_back/pallas_call | solution.py:106
  259.7 5.1 %collective-permute-start.46 = (bf16[2,240,480]{2,1,0:T(8,128)(2,1)S(1)}, bf16[2,240,480]{2,1,0:T(8,128)(2,1)S(1)}, u32[]{:S(2)}, u32[]{:S(2)}) collective-permute-start(bf16[2,240,480]{2,1,0:T(8,128)(2,1)S(1)} %pad_maximum_fusion), channel_id=1, source_target_pairs={{0,2},{1,3},{2,0},{3,1},{4,6},{5,7},{6,4},{7,5},{8,10},{9,11},{10,... | collective-permute-start | bytes 1382408 | tf_op jit(solution)/shard_map/ppermute | solution.py:58
  269.8 12.2 %collective-permute-done.45 = bf16[336,240]{1,0:T(8,128)(2,1)S(1)} collective-permute-done((bf16[336,240]{1,0:T(8,128)(2,1)S(1)}, bf16[336,240]{1,0:T(8,128)(2,1)S(1)}, u32[]{:S(2)}, u32[]{:S(2)}) %collective-permute-start.45) | collective-permute-done | bytes 161312 | tf_op jit(solution)/shard_map/ppermute | solution.py:58
  282.0 18.9 %collective-permute-done.44 = bf16[336,240]{1,0:T(8,128)(2,1)S(1)} collective-permute-done((bf16[336,240]{1,0:T(8,128)(2,1)S(1)}, bf16[336,240]{1,0:T(8,128)(2,1)S(1)}, u32[]{:S(2)}, u32[]{:S(2)}) %collective-permute-start.44) | collective-permute-done | bytes 161312 | tf_op jit(solution)/shard_map/ppermute | solution.py:58
  306.7 5.2 %collective-permute-done.57 = bf16[1,240,480]{2,1,0:T(8,128)(2,1)S(1)} collective-permute-done((bf16[1,240,480]{2,1,0:T(8,128)(2,1)S(1)}, bf16[1,240,480]{2,1,0:T(8,128)(2,1)S(1)}, u32[]{:S(2)}, u32[]{:S(2)}) %collective-permute-start.57) | collective-permute-done | bytes 230432 | tf_op jit(solution)/shard_map/ppermute | solution.py:58
  315.1 6.7 %feed_forward_out.1 = (f32[240,2560]{1,0:T(8,128)}, f32[240,2560]{1,0:T(8,128)}, f32[960,640]{1,0:T(8,128)}) custom-call(s32[4]{0:T(128)} %pad_add_fusion.1.spots, bf16[240,960]{1,0:T(8,128)(2,1)} %reduce-scatter.2.cloned.1.call-done.refs_0_, bf16[240,960]{1,0:T(8,128)(2,1)} %collective-permute-done.37.refs_1_, bf16[240,960]{1,0:T(8,128)(2,1)} %copy-done.27, ...), custom_call_target="tpu_custom_call" | custom-call | flops 8049999872 | tf_op jit(solution)/shard_map/feed_forward_out/pallas_call | solution.py:106
  324.5 4.7 %collective-permute-done.58 = bf16[240,480]{1,0:T(8,128)(2,1)S(1)} collective-permute-done((bf16[240,480]{1,0:T(8,128)(2,1)S(1)}, bf16[240,480]{1,0:T(8,128)(2,1)S(1)}, u32[]{:S(2)}, u32[]{:S(2)}) %collective-permute-start.58) | collective-permute-done | bytes 230432 | tf_op jit(solution)/shard_map/ppermute | solution.py:67
  (288 shorter events, 106.6 us)
Async XLA Ops:
  7.2 67.5 %all-gather.3.cloned.1.call-start = ((), (), s32[]{:S(2)}) async-start(), calls=%async_computation.1 | async-start | bytes 3538944 | tf_op jit(solution)/shard_map/all_gather | solution.py:711
  7.9 129.1 %all-gather.5.cloned.1.call-start = ((), (), s32[]{:S(2)}) async-start(), calls=%async_computation.2 | async-start | bytes 2457600 | tf_op jit(solution)/shard_map/all_gather | solution.py:761
  10.4 19.5 %collective-permute-start = (bf16[336,240]{1,0:T(8,128)(2,1)S(1)}, bf16[336,240]{1,0:T(8,128)(2,1)S(1)}, u32[]{:S(2)}, u32[]{:S(2)}) collective-permute-start(bf16[336,240]{1,0:T(8,128)(2,1)S(1)} %pad_maximum_fusion.1), channel_id=1, source_target_pairs={{0,1},{1,0},{2,3},{3,2},{4,5},{5,4},{6,7},{7,6},{8,9},{9,8},{10,11... | collective-permute-start | bytes 483848 | tf_op jit(solution)/shard_map/ppermute | solution.py:58
  13.5 16.4 %collective-permute-start.1 = (bf16[336,240]{1,0:T(8,128)(2,1)S(1)}, bf16[336,240]{1,0:T(8,128)(2,1)S(1)}, u32[]{:S(2)}, u32[]{:S(2)}) collective-permute-start(bf16[336,240]{1,0:T(8,128)(2,1)S(1)} %pad_maximum_fusion.1), channel_id=1, source_target_pairs={{0,2},{1,3},{2,0},{3,1},{4,6},{5,7},{6,4},{7,5},{8,10},{9,11},{10,... | collective-permute-start | bytes 483848 | tf_op jit(solution)/shard_map/ppermute | solution.py:58
  18.6 24.2 %collective-permute-start.6 = (bf16[240,240]{1,0:T(8,128)(2,1)}, bf16[240,240]{1,0:T(8,128)(2,1)S(1)}, u32[]{:S(2)}, u32[]{:S(2)}) collective-permute-start(bf16[240,240]{1,0:T(8,128)(2,1)} %get-tuple-element.114), channel_id=1, source_target_pairs={{0,1},{1,0},{2,3},{3,2},{4,5},{5,4},{6,7},{7,6},{8,9},{9,8},{10,11... | collective-permute-start | bytes 345608 | tf_op jit(solution)/shard_map/ppermute | solution.py:58
  19.5 25.7 %collective-permute-start.7 = (bf16[240,240]{1,0:T(8,128)(2,1)}, bf16[240,240]{1,0:T(8,128)(2,1)S(1)}, u32[]{:S(2)}, u32[]{:S(2)}) collective-permute-start(bf16[240,240]{1,0:T(8,128)(2,1)} %get-tuple-element.114), channel_id=1, source_target_pairs={{0,2},{1,3},{2,0},{3,1},{4,6},{5,7},{6,4},{7,5},{8,10},{9,11},{10,... | collective-permute-start | bytes 345608 | tf_op jit(solution)/shard_map/ppermute | solution.py:58
  42.8 20.5 %collective-permute-start.12 = (bf16[192,640]{1,0:T(8,128)(2,1)}, bf16[192,640]{1,0:T(8,128)(2,1)S(1)}, u32[]{:S(2)}, u32[]{:S(2)}) collective-permute-start(bf16[192,640]{1,0:T(8,128)(2,1)} %get-tuple-element.122.refs_10_.refs_0_.refs_9_), channel_id=1, source_target_pairs={{0,2},{1,3},{2,0},{3,1},{4,6},{5,7},{6,4},{7,5},{8,10},{9,11},{10,... | collective-permute-start | bytes 737288 | tf_op jit(solution)/shard_map/ppermute | solution.py:58
  42.8 20.5 %collective-permute-start.13 = (bf16[192,640]{1,0:T(8,128)(2,1)}, bf16[192,640]{1,0:T(8,128)(2,1)S(1)}, u32[]{:S(2)}, u32[]{:S(2)}) collective-permute-start(bf16[192,640]{1,0:T(8,128)(2,1)} %get-tuple-element.122.refs_10_.refs_0_.refs_9_), channel_id=1, source_target_pairs={{0,3},{1,2},{2,1},{3,0},{4,7},{5,6},{6,5},{7,4},{8,11},{9,10},{10,... | collective-permute-start | bytes 737288 | tf_op jit(solution)/shard_map/ppermute | solution.py:58
  48.3 14.9 %collective-permute-start.10 = (bf16[720,240]{1,0:T(8,128)(2,1)}, bf16[720,240]{1,0:T(8,128)(2,1)S(1)}, u32[]{:S(2)}, u32[]{:S(2)}) collective-permute-start(bf16[720,240]{1,0:T(8,128)(2,1)} %stack_quarters.2.refs_6_.refs_0_), channel_id=1, source_target_pairs={{0,16},{4,20},{8,24},{12,28},{16,0},{20,4},{24,8},{28,12},{1,17},{... | collective-permute-start | bytes 1036808 | tf_op jit(solution)/shard_map/ppermute | solution.py:67
  49.9 25.0 %collective-permute-start.9 = (bf16[720,240]{1,0:T(8,128)(2,1)}, bf16[720,240]{1,0:T(8,128)(2,1)S(1)}, u32[]{:S(2)}, u32[]{:S(2)}) collective-permute-start(bf16[720,240]{1,0:T(8,128)(2,1)} %stack_quarters.2.refs_6_.refs_0_), channel_id=1, source_target_pairs={{0,8},{4,12},{8,0},{12,4},{16,24},{20,28},{24,16},{28,20},{1,9},{5... | collective-permute-start | bytes 1036808 | tf_op jit(solution)/shard_map/ppermute | solution.py:67
  65.1 21.0 %collective-permute-start.16 = (bf16[240,240]{1,0:T(8,128)(2,1)S(1)}, bf16[240,240]{1,0:T(8,128)(2,1)S(1)}, u32[]{:S(2)}, u32[]{:S(2)}) collective-permute-start(bf16[240,240]{1,0:T(8,128)(2,1)S(1)} %copy-done.58), channel_id=1, source_target_pairs={{0,1},{1,0},{2,3},{3,2},{4,5},{5,4},{6,7},{7,6},{8,9},{9,8},{10,11... | collective-permute-start | bytes 345608 | tf_op jit(solution)/shard_map/ppermute | solution.py:58
  69.9 16.1 %collective-permute-start.17 = (bf16[240,240]{1,0:T(8,128)(2,1)S(1)}, bf16[240,240]{1,0:T(8,128)(2,1)S(1)}, u32[]{:S(2)}, u32[]{:S(2)}) collective-permute-start(bf16[240,240]{1,0:T(8,128)(2,1)S(1)} %copy-done.58), channel_id=1, source_target_pairs={{0,2},{1,3},{2,0},{3,1},{4,6},{5,7},{6,4},{7,5},{8,10},{9,11},{10,... | collective-permute-start | bytes 345608 | tf_op jit(solution)/shard_map/ppermute | solution.py:58
  69.9 16.2 %collective-permute-start.18 = (bf16[240,240]{1,0:T(8,128)(2,1)S(1)}, bf16[240,240]{1,0:T(8,128)(2,1)S(1)}, u32[]{:S(2)}, u32[]{:S(2)}) collective-permute-start(bf16[240,240]{1,0:T(8,128)(2,1)S(1)} %copy-done.58), channel_id=1, source_target_pairs={{0,3},{1,2},{2,1},{3,0},{4,7},{5,6},{6,5},{7,4},{8,11},{9,10},{10,... | collective-permute-start | bytes 345608 | tf_op jit(solution)/shard_map/ppermute | solution.py:58
  74.7 150.2 %reduce-scatter.2.cloned.1.call-start = ((), (), s32[]{:S(2)}) async-start(), calls=%async_computation.3 | async-start | bytes 2457600 | tf_op jit(solution)/shard_map/reduce_scatter | solution.py:833
  74.9 24.0 %collective-permute-start.15 = (bf16[768,640]{1,0:T(8,128)(2,1)}, bf16[768,640]{1,0:T(8,128)(2,1)S(1)}, u32[]{:S(2)}, u32[]{:S(2)}) collective-permute-start(bf16[768,640]{1,0:T(8,128)(2,1)} %stack_keys_values.1), channel_id=1, source_target_pairs={{0,4},{4,0},{1,5},{5,1},{2,6},{6,2},{3,7},{7,3},{8,12},{12,8},{9,1... | collective-permute-start | bytes 2949128 | tf_op jit(solution)/shard_map/ppermute | solution.py:58
  91.1 17.8 %collective-permute-start.19 = (bf16[720,240]{1,0:T(8,128)(2,1)}, bf16[720,240]{1,0:T(8,128)(2,1)S(1)}, u32[]{:S(2)}, u32[]{:S(2)}) collective-permute-start(bf16[720,240]{1,0:T(8,128)(2,1)} %stack_quarters.3.refs_4_.refs_10_), channel_id=1, source_target_pairs={{0,8},{4,12},{8,0},{12,4},{16,24},{20,28},{24,16},{28,20},{1,9},{5... | collective-permute-start | bytes 1036808 | tf_op jit(solution)/shard_map/ppermute | solution.py:67
  116.9 18.4 %collective-permute-start.24 = (bf16[192,960]{1,0:T(8,128)(2,1)}, bf16[192,960]{1,0:T(8,128)(2,1)S(1)}, u32[]{:S(2)}, u32[]{:S(2)}) collective-permute-start(bf16[192,960]{1,0:T(8,128)(2,1)} %get-tuple-element.140.refs_2_.refs_6_), channel_id=1, source_target_pairs={{0,20},{4,16},{8,28},{12,24},{16,4},{20,0},{24,12},{28,8},{1,21},{... | collective-permute-start | bytes 1105928 | tf_op jit(solution)/shard_map/ppermute | solution.py:67
  117.5 17.8 %collective-permute-start.25 = (bf16[192,960]{1,0:T(8,128)(2,1)}, bf16[192,960]{1,0:T(8,128)(2,1)S(1)}, u32[]{:S(2)}, u32[]{:S(2)}) collective-permute-start(bf16[192,960]{1,0:T(8,128)(2,1)} %get-tuple-element.140.refs_2_.refs_6_), channel_id=1, source_target_pairs={{0,8},{4,12},{8,0},{12,4},{16,24},{20,28},{24,16},{28,20},{1,9},{5... | collective-permute-start | bytes 1105928 | tf_op jit(solution)/shard_map/ppermute | solution.py:67
  157.4 15.7 %collective-permute-start.30 = (bf16[192,960]{1,0:T(8,128)(2,1)S(1)}, bf16[192,960]{1,0:T(8,128)(2,1)S(1)}, u32[]{:S(2)}, u32[]{:S(2)}) collective-permute-start(bf16[192,960]{1,0:T(8,128)(2,1)S(1)} %get-tuple-element.217), channel_id=1, source_target_pairs={{0,4},{4,0},{8,12},{12,8},{16,20},{20,16},{24,28},{28,24},{1,5},{5... | collective-permute-start | bytes 1105928 | tf_op jit(solution)/shard_map/ppermute | solution.py:67
  158.0 15.1 %collective-permute-start.31 = (bf16[192,960]{1,0:T(8,128)(2,1)S(1)}, bf16[192,960]{1,0:T(8,128)(2,1)S(1)}, u32[]{:S(2)}, u32[]{:S(2)}) collective-permute-start(bf16[192,960]{1,0:T(8,128)(2,1)S(1)} %get-tuple-element.216), channel_id=1, source_target_pairs={{0,16},{4,20},{8,24},{12,28},{16,0},{20,4},{24,8},{28,12},{1,17},{... | collective-permute-start | bytes 1105928 | tf_op jit(solution)/shard_map/ppermute | solution.py:67
  159.4 19.0 %collective-permute-start.32 = (bf16[192,960]{1,0:T(8,128)(2,1)S(1)}, bf16[192,960]{1,0:T(8,128)(2,1)S(1)}, u32[]{:S(2)}, u32[]{:S(2)}) collective-permute-start(bf16[192,960]{1,0:T(8,128)(2,1)S(1)} %get-tuple-element.215), channel_id=1, source_target_pairs={{0,20},{4,16},{8,28},{12,24},{16,4},{20,0},{24,12},{28,8},{1,21},{... | collective-permute-start | bytes 1105928 | tf_op jit(solution)/shard_map/ppermute | solution.py:67
  195.2 24.4 %collective-permute-start.34 = (bf16[4,192,640]{2,1,0:T(8,128)(2,1)}, bf16[4,192,640]{2,1,0:T(8,128)(2,1)S(1)}, u32[]{:S(2)}, u32[]{:S(2)}) collective-permute-start(bf16[4,192,640]{2,1,0:T(8,128)(2,1)} %get-tuple-element.167), channel_id=1, source_target_pairs={{0,4},{4,0},{1,5},{5,1},{2,6},{6,2},{3,7},{7,3},{8,12},{12,8},{9,1... | collective-permute-start | bytes 2949128 | tf_op jit(solution)/shard_map/ppermute | solution.py:58
  196.0 23.6 %collective-permute-start.35 = (bf16[2,192,960]{2,1,0:T(8,128)(2,1)S(1)}, bf16[2,192,960]{2,1,0:T(8,128)(2,1)}, u32[]{:S(2)}, u32[]{:S(2)}) collective-permute-start(bf16[2,192,960]{2,1,0:T(8,128)(2,1)S(1)} %add_convert_fusion.1), channel_id=1, source_target_pairs={{0,16},{4,20},{8,24},{12,28},{16,0},{20,4},{24,8},{28,12},{1,17},{... | collective-permute-start | bytes 2211848 | tf_op jit(solution)/shard_map/ppermute | solution.py:67
  227.0 20.5 %collective-permute-start.39 = (bf16[192,640]{1,0:T(8,128)(2,1)}, bf16[192,640]{1,0:T(8,128)(2,1)S(1)}, u32[]{:S(2)}, u32[]{:S(2)}) collective-permute-start(bf16[192,640]{1,0:T(8,128)(2,1)} %get-tuple-element.227), channel_id=1, source_target_pairs={{0,2},{1,3},{2,0},{3,1},{4,6},{5,7},{6,4},{7,5},{8,10},{9,11},{10,... | collective-permute-start | bytes 737288 | tf_op jit(solution)/shard_map/ppermute | solution.py:58
  228.5 19.1 %collective-permute-start.40 = (bf16[192,640]{1,0:T(8,128)(2,1)}, bf16[192,640]{1,0:T(8,128)(2,1)S(1)}, u32[]{:S(2)}, u32[]{:S(2)}) collective-permute-start(bf16[192,640]{1,0:T(8,128)(2,1)} %get-tuple-element.226), channel_id=1, source_target_pairs={{0,3},{1,2},{2,1},{3,0},{4,7},{5,6},{6,5},{7,4},{8,11},{9,10},{10,... | collective-permute-start | bytes 737288 | tf_op jit(solution)/shard_map/ppermute | solution.py:58
  232.2 26.1 %collective-permute-start.41 = (bf16[960,480]{1,0:T(8,128)(2,1)S(1)}, bf16[960,480]{1,0:T(8,128)(2,1)S(1)}, u32[]{:S(2)}, u32[]{:S(2)}) collective-permute-start(bf16[960,480]{1,0:T(8,128)(2,1)S(1)} %fusion), channel_id=1, source_target_pairs={{0,16},{4,20},{8,24},{12,28},{16,0},{20,4},{24,8},{28,12},{1,17},{... | collective-permute-start | bytes 2764808 | tf_op jit(solution)/shard_map/ppermute | solution.py:67
  259.7 41.3 %collective-permute-start.46 = (bf16[2,240,480]{2,1,0:T(8,128)(2,1)S(1)}, bf16[2,240,480]{2,1,0:T(8,128)(2,1)S(1)}, u32[]{:S(2)}, u32[]{:S(2)}) collective-permute-start(bf16[2,240,480]{2,1,0:T(8,128)(2,1)S(1)} %pad_maximum_fusion), channel_id=1, source_target_pairs={{0,2},{1,3},{2,0},{3,1},{4,6},{5,7},{6,4},{7,5},{8,10},{9,11},{10,... | collective-permute-start | bytes 1382408 | tf_op jit(solution)/shard_map/ppermute | solution.py:58
  264.8 17.2 %collective-permute-start.45 = (bf16[336,240]{1,0:T(8,128)(2,1)S(1)}, bf16[336,240]{1,0:T(8,128)(2,1)S(1)}, u32[]{:S(2)}, u32[]{:S(2)}) collective-permute-start(bf16[336,240]{1,0:T(8,128)(2,1)S(1)} %get-tuple-element.193), channel_id=1, source_target_pairs={{0,3},{1,2},{2,1},{3,0},{4,7},{5,6},{6,5},{7,4},{8,11},{9,10},{10,... | collective-permute-start | bytes 483848 | tf_op jit(solution)/shard_map/ppermute | solution.py:58
  266.1 34.8 %collective-permute-start.44 = (bf16[336,240]{1,0:T(8,128)(2,1)S(1)}, bf16[336,240]{1,0:T(8,128)(2,1)S(1)}, u32[]{:S(2)}, u32[]{:S(2)}) collective-permute-start(bf16[336,240]{1,0:T(8,128)(2,1)S(1)} %get-tuple-element.192), channel_id=1, source_target_pairs={{0,2},{1,3},{2,0},{3,1},{4,6},{5,7},{6,4},{7,5},{8,10},{9,11},{10,... | collective-permute-start | bytes 483848 | tf_op jit(solution)/shard_map/ppermute | solution.py:58
  266.1 34.8 %collective-permute-start.43 = (bf16[336,240]{1,0:T(8,128)(2,1)S(1)}, bf16[336,240]{1,0:T(8,128)(2,1)S(1)}, u32[]{:S(2)}, u32[]{:S(2)}) collective-permute-start(bf16[336,240]{1,0:T(8,128)(2,1)S(1)} %get-tuple-element.191), channel_id=1, source_target_pairs={{0,1},{1,0},{2,3},{3,2},{4,5},{5,4},{6,7},{7,6},{8,9},{9,8},{10,11... | collective-permute-start | bytes 483848 | tf_op jit(solution)/shard_map/ppermute | solution.py:58
  269.2 34.4 %collective-permute-start.52 = (bf16[240,960]{1,0:T(8,128)(2,1)S(1)}, bf16[240,960]{1,0:T(8,128)(2,1)S(1)}, u32[]{:S(2)}, u32[]{:S(2)}) collective-permute-start(bf16[240,960]{1,0:T(8,128)(2,1)S(1)} %collective-permute-done.51.refs_4_), channel_id=1, source_target_pairs={{0,4},{4,0},{8,12},{12,8},{16,20},{20,16},{24,28},{28,24},{1,5},{5... | collective-permute-start | bytes 1382408 | tf_op jit(solution)/shard_map/ppermute | solution.py:67
  312.6 16.6 %collective-permute-start.58 = (bf16[240,480]{1,0:T(8,128)(2,1)S(1)}, bf16[240,480]{1,0:T(8,128)(2,1)S(1)}, u32[]{:S(2)}, u32[]{:S(2)}) collective-permute-start(bf16[240,480]{1,0:T(8,128)(2,1)S(1)} %fusion.3), channel_id=1, source_target_pairs={{0,4},{4,0},{8,12},{12,8},{16,20},{20,16},{24,28},{28,24},{1,5},{5... | collective-permute-start | bytes 691208 | tf_op jit(solution)/shard_map/ppermute | solution.py:67
  (94 other events, 747.1 us)
Sparse Core Ops, SparseCore 0:
  9.9 35.0 all-gather.2
  74.8 42.6 all-gather.4
  185.0 39.7 reduce-scatter.1

commit v9 on v8

--- a/solution.py
+++ b/solution.py
@@ -32,7 +32,8 @@
     "residual_back": 6,
     "attention_back_far": 13,
     "attention_back_near": 14,
-    "query_output_weight_grads": 0,
+    "output_weight_grad": 3,
+    "query_weight_grad": 0,
     "query_back": 0,
     "stack_quarters": 0,
     "quarter_columns": 0,
@@ -457,21 +458,13 @@
     return join_lanes(out_blocks)
 
 
-def weight_grads_kernel(members, spots, *refs):
-    lefts, lows, (keep_ref, send_ref, blocks) = refs[0:4:2], refs[1:4:2], refs[4:]
+def weight_grad_kernel(members, spots, left_ref, low_ref, keep_ref, send_ref, blocks):
     dp = spots[2]
-    for k, (left_ref, low_ref) in enumerate(zip(lefts, lows)):
-        for i, block in enumerate(lane_blocks(low_ref[...], members)):
-            blocks[k * members + i] = block
+    for i, block in enumerate(lane_blocks(low_ref[...], members)):
+        blocks[i] = block
     for j in (1, 3, 0, 2):
         out_ref = send_ref if j & 1 else keep_ref
-        out_ref[j // 2] = jnp.concatenate(
-            [
-                dot_first(left_ref[...], blocks[k * members + (dp ^ j)])
-                for k, left_ref in enumerate(lefts)
-            ],
-            axis=1,
-        ).astype(BF16)
+        out_ref[j // 2] = dot_first(left_ref[...], blocks[dp ^ j]).astype(BF16)
 
 
 def join_kernel(members, spots, own_ref, across_ref, core_ref, core_across_ref, *refs):
@@ -747,15 +740,14 @@
     near = [kv_own] + direct_fsdp(kv_own)
     query_pieces = lax.optimization_barrier((kv_own, *query_pieces))[1:]
     stacked, across = stack(query_pieces)
-    output_quarter = after(output_quarter, near[1])
     across, *near = lax.optimization_barrier((across, *near))
     query_stacks = four(stacked, across)
-    output_pieces = direct_fsdp(output_quarter)
     (near_all,) = call(
         stack_kernel, spots, near, [((near_count, 2 * kv_width), BF16)],
         name="stack_keys_values",
     )
     far = [swap(near_all, "ctx", d) for d in range(1, ctx_count)]
+    output_pieces = direct_fsdp(after(output_quarter, near_all))
 
     pack, cot_all, _ = lax.optimization_barrier((pack, cot_all, near[-1]))
     pack_all = lax.all_gather(pack, "fsdp", axis=0, tiled=True)
@@ -779,7 +771,9 @@
         scratch=[((far_count, 2 * kv_width), BF16)], name="attention_far",
     )
     output_pieces = lax.optimization_barrier((queries, *output_pieces))[1:]
-    output_stacks = four(*stack(output_pieces))
+    output_stacked, output_across = stack(output_pieces)
+    attended, output_across = lax.optimization_barrier((attended, output_across))
+    output_stacks = four(output_stacked, output_across)
     residual, inverse_two, normed_two = call(
         functools.partial(project_kernel, shards, dp_count), spots,
         [attended, tokens, gains, output_weight, *output_stacks],
@@ -832,7 +826,9 @@
     )
     pack_share = sum_far(lax.psum_scatter(pack_grad, "fsdp", scatter_dimension=0, tiled=True))
 
-    pack_grad, *grad_chips = lax.optimization_barrier((pack_grad, *grad_chips))
+    pack_grad, result_b, *grad_chips = lax.optimization_barrier(
+        (pack_grad, result_b, *grad_chips)
+    )
     residual_grad, residual_low, attended_grad, second_gain_grad = call(
         functools.partial(middle_kernel, shards, dp_count), spots,
         [
@@ -844,8 +840,20 @@
         name="residual_back",
     )
 
-    result_core = swap_core(after(result_b, residual_low))
-    attended_grad, result_a = lax.optimization_barrier((attended_grad, result_a))
+    result_core = swap_core(result_b)
+    result_sent = (result_a[2:].astype(F32) + result_core[2:].astype(F32)).astype(BF16)
+
+    def weight_grad(left, low, name):
+        pair = ((2, width, quarter), BF16)
+        return call(
+            functools.partial(weight_grad_kernel, dp_count), spots, [left, low], [pair, pair],
+            scratch=[((dp_count, rows, quarter), BF16)], name=name,
+        )
+
+    output_keep, output_send = weight_grad(attended, residual_low, "output_weight_grad")
+    attended_grad, result_sent, output_send = lax.optimization_barrier(
+        (attended_grad, result_sent, output_send)
+    )
 
     def sum_x(keep, away):
         sent = (keep[1].astype(F32) + away[1].astype(F32)).astype(BF16)
@@ -913,25 +921,20 @@
             d == 1, False, query_partial, far_pos[at : at + near_count], far[d - 1 : d]
         )
         far_grads.append(swap(grads[0], "ctx", d))
-    result_sent = (result_a[2:].astype(F32) + result_core[2:].astype(F32)).astype(BF16)
-    query_partial, result_sent = lax.optimization_barrier((query_partial, result_sent))
+    output_sent, output_terms = sum_x(output_keep, swap_core(output_send))
+    query_partial = after(query_partial, output_sent)
     result_across = swap_plane(result_sent, 2, 0)
     query_low, near_grads = back(False, True, query_partial, near_pos, near)
-    pair_shape = ((2, width, 2 * quarter), BF16)
-    weights_keep, weights_send = call(
-        functools.partial(weight_grads_kernel, dp_count), spots,
-        [attended, residual_low, normed_one, query_low], [pair_shape, pair_shape],
-        scratch=[((2 * dp_count, rows, quarter), BF16)], name="query_output_weight_grads",
-    )
-    weights_send, far_grads[-1], result_across = lax.optimization_barrier(
-        (weights_send, far_grads[-1], result_across)
-    )
-    result_own, result_along = [
-        (result_a[k].astype(F32) + result_core[k].astype(F32)) + result_across[k].astype(F32)
-        for k in (0, 1)
-    ]
-    result_along = swap_plane(result_along.astype(BF16), 0, 1)
-
+    query_low, result_across, *output_terms = lax.optimization_barrier(
+        (query_low, result_across, *output_terms)
+    )
+    output_half_pieces = pieces_z(output_terms)
+    query_low, *output_half_pieces = lax.optimization_barrier((query_low, *output_half_pieces))
+    output_half = halve_z(output_half_pieces, shards // 2)
+    weights_keep, weights_send = weight_grad(normed_one, query_low, "query_weight_grad")
+    weights_send, pack_share, far_grads[-1], *output_half = lax.optimization_barrier(
+        (weights_send, pack_share, far_grads[-1], *output_half)
+    )
     def home(r):
         return sum(grads[r].astype(F32) for grads in far_grads)
 
@@ -939,11 +942,10 @@
         r: (near_grads[r].astype(F32) + home(r)).astype(BF16) for r in range(1, shards)
     }
     kv_arrived = {r: swap(kv_sums[r], "fsdp", r) for r in reversed(range(1, shards))}
-    query_low, pack_share, *_ = lax.optimization_barrier(
-        (query_low, pack_share, *kv_sums.values())
-    )
-
-    weights_away = swap_core(weights_send)
+    query_low, weights_away, *_ = lax.optimization_barrier(
+        (query_low, swap_core(weights_send), *kv_sums.values())
+    )
+
     weights_sent, weights_terms = sum_x(weights_keep, weights_away)
     query_turn = after(query_low, weights_sent)
     (query_back,) = call(
@@ -952,9 +954,15 @@
         scratch=[((dp_count, rows, quarter), BF16), ((shards, rows, weight_rows), F32)],
         name="query_back",
     )
-    query_back, share_along = lax.optimization_barrier(
-        (query_back, swap_plane(pack_share, 0, 1))
-    )
+    weights_pieces = pieces_z(weights_terms)
+    query_back, share_along, result_across, *weights_pieces = lax.optimization_barrier(
+        (query_back, swap_plane(pack_share, 0, 1), result_across, *weights_pieces)
+    )
+    result_own, result_along = [
+        (result_a[k].astype(F32) + result_core[k].astype(F32)) + result_across[k].astype(F32)
+        for k in (0, 1)
+    ]
+    result_along = swap_plane(result_along.astype(BF16), 0, 1)
     share_across = swap_plane(after(pack_share, weights_sent), 2, 0)
     span = kv_width + EXTRA_ROWS
     packed_shape = ((shards, span, weight_rows), BF16)
@@ -973,19 +981,19 @@
         name="keys_values_back",
     )
     kv_away = swap_core(kv_send)
-    kv_keep, *weights_terms = lax.optimization_barrier((kv_keep, *weights_terms))
-    weights_pieces = pieces_z(weights_terms)
     pieces = [
         (lax.dynamic_index_in_dim(kv_keep, shard ^ r, 0, keepdims=False).astype(F32)
          + lax.dynamic_index_in_dim(kv_away, shard ^ r, 0, keepdims=False).astype(F32)).astype(BF16)
         for r in range(shards)
     ]
-    weights_pieces, *pieces = lax.optimization_barrier((weights_pieces, *pieces))
     share_across = lax.optimization_barrier((share_across, *pieces))[0]
     share_a = [pack_share, share_along, share_across, swap_plane(share_across, 0, 1)]
     share_b = [swap_core(piece) for piece in share_a]
     kv_share = sum_z(pieces)
-    weights_half = halve_z(weights_pieces, shards // 2)
+    weights_half = [
+        jnp.concatenate([left, right], axis=1)
+        for left, right in zip(output_half, halve_z(weights_pieces, shards // 2))
+    ]
     share_by_mask = [None] * members
     for k, (a, b) in enumerate(((0, 0),) + CHIP_MASKS):
         share_by_mask[2 * a + b] = share_a[k]
@@ -1000,16 +1008,15 @@
         name="feed_forward_out",
     )
     kv_share, weights_half = lax.optimization_barrier((kv_share, weights_half))
-    kv_share, result_along, *big = lax.optimization_barrier(
-        (sum_swap(kv_share, 2, 0), result_along, gate_weight_grad, up_weight_grad,
-         down_weight_grad)
-    )
-    gate_weight_grad, up_weight_grad, down_weight_grad = big
+    kv_share, result_along = lax.optimization_barrier((sum_swap(kv_share, 2, 0), result_along))
     span = shards // 2
     while span > 1:
         span //= 2
         weights_half = halve_z(weights_half, span)
-    weights_own = sum_y(weights_half[0].astype(BF16))
+    weights_own, *big = lax.optimization_barrier(
+        (sum_y(weights_half[0].astype(BF16)), gate_weight_grad, up_weight_grad, down_weight_grad)
+    )
+    gate_weight_grad, up_weight_grad, down_weight_grad = big
     result = residual + (result_own + result_along.astype(F32))
     output_weight_grad, query_weight_grad = finish_quarters(weights_own)
     low = sum_far(sum_swap(kv_share, 0, 1))

time: 355 us -> 369 us (1.039)
  starting transfers between devices: 66.7 us -> 75.4 us
  other arithmetic: 14.2 us -> 18.2 us
    ppermute x40 -> x42, waiting for transfers between devices: 44.9 us -> 64.9 us  [swap_plane(): return lax.ppermute(x, ('dp', 'ctx'), pairs)]
    ppermute x22 -> x23, waiting for transfers between devices: 65.7 us -> 52.5 us  [swap(): return lax.ppermute(x, axis, [(i, i ^ mask) for i in range(count)])]
    ppermute x22 -> x23, starting transfers between devices: 42.8 us -> 51.5 us  [swap(): return lax.ppermute(x, axis, [(i, i ^ mask) for i in range(count)])]
    unnamed x122 -> x124, local copies, waits for them, and re-layouts: 12.5 us -> 9.48 us
    pallas_call x20 -> x21, Pallas kernels: 118 us -> 119 us  [call(): pl.pallas_call(kernel, out_shape=outs, in_specs=specs, out_specs=tuple((p...]
    ppermute x40 -> x42, starting transfers between devices: 23.6 us -> 23.6 us  [swap_plane(): return lax.ppermute(x, ('dp', 'ctx'), pairs)]
  transfers between devices with their start and end apart: 65 -> 68, of which waited for: 21 -> 25; matrix products, arithmetic and copies ran while one was open for 6% -> 6% of each run, Pallas kernels for 29% -> 28%
where the time goes in v9:
time: 369 us; the launch traced here: 364 us
  Pallas kernels  119 us (32%)
  waiting for transfers between devices  118 us (32%)
  starting transfers between devices  75.4 us (20%)
  other arithmetic  18.2 us (5%)
  local copies, waits for them, and re-layouts  17.4 us (5%)
  between operations  15.6 us (4%)
    pallas_call x21, Pallas kernels, call(): pl.pallas_call(kernel, out_shape=outs, in_specs=specs, out_specs=tuple((p...  119 us
    ppermute x42, waiting for transfers between devices, swap_plane(): return lax.ppermute(x, ('dp', 'ctx'), pairs)  64.9 us
    ppermute x23, waiting for transfers between devices, swap(): return lax.ppermute(x, axis, [(i, i ^ mask) for i in range(count)])  52.5 us
    ppermute x23, starting transfers between devices, swap(): return lax.ppermute(x, axis, [(i, i ^ mask) for i in range(count)])  51.5 us
    ppermute x42, starting transfers between devices, swap_plane(): return lax.ppermute(x, ('dp', 'ctx'), pairs)  23.6 us
    unnamed x124, local copies, waits for them, and re-layouts  9.48 us
  transfers between devices with their start and end apart: 68, of which 25 were waited for; matrix products, arithmetic and copies ran while one was open for 6% of the time, Pallas kernels for 28%

profile of v9, /device:TPU:0, one launch (start us, length us, event | category | flops | bytes accessed | tf_op | source)
XLA Modules:
  0.0 363.7 jit_solution(8976396735527800044)
XLA Ops:
  24.9 4.2 %pack_weights.1 = bf16[240,960]{1,0:T(8,128)(2,1)} custom-call(s32[4]{0:T(128)} %pad_add_fusion.1.spots, bf16[240,2560]{1,0:T(8,128)(2,1)} %gate_ref.1, bf16[240,2560]{1,0:T(8,128)(2,1)} %up_ref.1, bf16[960,640]{1,0:T(8,128)(2,1)} %bitcast.131), custom_call_target="tpu_custom_call" | custom-call | flops 4600000000 | tf_op jit(solution)/shard_map/pack_weights/pallas_call | solution.py:107
  31.3 4.2 %collective-permute-start.8 = (bf16[240,240]{1,0:T(8,128)(2,1)S(1)}, bf16[240,240]{1,0:T(8,128)(2,1)S(1)}, u32[]{:S(2)}, u32[]{:S(2)}) collective-permute-start(bf16[240,240]{1,0:T(8,128)(2,1)S(1)} %copy-done.60), channel_id=1, source_target_pairs={{0,3},{1,2},{2,1},{3,0},{4,7},{5,6},{6,5},{7,4},{8,11},{9,10},{10,... | collective-permute-start | bytes 345608 | tf_op jit(solution)/shard_map/ppermute | solution.py:59
  36.3 3.6 norm_keys_values.1
  53.3 9.9 %collective-permute-done.12.refs_12_.refs_2_.refs_11_ = bf16[192,640]{1,0:T(8,128)(2,1)S(1)} collective-permute-done((bf16[192,640]{1,0:T(8,128)(2,1)}, bf16[192,640]{1,0:T(8,128)(2,1)S(1)}, u32[]{:S(2)}, u32[]{:S(2)}) %collective-permute-start.12) | collective-permute-done | bytes 245792 | tf_op jit(solution)/shard_map/ppermute | solution.py:59
  70.0 4.8 %collective-permute-start.16 = (bf16[240,240]{1,0:T(8,128)(2,1)S(1)}, bf16[240,240]{1,0:T(8,128)(2,1)S(1)}, u32[]{:S(2)}, u32[]{:S(2)}) collective-permute-start(bf16[240,240]{1,0:T(8,128)(2,1)S(1)} %copy-done.59), channel_id=1, source_target_pairs={{0,1},{1,0},{2,3},{3,2},{4,5},{5,4},{6,7},{7,6},{8,9},{9,8},{10,11... | collective-permute-start | bytes 345608 | tf_op jit(solution)/shard_map/ppermute | solution.py:59
  78.3 8.7 %attention_near.1 = (bf16[192,960]{1,0:T(8,128)(2,1)}, f32[5,576]{1,0:T(8,128)}, f32[5,576]{1,0:T(8,128)}, f32[5,64,576]{2,1,0:T(8,128)}) custom-call(s32[4]{0:T(128)} %pad_add_fusion.1.spots, bf16[192,960]{1,0:T(8,128)(2,1)} %get-tuple-element.126.refs_0_, s32[768,1]{1,0:T(8,128)} %slice.148.refs_1_, s32[1,576]{1,0:T(1,128)} %broadcast_in_dim.29.refs_2_, ...), custom_call_target="tpu_custom_call" | custom-call | flops 13799999488 | tf_op jit(solution)/shard_map/attention_near/pallas_call | solution.py:107
  93.9 9.1 %attention_far.1 = (bf16[192,960]{1,0:T(8,128)(2,1)}, f32[5,64,576]{2,1,0:T(8,128)}, f32[5,576]{1,0:T(8,128)}) custom-call(s32[4]{0:T(128)} %pad_add_fusion.1.spots, bf16[192,960]{1,0:T(8,128)(2,1)} %get-tuple-element.136.refs_0_, s32[768,1]{1,0:T(8,128)} %slice.149.refs_1_, s32[1,576]{1,0:T(1,128)} %broadcast_in_dim.29.refs_2_, ...), custom_call_target="tpu_custom_call" | custom-call | flops 13799999488 | tf_op jit(solution)/shard_map/attention_far/pallas_call | solution.py:107
  105.6 4.2 %project_residual.1 = (f32[192,960]{1,0:T(8,128)}, f32[192,1]{1,0:T(8,128)}, bf16[192,960]{1,0:T(8,128)(2,1)}) custom-call(s32[4]{0:T(128)} %pad_add_fusion.1.spots, bf16[192,960]{1,0:T(8,128)(2,1)} %get-tuple-element.146.refs_0_.left_ref, bf16[192,960]{1,0:T(8,128)(2,1)} %bitcast.133, f32[8,960]{1,0:T(8,128)} %get-tuple-element.147.refs_2_.refs_8_.refs_5_, ...), custom_call_target="tpu_custom_call" | custom-call | flops 2300000000 | tf_op jit(solution)/shard_map/project_residual/pallas_call | solution.py:107
  113.3 8.1 %collective-permute-done.22.refs_3_.refs_7_ = bf16[192,960]{1,0:T(8,128)(2,1)S(1)} collective-permute-done((bf16[192,960]{1,0:T(8,128)(2,1)}, bf16[192,960]{1,0:T(8,128)(2,1)S(1)}, u32[]{:S(2)}, u32[]{:S(2)}) %collective-permute-start.22) | collective-permute-done | bytes 368672 | tf_op jit(solution)/shard_map/ppermute | solution.py:68
  123.3 7.7 %collective-permute-done.24.refs_5_.refs_9_ = bf16[192,960]{1,0:T(8,128)(2,1)S(1)} collective-permute-done((bf16[192,960]{1,0:T(8,128)(2,1)}, bf16[192,960]{1,0:T(8,128)(2,1)S(1)}, u32[]{:S(2)}, u32[]{:S(2)}) %collective-permute-start.24) | collective-permute-done | bytes 368672 | tf_op jit(solution)/shard_map/ppermute | solution.py:68
  133.5 8.5 %feed_forward.3 = (bf16[4,192,960]{2,1,0:T(8,128)(2,1)}, bf16[768,320]{1,0:T(8,128)(2,1)}, bf16[768,640]{1,0:T(8,128)(2,1)}) custom-call(s32[4]{0:T(128)} %pad_add_fusion.1.spots, bf16[960,960]{1,0:T(8,128)(2,1)} %all-gather.5.cloned.1.call-done.refs_0_, bf16[8,192,960]{2,1,0:T(8,128)(2,1)} %all-gather.3.cloned.1.call-done.refs_1_.refs_5_, ...), custom_call_target="tpu_custom_call" | custom-call | flops 9200000000 | tf_op jit(solution)/shard_map/feed_forward/pallas_call | solution.py:107
  142.2 8.5 %feed_forward.2 = (bf16[4,192,960]{2,1,0:T(8,128)(2,1)}, bf16[768,320]{1,0:T(8,128)(2,1)}, bf16[768,640]{1,0:T(8,128)(2,1)}) custom-call(s32[4]{0:T(128)} %pad_add_fusion.1.spots, bf16[960,960]{1,0:T(8,128)(2,1)} %all-gather.5.cloned.1.call-done.refs_0_, bf16[8,192,960]{2,1,0:T(8,128)(2,1)} %all-gather.3.cloned.1.call-done.refs_1_.refs_5_, ...), custom_call_target="tpu_custom_call" | custom-call | flops 9200000000 | tf_op jit(solution)/shard_map/feed_forward/pallas_call | solution.py:107
  156.6 12.1 %feed_forward_weights.1 = (bf16[4,192,960]{2,1,0:T(8,128)(2,1)}, bf16[4,192,960]{2,1,0:T(8,128)(2,1)}, bf16[960,960]{1,0:T(8,128)(2,1)}) custom-call(s32[4]{0:T(128)} %pad_add_fusion.1.spots, bf16[960,960]{1,0:T(8,128)(2,1)} %all-gather.5.cloned.1.call-done.refs_0_, bf16[768,320]{1,0:T(8,128)(2,1)} %get-tuple-element.156.refs_1_, ...), custom_call_target="tpu_custom_call" | custom-call | flops 13799999488 | tf_op jit(solution)/shard_map/feed_forward_weights/pallas_call | solution.py:107
  168.8 5.3 %collective-permute-done.32.refs_4_ = bf16[192,960]{1,0:T(8,128)(2,1)S(1)} collective-permute-done((bf16[192,960]{1,0:T(8,128)(2,1)S(1)}, bf16[192,960]{1,0:T(8,128)(2,1)S(1)}, u32[]{:S(2)}, u32[]{:S(2)}) %collective-permute-start.32) | collective-permute-done | bytes 368672 | tf_op jit(solution)/shard_map/ppermute | solution.py:68
  174.9 5.6 %residual_back.1 = (f32[192,960]{1,0:T(8,128)}, bf16[192,960]{1,0:T(8,128)(2,1)}, bf16[192,960]{1,0:T(8,128)(2,1)}, f32[1,960]{1,0:T(1,128)}) custom-call(s32[4]{0:T(128)} %pad_add_fusion.1.spots, bf16[4,192,960]{2,1,0:T(8,128)(2,1)} %get-tuple-element.154.refs_0_, bf16[4,192,960]{2,1,0:T(8,128)(2,1)} %copy-done.3, bf16[192,960]{1,0:T(8,128)(2,1)} %copy-done.31, ...), custom_call_target="tpu_custom_call" | custom-call | flops 6899999744 | tf_op jit(solution)/shard_map/residual_back/pallas_call | solution.py:107
  186.2 10.6 %attention_back_far.1 = (f32[5,64,576]{2,1,0:T(8,128)}, bf16[4,192,640]{2,1,0:T(8,128)(2,1)}) custom-call(s32[4]{0:T(128)} %pad_add_fusion.1.spots, bf16[192,960]{1,0:T(8,128)(2,1)} %get-tuple-element.136.refs_0_, s32[768,1]{1,0:T(8,128)} %slice.149.refs_1_, s32[1,576]{1,0:T(1,128)} %broadcast_in_dim.29.refs_2_, ...), custom_call_target="tpu_custom_call" | custom-call | flops 14949999616 | tf_op jit(solution)/shard_map/attention_back_far/pallas_call | solution.py:107
  199.2 10.2 %attention_back_near.1 = (bf16[192,960]{1,0:T(8,128)(2,1)}, bf16[192,640]{1,0:T(8,128)(2,1)}, bf16[192,640]{1,0:T(8,128)(2,1)}, bf16[192,640]{1,0:T(8,128)(2,1)}, bf16[192,640]{1,0:T(8,128)(2,1)}) custom-call(s32[4]{0:T(128)} %pad_add_fusion.1.spots, bf16[192,960]{1,0:T(8,128)(2,1)} %get-tuple-element.136.refs_0_, s32[768,1]{1,0:T(8,128)} %slice.148.refs_1_, ...), custom_call_target="tpu_custom_call" | custom-call | flops 16099999744 | tf_op jit(solution)/shard_map/attention_back_near/pallas_call | solution.py:107
  209.5 6.1 %collective-permute-done.36 = bf16[960,240]{1,0:T(8,128)(2,1)S(1)} collective-permute-done((bf16[960,240]{1,0:T(8,128)(2,1)S(1)}, bf16[960,240]{1,0:T(8,128)(2,1)S(1)}, u32[]{:S(2)}, u32[]{:S(2)}) %collective-permute-start.36) | collective-permute-done | bytes 460832 | tf_op jit(solution)/shard_map/ppermute | solution.py:68
  215.9 10.5 %collective-permute-start.38 = (bf16[2,240,240]{2,1,0:T(8,128)(2,1)S(1)}, bf16[2,240,240]{2,1,0:T(8,128)(2,1)S(1)}, u32[]{:S(2)}, u32[]{:S(2)}) collective-permute-start(bf16[2,240,240]{2,1,0:T(8,128)(2,1)S(1)} %pad_maximum_fusion.2), channel_id=1, source_target_pairs={{0,2},{1,3},{2,0},{3,1},{4,6},{5,7},{6,4},{7,5},{8,10},{9,11},{10,... | collective-permute-start | bytes 691208 | tf_op jit(solution)/shard_map/ppermute | solution.py:59
  229.5 8.1 %collective-permute-done.38 = bf16[2,240,240]{2,1,0:T(8,128)(2,1)S(1)} collective-permute-done((bf16[2,240,240]{2,1,0:T(8,128)(2,1)S(1)}, bf16[2,240,240]{2,1,0:T(8,128)(2,1)S(1)}, u32[]{:S(2)}, u32[]{:S(2)}) %collective-permute-start.38) | collective-permute-done | bytes 230432 | tf_op jit(solution)/shard_map/ppermute | solution.py:59
  246.9 3.6 query_back.1.refs_6_
  250.5 4.1 %collective-permute-done.41 = bf16[960,240]{1,0:T(8,128)(2,1)S(1)} collective-permute-done((bf16[960,240]{1,0:T(8,128)(2,1)S(1)}, bf16[960,240]{1,0:T(8,128)(2,1)S(1)}, u32[]{:S(2)}, u32[]{:S(2)}) %collective-permute-start.41) | collective-permute-done | bytes 460832 | tf_op jit(solution)/shard_map/ppermute | solution.py:68
  256.3 11.7 %collective-permute-done.43.refs_14_ = bf16[192,640]{1,0:T(8,128)(2,1)S(1)} collective-permute-done((bf16[192,640]{1,0:T(8,128)(2,1)S(1)}, bf16[192,640]{1,0:T(8,128)(2,1)S(1)}, u32[]{:S(2)}, u32[]{:S(2)}) %collective-permute-start.43) | collective-permute-done | bytes 245792 | tf_op jit(solution)/shard_map/ppermute | solution.py:59
  268.8 6.2 %keys_values_back.1 = (f32[192,960]{1,0:T(8,128)}, bf16[4,336,240]{2,1,0:T(8,128)(2,1)}, bf16[4,336,240]{2,1,0:T(8,128)(2,1)}) custom-call(s32[4]{0:T(128)} %pad_add_fusion.1.spots, f32[192,128]{1,0:T(8,128)} %pad_maximum_fusion.5.refs_5_.refs_3_.refs_0_, f32[192,128]{1,0:T(8,128)} %pad_maximum_fusion.6.refs_6_.refs_4_.refs_1_, ...), custom_call_target="tpu_custom_call" | custom-call | flops 6899999744 | tf_op jit(solution)/shard_map/keys_values_back/pallas_call | solution.py:107
  282.1 5.0 %collective-permute-start.47 = (bf16[336,240]{1,0:T(8,128)(2,1)S(1)}, bf16[336,240]{1,0:T(8,128)(2,1)S(1)}, u32[]{:S(2)}, u32[]{:S(2)}) collective-permute-start(bf16[336,240]{1,0:T(8,128)(2,1)S(1)} %get-tuple-element.250), channel_id=1, source_target_pairs={{0,2},{1,3},{2,0},{3,1},{4,6},{5,7},{6,4},{7,5},{8,10},{9,11},{10,... | collective-permute-start | bytes 483848 | tf_op jit(solution)/shard_map/ppermute | solution.py:59
  288.2 11.0 %collective-permute-done.47 = bf16[336,240]{1,0:T(8,128)(2,1)S(1)} collective-permute-done((bf16[336,240]{1,0:T(8,128)(2,1)S(1)}, bf16[336,240]{1,0:T(8,128)(2,1)S(1)}, u32[]{:S(2)}, u32[]{:S(2)}) %collective-permute-start.47) | collective-permute-done | bytes 161312 | tf_op jit(solution)/shard_map/ppermute | solution.py:59
  306.4 7.4 %collective-permute-done.51 = bf16[192,960]{1,0:T(8,128)(2,1)S(1)} collective-permute-done((bf16[192,960]{1,0:T(8,128)(2,1)S(1)}, bf16[192,960]{1,0:T(8,128)(2,1)S(1)}, u32[]{:S(2)}, u32[]{:S(2)}) %collective-permute-start.51) | collective-permute-done | bytes 368672 | tf_op jit(solution)/shard_map/ppermute | solution.py:68
  314.9 5.0 %collective-permute-done.54 = bf16[1,240,480]{2,1,0:T(8,128)(2,1)S(1)} collective-permute-done((bf16[1,240,480]{2,1,0:T(8,128)(2,1)S(1)}, bf16[1,240,480]{2,1,0:T(8,128)(2,1)S(1)}, u32[]{:S(2)}, u32[]{:S(2)}) %collective-permute-start.54) | collective-permute-done | bytes 230432 | tf_op jit(solution)/shard_map/ppermute | solution.py:59
  321.7 5.0 %collective-permute-done.52 = bf16[336,240]{1,0:T(8,128)(2,1)S(1)} collective-permute-done((bf16[336,240]{1,0:T(8,128)(2,1)S(1)}, bf16[336,240]{1,0:T(8,128)(2,1)S(1)}, u32[]{:S(2)}, u32[]{:S(2)}) %collective-permute-start.52) | collective-permute-done | bytes 161312 | tf_op jit(solution)/shard_map/ppermute | solution.py:68
  328.6 4.8 %collective-permute-done.55 = bf16[240,480]{1,0:T(8,128)(2,1)S(1)} collective-permute-done((bf16[240,480]{1,0:T(8,128)(2,1)S(1)}, bf16[240,480]{1,0:T(8,128)(2,1)S(1)}, u32[]{:S(2)}, u32[]{:S(2)}) %collective-permute-start.55) | collective-permute-done | bytes 230432 | tf_op jit(solution)/shard_map/ppermute | solution.py:68
  336.6 6.7 %feed_forward_out.1 = (f32[240,2560]{1,0:T(8,128)}, f32[240,2560]{1,0:T(8,128)}, f32[960,640]{1,0:T(8,128)}) custom-call(s32[4]{0:T(128)} %pad_add_fusion.1.spots, bf16[240,960]{1,0:T(8,128)(2,1)} %reduce-scatter.2.cloned.1.call-done.refs_0_, bf16[240,960]{1,0:T(8,128)(2,1)} %copy-done.23, bf16[240,960]{1,0:T(8,128)(2,1)} %copy-done.26, ...), custom_call_target="tpu_custom_call" | custom-call | flops 8049999872 | tf_op jit(solution)/shard_map/feed_forward_out/pallas_call | solution.py:107
  344.6 7.1 %collective-permute-done.62.across_ref = bf16[240,480]{1,0:T(8,128)(2,1)S(1)} collective-permute-done((bf16[240,480]{1,0:T(8,128)(2,1)S(1)}, bf16[240,480]{1,0:T(8,128)(2,1)S(1)}, u32[]{:S(2)}, u32[]{:S(2)}) %collective-permute-start.62) | collective-permute-done | bytes 230432 | tf_op jit(solution)/shard_map/ppermute | solution.py:68
  (306 shorter events, 120.1 us)
Async XLA Ops:
  7.2 67.6 %all-gather.3.cloned.1.call-start = ((), (), s32[]{:S(2)}) async-start(), calls=%async_computation.1 | async-start | bytes 3538944 | tf_op jit(solution)/shard_map/all_gather | solution.py:704
  7.9 124.8 %all-gather.5.cloned.1.call-start = ((), (), s32[]{:S(2)}) async-start(), calls=%async_computation.2 | async-start | bytes 2457600 | tf_op jit(solution)/shard_map/all_gather | solution.py:753
  10.4 19.5 %collective-permute-start = (bf16[336,240]{1,0:T(8,128)(2,1)S(1)}, bf16[336,240]{1,0:T(8,128)(2,1)S(1)}, u32[]{:S(2)}, u32[]{:S(2)}) collective-permute-start(bf16[336,240]{1,0:T(8,128)(2,1)S(1)} %pad_maximum_fusion.4), channel_id=1, source_target_pairs={{0,1},{1,0},{2,3},{3,2},{4,5},{5,4},{6,7},{7,6},{8,9},{9,8},{10,11... | collective-permute-start | bytes 483848 | tf_op jit(solution)/shard_map/ppermute | solution.py:59
  13.5 16.4 %collective-permute-start.1 = (bf16[336,240]{1,0:T(8,128)(2,1)S(1)}, bf16[336,240]{1,0:T(8,128)(2,1)S(1)}, u32[]{:S(2)}, u32[]{:S(2)}) collective-permute-start(bf16[336,240]{1,0:T(8,128)(2,1)S(1)} %pad_maximum_fusion.4), channel_id=1, source_target_pairs={{0,2},{1,3},{2,0},{3,1},{4,6},{5,7},{6,4},{7,5},{8,10},{9,11},{10,... | collective-permute-start | bytes 483848 | tf_op jit(solution)/shard_map/ppermute | solution.py:59
  16.0 14.3 %collective-permute-start.2 = (bf16[336,240]{1,0:T(8,128)(2,1)S(1)}, bf16[336,240]{1,0:T(8,128)(2,1)S(1)}, u32[]{:S(2)}, u32[]{:S(2)}) collective-permute-start(bf16[336,240]{1,0:T(8,128)(2,1)S(1)} %pad_maximum_fusion.4), channel_id=1, source_target_pairs={{0,3},{1,2},{2,1},{3,0},{4,7},{5,6},{6,5},{7,4},{8,11},{9,10},{10,... | collective-permute-start | bytes 483848 | tf_op jit(solution)/shard_map/ppermute | solution.py:59
  18.6 24.1 %collective-permute-start.6 = (bf16[240,240]{1,0:T(8,128)(2,1)}, bf16[240,240]{1,0:T(8,128)(2,1)S(1)}, u32[]{:S(2)}, u32[]{:S(2)}) collective-permute-start(bf16[240,240]{1,0:T(8,128)(2,1)} %get-tuple-element.124), channel_id=1, source_target_pairs={{0,1},{1,0},{2,3},{3,2},{4,5},{5,4},{6,7},{7,6},{8,9},{9,8},{10,11... | collective-permute-start | bytes 345608 | tf_op jit(solution)/shard_map/ppermute | solution.py:59
  19.5 25.6 %collective-permute-start.7 = (bf16[240,240]{1,0:T(8,128)(2,1)}, bf16[240,240]{1,0:T(8,128)(2,1)S(1)}, u32[]{:S(2)}, u32[]{:S(2)}) collective-permute-start(bf16[240,240]{1,0:T(8,128)(2,1)} %get-tuple-element.124), channel_id=1, source_target_pairs={{0,2},{1,3},{2,0},{3,1},{4,6},{5,7},{6,4},{7,5},{8,10},{9,11},{10,... | collective-permute-start | bytes 345608 | tf_op jit(solution)/shard_map/ppermute | solution.py:59
  42.7 20.5 %collective-permute-start.12 = (bf16[192,640]{1,0:T(8,128)(2,1)}, bf16[192,640]{1,0:T(8,128)(2,1)S(1)}, u32[]{:S(2)}, u32[]{:S(2)}) collective-permute-start(bf16[192,640]{1,0:T(8,128)(2,1)} %get-tuple-element.132.refs_10_.refs_0_.refs_9_), channel_id=1, source_target_pairs={{0,2},{1,3},{2,0},{3,1},{4,6},{5,7},{6,4},{7,5},{8,10},{9,11},{10,... | collective-permute-start | bytes 737288 | tf_op jit(solution)/shard_map/ppermute | solution.py:59
  42.7 20.5 %collective-permute-start.13 = (bf16[192,640]{1,0:T(8,128)(2,1)}, bf16[192,640]{1,0:T(8,128)(2,1)S(1)}, u32[]{:S(2)}, u32[]{:S(2)}) collective-permute-start(bf16[192,640]{1,0:T(8,128)(2,1)} %get-tuple-element.132.refs_10_.refs_0_.refs_9_), channel_id=1, source_target_pairs={{0,3},{1,2},{2,1},{3,0},{4,7},{5,6},{6,5},{7,4},{8,11},{9,10},{10,... | collective-permute-start | bytes 737288 | tf_op jit(solution)/shard_map/ppermute | solution.py:59
  48.3 14.9 %collective-permute-start.10 = (bf16[720,240]{1,0:T(8,128)(2,1)}, bf16[720,240]{1,0:T(8,128)(2,1)S(1)}, u32[]{:S(2)}, u32[]{:S(2)}) collective-permute-start(bf16[720,240]{1,0:T(8,128)(2,1)} %stack_quarters.2.refs_6_.refs_0_), channel_id=1, source_target_pairs={{0,16},{4,20},{8,24},{12,28},{16,0},{20,4},{24,8},{28,12},{1,17},{... | collective-permute-start | bytes 1036808 | tf_op jit(solution)/shard_map/ppermute | solution.py:68
  49.9 25.2 %collective-permute-start.9 = (bf16[720,240]{1,0:T(8,128)(2,1)}, bf16[720,240]{1,0:T(8,128)(2,1)S(1)}, u32[]{:S(2)}, u32[]{:S(2)}) collective-permute-start(bf16[720,240]{1,0:T(8,128)(2,1)} %stack_quarters.2.refs_6_.refs_0_), channel_id=1, source_target_pairs={{0,8},{4,12},{8,0},{12,4},{16,24},{20,28},{24,16},{28,20},{1,9},{5... | collective-permute-start | bytes 1036808 | tf_op jit(solution)/shard_map/ppermute | solution.py:68
  68.4 24.5 %collective-permute-start.15 = (bf16[768,640]{1,0:T(8,128)(2,1)}, bf16[768,640]{1,0:T(8,128)(2,1)S(1)}, u32[]{:S(2)}, u32[]{:S(2)}) collective-permute-start(bf16[768,640]{1,0:T(8,128)(2,1)} %stack_keys_values.1), channel_id=1, source_target_pairs={{0,4},{4,0},{1,5},{5,1},{2,6},{6,2},{3,7},{7,3},{8,12},{12,8},{9,1... | collective-permute-start | bytes 2949128 | tf_op jit(solution)/shard_map/ppermute | solution.py:59
  70.0 17.1 %collective-permute-start.16 = (bf16[240,240]{1,0:T(8,128)(2,1)S(1)}, bf16[240,240]{1,0:T(8,128)(2,1)S(1)}, u32[]{:S(2)}, u32[]{:S(2)}) collective-permute-start(bf16[240,240]{1,0:T(8,128)(2,1)S(1)} %copy-done.59), channel_id=1, source_target_pairs={{0,1},{1,0},{2,3},{3,2},{4,5},{5,4},{6,7},{7,6},{8,9},{9,8},{10,11... | collective-permute-start | bytes 345608 | tf_op jit(solution)/shard_map/ppermute | solution.py:59
  74.8 163.5 %reduce-scatter.2.cloned.1.call-start = ((), (), s32[]{:S(2)}) async-start(), calls=%async_computation.3 | async-start | bytes 2457600 | tf_op jit(solution)/shard_map/reduce_scatter | solution.py:827
  112.6 18.4 %collective-permute-start.24 = (bf16[192,960]{1,0:T(8,128)(2,1)}, bf16[192,960]{1,0:T(8,128)(2,1)S(1)}, u32[]{:S(2)}, u32[]{:S(2)}) collective-permute-start(bf16[192,960]{1,0:T(8,128)(2,1)} %get-tuple-element.152.refs_2_.refs_6_), channel_id=1, source_target_pairs={{0,20},{4,16},{8,28},{12,24},{16,4},{20,0},{24,12},{28,8},{1,21},{... | collective-permute-start | bytes 1105928 | tf_op jit(solution)/shard_map/ppermute | solution.py:68
  113.3 17.7 %collective-permute-start.25 = (bf16[192,960]{1,0:T(8,128)(2,1)}, bf16[192,960]{1,0:T(8,128)(2,1)S(1)}, u32[]{:S(2)}, u32[]{:S(2)}) collective-permute-start(bf16[192,960]{1,0:T(8,128)(2,1)} %get-tuple-element.152.refs_2_.refs_6_), channel_id=1, source_target_pairs={{0,8},{4,12},{8,0},{12,4},{16,24},{20,28},{24,16},{28,20},{1,9},{5... | collective-permute-start | bytes 1105928 | tf_op jit(solution)/shard_map/ppermute | solution.py:68
  153.1 15.7 %collective-permute-start.30 = (bf16[192,960]{1,0:T(8,128)(2,1)S(1)}, bf16[192,960]{1,0:T(8,128)(2,1)S(1)}, u32[]{:S(2)}, u32[]{:S(2)}) collective-permute-start(bf16[192,960]{1,0:T(8,128)(2,1)S(1)} %get-tuple-element.239), channel_id=1, source_target_pairs={{0,4},{4,0},{8,12},{12,8},{16,20},{20,16},{24,28},{28,24},{1,5},{5... | collective-permute-start | bytes 1105928 | tf_op jit(solution)/shard_map/ppermute | solution.py:68
  154.2 14.6 %collective-permute-start.31 = (bf16[192,960]{1,0:T(8,128)(2,1)S(1)}, bf16[192,960]{1,0:T(8,128)(2,1)S(1)}, u32[]{:S(2)}, u32[]{:S(2)}) collective-permute-start(bf16[192,960]{1,0:T(8,128)(2,1)S(1)} %get-tuple-element.238), channel_id=1, source_target_pairs={{0,16},{4,20},{8,24},{12,28},{16,0},{20,4},{24,8},{28,12},{1,17},{... | collective-permute-start | bytes 1105928 | tf_op jit(solution)/shard_map/ppermute | solution.py:68
  155.7 18.4 %collective-permute-start.32 = (bf16[192,960]{1,0:T(8,128)(2,1)S(1)}, bf16[192,960]{1,0:T(8,128)(2,1)S(1)}, u32[]{:S(2)}, u32[]{:S(2)}) collective-permute-start(bf16[192,960]{1,0:T(8,128)(2,1)S(1)} %get-tuple-element.237), channel_id=1, source_target_pairs={{0,20},{4,16},{8,28},{12,24},{16,4},{20,0},{24,12},{28,8},{1,21},{... | collective-permute-start | bytes 1105928 | tf_op jit(solution)/shard_map/ppermute | solution.py:68
  185.1 24.4 %collective-permute-start.35 = (bf16[2,192,960]{2,1,0:T(8,128)(2,1)S(1)}, bf16[2,192,960]{2,1,0:T(8,128)(2,1)S(1)}, u32[]{:S(2)}, u32[]{:S(2)}) collective-permute-start(bf16[2,192,960]{2,1,0:T(8,128)(2,1)S(1)} %add_convert_fusion), channel_id=1, source_target_pairs={{0,16},{4,20},{8,24},{12,28},{16,0},{20,4},{24,8},{28,12},{1,17},{... | collective-permute-start | bytes 2211848 | tf_op jit(solution)/shard_map/ppermute | solution.py:68
  196.8 41.5 %collective-permute-start.37 = (bf16[4,192,640]{2,1,0:T(8,128)(2,1)}, bf16[4,192,640]{2,1,0:T(8,128)(2,1)}, u32[]{:S(2)}, u32[]{:S(2)}) collective-permute-start(bf16[4,192,640]{2,1,0:T(8,128)(2,1)} %get-tuple-element.187), channel_id=1, source_target_pairs={{0,4},{4,0},{1,5},{5,1},{2,6},{6,2},{3,7},{7,3},{8,12},{12,8},{9,1... | collective-permute-start | bytes 2949128 | tf_op jit(solution)/shard_map/ppermute | solution.py:59
  198.6 17.0 %collective-permute-start.36 = (bf16[960,240]{1,0:T(8,128)(2,1)S(1)}, bf16[960,240]{1,0:T(8,128)(2,1)S(1)}, u32[]{:S(2)}, u32[]{:S(2)}) collective-permute-start(bf16[960,240]{1,0:T(8,128)(2,1)S(1)} %fusion.2), channel_id=1, source_target_pairs={{0,16},{4,20},{8,24},{12,28},{16,0},{20,4},{24,8},{28,12},{1,17},{... | collective-permute-start | bytes 1382408 | tf_op jit(solution)/shard_map/ppermute | solution.py:68
  215.9 21.7 %collective-permute-start.38 = (bf16[2,240,240]{2,1,0:T(8,128)(2,1)S(1)}, bf16[2,240,240]{2,1,0:T(8,128)(2,1)S(1)}, u32[]{:S(2)}, u32[]{:S(2)}) collective-permute-start(bf16[2,240,240]{2,1,0:T(8,128)(2,1)S(1)} %pad_maximum_fusion.2), channel_id=1, source_target_pairs={{0,2},{1,3},{2,0},{3,1},{4,6},{5,7},{6,4},{7,5},{8,10},{9,11},{10,... | collective-permute-start | bytes 691208 | tf_op jit(solution)/shard_map/ppermute | solution.py:59
  242.4 25.6 %collective-permute-start.43 = (bf16[192,640]{1,0:T(8,128)(2,1)S(1)}, bf16[192,640]{1,0:T(8,128)(2,1)S(1)}, u32[]{:S(2)}, u32[]{:S(2)}) collective-permute-start(bf16[192,640]{1,0:T(8,128)(2,1)S(1)} %get-tuple-element.252), channel_id=1, source_target_pairs={{0,2},{1,3},{2,0},{3,1},{4,6},{5,7},{6,4},{7,5},{8,10},{9,11},{10,... | collective-permute-start | bytes 737288 | tf_op jit(solution)/shard_map/ppermute | solution.py:59
  243.8 24.2 %collective-permute-start.44 = (bf16[192,640]{1,0:T(8,128)(2,1)S(1)}, bf16[192,640]{1,0:T(8,128)(2,1)S(1)}, u32[]{:S(2)}, u32[]{:S(2)}) collective-permute-start(bf16[192,640]{1,0:T(8,128)(2,1)S(1)} %get-tuple-element.251), channel_id=1, source_target_pairs={{0,3},{1,2},{2,1},{3,0},{4,7},{5,6},{6,5},{7,4},{8,11},{9,10},{10,... | collective-permute-start | bytes 737288 | tf_op jit(solution)/shard_map/ppermute | solution.py:59
  256.3 21.0 %collective-permute-start.49 = (bf16[2,240,240]{2,1,0:T(8,128)(2,1)}, bf16[2,240,240]{2,1,0:T(8,128)(2,1)}, u32[]{:S(2)}, u32[]{:S(2)}) collective-permute-start(bf16[2,240,240]{2,1,0:T(8,128)(2,1)} %pad_maximum_fusion.3), channel_id=1, source_target_pairs={{0,2},{1,3},{2,0},{3,1},{4,6},{5,7},{6,4},{7,5},{8,10},{9,11},{10,... | collective-permute-start | bytes 691208 | tf_op jit(solution)/shard_map/ppermute | solution.py:59
  275.1 28.8 %collective-permute-start.58 = (bf16[240,960]{1,0:T(8,128)(2,1)}, bf16[240,960]{1,0:T(8,128)(2,1)S(1)}, u32[]{:S(2)}, u32[]{:S(2)}) collective-permute-start(bf16[240,960]{1,0:T(8,128)(2,1)} %reduce-scatter.2.cloned.1.call-done.refs_0_), channel_id=1, source_target_pairs={{0,16},{4,20},{8,24},{12,28},{16,0},{20,4},{24,8},{28,12},{1,17},{... | collective-permute-start | bytes 1382408 | tf_op jit(solution)/shard_map/ppermute | solution.py:68
  282.1 17.1 %collective-permute-start.47 = (bf16[336,240]{1,0:T(8,128)(2,1)S(1)}, bf16[336,240]{1,0:T(8,128)(2,1)S(1)}, u32[]{:S(2)}, u32[]{:S(2)}) collective-permute-start(bf16[336,240]{1,0:T(8,128)(2,1)S(1)} %get-tuple-element.250), channel_id=1, source_target_pairs={{0,2},{1,3},{2,0},{3,1},{4,6},{5,7},{6,4},{7,5},{8,10},{9,11},{10,... | collective-permute-start | bytes 483848 | tf_op jit(solution)/shard_map/ppermute | solution.py:59
  303.4 31.3 %collective-permute-start.56 = (bf16[240,960]{1,0:T(8,128)(2,1)S(1)}, bf16[240,960]{1,0:T(8,128)(2,1)S(1)}, u32[]{:S(2)}, u32[]{:S(2)}) collective-permute-start(bf16[240,960]{1,0:T(8,128)(2,1)S(1)} %copy-done.22), channel_id=1, source_target_pairs={{0,8},{4,12},{8,0},{12,4},{16,24},{20,28},{24,16},{28,20},{1,9},{5... | collective-permute-start | bytes 1382408 | tf_op jit(solution)/shard_map/ppermute | solution.py:68
  303.4 31.3 %collective-permute-start.57 = (bf16[240,960]{1,0:T(8,128)(2,1)S(1)}, bf16[240,960]{1,0:T(8,128)(2,1)S(1)}, u32[]{:S(2)}, u32[]{:S(2)}) collective-permute-start(bf16[240,960]{1,0:T(8,128)(2,1)S(1)} %copy-done.24), channel_id=1, source_target_pairs={{0,8},{4,12},{8,0},{12,4},{16,24},{20,28},{24,16},{28,20},{1,9},{5... | collective-permute-start | bytes 1382408 | tf_op jit(solution)/shard_map/ppermute | solution.py:68
  303.9 24.5 %collective-permute-start.59 = (bf16[240,960]{1,0:T(8,128)(2,1)S(1)}, bf16[240,960]{1,0:T(8,128)(2,1)S(1)}, u32[]{:S(2)}, u32[]{:S(2)}) collective-permute-start(bf16[240,960]{1,0:T(8,128)(2,1)S(1)} %collective-permute-done.58.refs_4_), channel_id=1, source_target_pairs={{0,4},{4,0},{8,12},{12,8},{16,20},{20,16},{24,28},{28,24},{1,5},{5... | collective-permute-start | bytes 1382408 | tf_op jit(solution)/shard_map/ppermute | solution.py:68
  306.3 28.4 %collective-permute-start.60 = (bf16[240,960]{1,0:T(8,128)(2,1)S(1)}, bf16[240,960]{1,0:T(8,128)(2,1)S(1)}, u32[]{:S(2)}, u32[]{:S(2)}) collective-permute-start(bf16[240,960]{1,0:T(8,128)(2,1)S(1)} %collective-permute-done.58.refs_4_), channel_id=1, source_target_pairs={{0,8},{4,12},{8,0},{12,4},{16,24},{20,28},{24,16},{28,20},{1,9},{5... | collective-permute-start | bytes 1382408 | tf_op jit(solution)/shard_map/ppermute | solution.py:68
  (98 other events, 711.0 us)
Sparse Core Ops, SparseCore 0:
  9.9 34.9 all-gather.2
  75.0 45.7 all-gather.4
  174.3 47.8 reduce-scatter.1

commit v10 on v8

--- a/solution.py
+++ b/solution.py
@@ -747,15 +747,14 @@
     near = [kv_own] + direct_fsdp(kv_own)
     query_pieces = lax.optimization_barrier((kv_own, *query_pieces))[1:]
     stacked, across = stack(query_pieces)
-    output_quarter = after(output_quarter, near[1])
     across, *near = lax.optimization_barrier((across, *near))
     query_stacks = four(stacked, across)
-    output_pieces = direct_fsdp(output_quarter)
     (near_all,) = call(
         stack_kernel, spots, near, [((near_count, 2 * kv_width), BF16)],
         name="stack_keys_values",
     )
     far = [swap(near_all, "ctx", d) for d in range(1, ctx_count)]
+    output_pieces = direct_fsdp(after(output_quarter, near_all))
 
     pack, cot_all, _ = lax.optimization_barrier((pack, cot_all, near[-1]))
     pack_all = lax.all_gather(pack, "fsdp", axis=0, tiled=True)
@@ -779,7 +778,9 @@
         scratch=[((far_count, 2 * kv_width), BF16)], name="attention_far",
     )
     output_pieces = lax.optimization_barrier((queries, *output_pieces))[1:]
-    output_stacks = four(*stack(output_pieces))
+    output_stacked, output_across = stack(output_pieces)
+    attended, output_across = lax.optimization_barrier((attended, output_across))
+    output_stacks = four(output_stacked, output_across)
     residual, inverse_two, normed_two = call(
         functools.partial(project_kernel, shards, dp_count), spots,
         [attended, tokens, gains, output_weight, *output_stacks],
@@ -832,7 +833,9 @@
     )
     pack_share = sum_far(lax.psum_scatter(pack_grad, "fsdp", scatter_dimension=0, tiled=True))
 
-    pack_grad, *grad_chips = lax.optimization_barrier((pack_grad, *grad_chips))
+    pack_grad, result_b, *grad_chips = lax.optimization_barrier(
+        (pack_grad, result_b, *grad_chips)
+    )
     residual_grad, residual_low, attended_grad, second_gain_grad = call(
         functools.partial(middle_kernel, shards, dp_count), spots,
         [
@@ -844,7 +847,7 @@
         name="residual_back",
     )
 
-    result_core = swap_core(after(result_b, residual_low))
+    result_core = swap_core(result_b)
     attended_grad, result_a = lax.optimization_barrier((attended_grad, result_a))
 
     def sum_x(keep, away):
@@ -923,8 +926,8 @@
         [attended, residual_low, normed_one, query_low], [pair_shape, pair_shape],
         scratch=[((2 * dp_count, rows, quarter), BF16)], name="query_output_weight_grads",
     )
-    weights_send, far_grads[-1], result_across = lax.optimization_barrier(
-        (weights_send, far_grads[-1], result_across)
+    weights_send, pack_share, far_grads[-1], result_across = lax.optimization_barrier(
+        (weights_send, pack_share, far_grads[-1], result_across)
     )
     result_own, result_along = [
         (result_a[k].astype(F32) + result_core[k].astype(F32)) + result_across[k].astype(F32)
@@ -939,9 +942,7 @@
         r: (near_grads[r].astype(F32) + home(r)).astype(BF16) for r in range(1, shards)
     }
     kv_arrived = {r: swap(kv_sums[r], "fsdp", r) for r in reversed(range(1, shards))}
-    query_low, pack_share, *_ = lax.optimization_barrier(
-        (query_low, pack_share, *kv_sums.values())
-    )
+    query_low = lax.optimization_barrier((query_low, *kv_sums.values()))[0]
 
     weights_away = swap_core(weights_send)
     weights_sent, weights_terms = sum_x(weights_keep, weights_away)

time: 355 us -> 354 us (level)
  waiting for transfers between devices: 115 us -> 102 us
  starting transfers between devices: 66.7 us -> 79.6 us
    ppermute x40, waiting for transfers between devices: 44.9 us -> 32.4 us  [swap_plane(): return lax.ppermute(x, ('dp', 'ctx'), pairs)]
    ppermute x22, starting transfers between devices: 42.8 us -> 55 us  [swap(): return lax.ppermute(x, axis, [(i, i ^ mask) for i in range(count)])]
    unnamed x122 -> x118, local copies, waits for them, and re-layouts: 12.5 us -> 10.6 us
  transfers between devices with their start and end apart: 65 -> 65, of which waited for: 21 -> 20; matrix products, arithmetic and copies ran while one was open for 6% -> 6% of each run, Pallas kernels for 29% -> 31%
where the time goes in v10:
time: 354 us; the launch traced here: 349 us
  Pallas kernels  118 us (33%)
  waiting for transfers between devices  102 us (29%)
  starting transfers between devices  79.6 us (22%)
  local copies, waits for them, and re-layouts  18.6 us (5%)
  between operations  15.6 us (4%)
  other arithmetic  14.8 us (4%)
    pallas_call x20, Pallas kernels, call(): pl.pallas_call(kernel, out_shape=outs, in_specs=specs, out_specs=tuple((p...  118 us
    ppermute x22, waiting for transfers between devices, swap(): return lax.ppermute(x, axis, [(i, i ^ mask) for i in range(count)])  67.3 us
    ppermute x22, starting transfers between devices, swap(): return lax.ppermute(x, axis, [(i, i ^ mask) for i in range(count)])  55 us
    ppermute x40, waiting for transfers between devices, swap_plane(): return lax.ppermute(x, ('dp', 'ctx'), pairs)  32.4 us
    ppermute x40, starting transfers between devices, swap_plane(): return lax.ppermute(x, ('dp', 'ctx'), pairs)  24.4 us
    unnamed x118, local copies, waits for them, and re-layouts  10.6 us
  transfers between devices with their start and end apart: 65, of which 20 were waited for; matrix products, arithmetic and copies ran while one was open for 6% of the time, Pallas kernels for 31%

profile of v10, /device:TPU:0, one launch (start us, length us, event | category | flops | bytes accessed | tf_op | source)
XLA Modules:
  0.0 348.6 jit_solution(10502528713719771782)
XLA Ops:
  19.5 3.5 %collective-permute-start.7 = (bf16[240,240]{1,0:T(8,128)(2,1)}, bf16[240,240]{1,0:T(8,128)(2,1)S(1)}, u32[]{:S(2)}, u32[]{:S(2)}) collective-permute-start(bf16[240,240]{1,0:T(8,128)(2,1)} %get-tuple-element.116), channel_id=1, source_target_pairs={{0,2},{1,3},{2,0},{3,1},{4,6},{5,7},{6,4},{7,5},{8,10},{9,11},{10,... | collective-permute-start | bytes 345608 | tf_op jit(solution)/shard_map/ppermute | solution.py:58
  24.8 4.2 %pack_weights.1 = bf16[240,960]{1,0:T(8,128)(2,1)} custom-call(s32[4]{0:T(128)} %pad_add_fusion.1.spots, bf16[240,2560]{1,0:T(8,128)(2,1)} %gate_ref.1, bf16[240,2560]{1,0:T(8,128)(2,1)} %up_ref.1, bf16[960,640]{1,0:T(8,128)(2,1)} %bitcast.98), custom_call_target="tpu_custom_call" | custom-call | flops 4600000000 | tf_op jit(solution)/shard_map/pack_weights/pallas_call | solution.py:106
  31.3 4.3 %collective-permute-start.8 = (bf16[240,240]{1,0:T(8,128)(2,1)S(1)}, bf16[240,240]{1,0:T(8,128)(2,1)S(1)}, u32[]{:S(2)}, u32[]{:S(2)}) collective-permute-start(bf16[240,240]{1,0:T(8,128)(2,1)S(1)} %copy-done.57), channel_id=1, source_target_pairs={{0,3},{1,2},{2,1},{3,0},{4,7},{5,6},{6,5},{7,4},{8,11},{9,10},{10,... | collective-permute-start | bytes 345608 | tf_op jit(solution)/shard_map/ppermute | solution.py:58
  36.3 3.6 %norm_keys_values.1 = (bf16[192,640]{1,0:T(8,128)(2,1)}, bf16[192,960]{1,0:T(8,128)(2,1)}, bf16[192,960]{1,0:T(8,128)(2,1)}, f32[192,1]{1,0:T(8,128)}, f32[8,960]{1,0:T(8,128)}) custom-call(s32[4]{0:T(128)} %pad_add_fusion.1.spots, bf16[192,960]{1,0:T(8,128)(2,1)} %bitcast.99, bf16[1,240]{1,0:T(2,128)(2,1)} %copy-done.18, bf16[1,240]{1,0:T(2,128)(2,1)} %copy-done.17, ...), custom_call_target="tpu_custom_call" | custom-call | flops 4600000000 | tf_op jit(solution)/shard_map/norm_keys_values/pallas_call | solution.py:106
  49.9 3.4 collective-permute-done.11.refs_11_.refs_1_.refs_10_
  53.3 9.9 %collective-permute-done.12.refs_12_.refs_2_.refs_11_ = bf16[192,640]{1,0:T(8,128)(2,1)S(1)} collective-permute-done((bf16[192,640]{1,0:T(8,128)(2,1)}, bf16[192,640]{1,0:T(8,128)(2,1)S(1)}, u32[]{:S(2)}, u32[]{:S(2)}) %collective-permute-start.12) | collective-permute-done | bytes 245792 | tf_op jit(solution)/shard_map/ppermute | solution.py:58
  70.0 4.8 %collective-permute-start.16 = (bf16[240,240]{1,0:T(8,128)(2,1)S(1)}, bf16[240,240]{1,0:T(8,128)(2,1)S(1)}, u32[]{:S(2)}, u32[]{:S(2)}) collective-permute-start(bf16[240,240]{1,0:T(8,128)(2,1)S(1)} %copy-done.56), channel_id=1, source_target_pairs={{0,1},{1,0},{2,3},{3,2},{4,5},{5,4},{6,7},{7,6},{8,9},{9,8},{10,11... | collective-permute-start | bytes 345608 | tf_op jit(solution)/shard_map/ppermute | solution.py:58
  78.3 8.7 %attention_near.1 = (bf16[192,960]{1,0:T(8,128)(2,1)}, f32[5,576]{1,0:T(8,128)}, f32[5,576]{1,0:T(8,128)}, f32[5,64,576]{2,1,0:T(8,128)}) custom-call(s32[4]{0:T(128)} %pad_add_fusion.1.spots, bf16[192,960]{1,0:T(8,128)(2,1)} %get-tuple-element.118.refs_0_, s32[768,1]{1,0:T(8,128)} %slice.124.refs_1_, s32[1,576]{1,0:T(1,128)} %broadcast_in_dim.29.refs_2_, ...), custom_call_target="tpu_custom_call" | custom-call | flops 13799999488 | tf_op jit(solution)/shard_map/attention_near/pallas_call | solution.py:106
  93.9 9.0 %attention_far.1 = (bf16[192,960]{1,0:T(8,128)(2,1)}, f32[5,64,576]{2,1,0:T(8,128)}, f32[5,576]{1,0:T(8,128)}) custom-call(s32[4]{0:T(128)} %pad_add_fusion.1.spots, bf16[192,960]{1,0:T(8,128)(2,1)} %get-tuple-element.128.refs_0_, s32[768,1]{1,0:T(8,128)} %slice.125.refs_1_, s32[1,576]{1,0:T(1,128)} %broadcast_in_dim.29.refs_2_, ...), custom_call_target="tpu_custom_call" | custom-call | flops 13799999488 | tf_op jit(solution)/shard_map/attention_far/pallas_call | solution.py:106
  105.5 4.2 %project_residual.1 = (f32[192,960]{1,0:T(8,128)}, f32[192,1]{1,0:T(8,128)}, bf16[192,960]{1,0:T(8,128)(2,1)}) custom-call(s32[4]{0:T(128)} %pad_add_fusion.1.spots, bf16[192,960]{1,0:T(8,128)(2,1)} %get-tuple-element.138.refs_0_, bf16[192,960]{1,0:T(8,128)(2,1)} %bitcast.100, f32[8,960]{1,0:T(8,128)} %get-tuple-element.139.refs_2_.refs_8_.refs_5_, ...), custom_call_target="tpu_custom_call" | custom-call | flops 2300000000 | tf_op jit(solution)/shard_map/project_residual/pallas_call | solution.py:106
  113.2 8.1 %collective-permute-done.22.refs_3_.refs_7_ = bf16[192,960]{1,0:T(8,128)(2,1)S(1)} collective-permute-done((bf16[192,960]{1,0:T(8,128)(2,1)}, bf16[192,960]{1,0:T(8,128)(2,1)S(1)}, u32[]{:S(2)}, u32[]{:S(2)}) %collective-permute-start.22) | collective-permute-done | bytes 368672 | tf_op jit(solution)/shard_map/ppermute | solution.py:67
  123.3 7.7 %collective-permute-done.24.refs_5_.refs_9_ = bf16[192,960]{1,0:T(8,128)(2,1)S(1)} collective-permute-done((bf16[192,960]{1,0:T(8,128)(2,1)}, bf16[192,960]{1,0:T(8,128)(2,1)S(1)}, u32[]{:S(2)}, u32[]{:S(2)}) %collective-permute-start.24) | collective-permute-done | bytes 368672 | tf_op jit(solution)/shard_map/ppermute | solution.py:67
  133.4 8.5 %feed_forward.3 = (bf16[4,192,960]{2,1,0:T(8,128)(2,1)}, bf16[768,320]{1,0:T(8,128)(2,1)}, bf16[768,640]{1,0:T(8,128)(2,1)}) custom-call(s32[4]{0:T(128)} %pad_add_fusion.1.spots, bf16[960,960]{1,0:T(8,128)(2,1)} %all-gather.5.cloned.1.call-done.refs_0_, bf16[8,192,960]{2,1,0:T(8,128)(2,1)} %all-gather.3.cloned.1.call-done.refs_1_.refs_5_, ...), custom_call_target="tpu_custom_call" | custom-call | flops 9200000000 | tf_op jit(solution)/shard_map/feed_forward/pallas_call | solution.py:106
  142.2 8.5 %feed_forward.2 = (bf16[4,192,960]{2,1,0:T(8,128)(2,1)}, bf16[768,320]{1,0:T(8,128)(2,1)}, bf16[768,640]{1,0:T(8,128)(2,1)}) custom-call(s32[4]{0:T(128)} %pad_add_fusion.1.spots, bf16[960,960]{1,0:T(8,128)(2,1)} %all-gather.5.cloned.1.call-done.refs_0_, bf16[8,192,960]{2,1,0:T(8,128)(2,1)} %all-gather.3.cloned.1.call-done.refs_1_.refs_5_, ...), custom_call_target="tpu_custom_call" | custom-call | flops 9200000000 | tf_op jit(solution)/shard_map/feed_forward/pallas_call | solution.py:106
  156.6 12.1 %feed_forward_weights.1 = (bf16[4,192,960]{2,1,0:T(8,128)(2,1)}, bf16[4,192,960]{2,1,0:T(8,128)(2,1)}, bf16[960,960]{1,0:T(8,128)(2,1)}) custom-call(s32[4]{0:T(128)} %pad_add_fusion.1.spots, bf16[960,960]{1,0:T(8,128)(2,1)} %all-gather.5.cloned.1.call-done.refs_0_, bf16[768,320]{1,0:T(8,128)(2,1)} %get-tuple-element.148.refs_1_, ...), custom_call_target="tpu_custom_call" | custom-call | flops 13799999488 | tf_op jit(solution)/shard_map/feed_forward_weights/pallas_call | solution.py:106
  168.8 5.4 %collective-permute-done.32.refs_4_ = bf16[192,960]{1,0:T(8,128)(2,1)} collective-permute-done((bf16[192,960]{1,0:T(8,128)(2,1)S(1)}, bf16[192,960]{1,0:T(8,128)(2,1)}, u32[]{:S(2)}, u32[]{:S(2)}) %collective-permute-start.32) | collective-permute-done | bytes 368672 | tf_op jit(solution)/shard_map/ppermute | solution.py:67
  174.2 5.5 %residual_back.1 = (f32[192,960]{1,0:T(8,128)}, bf16[192,960]{1,0:T(8,128)(2,1)}, bf16[192,960]{1,0:T(8,128)(2,1)}, f32[1,960]{1,0:T(1,128)}) custom-call(s32[4]{0:T(128)} %pad_add_fusion.1.spots, bf16[4,192,960]{2,1,0:T(8,128)(2,1)} %get-tuple-element.145.refs_0_, bf16[4,192,960]{2,1,0:T(8,128)(2,1)} %copy-done.4, bf16[192,960]{1,0:T(8,128)(2,1)} %copy-done.35, ...), custom_call_target="tpu_custom_call" | custom-call | flops 6899999744 | tf_op jit(solution)/shard_map/residual_back/pallas_call | solution.py:106
  179.8 10.6 %attention_back_far.1 = (f32[5,64,576]{2,1,0:T(8,128)}, bf16[4,192,640]{2,1,0:T(8,128)(2,1)}) custom-call(s32[4]{0:T(128)} %pad_add_fusion.1.spots, bf16[192,960]{1,0:T(8,128)(2,1)} %get-tuple-element.128.refs_0_, s32[768,1]{1,0:T(8,128)} %slice.125.refs_1_, s32[1,576]{1,0:T(1,128)} %broadcast_in_dim.29.refs_2_, ...), custom_call_target="tpu_custom_call" | custom-call | flops 14949999616 | tf_op jit(solution)/shard_map/attention_back_far/pallas_call | solution.py:106
  193.2 10.4 %attention_back_near.1 = (bf16[192,960]{1,0:T(8,128)(2,1)}, bf16[192,640]{1,0:T(8,128)(2,1)}, bf16[192,640]{1,0:T(8,128)(2,1)}, bf16[192,640]{1,0:T(8,128)(2,1)}, bf16[192,640]{1,0:T(8,128)(2,1)}) custom-call(s32[4]{0:T(128)} %pad_add_fusion.1.spots, bf16[192,960]{1,0:T(8,128)(2,1)} %get-tuple-element.128.refs_0_, s32[768,1]{1,0:T(8,128)} %slice.124.refs_1_, ...), custom_call_target="tpu_custom_call" | custom-call | flops 16099999744 | tf_op jit(solution)/shard_map/attention_back_near/pallas_call | solution.py:106
  203.6 5.0 %query_output_weight_grads.1 = (bf16[2,960,480]{2,1,0:T(8,128)(2,1)}, bf16[2,960,480]{2,1,0:T(8,128)(2,1)}) custom-call(s32[4]{0:T(128)} %pad_add_fusion.1.spots, bf16[192,960]{1,0:T(8,128)(2,1)} %get-tuple-element.138.refs_0_, bf16[192,960]{1,0:T(8,128)(2,1)} %get-tuple-element.162.refs_1_, bf16[192,960]{1,0:T(8,128)(2,1)} %get-tuple-element.163.refs_2_, ...), custom_call_target="tpu_custom_call" | custom-call | tf_op jit(solution)/shard_map/query_output_weight_grads/pallas_call | solution.py:106
  208.7 6.2 %collective-permute-done.34.refs_12_ = bf16[4,192,640]{2,1,0:T(8,128)(2,1)} collective-permute-done((bf16[4,192,640]{2,1,0:T(8,128)(2,1)}, bf16[4,192,640]{2,1,0:T(8,128)(2,1)}, u32[]{:S(2)}, u32[]{:S(2)}) %collective-permute-start.34) | collective-permute-done | bytes 983072 | tf_op jit(solution)/shard_map/ppermute | solution.py:58
  219.7 6.2 %collective-permute-start.38 = (bf16[192,640]{1,0:T(8,128)(2,1)S(1)}, bf16[192,640]{1,0:T(8,128)(2,1)S(1)}, u32[]{:S(2)}, u32[]{:S(2)}) collective-permute-start(bf16[192,640]{1,0:T(8,128)(2,1)S(1)} %get-tuple-element.232), channel_id=1, source_target_pairs={{0,1},{1,0},{2,3},{3,2},{4,5},{5,4},{6,7},{7,6},{8,9},{9,8},{10,11... | collective-permute-start | bytes 737288 | tf_op jit(solution)/shard_map/ppermute | solution.py:58
  231.1 3.6 %query_back.1.refs_6_ = f32[192,960]{1,0:T(8,128)} custom-call(s32[4]{0:T(128)} %pad_add_fusion.1.spots, bf16[192,960]{1,0:T(8,128)(2,1)} %get-tuple-element.182.refs_3_.low_ref, bf16[240,960]{1,0:T(8,128)(2,1)} %local_ref.1, bf16[720,240]{1,0:T(8,128)(2,1)} %stack_quarters.2.refs_6_.refs_0_, bf16[720,240]{1,0:T(8,128)(2,1)} %copy-done.8, ...), custom_call_target="tpu_custom_call" | custom-call | tf_op jit(solution)/shard_map/query_back/pallas_call | solution.py:106
  237.0 9.2 %collective-permute-done.39.refs_14_ = bf16[192,640]{1,0:T(8,128)(2,1)S(1)} collective-permute-done((bf16[192,640]{1,0:T(8,128)(2,1)S(1)}, bf16[192,640]{1,0:T(8,128)(2,1)S(1)}, u32[]{:S(2)}, u32[]{:S(2)}) %collective-permute-start.39) | collective-permute-done | bytes 245792 | tf_op jit(solution)/shard_map/ppermute | solution.py:58
  246.9 6.2 %keys_values_back.1 = (f32[192,960]{1,0:T(8,128)}, bf16[4,336,240]{2,1,0:T(8,128)(2,1)}, bf16[4,336,240]{2,1,0:T(8,128)(2,1)}) custom-call(s32[4]{0:T(128)} %pad_add_fusion.1.spots, f32[192,128]{1,0:T(8,128)} %pad_maximum_fusion.2.refs_5_.refs_3_.refs_0_, f32[192,128]{1,0:T(8,128)} %pad_maximum_fusion.3.refs_6_.refs_4_.refs_1_, ...), custom_call_target="tpu_custom_call" | custom-call | flops 6899999744 | tf_op jit(solution)/shard_map/keys_values_back/pallas_call | solution.py:106
  257.5 6.2 %collective-permute-start.46 = (bf16[2,240,480]{2,1,0:T(8,128)(2,1)S(1)}, bf16[2,240,480]{2,1,0:T(8,128)(2,1)S(1)}, u32[]{:S(2)}, u32[]{:S(2)}) collective-permute-start(bf16[2,240,480]{2,1,0:T(8,128)(2,1)S(1)} %pad_maximum_fusion), channel_id=1, source_target_pairs={{0,2},{1,3},{2,0},{3,1},{4,6},{5,7},{6,4},{7,5},{8,10},{9,11},{10,... | collective-permute-start | bytes 1382408 | tf_op jit(solution)/shard_map/ppermute | solution.py:58
  264.6 3.5 %collective-permute-start.43 = (bf16[336,240]{1,0:T(8,128)(2,1)S(1)}, bf16[336,240]{1,0:T(8,128)(2,1)S(1)}, u32[]{:S(2)}, u32[]{:S(2)}) collective-permute-start(bf16[336,240]{1,0:T(8,128)(2,1)S(1)} %get-tuple-element.195), channel_id=1, source_target_pairs={{0,1},{1,0},{2,3},{3,2},{4,5},{5,4},{6,7},{7,6},{8,9},{9,8},{10,11... | collective-permute-start | bytes 483848 | tf_op jit(solution)/shard_map/ppermute | solution.py:58
  268.2 12.4 %collective-permute-done.45 = bf16[336,240]{1,0:T(8,128)(2,1)S(1)} collective-permute-done((bf16[336,240]{1,0:T(8,128)(2,1)S(1)}, bf16[336,240]{1,0:T(8,128)(2,1)S(1)}, u32[]{:S(2)}, u32[]{:S(2)}) %collective-permute-start.45) | collective-permute-done | bytes 161312 | tf_op jit(solution)/shard_map/ppermute | solution.py:58
  281.9 17.9 %collective-permute-done.44 = bf16[336,240]{1,0:T(8,128)(2,1)S(1)} collective-permute-done((bf16[336,240]{1,0:T(8,128)(2,1)S(1)}, bf16[336,240]{1,0:T(8,128)(2,1)S(1)}, u32[]{:S(2)}, u32[]{:S(2)}) %collective-permute-start.44) | collective-permute-done | bytes 161312 | tf_op jit(solution)/shard_map/ppermute | solution.py:58
  303.1 6.1 %collective-permute-start.57 = (bf16[1,240,480]{2,1,0:T(8,128)(2,1)S(1)}, bf16[1,240,480]{2,1,0:T(8,128)(2,1)S(1)}, u32[]{:S(2)}, u32[]{:S(2)}) collective-permute-start(bf16[1,240,480]{2,1,0:T(8,128)(2,1)S(1)} %bitcast.91), channel_id=1, source_target_pairs={{0,1},{1,0},{2,3},{3,2},{4,5},{5,4},{6,7},{7,6},{8,9},{9,8},{10,11... | collective-permute-start | bytes 691208 | tf_op jit(solution)/shard_map/ppermute | solution.py:58
  309.3 4.1 %collective-permute-done.57 = bf16[1,240,480]{2,1,0:T(8,128)(2,1)S(1)} collective-permute-done((bf16[1,240,480]{2,1,0:T(8,128)(2,1)S(1)}, bf16[1,240,480]{2,1,0:T(8,128)(2,1)S(1)}, u32[]{:S(2)}, u32[]{:S(2)}) %collective-permute-start.57) | collective-permute-done | bytes 230432 | tf_op jit(solution)/shard_map/ppermute | solution.py:58
  316.5 6.7 %feed_forward_out.1 = (f32[240,2560]{1,0:T(8,128)}, f32[240,2560]{1,0:T(8,128)}, f32[960,640]{1,0:T(8,128)}) custom-call(s32[4]{0:T(128)} %pad_add_fusion.1.spots, bf16[240,960]{1,0:T(8,128)(2,1)} %reduce-scatter.2.cloned.1.call-done.refs_0_, bf16[240,960]{1,0:T(8,128)(2,1)} %copy-done.22, bf16[240,960]{1,0:T(8,128)(2,1)} %copy-done.25, ...), custom_call_target="tpu_custom_call" | custom-call | flops 8049999872 | tf_op jit(solution)/shard_map/feed_forward_out/pallas_call | solution.py:106
  (284 shorter events, 107.0 us)
Async XLA Ops:
  7.2 67.7 %all-gather.3.cloned.1.call-start = ((), (), s32[]{:S(2)}) async-start(), calls=%async_computation.1 | async-start | bytes 3538944 | tf_op jit(solution)/shard_map/all_gather | solution.py:711
  7.9 124.7 %all-gather.5.cloned.1.call-start = ((), (), s32[]{:S(2)}) async-start(), calls=%async_computation.2 | async-start | bytes 2457600 | tf_op jit(solution)/shard_map/all_gather | solution.py:760
  10.4 19.4 %collective-permute-start = (bf16[336,240]{1,0:T(8,128)(2,1)S(1)}, bf16[336,240]{1,0:T(8,128)(2,1)S(1)}, u32[]{:S(2)}, u32[]{:S(2)}) collective-permute-start(bf16[336,240]{1,0:T(8,128)(2,1)S(1)} %pad_maximum_fusion.1), channel_id=1, source_target_pairs={{0,1},{1,0},{2,3},{3,2},{4,5},{5,4},{6,7},{7,6},{8,9},{9,8},{10,11... | collective-permute-start | bytes 483848 | tf_op jit(solution)/shard_map/ppermute | solution.py:58
  13.5 16.3 %collective-permute-start.1 = (bf16[336,240]{1,0:T(8,128)(2,1)S(1)}, bf16[336,240]{1,0:T(8,128)(2,1)S(1)}, u32[]{:S(2)}, u32[]{:S(2)}) collective-permute-start(bf16[336,240]{1,0:T(8,128)(2,1)S(1)} %pad_maximum_fusion.1), channel_id=1, source_target_pairs={{0,2},{1,3},{2,0},{3,1},{4,6},{5,7},{6,4},{7,5},{8,10},{9,11},{10,... | collective-permute-start | bytes 483848 | tf_op jit(solution)/shard_map/ppermute | solution.py:58
  18.6 24.2 %collective-permute-start.6 = (bf16[240,240]{1,0:T(8,128)(2,1)}, bf16[240,240]{1,0:T(8,128)(2,1)S(1)}, u32[]{:S(2)}, u32[]{:S(2)}) collective-permute-start(bf16[240,240]{1,0:T(8,128)(2,1)} %get-tuple-element.116), channel_id=1, source_target_pairs={{0,1},{1,0},{2,3},{3,2},{4,5},{5,4},{6,7},{7,6},{8,9},{9,8},{10,11... | collective-permute-start | bytes 345608 | tf_op jit(solution)/shard_map/ppermute | solution.py:58
  19.5 25.7 %collective-permute-start.7 = (bf16[240,240]{1,0:T(8,128)(2,1)}, bf16[240,240]{1,0:T(8,128)(2,1)S(1)}, u32[]{:S(2)}, u32[]{:S(2)}) collective-permute-start(bf16[240,240]{1,0:T(8,128)(2,1)} %get-tuple-element.116), channel_id=1, source_target_pairs={{0,2},{1,3},{2,0},{3,1},{4,6},{5,7},{6,4},{7,5},{8,10},{9,11},{10,... | collective-permute-start | bytes 345608 | tf_op jit(solution)/shard_map/ppermute | solution.py:58
  42.8 20.5 %collective-permute-start.12 = (bf16[192,640]{1,0:T(8,128)(2,1)}, bf16[192,640]{1,0:T(8,128)(2,1)S(1)}, u32[]{:S(2)}, u32[]{:S(2)}) collective-permute-start(bf16[192,640]{1,0:T(8,128)(2,1)} %get-tuple-element.124.refs_10_.refs_0_.refs_9_), channel_id=1, source_target_pairs={{0,2},{1,3},{2,0},{3,1},{4,6},{5,7},{6,4},{7,5},{8,10},{9,11},{10,... | collective-permute-start | bytes 737288 | tf_op jit(solution)/shard_map/ppermute | solution.py:58
  42.8 20.5 %collective-permute-start.13 = (bf16[192,640]{1,0:T(8,128)(2,1)}, bf16[192,640]{1,0:T(8,128)(2,1)S(1)}, u32[]{:S(2)}, u32[]{:S(2)}) collective-permute-start(bf16[192,640]{1,0:T(8,128)(2,1)} %get-tuple-element.124.refs_10_.refs_0_.refs_9_), channel_id=1, source_target_pairs={{0,3},{1,2},{2,1},{3,0},{4,7},{5,6},{6,5},{7,4},{8,11},{9,10},{10,... | collective-permute-start | bytes 737288 | tf_op jit(solution)/shard_map/ppermute | solution.py:58
  48.3 15.0 %collective-permute-start.10 = (bf16[720,240]{1,0:T(8,128)(2,1)}, bf16[720,240]{1,0:T(8,128)(2,1)S(1)}, u32[]{:S(2)}, u32[]{:S(2)}) collective-permute-start(bf16[720,240]{1,0:T(8,128)(2,1)} %stack_quarters.2.refs_6_.refs_0_), channel_id=1, source_target_pairs={{0,16},{4,20},{8,24},{12,28},{16,0},{20,4},{24,8},{28,12},{1,17},{... | collective-permute-start | bytes 1036808 | tf_op jit(solution)/shard_map/ppermute | solution.py:67
  49.9 25.3 %collective-permute-start.9 = (bf16[720,240]{1,0:T(8,128)(2,1)}, bf16[720,240]{1,0:T(8,128)(2,1)S(1)}, u32[]{:S(2)}, u32[]{:S(2)}) collective-permute-start(bf16[720,240]{1,0:T(8,128)(2,1)} %stack_quarters.2.refs_6_.refs_0_), channel_id=1, source_target_pairs={{0,8},{4,12},{8,0},{12,4},{16,24},{20,28},{24,16},{28,20},{1,9},{5... | collective-permute-start | bytes 1036808 | tf_op jit(solution)/shard_map/ppermute | solution.py:67
  68.5 24.4 %collective-permute-start.15 = (bf16[768,640]{1,0:T(8,128)(2,1)}, bf16[768,640]{1,0:T(8,128)(2,1)S(1)}, u32[]{:S(2)}, u32[]{:S(2)}) collective-permute-start(bf16[768,640]{1,0:T(8,128)(2,1)} %stack_keys_values.1), channel_id=1, source_target_pairs={{0,4},{4,0},{1,5},{5,1},{2,6},{6,2},{3,7},{7,3},{8,12},{12,8},{9,1... | collective-permute-start | bytes 2949128 | tf_op jit(solution)/shard_map/ppermute | solution.py:58
  70.0 17.1 %collective-permute-start.16 = (bf16[240,240]{1,0:T(8,128)(2,1)S(1)}, bf16[240,240]{1,0:T(8,128)(2,1)S(1)}, u32[]{:S(2)}, u32[]{:S(2)}) collective-permute-start(bf16[240,240]{1,0:T(8,128)(2,1)S(1)} %copy-done.56), channel_id=1, source_target_pairs={{0,1},{1,0},{2,3},{3,2},{4,5},{5,4},{6,7},{7,6},{8,9},{9,8},{10,11... | collective-permute-start | bytes 345608 | tf_op jit(solution)/shard_map/ppermute | solution.py:58
  74.9 141.7 %reduce-scatter.2.cloned.1.call-start = ((), (), s32[]{:S(2)}) async-start(), calls=%async_computation.3 | async-start | bytes 2457600 | tf_op jit(solution)/shard_map/reduce_scatter | solution.py:834
  112.5 18.4 %collective-permute-start.24 = (bf16[192,960]{1,0:T(8,128)(2,1)}, bf16[192,960]{1,0:T(8,128)(2,1)S(1)}, u32[]{:S(2)}, u32[]{:S(2)}) collective-permute-start(bf16[192,960]{1,0:T(8,128)(2,1)} %get-tuple-element.144.refs_2_.refs_6_), channel_id=1, source_target_pairs={{0,20},{4,16},{8,28},{12,24},{16,4},{20,0},{24,12},{28,8},{1,21},{... | collective-permute-start | bytes 1105928 | tf_op jit(solution)/shard_map/ppermute | solution.py:67
  113.2 17.7 %collective-permute-start.25 = (bf16[192,960]{1,0:T(8,128)(2,1)}, bf16[192,960]{1,0:T(8,128)(2,1)S(1)}, u32[]{:S(2)}, u32[]{:S(2)}) collective-permute-start(bf16[192,960]{1,0:T(8,128)(2,1)} %get-tuple-element.144.refs_2_.refs_6_), channel_id=1, source_target_pairs={{0,8},{4,12},{8,0},{12,4},{16,24},{20,28},{24,16},{28,20},{1,9},{5... | collective-permute-start | bytes 1105928 | tf_op jit(solution)/shard_map/ppermute | solution.py:67
  153.0 15.7 %collective-permute-start.30 = (bf16[192,960]{1,0:T(8,128)(2,1)S(1)}, bf16[192,960]{1,0:T(8,128)(2,1)S(1)}, u32[]{:S(2)}, u32[]{:S(2)}) collective-permute-start(bf16[192,960]{1,0:T(8,128)(2,1)S(1)} %get-tuple-element.221), channel_id=1, source_target_pairs={{0,4},{4,0},{8,12},{12,8},{16,20},{20,16},{24,28},{28,24},{1,5},{5... | collective-permute-start | bytes 1105928 | tf_op jit(solution)/shard_map/ppermute | solution.py:67
  154.2 14.6 %collective-permute-start.31 = (bf16[192,960]{1,0:T(8,128)(2,1)S(1)}, bf16[192,960]{1,0:T(8,128)(2,1)S(1)}, u32[]{:S(2)}, u32[]{:S(2)}) collective-permute-start(bf16[192,960]{1,0:T(8,128)(2,1)S(1)} %get-tuple-element.220), channel_id=1, source_target_pairs={{0,16},{4,20},{8,24},{12,28},{16,0},{20,4},{24,8},{28,12},{1,17},{... | collective-permute-start | bytes 1105928 | tf_op jit(solution)/shard_map/ppermute | solution.py:67
  155.7 18.5 %collective-permute-start.32 = (bf16[192,960]{1,0:T(8,128)(2,1)S(1)}, bf16[192,960]{1,0:T(8,128)(2,1)}, u32[]{:S(2)}, u32[]{:S(2)}) collective-permute-start(bf16[192,960]{1,0:T(8,128)(2,1)S(1)} %get-tuple-element.219), channel_id=1, source_target_pairs={{0,20},{4,16},{8,28},{12,24},{16,4},{20,0},{24,12},{28,8},{1,21},{... | collective-permute-start | bytes 1105928 | tf_op jit(solution)/shard_map/ppermute | solution.py:67
  174.2 17.1 %collective-permute-start.33 = (bf16[4,192,960]{2,1,0:T(8,128)(2,1)S(1)}, bf16[4,192,960]{2,1,0:T(8,128)(2,1)S(1)}, u32[]{:S(2)}, u32[]{:S(2)}) collective-permute-start(bf16[4,192,960]{2,1,0:T(8,128)(2,1)S(1)} %copy-done.19), channel_id=1, source_target_pairs={{0,8},{4,12},{8,0},{12,4},{16,24},{20,28},{24,16},{28,20},{1,9},{5... | collective-permute-start | bytes 4423688 | tf_op jit(solution)/shard_map/ppermute | solution.py:67
  190.4 24.5 %collective-permute-start.34 = (bf16[4,192,640]{2,1,0:T(8,128)(2,1)}, bf16[4,192,640]{2,1,0:T(8,128)(2,1)}, u32[]{:S(2)}, u32[]{:S(2)}) collective-permute-start(bf16[4,192,640]{2,1,0:T(8,128)(2,1)} %get-tuple-element.171), channel_id=1, source_target_pairs={{0,4},{4,0},{1,5},{5,1},{2,6},{6,2},{3,7},{7,3},{8,12},{12,8},{9,1... | collective-permute-start | bytes 2949128 | tf_op jit(solution)/shard_map/ppermute | solution.py:58
  191.6 23.2 %collective-permute-start.35 = (bf16[2,192,960]{2,1,0:T(8,128)(2,1)S(1)}, bf16[2,192,960]{2,1,0:T(8,128)(2,1)}, u32[]{:S(2)}, u32[]{:S(2)}) collective-permute-start(bf16[2,192,960]{2,1,0:T(8,128)(2,1)S(1)} %add_convert_fusion.1), channel_id=1, source_target_pairs={{0,16},{4,20},{8,24},{12,28},{16,0},{20,4},{24,8},{28,12},{1,17},{... | collective-permute-start | bytes 2211848 | tf_op jit(solution)/shard_map/ppermute | solution.py:67
  216.6 18.1 %collective-permute-start.37 = (bf16[240,960]{1,0:T(8,128)(2,1)}, bf16[240,960]{1,0:T(8,128)(2,1)S(1)}, u32[]{:S(2)}, u32[]{:S(2)}) collective-permute-start(bf16[240,960]{1,0:T(8,128)(2,1)} %reduce-scatter.2.cloned.1.call-done.refs_0_), channel_id=1, source_target_pairs={{0,4},{4,0},{8,12},{12,8},{16,20},{20,16},{24,28},{28,24},{1,5},{5... | collective-permute-start | bytes 1382408 | tf_op jit(solution)/shard_map/ppermute | solution.py:67
  219.7 17.3 %collective-permute-start.38 = (bf16[192,640]{1,0:T(8,128)(2,1)S(1)}, bf16[192,640]{1,0:T(8,128)(2,1)S(1)}, u32[]{:S(2)}, u32[]{:S(2)}) collective-permute-start(bf16[192,640]{1,0:T(8,128)(2,1)S(1)} %get-tuple-element.232), channel_id=1, source_target_pairs={{0,1},{1,0},{2,3},{3,2},{4,5},{5,4},{6,7},{7,6},{8,9},{9,8},{10,11... | collective-permute-start | bytes 737288 | tf_op jit(solution)/shard_map/ppermute | solution.py:58
  225.9 20.3 %collective-permute-start.39 = (bf16[192,640]{1,0:T(8,128)(2,1)S(1)}, bf16[192,640]{1,0:T(8,128)(2,1)S(1)}, u32[]{:S(2)}, u32[]{:S(2)}) collective-permute-start(bf16[192,640]{1,0:T(8,128)(2,1)S(1)} %get-tuple-element.231), channel_id=1, source_target_pairs={{0,2},{1,3},{2,0},{3,1},{4,6},{5,7},{6,4},{7,5},{8,10},{9,11},{10,... | collective-permute-start | bytes 737288 | tf_op jit(solution)/shard_map/ppermute | solution.py:58
  227.2 18.9 %collective-permute-start.40 = (bf16[192,640]{1,0:T(8,128)(2,1)S(1)}, bf16[192,640]{1,0:T(8,128)(2,1)S(1)}, u32[]{:S(2)}, u32[]{:S(2)}) collective-permute-start(bf16[192,640]{1,0:T(8,128)(2,1)S(1)} %get-tuple-element.230), channel_id=1, source_target_pairs={{0,3},{1,2},{2,1},{3,0},{4,7},{5,6},{6,5},{7,4},{8,11},{9,10},{10,... | collective-permute-start | bytes 737288 | tf_op jit(solution)/shard_map/ppermute | solution.py:58
  230.1 26.0 %collective-permute-start.41 = (bf16[960,480]{1,0:T(8,128)(2,1)S(1)}, bf16[960,480]{1,0:T(8,128)(2,1)S(1)}, u32[]{:S(2)}, u32[]{:S(2)}) collective-permute-start(bf16[960,480]{1,0:T(8,128)(2,1)S(1)} %fusion), channel_id=1, source_target_pairs={{0,16},{4,20},{8,24},{12,28},{16,0},{20,4},{24,8},{28,12},{1,17},{... | collective-permute-start | bytes 2764808 | tf_op jit(solution)/shard_map/ppermute | solution.py:67
  257.5 42.4 %collective-permute-start.46 = (bf16[2,240,480]{2,1,0:T(8,128)(2,1)S(1)}, bf16[2,240,480]{2,1,0:T(8,128)(2,1)S(1)}, u32[]{:S(2)}, u32[]{:S(2)}) collective-permute-start(bf16[2,240,480]{2,1,0:T(8,128)(2,1)S(1)} %pad_maximum_fusion), channel_id=1, source_target_pairs={{0,2},{1,3},{2,0},{3,1},{4,6},{5,7},{6,4},{7,5},{8,10},{9,11},{10,... | collective-permute-start | bytes 1382408 | tf_op jit(solution)/shard_map/ppermute | solution.py:58
  263.8 16.8 %collective-permute-start.45 = (bf16[336,240]{1,0:T(8,128)(2,1)S(1)}, bf16[336,240]{1,0:T(8,128)(2,1)S(1)}, u32[]{:S(2)}, u32[]{:S(2)}) collective-permute-start(bf16[336,240]{1,0:T(8,128)(2,1)S(1)} %get-tuple-element.197), channel_id=1, source_target_pairs={{0,3},{1,2},{2,1},{3,0},{4,7},{5,6},{6,5},{7,4},{8,11},{9,10},{10,... | collective-permute-start | bytes 483848 | tf_op jit(solution)/shard_map/ppermute | solution.py:58
  264.6 35.2 %collective-permute-start.44 = (bf16[336,240]{1,0:T(8,128)(2,1)S(1)}, bf16[336,240]{1,0:T(8,128)(2,1)S(1)}, u32[]{:S(2)}, u32[]{:S(2)}) collective-permute-start(bf16[336,240]{1,0:T(8,128)(2,1)S(1)} %get-tuple-element.196), channel_id=1, source_target_pairs={{0,2},{1,3},{2,0},{3,1},{4,6},{5,7},{6,4},{7,5},{8,10},{9,11},{10,... | collective-permute-start | bytes 483848 | tf_op jit(solution)/shard_map/ppermute | solution.py:58
  264.6 35.2 %collective-permute-start.43 = (bf16[336,240]{1,0:T(8,128)(2,1)S(1)}, bf16[336,240]{1,0:T(8,128)(2,1)S(1)}, u32[]{:S(2)}, u32[]{:S(2)}) collective-permute-start(bf16[336,240]{1,0:T(8,128)(2,1)S(1)} %get-tuple-element.195), channel_id=1, source_target_pairs={{0,1},{1,0},{2,3},{3,2},{4,5},{5,4},{6,7},{7,6},{8,9},{9,8},{10,11... | collective-permute-start | bytes 483848 | tf_op jit(solution)/shard_map/ppermute | solution.py:58
  268.1 46.6 %collective-permute-start.49 = (bf16[240,960]{1,0:T(8,128)(2,1)S(1)}, bf16[240,960]{1,0:T(8,128)(2,1)S(1)}, u32[]{:S(2)}, u32[]{:S(2)}) collective-permute-start(bf16[240,960]{1,0:T(8,128)(2,1)S(1)} %copy-done.21), channel_id=1, source_target_pairs={{0,8},{4,12},{8,0},{12,4},{16,24},{20,28},{24,16},{28,20},{1,9},{5... | collective-permute-start | bytes 1382408 | tf_op jit(solution)/shard_map/ppermute | solution.py:67
  280.5 22.6 %collective-permute-start.52 = (bf16[240,960]{1,0:T(8,128)(2,1)S(1)}, bf16[240,960]{1,0:T(8,128)(2,1)S(1)}, u32[]{:S(2)}, u32[]{:S(2)}) collective-permute-start(bf16[240,960]{1,0:T(8,128)(2,1)S(1)} %collective-permute-done.51.refs_4_), channel_id=1, source_target_pairs={{0,4},{4,0},{8,12},{12,8},{16,20},{20,16},{24,28},{28,24},{1,5},{5... | collective-permute-start | bytes 1382408 | tf_op jit(solution)/shard_map/ppermute | solution.py:67
  (92 other events, 693.6 us)
Sparse Core Ops, SparseCore 0:
  9.9 35.0 all-gather.2
  75.0 45.7 all-gather.4
  168.9 47.6 reduce-scatter.1

commit v11 on v10

--- a/solution.py
+++ b/solution.py
@@ -1000,7 +1000,9 @@
         scratch=[((members, weight_rows, 3 * part), BF16)],
         name="feed_forward_out",
     )
-    kv_share, weights_half = lax.optimization_barrier((kv_share, weights_half))
+    kv_share, weights_half, result_along = lax.optimization_barrier(
+        (kv_share, weights_half, result_along)
+    )
     kv_share, result_along, *big = lax.optimization_barrier(
         (sum_swap(kv_share, 2, 0), result_along, gate_weight_grad, up_weight_grad,
          down_weight_grad)

time: 354 us -> 345 us (0.975)
  starting transfers between devices: 79.6 us -> 72.2 us
    ppermute x22, starting transfers between devices: 55 us -> 48.1 us  [swap(): return lax.ppermute(x, axis, [(i, i ^ mask) for i in range(count)])]
    ppermute x22, waiting for transfers between devices: 67.3 us -> 63.3 us  [swap(): return lax.ppermute(x, axis, [(i, i ^ mask) for i in range(count)])]
  transfers between devices with their start and end apart: 65 -> 65, of which waited for: 20 -> 18; matrix products, arithmetic and copies ran while one was open for 6% -> 6% of each run, Pallas kernels for 31% -> 31%
where the time goes in v11:
time: 345 us; the launch traced here: 340 us
  Pallas kernels  118 us (34%)
  waiting for transfers between devices  100 us (29%)
  starting transfers between devices  72.2 us (21%)
  local copies, waits for them, and re-layouts  18.8 us (5%)
  between operations  15.5 us (4%)
  other arithmetic  14.8 us (4%)
    pallas_call x20, Pallas kernels, call(): pl.pallas_call(kernel, out_shape=outs, in_specs=specs, out_specs=tuple((p...  118 us
    ppermute x22, waiting for transfers between devices, swap(): return lax.ppermute(x, axis, [(i, i ^ mask) for i in range(count)])  63.3 us
    ppermute x22, starting transfers between devices, swap(): return lax.ppermute(x, axis, [(i, i ^ mask) for i in range(count)])  48.1 us
    ppermute x40, waiting for transfers between devices, swap_plane(): return lax.ppermute(x, ('dp', 'ctx'), pairs)  34.7 us
    ppermute x40, starting transfers between devices, swap_plane(): return lax.ppermute(x, ('dp', 'ctx'), pairs)  23.8 us
    unnamed x118, local copies, waits for them, and re-layouts  10.7 us
  transfers between devices with their start and end apart: 65, of which 18 were waited for; matrix products, arithmetic and copies ran while one was open for 6% of the time, Pallas kernels for 31%

profile of v11, /device:TPU:0, one launch (start us, length us, event | category | flops | bytes accessed | tf_op | source)
XLA Modules:
  0.0 339.6 jit_solution(18002763563465004268)
XLA Ops:
  19.5 3.5 %collective-permute-start.7 = (bf16[240,240]{1,0:T(8,128)(2,1)}, bf16[240,240]{1,0:T(8,128)(2,1)S(1)}, u32[]{:S(2)}, u32[]{:S(2)}) collective-permute-start(bf16[240,240]{1,0:T(8,128)(2,1)} %get-tuple-element.117), channel_id=1, source_target_pairs={{0,2},{1,3},{2,0},{3,1},{4,6},{5,7},{6,4},{7,5},{8,10},{9,11},{10,... | collective-permute-start | bytes 345608 | tf_op jit(solution)/shard_map/ppermute | solution.py:58
  24.8 4.2 %pack_weights.1 = bf16[240,960]{1,0:T(8,128)(2,1)} custom-call(s32[4]{0:T(128)} %pad_add_fusion.1.spots, bf16[240,2560]{1,0:T(8,128)(2,1)} %gate_ref.1, bf16[240,2560]{1,0:T(8,128)(2,1)} %up_ref.1, bf16[960,640]{1,0:T(8,128)(2,1)} %bitcast.98), custom_call_target="tpu_custom_call" | custom-call | flops 4600000000 | tf_op jit(solution)/shard_map/pack_weights/pallas_call | solution.py:106
  31.3 4.3 %collective-permute-start.8 = (bf16[240,240]{1,0:T(8,128)(2,1)S(1)}, bf16[240,240]{1,0:T(8,128)(2,1)S(1)}, u32[]{:S(2)}, u32[]{:S(2)}) collective-permute-start(bf16[240,240]{1,0:T(8,128)(2,1)S(1)} %copy-done.57), channel_id=1, source_target_pairs={{0,3},{1,2},{2,1},{3,0},{4,7},{5,6},{6,5},{7,4},{8,11},{9,10},{10,... | collective-permute-start | bytes 345608 | tf_op jit(solution)/shard_map/ppermute | solution.py:58
  36.3 3.6 %norm_keys_values.1 = (bf16[192,640]{1,0:T(8,128)(2,1)}, bf16[192,960]{1,0:T(8,128)(2,1)}, bf16[192,960]{1,0:T(8,128)(2,1)}, f32[192,1]{1,0:T(8,128)}, f32[8,960]{1,0:T(8,128)}) custom-call(s32[4]{0:T(128)} %pad_add_fusion.1.spots, bf16[192,960]{1,0:T(8,128)(2,1)} %bitcast.99, bf16[1,240]{1,0:T(2,128)(2,1)} %copy-done.18, bf16[1,240]{1,0:T(2,128)(2,1)} %copy-done.17, ...), custom_call_target="tpu_custom_call" | custom-call | flops 4600000000 | tf_op jit(solution)/shard_map/norm_keys_values/pallas_call | solution.py:106
  49.9 3.4 %collective-permute-done.11.refs_11_.refs_1_.refs_10_ = bf16[192,640]{1,0:T(8,128)(2,1)S(1)} collective-permute-done((bf16[192,640]{1,0:T(8,128)(2,1)}, bf16[192,640]{1,0:T(8,128)(2,1)S(1)}, u32[]{:S(2)}, u32[]{:S(2)}) %collective-permute-start.11) | collective-permute-done | bytes 245792 | tf_op jit(solution)/shard_map/ppermute | solution.py:58
  53.3 9.9 %collective-permute-done.12.refs_12_.refs_2_.refs_11_ = bf16[192,640]{1,0:T(8,128)(2,1)S(1)} collective-permute-done((bf16[192,640]{1,0:T(8,128)(2,1)}, bf16[192,640]{1,0:T(8,128)(2,1)S(1)}, u32[]{:S(2)}, u32[]{:S(2)}) %collective-permute-start.12) | collective-permute-done | bytes 245792 | tf_op jit(solution)/shard_map/ppermute | solution.py:58
  70.0 4.8 %collective-permute-start.16 = (bf16[240,240]{1,0:T(8,128)(2,1)S(1)}, bf16[240,240]{1,0:T(8,128)(2,1)S(1)}, u32[]{:S(2)}, u32[]{:S(2)}) collective-permute-start(bf16[240,240]{1,0:T(8,128)(2,1)S(1)} %copy-done.56), channel_id=1, source_target_pairs={{0,1},{1,0},{2,3},{3,2},{4,5},{5,4},{6,7},{7,6},{8,9},{9,8},{10,11... | collective-permute-start | bytes 345608 | tf_op jit(solution)/shard_map/ppermute | solution.py:58
  78.3 8.7 %attention_near.1 = (bf16[192,960]{1,0:T(8,128)(2,1)}, f32[5,576]{1,0:T(8,128)}, f32[5,576]{1,0:T(8,128)}, f32[5,64,576]{2,1,0:T(8,128)}) custom-call(s32[4]{0:T(128)} %pad_add_fusion.1.spots, bf16[192,960]{1,0:T(8,128)(2,1)} %get-tuple-element.119.refs_0_, s32[768,1]{1,0:T(8,128)} %slice.124.refs_1_, s32[1,576]{1,0:T(1,128)} %broadcast_in_dim.29.refs_2_, ...), custom_call_target="tpu_custom_call" | custom-call | flops 13799999488 | tf_op jit(solution)/shard_map/attention_near/pallas_call | solution.py:106
  93.9 9.0 %attention_far.1 = (bf16[192,960]{1,0:T(8,128)(2,1)}, f32[5,64,576]{2,1,0:T(8,128)}, f32[5,576]{1,0:T(8,128)}) custom-call(s32[4]{0:T(128)} %pad_add_fusion.1.spots, bf16[192,960]{1,0:T(8,128)(2,1)} %get-tuple-element.129.refs_0_, s32[768,1]{1,0:T(8,128)} %slice.125.refs_1_, s32[1,576]{1,0:T(1,128)} %broadcast_in_dim.29.refs_2_, ...), custom_call_target="tpu_custom_call" | custom-call | flops 13799999488 | tf_op jit(solution)/shard_map/attention_far/pallas_call | solution.py:106
  105.5 4.2 %project_residual.1 = (f32[192,960]{1,0:T(8,128)}, f32[192,1]{1,0:T(8,128)}, bf16[192,960]{1,0:T(8,128)(2,1)}) custom-call(s32[4]{0:T(128)} %pad_add_fusion.1.spots, bf16[192,960]{1,0:T(8,128)(2,1)} %get-tuple-element.139.refs_0_, bf16[192,960]{1,0:T(8,128)(2,1)} %bitcast.100, f32[8,960]{1,0:T(8,128)} %get-tuple-element.140.refs_2_.refs_8_.refs_5_, ...), custom_call_target="tpu_custom_call" | custom-call | flops 2300000000 | tf_op jit(solution)/shard_map/project_residual/pallas_call | solution.py:106
  113.2 8.1 %collective-permute-done.22.refs_3_.refs_7_ = bf16[192,960]{1,0:T(8,128)(2,1)S(1)} collective-permute-done((bf16[192,960]{1,0:T(8,128)(2,1)}, bf16[192,960]{1,0:T(8,128)(2,1)S(1)}, u32[]{:S(2)}, u32[]{:S(2)}) %collective-permute-start.22) | collective-permute-done | bytes 368672 | tf_op jit(solution)/shard_map/ppermute | solution.py:67
  123.3 7.7 %collective-permute-done.24.refs_5_.refs_9_ = bf16[192,960]{1,0:T(8,128)(2,1)S(1)} collective-permute-done((bf16[192,960]{1,0:T(8,128)(2,1)}, bf16[192,960]{1,0:T(8,128)(2,1)S(1)}, u32[]{:S(2)}, u32[]{:S(2)}) %collective-permute-start.24) | collective-permute-done | bytes 368672 | tf_op jit(solution)/shard_map/ppermute | solution.py:67
  133.4 8.5 %feed_forward.3 = (bf16[4,192,960]{2,1,0:T(8,128)(2,1)}, bf16[768,320]{1,0:T(8,128)(2,1)}, bf16[768,640]{1,0:T(8,128)(2,1)}) custom-call(s32[4]{0:T(128)} %pad_add_fusion.1.spots, bf16[960,960]{1,0:T(8,128)(2,1)} %all-gather.5.cloned.1.call-done.refs_0_, bf16[8,192,960]{2,1,0:T(8,128)(2,1)} %all-gather.3.cloned.1.call-done.refs_1_.refs_5_, ...), custom_call_target="tpu_custom_call" | custom-call | flops 9200000000 | tf_op jit(solution)/shard_map/feed_forward/pallas_call | solution.py:106
  142.2 8.5 %feed_forward.2 = (bf16[4,192,960]{2,1,0:T(8,128)(2,1)}, bf16[768,320]{1,0:T(8,128)(2,1)}, bf16[768,640]{1,0:T(8,128)(2,1)}) custom-call(s32[4]{0:T(128)} %pad_add_fusion.1.spots, bf16[960,960]{1,0:T(8,128)(2,1)} %all-gather.5.cloned.1.call-done.refs_0_, bf16[8,192,960]{2,1,0:T(8,128)(2,1)} %all-gather.3.cloned.1.call-done.refs_1_.refs_5_, ...), custom_call_target="tpu_custom_call" | custom-call | flops 9200000000 | tf_op jit(solution)/shard_map/feed_forward/pallas_call | solution.py:106
  156.6 12.1 %feed_forward_weights.1 = (bf16[4,192,960]{2,1,0:T(8,128)(2,1)}, bf16[4,192,960]{2,1,0:T(8,128)(2,1)}, bf16[960,960]{1,0:T(8,128)(2,1)}) custom-call(s32[4]{0:T(128)} %pad_add_fusion.1.spots, bf16[960,960]{1,0:T(8,128)(2,1)} %all-gather.5.cloned.1.call-done.refs_0_, bf16[768,320]{1,0:T(8,128)(2,1)} %get-tuple-element.149.refs_1_, ...), custom_call_target="tpu_custom_call" | custom-call | flops 13799999488 | tf_op jit(solution)/shard_map/feed_forward_weights/pallas_call | solution.py:106
  168.8 5.4 %collective-permute-done.32.refs_4_ = bf16[192,960]{1,0:T(8,128)(2,1)} collective-permute-done((bf16[192,960]{1,0:T(8,128)(2,1)S(1)}, bf16[192,960]{1,0:T(8,128)(2,1)}, u32[]{:S(2)}, u32[]{:S(2)}) %collective-permute-start.32) | collective-permute-done | bytes 368672 | tf_op jit(solution)/shard_map/ppermute | solution.py:67
  174.2 5.5 %residual_back.1 = (f32[192,960]{1,0:T(8,128)}, bf16[192,960]{1,0:T(8,128)(2,1)}, bf16[192,960]{1,0:T(8,128)(2,1)}, f32[1,960]{1,0:T(1,128)}) custom-call(s32[4]{0:T(128)} %pad_add_fusion.1.spots, bf16[4,192,960]{2,1,0:T(8,128)(2,1)} %get-tuple-element.146.refs_0_, bf16[4,192,960]{2,1,0:T(8,128)(2,1)} %copy-done.4, bf16[192,960]{1,0:T(8,128)(2,1)} %copy-done.35, ...), custom_call_target="tpu_custom_call" | custom-call | flops 6899999744 | tf_op jit(solution)/shard_map/residual_back/pallas_call | solution.py:106
  179.8 10.6 %attention_back_far.1 = (f32[5,64,576]{2,1,0:T(8,128)}, bf16[4,192,640]{2,1,0:T(8,128)(2,1)}) custom-call(s32[4]{0:T(128)} %pad_add_fusion.1.spots, bf16[192,960]{1,0:T(8,128)(2,1)} %get-tuple-element.129.refs_0_, s32[768,1]{1,0:T(8,128)} %slice.125.refs_1_, s32[1,576]{1,0:T(1,128)} %broadcast_in_dim.29.refs_2_, ...), custom_call_target="tpu_custom_call" | custom-call | flops 14949999616 | tf_op jit(solution)/shard_map/attention_back_far/pallas_call | solution.py:106
  193.2 10.4 %attention_back_near.1 = (bf16[192,960]{1,0:T(8,128)(2,1)}, bf16[192,640]{1,0:T(8,128)(2,1)}, bf16[192,640]{1,0:T(8,128)(2,1)}, bf16[192,640]{1,0:T(8,128)(2,1)}, bf16[192,640]{1,0:T(8,128)(2,1)}) custom-call(s32[4]{0:T(128)} %pad_add_fusion.1.spots, bf16[192,960]{1,0:T(8,128)(2,1)} %get-tuple-element.129.refs_0_, s32[768,1]{1,0:T(8,128)} %slice.124.refs_1_, ...), custom_call_target="tpu_custom_call" | custom-call | flops 16099999744 | tf_op jit(solution)/shard_map/attention_back_near/pallas_call | solution.py:106
  203.6 5.0 %query_output_weight_grads.1 = (bf16[2,960,480]{2,1,0:T(8,128)(2,1)}, bf16[2,960,480]{2,1,0:T(8,128)(2,1)}) custom-call(s32[4]{0:T(128)} %pad_add_fusion.1.spots, bf16[192,960]{1,0:T(8,128)(2,1)} %get-tuple-element.139.refs_0_, bf16[192,960]{1,0:T(8,128)(2,1)} %get-tuple-element.163.refs_1_, bf16[192,960]{1,0:T(8,128)(2,1)} %get-tuple-element.164.refs_2_, ...), custom_call_target="tpu_custom_call" | custom-call | tf_op jit(solution)/shard_map/query_output_weight_grads/pallas_call | solution.py:106
  208.7 6.2 %collective-permute-done.34.refs_12_ = bf16[4,192,640]{2,1,0:T(8,128)(2,1)} collective-permute-done((bf16[4,192,640]{2,1,0:T(8,128)(2,1)}, bf16[4,192,640]{2,1,0:T(8,128)(2,1)}, u32[]{:S(2)}, u32[]{:S(2)}) %collective-permute-start.34) | collective-permute-done | bytes 983072 | tf_op jit(solution)/shard_map/ppermute | solution.py:58
  219.7 6.2 %collective-permute-start.38 = (bf16[192,640]{1,0:T(8,128)(2,1)S(1)}, bf16[192,640]{1,0:T(8,128)(2,1)S(1)}, u32[]{:S(2)}, u32[]{:S(2)}) collective-permute-start(bf16[192,640]{1,0:T(8,128)(2,1)S(1)} %get-tuple-element.234), channel_id=1, source_target_pairs={{0,1},{1,0},{2,3},{3,2},{4,5},{5,4},{6,7},{7,6},{8,9},{9,8},{10,11... | collective-permute-start | bytes 737288 | tf_op jit(solution)/shard_map/ppermute | solution.py:58
  231.1 3.6 %query_back.1.refs_6_ = f32[192,960]{1,0:T(8,128)} custom-call(s32[4]{0:T(128)} %pad_add_fusion.1.spots, bf16[192,960]{1,0:T(8,128)(2,1)} %get-tuple-element.183.refs_3_.low_ref, bf16[240,960]{1,0:T(8,128)(2,1)} %local_ref.1, bf16[720,240]{1,0:T(8,128)(2,1)} %stack_quarters.2.refs_6_.refs_0_, bf16[720,240]{1,0:T(8,128)(2,1)} %copy-done.8, ...), custom_call_target="tpu_custom_call" | custom-call | tf_op jit(solution)/shard_map/query_back/pallas_call | solution.py:106
  237.0 9.2 %collective-permute-done.39.refs_14_ = bf16[192,640]{1,0:T(8,128)(2,1)S(1)} collective-permute-done((bf16[192,640]{1,0:T(8,128)(2,1)S(1)}, bf16[192,640]{1,0:T(8,128)(2,1)S(1)}, u32[]{:S(2)}, u32[]{:S(2)}) %collective-permute-start.39) | collective-permute-done | bytes 245792 | tf_op jit(solution)/shard_map/ppermute | solution.py:58
  246.9 6.2 %keys_values_back.1 = (f32[192,960]{1,0:T(8,128)}, bf16[4,336,240]{2,1,0:T(8,128)(2,1)}, bf16[4,336,240]{2,1,0:T(8,128)(2,1)}) custom-call(s32[4]{0:T(128)} %pad_add_fusion.1.spots, f32[192,128]{1,0:T(8,128)} %pad_maximum_fusion.2.refs_5_.refs_3_.refs_0_, f32[192,128]{1,0:T(8,128)} %pad_maximum_fusion.3.refs_6_.refs_4_.refs_1_, ...), custom_call_target="tpu_custom_call" | custom-call | flops 6899999744 | tf_op jit(solution)/shard_map/keys_values_back/pallas_call | solution.py:106
  260.5 3.3 collective-permute-start.44
  270.6 16.2 %collective-permute-done.44 = bf16[336,240]{1,0:T(8,128)(2,1)S(1)} collective-permute-done((bf16[336,240]{1,0:T(8,128)(2,1)S(1)}, bf16[336,240]{1,0:T(8,128)(2,1)S(1)}, u32[]{:S(2)}, u32[]{:S(2)}) %collective-permute-start.44) | collective-permute-done | bytes 161312 | tf_op jit(solution)/shard_map/ppermute | solution.py:58
  286.9 10.2 %collective-permute-done.46 = bf16[2,240,480]{2,1,0:T(8,128)(2,1)S(1)} collective-permute-done((bf16[2,240,480]{2,1,0:T(8,128)(2,1)S(1)}, bf16[2,240,480]{2,1,0:T(8,128)(2,1)S(1)}, u32[]{:S(2)}, u32[]{:S(2)}) %collective-permute-start.46) | collective-permute-done | bytes 460832 | tf_op jit(solution)/shard_map/ppermute | solution.py:58
  299.3 4.2 %collective-permute-done.48 = bf16[336,240]{1,0:T(8,128)(2,1)S(1)} collective-permute-done((bf16[336,240]{1,0:T(8,128)(2,1)S(1)}, bf16[336,240]{1,0:T(8,128)(2,1)S(1)}, u32[]{:S(2)}, u32[]{:S(2)}) %collective-permute-start.48) | collective-permute-done | bytes 161312 | tf_op jit(solution)/shard_map/ppermute | solution.py:67
  303.6 4.0 %collective-permute-done.57 = bf16[1,240,480]{2,1,0:T(8,128)(2,1)S(1)} collective-permute-done((bf16[1,240,480]{2,1,0:T(8,128)(2,1)S(1)}, bf16[1,240,480]{2,1,0:T(8,128)(2,1)S(1)}, u32[]{:S(2)}, u32[]{:S(2)}) %collective-permute-start.57) | collective-permute-done | bytes 230432 | tf_op jit(solution)/shard_map/ppermute | solution.py:58
  310.4 6.7 %feed_forward_out.1 = (f32[240,2560]{1,0:T(8,128)}, f32[240,2560]{1,0:T(8,128)}, f32[960,640]{1,0:T(8,128)}) custom-call(s32[4]{0:T(128)} %pad_add_fusion.1.spots, bf16[240,960]{1,0:T(8,128)(2,1)} %reduce-scatter.2.cloned.1.call-done.refs_0_, bf16[240,960]{1,0:T(8,128)(2,1)} %copy-done.22, bf16[240,960]{1,0:T(8,128)(2,1)} %copy-done.26, ...), custom_call_target="tpu_custom_call" | custom-call | flops 8049999872 | tf_op jit(solution)/shard_map/feed_forward_out/pallas_call | solution.py:106
  318.4 4.3 %collective-permute-done.55 = bf16[336,240]{1,0:T(8,128)(2,1)S(1)} collective-permute-done((bf16[336,240]{1,0:T(8,128)(2,1)S(1)}, bf16[336,240]{1,0:T(8,128)(2,1)S(1)}, u32[]{:S(2)}, u32[]{:S(2)}) %collective-permute-start.55) | collective-permute-done | bytes 161312 | tf_op jit(solution)/shard_map/ppermute | solution.py:67
  (284 shorter events, 105.9 us)
Async XLA Ops:
  7.2 67.7 %all-gather.3.cloned.1.call-start = ((), (), s32[]{:S(2)}) async-start(), calls=%async_computation.1 | async-start | bytes 3538944 | tf_op jit(solution)/shard_map/all_gather | solution.py:711
  7.9 124.7 %all-gather.5.cloned.1.call-start = ((), (), s32[]{:S(2)}) async-start(), calls=%async_computation.2 | async-start | bytes 2457600 | tf_op jit(solution)/shard_map/all_gather | solution.py:760
  10.4 19.4 %collective-permute-start = (bf16[336,240]{1,0:T(8,128)(2,1)S(1)}, bf16[336,240]{1,0:T(8,128)(2,1)S(1)}, u32[]{:S(2)}, u32[]{:S(2)}) collective-permute-start(bf16[336,240]{1,0:T(8,128)(2,1)S(1)} %pad_maximum_fusion.1), channel_id=1, source_target_pairs={{0,1},{1,0},{2,3},{3,2},{4,5},{5,4},{6,7},{7,6},{8,9},{9,8},{10,11... | collective-permute-start | bytes 483848 | tf_op jit(solution)/shard_map/ppermute | solution.py:58
  13.5 16.3 %collective-permute-start.1 = (bf16[336,240]{1,0:T(8,128)(2,1)S(1)}, bf16[336,240]{1,0:T(8,128)(2,1)S(1)}, u32[]{:S(2)}, u32[]{:S(2)}) collective-permute-start(bf16[336,240]{1,0:T(8,128)(2,1)S(1)} %pad_maximum_fusion.1), channel_id=1, source_target_pairs={{0,2},{1,3},{2,0},{3,1},{4,6},{5,7},{6,4},{7,5},{8,10},{9,11},{10,... | collective-permute-start | bytes 483848 | tf_op jit(solution)/shard_map/ppermute | solution.py:58
  18.6 24.2 %collective-permute-start.6 = (bf16[240,240]{1,0:T(8,128)(2,1)}, bf16[240,240]{1,0:T(8,128)(2,1)S(1)}, u32[]{:S(2)}, u32[]{:S(2)}) collective-permute-start(bf16[240,240]{1,0:T(8,128)(2,1)} %get-tuple-element.117), channel_id=1, source_target_pairs={{0,1},{1,0},{2,3},{3,2},{4,5},{5,4},{6,7},{7,6},{8,9},{9,8},{10,11... | collective-permute-start | bytes 345608 | tf_op jit(solution)/shard_map/ppermute | solution.py:58
  19.5 25.7 %collective-permute-start.7 = (bf16[240,240]{1,0:T(8,128)(2,1)}, bf16[240,240]{1,0:T(8,128)(2,1)S(1)}, u32[]{:S(2)}, u32[]{:S(2)}) collective-permute-start(bf16[240,240]{1,0:T(8,128)(2,1)} %get-tuple-element.117), channel_id=1, source_target_pairs={{0,2},{1,3},{2,0},{3,1},{4,6},{5,7},{6,4},{7,5},{8,10},{9,11},{10,... | collective-permute-start | bytes 345608 | tf_op jit(solution)/shard_map/ppermute | solution.py:58
  42.8 20.5 %collective-permute-start.12 = (bf16[192,640]{1,0:T(8,128)(2,1)}, bf16[192,640]{1,0:T(8,128)(2,1)S(1)}, u32[]{:S(2)}, u32[]{:S(2)}) collective-permute-start(bf16[192,640]{1,0:T(8,128)(2,1)} %get-tuple-element.125.refs_10_.refs_0_.refs_9_), channel_id=1, source_target_pairs={{0,2},{1,3},{2,0},{3,1},{4,6},{5,7},{6,4},{7,5},{8,10},{9,11},{10,... | collective-permute-start | bytes 737288 | tf_op jit(solution)/shard_map/ppermute | solution.py:58
  42.8 20.5 %collective-permute-start.13 = (bf16[192,640]{1,0:T(8,128)(2,1)}, bf16[192,640]{1,0:T(8,128)(2,1)S(1)}, u32[]{:S(2)}, u32[]{:S(2)}) collective-permute-start(bf16[192,640]{1,0:T(8,128)(2,1)} %get-tuple-element.125.refs_10_.refs_0_.refs_9_), channel_id=1, source_target_pairs={{0,3},{1,2},{2,1},{3,0},{4,7},{5,6},{6,5},{7,4},{8,11},{9,10},{10,... | collective-permute-start | bytes 737288 | tf_op jit(solution)/shard_map/ppermute | solution.py:58
  48.3 15.0 %collective-permute-start.10 = (bf16[720,240]{1,0:T(8,128)(2,1)}, bf16[720,240]{1,0:T(8,128)(2,1)S(1)}, u32[]{:S(2)}, u32[]{:S(2)}) collective-permute-start(bf16[720,240]{1,0:T(8,128)(2,1)} %stack_quarters.2.refs_6_.refs_0_), channel_id=1, source_target_pairs={{0,16},{4,20},{8,24},{12,28},{16,0},{20,4},{24,8},{28,12},{1,17},{... | collective-permute-start | bytes 1036808 | tf_op jit(solution)/shard_map/ppermute | solution.py:67
  49.9 25.3 %collective-permute-start.9 = (bf16[720,240]{1,0:T(8,128)(2,1)}, bf16[720,240]{1,0:T(8,128)(2,1)S(1)}, u32[]{:S(2)}, u32[]{:S(2)}) collective-permute-start(bf16[720,240]{1,0:T(8,128)(2,1)} %stack_quarters.2.refs_6_.refs_0_), channel_id=1, source_target_pairs={{0,8},{4,12},{8,0},{12,4},{16,24},{20,28},{24,16},{28,20},{1,9},{5... | collective-permute-start | bytes 1036808 | tf_op jit(solution)/shard_map/ppermute | solution.py:67
  68.5 24.4 %collective-permute-start.15 = (bf16[768,640]{1,0:T(8,128)(2,1)}, bf16[768,640]{1,0:T(8,128)(2,1)S(1)}, u32[]{:S(2)}, u32[]{:S(2)}) collective-permute-start(bf16[768,640]{1,0:T(8,128)(2,1)} %stack_keys_values.1), channel_id=1, source_target_pairs={{0,4},{4,0},{1,5},{5,1},{2,6},{6,2},{3,7},{7,3},{8,12},{12,8},{9,1... | collective-permute-start | bytes 2949128 | tf_op jit(solution)/shard_map/ppermute | solution.py:58
  70.0 17.1 %collective-permute-start.16 = (bf16[240,240]{1,0:T(8,128)(2,1)S(1)}, bf16[240,240]{1,0:T(8,128)(2,1)S(1)}, u32[]{:S(2)}, u32[]{:S(2)}) collective-permute-start(bf16[240,240]{1,0:T(8,128)(2,1)S(1)} %copy-done.56), channel_id=1, source_target_pairs={{0,1},{1,0},{2,3},{3,2},{4,5},{5,4},{6,7},{7,6},{8,9},{9,8},{10,11... | collective-permute-start | bytes 345608 | tf_op jit(solution)/shard_map/ppermute | solution.py:58
  74.9 141.7 %reduce-scatter.2.cloned.1.call-start = ((), (), s32[]{:S(2)}) async-start(), calls=%async_computation.3 | async-start | bytes 2457600 | tf_op jit(solution)/shard_map/reduce_scatter | solution.py:834
  112.5 18.4 %collective-permute-start.24 = (bf16[192,960]{1,0:T(8,128)(2,1)}, bf16[192,960]{1,0:T(8,128)(2,1)S(1)}, u32[]{:S(2)}, u32[]{:S(2)}) collective-permute-start(bf16[192,960]{1,0:T(8,128)(2,1)} %get-tuple-element.145.refs_2_.refs_6_), channel_id=1, source_target_pairs={{0,20},{4,16},{8,28},{12,24},{16,4},{20,0},{24,12},{28,8},{1,21},{... | collective-permute-start | bytes 1105928 | tf_op jit(solution)/shard_map/ppermute | solution.py:67
  113.2 17.7 %collective-permute-start.25 = (bf16[192,960]{1,0:T(8,128)(2,1)}, bf16[192,960]{1,0:T(8,128)(2,1)S(1)}, u32[]{:S(2)}, u32[]{:S(2)}) collective-permute-start(bf16[192,960]{1,0:T(8,128)(2,1)} %get-tuple-element.145.refs_2_.refs_6_), channel_id=1, source_target_pairs={{0,8},{4,12},{8,0},{12,4},{16,24},{20,28},{24,16},{28,20},{1,9},{5... | collective-permute-start | bytes 1105928 | tf_op jit(solution)/shard_map/ppermute | solution.py:67
  153.0 15.7 %collective-permute-start.30 = (bf16[192,960]{1,0:T(8,128)(2,1)S(1)}, bf16[192,960]{1,0:T(8,128)(2,1)S(1)}, u32[]{:S(2)}, u32[]{:S(2)}) collective-permute-start(bf16[192,960]{1,0:T(8,128)(2,1)S(1)} %get-tuple-element.223), channel_id=1, source_target_pairs={{0,4},{4,0},{8,12},{12,8},{16,20},{20,16},{24,28},{28,24},{1,5},{5... | collective-permute-start | bytes 1105928 | tf_op jit(solution)/shard_map/ppermute | solution.py:67
  154.2 14.6 %collective-permute-start.31 = (bf16[192,960]{1,0:T(8,128)(2,1)S(1)}, bf16[192,960]{1,0:T(8,128)(2,1)S(1)}, u32[]{:S(2)}, u32[]{:S(2)}) collective-permute-start(bf16[192,960]{1,0:T(8,128)(2,1)S(1)} %get-tuple-element.222), channel_id=1, source_target_pairs={{0,16},{4,20},{8,24},{12,28},{16,0},{20,4},{24,8},{28,12},{1,17},{... | collective-permute-start | bytes 1105928 | tf_op jit(solution)/shard_map/ppermute | solution.py:67
  155.7 18.5 %collective-permute-start.32 = (bf16[192,960]{1,0:T(8,128)(2,1)S(1)}, bf16[192,960]{1,0:T(8,128)(2,1)}, u32[]{:S(2)}, u32[]{:S(2)}) collective-permute-start(bf16[192,960]{1,0:T(8,128)(2,1)S(1)} %get-tuple-element.221), channel_id=1, source_target_pairs={{0,20},{4,16},{8,28},{12,24},{16,4},{20,0},{24,12},{28,8},{1,21},{... | collective-permute-start | bytes 1105928 | tf_op jit(solution)/shard_map/ppermute | solution.py:67
  174.2 17.1 %collective-permute-start.33 = (bf16[4,192,960]{2,1,0:T(8,128)(2,1)S(1)}, bf16[4,192,960]{2,1,0:T(8,128)(2,1)S(1)}, u32[]{:S(2)}, u32[]{:S(2)}) collective-permute-start(bf16[4,192,960]{2,1,0:T(8,128)(2,1)S(1)} %copy-done.19), channel_id=1, source_target_pairs={{0,8},{4,12},{8,0},{12,4},{16,24},{20,28},{24,16},{28,20},{1,9},{5... | collective-permute-start | bytes 4423688 | tf_op jit(solution)/shard_map/ppermute | solution.py:67
  190.4 24.5 %collective-permute-start.34 = (bf16[4,192,640]{2,1,0:T(8,128)(2,1)}, bf16[4,192,640]{2,1,0:T(8,128)(2,1)}, u32[]{:S(2)}, u32[]{:S(2)}) collective-permute-start(bf16[4,192,640]{2,1,0:T(8,128)(2,1)} %get-tuple-element.172), channel_id=1, source_target_pairs={{0,4},{4,0},{1,5},{5,1},{2,6},{6,2},{3,7},{7,3},{8,12},{12,8},{9,1... | collective-permute-start | bytes 2949128 | tf_op jit(solution)/shard_map/ppermute | solution.py:58
  191.6 23.2 %collective-permute-start.35 = (bf16[2,192,960]{2,1,0:T(8,128)(2,1)S(1)}, bf16[2,192,960]{2,1,0:T(8,128)(2,1)}, u32[]{:S(2)}, u32[]{:S(2)}) collective-permute-start(bf16[2,192,960]{2,1,0:T(8,128)(2,1)S(1)} %add_convert_fusion.1), channel_id=1, source_target_pairs={{0,16},{4,20},{8,24},{12,28},{16,0},{20,4},{24,8},{28,12},{1,17},{... | collective-permute-start | bytes 2211848 | tf_op jit(solution)/shard_map/ppermute | solution.py:67
  216.6 18.1 %collective-permute-start.37 = (bf16[240,960]{1,0:T(8,128)(2,1)}, bf16[240,960]{1,0:T(8,128)(2,1)S(1)}, u32[]{:S(2)}, u32[]{:S(2)}) collective-permute-start(bf16[240,960]{1,0:T(8,128)(2,1)} %reduce-scatter.2.cloned.1.call-done.refs_0_), channel_id=1, source_target_pairs={{0,4},{4,0},{8,12},{12,8},{16,20},{20,16},{24,28},{28,24},{1,5},{5... | collective-permute-start | bytes 1382408 | tf_op jit(solution)/shard_map/ppermute | solution.py:67
  219.7 17.3 %collective-permute-start.38 = (bf16[192,640]{1,0:T(8,128)(2,1)S(1)}, bf16[192,640]{1,0:T(8,128)(2,1)S(1)}, u32[]{:S(2)}, u32[]{:S(2)}) collective-permute-start(bf16[192,640]{1,0:T(8,128)(2,1)S(1)} %get-tuple-element.234), channel_id=1, source_target_pairs={{0,1},{1,0},{2,3},{3,2},{4,5},{5,4},{6,7},{7,6},{8,9},{9,8},{10,11... | collective-permute-start | bytes 737288 | tf_op jit(solution)/shard_map/ppermute | solution.py:58
  225.9 20.3 %collective-permute-start.39 = (bf16[192,640]{1,0:T(8,128)(2,1)S(1)}, bf16[192,640]{1,0:T(8,128)(2,1)S(1)}, u32[]{:S(2)}, u32[]{:S(2)}) collective-permute-start(bf16[192,640]{1,0:T(8,128)(2,1)S(1)} %get-tuple-element.233), channel_id=1, source_target_pairs={{0,2},{1,3},{2,0},{3,1},{4,6},{5,7},{6,4},{7,5},{8,10},{9,11},{10,... | collective-permute-start | bytes 737288 | tf_op jit(solution)/shard_map/ppermute | solution.py:58
  227.2 18.9 %collective-permute-start.40 = (bf16[192,640]{1,0:T(8,128)(2,1)S(1)}, bf16[192,640]{1,0:T(8,128)(2,1)S(1)}, u32[]{:S(2)}, u32[]{:S(2)}) collective-permute-start(bf16[192,640]{1,0:T(8,128)(2,1)S(1)} %get-tuple-element.232), channel_id=1, source_target_pairs={{0,3},{1,2},{2,1},{3,0},{4,7},{5,6},{6,5},{7,4},{8,11},{9,10},{10,... | collective-permute-start | bytes 737288 | tf_op jit(solution)/shard_map/ppermute | solution.py:58
  230.1 26.0 %collective-permute-start.41 = (bf16[960,480]{1,0:T(8,128)(2,1)S(1)}, bf16[960,480]{1,0:T(8,128)(2,1)S(1)}, u32[]{:S(2)}, u32[]{:S(2)}) collective-permute-start(bf16[960,480]{1,0:T(8,128)(2,1)S(1)} %fusion), channel_id=1, source_target_pairs={{0,16},{4,20},{8,24},{12,28},{16,0},{20,4},{24,8},{28,12},{1,17},{... | collective-permute-start | bytes 2764808 | tf_op jit(solution)/shard_map/ppermute | solution.py:67
  254.2 14.3 %collective-permute-start.51 = (bf16[240,960]{1,0:T(8,128)(2,1)S(1)}, bf16[240,960]{1,0:T(8,128)(2,1)S(1)}, u32[]{:S(2)}, u32[]{:S(2)}) collective-permute-start(bf16[240,960]{1,0:T(8,128)(2,1)S(1)} %copy-done.21), channel_id=1, source_target_pairs={{0,16},{4,20},{8,24},{12,28},{16,0},{20,4},{24,8},{28,12},{1,17},{... | collective-permute-start | bytes 1382408 | tf_op jit(solution)/shard_map/ppermute | solution.py:67
  260.5 26.4 %collective-permute-start.44 = (bf16[336,240]{1,0:T(8,128)(2,1)S(1)}, bf16[336,240]{1,0:T(8,128)(2,1)S(1)}, u32[]{:S(2)}, u32[]{:S(2)}) collective-permute-start(bf16[336,240]{1,0:T(8,128)(2,1)S(1)} %get-tuple-element.197), channel_id=1, source_target_pairs={{0,2},{1,3},{2,0},{3,1},{4,6},{5,7},{6,4},{7,5},{8,10},{9,11},{10,... | collective-permute-start | bytes 483848 | tf_op jit(solution)/shard_map/ppermute | solution.py:58
  263.8 23.1 %collective-permute-start.43 = (bf16[336,240]{1,0:T(8,128)(2,1)S(1)}, bf16[336,240]{1,0:T(8,128)(2,1)S(1)}, u32[]{:S(2)}, u32[]{:S(2)}) collective-permute-start(bf16[336,240]{1,0:T(8,128)(2,1)S(1)} %get-tuple-element.196), channel_id=1, source_target_pairs={{0,1},{1,0},{2,3},{3,2},{4,5},{5,4},{6,7},{7,6},{8,9},{9,8},{10,11... | collective-permute-start | bytes 483848 | tf_op jit(solution)/shard_map/ppermute | solution.py:58
  264.3 32.8 %collective-permute-start.46 = (bf16[2,240,480]{2,1,0:T(8,128)(2,1)S(1)}, bf16[2,240,480]{2,1,0:T(8,128)(2,1)S(1)}, u32[]{:S(2)}, u32[]{:S(2)}) collective-permute-start(bf16[2,240,480]{2,1,0:T(8,128)(2,1)S(1)} %pad_maximum_fusion), channel_id=1, source_target_pairs={{0,2},{1,3},{2,0},{3,1},{4,6},{5,7},{6,4},{7,5},{8,10},{9,11},{10,... | collective-permute-start | bytes 1382408 | tf_op jit(solution)/shard_map/ppermute | solution.py:58
  268.5 28.8 %collective-permute-start.47 = (bf16[192,960]{1,0:T(8,128)(2,1)S(1)}, bf16[192,960]{1,0:T(8,128)(2,1)S(1)}, u32[]{:S(2)}, u32[]{:S(2)}) collective-permute-start(bf16[192,960]{1,0:T(8,128)(2,1)S(1)} %fusion.10), channel_id=1, source_target_pairs={{0,4},{4,0},{8,12},{12,8},{16,20},{20,16},{24,28},{28,24},{1,5},{5... | collective-permute-start | bytes 1105928 | tf_op jit(solution)/shard_map/ppermute | solution.py:67
  269.9 29.3 %collective-permute-start.52 = (bf16[240,960]{1,0:T(8,128)(2,1)S(1)}, bf16[240,960]{1,0:T(8,128)(2,1)S(1)}, u32[]{:S(2)}, u32[]{:S(2)}) collective-permute-start(bf16[240,960]{1,0:T(8,128)(2,1)S(1)} %collective-permute-done.51.refs_4_), channel_id=1, source_target_pairs={{0,4},{4,0},{8,12},{12,8},{16,20},{20,16},{24,28},{28,24},{1,5},{5... | collective-permute-start | bytes 1382408 | tf_op jit(solution)/shard_map/ppermute | solution.py:67
  (92 other events, 673.4 us)
Sparse Core Ops, SparseCore 0:
  9.9 35.0 all-gather.2
  75.0 45.7 all-gather.4
  168.9 47.6 reduce-scatter.1
